TPU v7x, 32 devices: a whole 2x2x4 slice. The times are simulated.
32 devices in a mesh: dp: 8 (over z, y), fsdp: 4 (over x, core).
Axes of the slice: x: 2, y: 2, z: 4, core: 2. Of those that a mesh axis runs over, the one named last changes fastest.
Arguments:
- tokens: bfloat16 [8, 2064, 1024], P('dp', 'fsdp'), may hold values from -6 to 6
- cotangent: bfloat16 [8, 2064, 1024], P('dp', 'fsdp'), may hold values from -6 to 6
- frame_counts: int32 [8, 2], P('dp'), may hold values from 0 to 8, as said below
- presence: int32 [8, 8, 2], P('dp'), may hold values 0 or 1
- attend_gain: bfloat16 [1024], P('dp'), may hold values from 0.5 to 1.5
- attend_shift: bfloat16 [1024], P('dp'), may hold values from -1.75 to 1.75
- triple_weight: bfloat16 [1024, 3072], P('fsdp', 'dp'), may hold values from -0.1875 to 0.1875
- triple_bias: bfloat16 [3072], P('dp'), may hold values from -3 to 3
- output_weight: bfloat16 [1024, 1024], P('fsdp', 'dp'), may hold values from -0.75 to 0.75
- output_bias: bfloat16 [1024], P('dp'), may hold values from -1.75 to 1.75
- second_gain: bfloat16 [1024], P('dp'), may hold values from 0.5 to 1.5
- second_shift: bfloat16 [1024], P('dp'), may hold values from -1.75 to 1.75
- expand_weight: bfloat16 [1024, 4096], P('fsdp', 'dp'), may hold values from -0.1875 to 0.1875
- expand_bias: bfloat16 [4096], P('dp'), may hold values from -3 to 3
- reduce_weight: bfloat16 [4096, 1024], P('fsdp', 'dp'), may hold values from -0.09375 to 0.09375
- reduce_bias: bfloat16 [1024], P('dp'), may hold values from -1.75 to 1.75
Outputs:
- block_output: bfloat16 [8, 2064, 1024], P('dp', 'fsdp')
- tokens_grad: float32 [8, 2064, 1024], P('dp', 'fsdp')
- attend_gain_grad: float32 [1024], P('dp')
- attend_shift_grad: float32 [1024], P('dp')
- triple_weight_grad: float32 [1024, 3072], P('fsdp', 'dp')
- triple_bias_grad: float32 [3072], P('dp')
- output_weight_grad: float32 [1024, 1024], P('fsdp', 'dp')
- output_bias_grad: float32 [1024], P('dp')
- second_gain_grad: float32 [1024], P('dp')
- second_shift_grad: float32 [1024], P('dp')
- expand_weight_grad: float32 [1024, 4096], P('fsdp', 'dp')
- expand_bias_grad: float32 [4096], P('dp')
- reduce_weight_grad: float32 [4096, 1024], P('fsdp', 'dp')
- reduce_bias_grad: float32 [1024], P('dp')
Inputs may be any that keep to these rules, and one draw needn't show every extreme that they name: `frame_counts`: column 0 is the first clip of a sequence, 4 to 8 frames, exactly 8 in sequence 0; column 1 is a second clip of 0 frames or of 4 or more, at most 8 minus column 0; frames after both clips are padding.
All inputs are finite; a program needn't handle non-finite values. No bound on the sum of `presence` on one device may be relied on, other than what follows from the above.
Results may differ from a plain program's by a relative error of at most 0.017.
Values may be sent and summed in bfloat16 or wider, within the bound.
No kernel may reach another device: no remote copies, remote signals or barrier semaphores. Data moves between devices by JAX's collectives and lax.ppermute only.
A program may use at most 256 MiB of HBM per device.

v0:
```python
import jax
import jax.numpy as jnp
from jax import lax
from jax.sharding import PartitionSpec as P

D = 1024
HEADS = 16
HEAD = 64
FF = 4096
GRID = 16


EPSILON = 1e-06
NEGATIVE = -1000000000.0


def norm_affine(values, gain, shift):
    center = values - jnp.mean(values, -1, keepdims=True)
    spread = jnp.mean(center * center, -1, keepdims=True)
    return center * lax.rsqrt(spread + EPSILON) * gain + shift


def gelu_exact(values):
    return jax.nn.gelu(values, approximate=False)


def rotary(values, cosine, sine):
    pairs = cosine.shape[-1]
    span = 6 * pairs
    leading = values.shape[:-1]
    turned_part = values[..., :span].reshape(leading + (3, 2, pairs))
    first = turned_part[..., 0, :]
    second = turned_part[..., 1, :]
    cos_b = cosine[..., None, :, :]
    sin_b = sine[..., None, :, :]
    new_first = first * cos_b - second * sin_b
    new_second = second * cos_b + first * sin_b
    turned = jnp.stack([new_first, new_second], -2).reshape(leading + (span,))
    return jnp.concatenate([turned, values[..., span:]], -1)


def row_tables(counts, present, row_frame, grid, pairs):
    frames = present.shape[0]
    frame_ids = jnp.arange(frames, dtype=jnp.int32)
    first = counts[0]
    second = counts[1]
    clip_frame = jnp.where(
        frame_ids < first, 0, jnp.where(frame_ids < first + second, 1, 2)
    ).astype(jnp.int32)
    start = jnp.where(frame_ids < first, 0, first)
    time_frame = (frame_ids - start).astype(jnp.float32)
    within = jnp.arange(row_frame, dtype=jnp.int32)
    patch = jnp.maximum(within - 2, 0)
    grid_row = jnp.where(within >= 2, patch // grid, 0).astype(jnp.float32)
    grid_col = jnp.where(within >= 2, patch % grid, 0).astype(jnp.float32)
    inclip = clip_frame < 2
    action_on = present[:, 0] == 1
    state_on = present[:, 1] == 1
    live = inclip[:, None] & (
        (within[None, :] >= 2)
        | (within[None, :] == 0) & action_on[:, None]
        | (within[None, :] == 1) & state_on[:, None]
    )
    shape = (frames, row_frame)
    clip = jnp.broadcast_to(clip_frame[:, None], shape).reshape(-1)
    times = jnp.broadcast_to(time_frame[:, None], shape).reshape(-1)
    rows_pos = jnp.broadcast_to(grid_row[None, :], shape).reshape(-1)
    cols_pos = jnp.broadcast_to(grid_col[None, :], shape).reshape(-1)
    position = jnp.stack([times, rows_pos, cols_pos], -1)
    freq = 10000.0 ** (-jnp.arange(pairs, dtype=jnp.float32) / pairs)
    angle = position[:, :, None] * freq
    return (clip, times, live.reshape(-1).astype(jnp.float32), jnp.cos(angle), jnp.sin(angle))


def over_rows(left, right):
    return lax.dot_general(
        left, right, (((0,), (0,)), ((), ())), preferred_element_type=jnp.float32
    )


def against(left, right):
    return lax.dot_general(
        left, right, (((1,), (1,)), ((), ())), preferred_element_type=jnp.float32
    )


def split_heads(array):
    return array.reshape(array.shape[0], HEADS, HEAD).transpose(1, 0, 2)


def merge_heads(array):
    return array.transpose(1, 0, 2).reshape(array.shape[1], HEADS * HEAD)


def mask_for(clip_rows, time_rows, clip_keys, time_keys, live_keys):
    return (
        (clip_rows[:, None] == clip_keys[None, :])
        & (time_keys[None, :] <= time_rows[:, None])
        & (live_keys[None, :] > 0.5)
    )


def head_forward(allowed, item):
    query, key_rows, value_rows = item
    scores = jnp.einsum("qd,kd->qk", query, key_rows, preferred_element_type=jnp.float32) * 0.125
    scores = jnp.where(allowed, scores, NEGATIVE)
    top = jnp.max(scores, -1, keepdims=True)
    weights = jnp.exp(scores - top)
    total = jnp.sum(weights, -1, keepdims=True)
    probs = (weights / total).astype(jnp.bfloat16)
    result = jnp.einsum("qk,kd->qd", probs, value_rows, preferred_element_type=jnp.float32)
    return (result, (top + jnp.log(total))[:, 0])


def head_backward(allowed, item):
    query, key_rows, value_rows, grad_rows, log_total = item
    scores = jnp.einsum("qd,kd->qk", query, key_rows, preferred_element_type=jnp.float32) * 0.125
    scores = jnp.where(allowed, scores, NEGATIVE)
    probs = jnp.exp(scores - log_total[:, None])
    inner = jnp.einsum("qd,kd->qk", grad_rows, value_rows, preferred_element_type=jnp.float32)
    center = jnp.sum(probs * inner, -1, keepdims=True)
    score_grad = (probs * (inner - center)).astype(jnp.bfloat16)
    query_grad = (
        jnp.einsum("qk,kd->qd", score_grad, key_rows, preferred_element_type=jnp.float32) * 0.125
    )
    key_grad = (
        jnp.einsum("qk,qd->kd", score_grad, query, preferred_element_type=jnp.float32) * 0.125
    )
    value_grad = jnp.einsum(
        "qk,qd->kd", probs.astype(jnp.bfloat16), grad_rows, preferred_element_type=jnp.float32
    )
    return (query_grad, key_grad, value_grad)


def sequence_forward(item):
    query, key_all, value_all, clip_rows, time_rows, clip_keys, time_keys, live_keys = item
    allowed = mask_for(clip_rows, time_rows, clip_keys, time_keys, live_keys)

    def run_head(head_item):
        return head_forward(allowed, head_item)

    result, log_total = lax.map(
        run_head, (split_heads(query), split_heads(key_all), split_heads(value_all))
    )
    return (merge_heads(result), log_total)


def sequence_backward(item):
    (
        query,
        key_all,
        value_all,
        grad_rows,
        log_total,
        clip_rows,
        time_rows,
        clip_keys,
        time_keys,
        live_keys,
    ) = item
    allowed = mask_for(clip_rows, time_rows, clip_keys, time_keys, live_keys)

    def run_head(head_item):
        return head_backward(allowed, head_item)

    query_grad, key_grad, value_grad = lax.map(
        run_head,
        (
            split_heads(query),
            split_heads(key_all),
            split_heads(value_all),
            split_heads(grad_rows),
            log_total,
        ),
    )
    return (merge_heads(query_grad), merge_heads(key_grad), merge_heads(value_grad))


def shards(
    tokens,
    cotangent,
    frame_counts,
    presence,
    attend_gain,
    attend_shift,
    triple_weight,
    triple_bias,
    output_weight,
    output_bias,
    second_gain,
    second_shift,
    expand_weight,
    expand_bias,
    reduce_weight,
    reduce_bias,
):
    seq_count = tokens.shape[0]
    local_rows = tokens.shape[1]
    flat_rows = seq_count * local_rows
    shard_index = lax.axis_index("fsdp")
    row_frame = GRID * GRID + 2
    pairs = HEAD // 3 // 2
    triple_full, output_full, expand_full, reduce_full = (
        lax.all_gather(triple_weight, "fsdp", axis=0, tiled=True),
        lax.all_gather(output_weight, "fsdp", axis=0, tiled=True),
        lax.all_gather(expand_weight, "fsdp", axis=0, tiled=True),
        lax.all_gather(reduce_weight, "fsdp", axis=0, tiled=True),
    )
    (
        triple_full,
        output_full,
        expand_full,
        reduce_full,
        norm_gain_one,
        norm_shift_one,
        triple_add,
        output_add,
        norm_gain_two,
        norm_shift_two,
        expand_add,
        reduce_add,
    ) = (
        lax.all_gather(triple_full, "dp", axis=1, tiled=True),
        lax.all_gather(output_full, "dp", axis=1, tiled=True),
        lax.all_gather(expand_full, "dp", axis=1, tiled=True),
        lax.all_gather(reduce_full, "dp", axis=1, tiled=True),
        lax.all_gather(attend_gain, "dp", axis=0, tiled=True),
        lax.all_gather(attend_shift, "dp", axis=0, tiled=True),
        lax.all_gather(triple_bias, "dp", axis=0, tiled=True),
        lax.all_gather(output_bias, "dp", axis=0, tiled=True),
        lax.all_gather(second_gain, "dp", axis=0, tiled=True),
        lax.all_gather(second_shift, "dp", axis=0, tiled=True),
        lax.all_gather(expand_bias, "dp", axis=0, tiled=True),
        lax.all_gather(reduce_bias, "dp", axis=0, tiled=True),
    )
    gain_one = norm_gain_one.astype(jnp.float32)
    shift_one = norm_shift_one.astype(jnp.float32)
    gain_two = norm_gain_two.astype(jnp.float32)
    shift_two = norm_shift_two.astype(jnp.float32)
    clip_all, time_all, live_all, cosine_all, sine_all = jax.vmap(
        lambda counts, present: row_tables(counts, present, row_frame, GRID, pairs)
    )(frame_counts, presence)
    offset = shard_index * local_rows

    def local_part(array):
        return lax.dynamic_slice_in_dim(array, offset, local_rows, 1)

    clip_rows = local_part(clip_all)
    time_rows = local_part(time_all)
    live_rows = local_part(live_all)
    cosine = local_part(cosine_all)
    sine = local_part(sine_all)
    mask_col = live_rows[..., None]
    entered = tokens.astype(jnp.float32) * mask_col
    normed_low = norm_affine(entered, gain_one, shift_one).astype(jnp.bfloat16)
    triple = jnp.dot(
        normed_low, triple_full, preferred_element_type=jnp.float32
    ) + triple_add.astype(jnp.float32)
    head_shape = (seq_count, local_rows, HEADS, HEAD)
    query = (
        rotary(triple[..., :D].reshape(head_shape), cosine, sine)
        .reshape(seq_count, local_rows, D)
        .astype(jnp.bfloat16)
    )
    keys_low = (
        rotary(triple[..., D : 2 * D].reshape(head_shape), cosine, sine)
        .reshape(seq_count, local_rows, D)
        .astype(jnp.bfloat16)
    )
    value_low = triple[..., 2 * D :].astype(jnp.bfloat16)
    key_all, value_all = (
        lax.all_gather(keys_low, "fsdp", axis=1, tiled=True),
        lax.all_gather(value_low, "fsdp", axis=1, tiled=True),
    )
    attended, log_total = lax.map(
        sequence_forward,
        (query, key_all, value_all, clip_rows, time_rows, clip_all, time_all, live_all),
    )
    mixed_low = attended.astype(jnp.bfloat16)
    middle = (
        entered
        + jnp.dot(mixed_low, output_full, preferred_element_type=jnp.float32)
        + output_add.astype(jnp.float32)
    )
    second_low = norm_affine(middle, gain_two, shift_two).astype(jnp.bfloat16)
    hidden = jnp.dot(
        second_low, expand_full, preferred_element_type=jnp.float32
    ) + expand_add.astype(jnp.float32)
    active_low = gelu_exact(hidden).astype(jnp.bfloat16)
    final = jnp.dot(
        active_low, reduce_full, preferred_element_type=jnp.float32
    ) + reduce_add.astype(jnp.float32)
    block_output = ((middle + final) * mask_col).astype(jnp.bfloat16)
    triple_full, output_full, expand_full, reduce_full = (
        lax.all_gather(triple_weight, "fsdp", axis=0, tiled=True),
        lax.all_gather(output_weight, "fsdp", axis=0, tiled=True),
        lax.all_gather(expand_weight, "fsdp", axis=0, tiled=True),
        lax.all_gather(reduce_weight, "fsdp", axis=0, tiled=True),
    )
    triple_full, output_full, expand_full, reduce_full, norm_gain_one, norm_gain_two = (
        lax.all_gather(triple_full, "dp", axis=1, tiled=True),
        lax.all_gather(output_full, "dp", axis=1, tiled=True),
        lax.all_gather(expand_full, "dp", axis=1, tiled=True),
        lax.all_gather(reduce_full, "dp", axis=1, tiled=True),
        lax.all_gather(attend_gain, "dp", axis=0, tiled=True),
        lax.all_gather(second_gain, "dp", axis=0, tiled=True),
    )
    gain_one = norm_gain_one.astype(jnp.float32)
    gain_two = norm_gain_two.astype(jnp.float32)
    outer = (cotangent.astype(jnp.float32) * mask_col).reshape(flat_rows, D)
    outer_low = outer.astype(jnp.bfloat16)
    reduce_weight_grad = over_rows(active_low.reshape(flat_rows, FF), outer_low)
    reduce_bias_grad = jnp.sum(outer_low.astype(jnp.float32), 0)
    active_grad = against(outer_low, reduce_full)
    gelu_value, gelu_pull = jax.vjp(gelu_exact, hidden.reshape(flat_rows, FF))
    hidden_grad = gelu_pull(active_grad)[0].astype(jnp.bfloat16)
    expand_weight_grad = over_rows(second_low.reshape(flat_rows, D), hidden_grad)
    expand_bias_grad = jnp.sum(hidden_grad.astype(jnp.float32), 0)
    second_grad = against(hidden_grad, expand_full)
    norm_value, second_pull = jax.vjp(
        norm_affine, middle.reshape(flat_rows, D), gain_two, shift_two
    )
    middle_norm, second_gain_grad, second_shift_grad = second_pull(second_grad)
    middle_grad = outer + middle_norm
    branch_low = middle_grad.astype(jnp.bfloat16)
    output_weight_grad = over_rows(mixed_low.reshape(flat_rows, D), branch_low)
    output_bias_grad = jnp.sum(branch_low.astype(jnp.float32), 0)
    mixed_grad = (
        against(branch_low, output_full).astype(jnp.bfloat16).reshape(seq_count, local_rows, D)
    )
    query_grad, key_part, value_part = lax.map(
        sequence_backward,
        (
            query,
            key_all,
            value_all,
            mixed_grad,
            log_total,
            clip_rows,
            time_rows,
            clip_all,
            time_all,
            live_all,
        ),
    )
    key_grad, value_grad = (
        lax.psum_scatter(
            key_part.astype(jnp.bfloat16), "fsdp", scatter_dimension=1, tiled=True
        ).astype(jnp.float32),
        lax.psum_scatter(
            value_part.astype(jnp.bfloat16), "fsdp", scatter_dimension=1, tiled=True
        ).astype(jnp.float32),
    )
    query_back = rotary(query_grad.reshape(head_shape), cosine, -sine).reshape(
        seq_count, local_rows, D
    )
    key_back = rotary(key_grad.reshape(head_shape), cosine, -sine).reshape(seq_count, local_rows, D)
    triple_grad = (
        jnp.concatenate([query_back, key_back, value_grad], -1)
        .astype(jnp.bfloat16)
        .reshape(flat_rows, 3 * D)
    )
    triple_weight_grad = over_rows(normed_low.reshape(flat_rows, D), triple_grad)
    triple_bias_grad = jnp.sum(triple_grad.astype(jnp.float32), 0)
    normed_grad = against(triple_grad, triple_full)
    first_value, first_pull = jax.vjp(
        norm_affine, entered.reshape(flat_rows, D), gain_one, shift_one
    )
    entered_norm, attend_gain_grad, attend_shift_grad = first_pull(normed_grad)
    tokens_grad = ((middle_grad + entered_norm) * mask_col.reshape(flat_rows, 1)).reshape(
        seq_count, local_rows, D
    )
    (
        triple_weight_grad,
        output_weight_grad,
        expand_weight_grad,
        reduce_weight_grad,
        attend_gain_grad,
        attend_shift_grad,
        triple_bias_grad,
        output_bias_grad,
        second_gain_grad,
        second_shift_grad,
        expand_bias_grad,
        reduce_bias_grad,
    ) = (
        lax.psum_scatter(
            triple_weight_grad.astype(jnp.bfloat16), "dp", scatter_dimension=1, tiled=True
        ).astype(jnp.float32),
        lax.psum_scatter(
            output_weight_grad.astype(jnp.bfloat16), "dp", scatter_dimension=1, tiled=True
        ).astype(jnp.float32),
        lax.psum_scatter(
            expand_weight_grad.astype(jnp.bfloat16), "dp", scatter_dimension=1, tiled=True
        ).astype(jnp.float32),
        lax.psum_scatter(
            reduce_weight_grad.astype(jnp.bfloat16), "dp", scatter_dimension=1, tiled=True
        ).astype(jnp.float32),
        lax.psum_scatter(
            attend_gain_grad.astype(jnp.bfloat16), "dp", scatter_dimension=0, tiled=True
        ).astype(jnp.float32),
        lax.psum_scatter(
            attend_shift_grad.astype(jnp.bfloat16), "dp", scatter_dimension=0, tiled=True
        ).astype(jnp.float32),
        lax.psum_scatter(
            triple_bias_grad.astype(jnp.bfloat16), "dp", scatter_dimension=0, tiled=True
        ).astype(jnp.float32),
        lax.psum_scatter(
            output_bias_grad.astype(jnp.bfloat16), "dp", scatter_dimension=0, tiled=True
        ).astype(jnp.float32),
        lax.psum_scatter(
            second_gain_grad.astype(jnp.bfloat16), "dp", scatter_dimension=0, tiled=True
        ).astype(jnp.float32),
        lax.psum_scatter(
            second_shift_grad.astype(jnp.bfloat16), "dp", scatter_dimension=0, tiled=True
        ).astype(jnp.float32),
        lax.psum_scatter(
            expand_bias_grad.astype(jnp.bfloat16), "dp", scatter_dimension=0, tiled=True
        ).astype(jnp.float32),
        lax.psum_scatter(
            reduce_bias_grad.astype(jnp.bfloat16), "dp", scatter_dimension=0, tiled=True
        ).astype(jnp.float32),
    )
    triple_weight_grad, output_weight_grad, expand_weight_grad, reduce_weight_grad = (
        lax.psum_scatter(
            triple_weight_grad.astype(jnp.bfloat16), "fsdp", scatter_dimension=0, tiled=True
        ).astype(jnp.float32),
        lax.psum_scatter(
            output_weight_grad.astype(jnp.bfloat16), "fsdp", scatter_dimension=0, tiled=True
        ).astype(jnp.float32),
        lax.psum_scatter(
            expand_weight_grad.astype(jnp.bfloat16), "fsdp", scatter_dimension=0, tiled=True
        ).astype(jnp.float32),
        lax.psum_scatter(
            reduce_weight_grad.astype(jnp.bfloat16), "fsdp", scatter_dimension=0, tiled=True
        ).astype(jnp.float32),
    )
    (
        attend_gain_grad,
        attend_shift_grad,
        triple_bias_grad,
        output_bias_grad,
        second_gain_grad,
        second_shift_grad,
        expand_bias_grad,
        reduce_bias_grad,
    ) = lax.psum(
        (
            attend_gain_grad,
            attend_shift_grad,
            triple_bias_grad,
            output_bias_grad,
            second_gain_grad,
            second_shift_grad,
            expand_bias_grad,
            reduce_bias_grad,
        ),
        "fsdp",
    )
    return (
        block_output,
        tokens_grad,
        attend_gain_grad,
        attend_shift_grad,
        triple_weight_grad,
        triple_bias_grad,
        output_weight_grad,
        output_bias_grad,
        second_gain_grad,
        second_shift_grad,
        expand_weight_grad,
        expand_bias_grad,
        reduce_weight_grad,
        reduce_bias_grad,
    )


def solution(mesh):
    placed = (
        P("dp", "fsdp", None),
        P("dp", "fsdp", None),
        P("dp", None),
        P("dp", None, None),
        P("dp"),
        P("dp"),
        P("fsdp", "dp"),
        P("dp"),
        P("fsdp", "dp"),
        P("dp"),
        P("dp"),
        P("dp"),
        P("fsdp", "dp"),
        P("dp"),
        P("fsdp", "dp"),
        P("dp"),
    )
    return jax.shard_map(
        shards,
        mesh=mesh,
        in_specs=placed,
        out_specs=(
            P("dp", "fsdp", None),
            P("dp", "fsdp", None),
            P("dp"),
            P("dp"),
            P("fsdp", "dp"),
            P("dp"),
            P("fsdp", "dp"),
            P("dp"),
            P("dp"),
            P("dp"),
            P("fsdp", "dp"),
            P("dp"),
            P("fsdp", "dp"),
            P("dp"),
        ),
        check_vma=False,
    )
```

profile of v0, /device:TPU:0, one launch (start us, length us, event | category | flops | bytes accessed | tf_op | source)
XLA Modules:
  0.0 1703.3 jit_solution(5392114978707453176)
XLA Ops:
  7.3 11.8 all_gather.66
  25.9 20.9 %all-gather = bf16[8,1,128]{2,1,0:T(2,128)(2,1)S(1)} all-gather(bf16[1,1,128]{2,1,0:T(2,128)(2,1)S(1)} %bitcast.316), channel_id=1, replica_groups=mesh['dp'=8,'fsdp'=4] {'dp'}, dimensions={0}, use_global_device_ids=true | all-gather | bytes 2304 | tf_op jit(solution)/shard_map/all_gather | solution.py:227
  46.8 16.2 all-gather.1
  63.0 28.0 %all-gather.2 = bf16[8,1,384]{2,1,0:T(2,128)(2,1)S(1)} all-gather(bf16[1,1,384]{2,1,0:T(2,128)(2,1)S(1)} %reshape.834), channel_id=1, replica_groups=mesh['dp'=8,'fsdp'=4] {'dp'}, dimensions={0}, use_global_device_ids=true | all-gather | bytes 6912 | tf_op jit(solution)/shard_map/all_gather | solution.py:229
  92.8 27.0 %all-gather.17.cloned.1.call-done = bf16[1024,3072]{1,0:T(8,128)(2,1)} async-done(((bf16[1024,384]{1,0:T(8,128)(2,1)}), bf16[1024,3072]{1,0:T(8,128)(2,1)}) %all-gather.17.cloned.1.call-update) | async-done | bytes 6291472 | tf_op jit(solution)/shard_map/all_gather | solution.py:223
  163.2 17.7 %all-gather.3 = bf16[8,1,128]{2,1,0:T(2,128)(2,1)S(1)} all-gather(bf16[1,1,128]{2,1,0:T(2,128)(2,1)S(1)} %bitcast.318), channel_id=1, replica_groups=mesh['dp'=8,'fsdp'=4] {'dp'}, dimensions={0}, use_global_device_ids=true | all-gather | bytes 2304 | tf_op jit(solution)/shard_map/all_gather | solution.py:230
  180.9 16.6 all-gather.4
  197.5 26.0 %all-gather.6 = bf16[8,1,512]{2,1,0:T(2,128)(2,1)S(1)} all-gather(bf16[1,1,512]{2,1,0:T(2,128)(2,1)S(1)} %reshape.842), channel_id=1, replica_groups=mesh['dp'=8,'fsdp'=4] {'dp'}, dimensions={0}, use_global_device_ids=true | all-gather | bytes 9216 | tf_op jit(solution)/shard_map/all_gather | solution.py:233
  223.5 16.2 all-gather.5
  244.3 20.8 %copy.112 = bf16[1,2064,1024]{1,2,0:T(8,128)(2,1)} copy(bf16[1,2064,1024]{2,0,1:T(2,128)(2,1)} %all-gather.19.cloned.1.call-done) | data formatting | bytes 8454144 | tf_op jit(solution)/shard_map/all_gather | solution.py:272
  265.1 9.0 copy.116
  275.4 20.8 %copy.114 = bf16[1,2064,1024]{1,2,0:T(8,128)(2,1)} copy(bf16[1,2064,1024]{2,0,1:T(2,128)(2,1)} %all-gather.21.cloned.1.call-done) | data formatting | bytes 8454144 | tf_op jit(solution)/shard_map/all_gather | solution.py:273
  296.2 9.2 copy.117
  305.4 134.7 %while.48 = (s32[]{:T(128)}, bf16[16,516,64]{1,2,0:T(8,128)(2,1)S(1)}, f32[16,516]{1,0:T(8,128)S(1)}, bf16[16,516,64]{2,1,0:T(8,128)(2,1)}, bf16[16,2064,64]{2,1...) while((s32[]{:T(128)}, ...), condition=%wide.region_5.6_spmd.clone, body=%wide.region_2.5_spmd.clone.sunk | while | flops 285425920 | bytes 31494124 | solution.py:142
  454.1 28.9 %multiply_convert_fusion.1 = (bf16[516,4096]{1,0:T(8,128)(2,1)}, f32[516,4096]{1,0:T(8,128)}, f32[516,4096]{1,0:T(8,128)}) fusion(f32[4096]{0:T(1024)S(1)} %bitcast.299, bf16[1024,4096]{1,0:T(8,128)(2,1)} %all-gather.27.cloned.1.call-done, f32[1,516,1024]{2,1,0:T(8,128)S(1)} %get-tuple-element.531, f32[1024]{0:T(1024)S(1)} %bitcast.312, ...), kind=kOutput, calls=%fused_computation.57 | convolution fusion | flops 4470657024 | bytes 31666208 | tf_op jit(solution)/shard_map/dot_general | solution.py:286
  483.0 96.7 %all-gather.31.cloned.1.call-done = bf16[4096,1024]{1,0:T(8,128)(2,1)} async-done(((bf16[4096,128]{1,0:T(8,128)(2,1)}), bf16[4096,1024]{1,0:T(8,128)(2,1)}) %all-gather.31.cloned.1.call-update) | async-done | bytes 8388624 | tf_op jit(solution)/shard_map/all_gather | solution.py:226
  579.7 14.5 fusion.98
  594.2 10.5 multiply_reduce_fusion.1
  612.0 323.7 %while.49 = (s32[]{:T(128)}, f32[16,516,64]{1,0,2:T(8,128)}, bf16[16,2064,64]{1,2,0:T(8,128)(2,1)}, bf16[16,2064,64]{1,2,0:T(8,128)(2,1)}, bf16[16,516,64]{2,1,0...) while((s32[]{:T(128)}, f32[16,516,64]{1,0,2:T(8,128)}, ...), condition=%wide.region_13.14_spmd.clone, body=%wide.region_11.13_spmd.clone.sunk | while | flops 695625280 | bytes 61538928 | solution.py:166
  951.1 144.7 %all-reduce.15.cloned.1.call-done = (bf16[1,2064,1024]{1,2,0:T(8,128)(2,1)}, bf16[1,2064,1024]{1,2,0:T(8,128)(2,1)}) async-done(((bf16[1,2064,1024]{1,2,0:T(8,128)(2,1)}, bf16[1,2064,1024]{1,2,0:T(8,128)(2,1)}), (bf16[1,2064,1024]{1,2,0:T(8,128)(2,1)}, bf16[1,2064,1024]{1,2,0:T(8,128)(2,1)})) %all-reduce.15.cloned.1.call-update) | async-done | bytes 8454160
  1106.0 10.9 convolution_convert_fusion.2
  1125.9 11.6 convolution_convert_fusion.1
  1137.5 11.2 convolution_convert_fusion
  1148.7 11.7 copy.137
  1169.0 118.8 %reduce-scatter.27.cloned.1.call-done = bf16[384,1024]{1,0:T(8,128)(2,1)} async-done(((bf16[3072,1024]{1,0:T(8,128)(2,1)}), bf16[384,1024]{1,0:T(8,128)(2,1)}) %reduce-scatter.27.cloned.1.call-update) | async-done | bytes 786448
  1292.7 18.8 %all-gather.7 = bf16[8,1,128]{2,1,0:T(2,128)(2,1)S(1)} all-gather(bf16[1,1,128]{2,1,0:T(2,128)(2,1)S(1)} %bitcast.321), channel_id=1, replica_groups=mesh['dp'=8,'fsdp'=4] {'dp'}, dimensions={0}, use_global_device_ids=true | all-gather | bytes 2304 | tf_op jit(solution)/shard_map/all_gather | solution.py:234
  1312.0 127.9 %reduce-scatter.21.cloned.1.call-done = bf16[1024,512]{1,0:T(8,128)(2,1)} async-done(((bf16[1024,4096]{1,0:T(8,128)(2,1)}), bf16[1024,512]{1,0:T(8,128)(2,1)}) %reduce-scatter.21.cloned.1.call-update) | async-done | bytes 1048592 | tf_op jit(solution)/shard_map/reduce_scatter | solution.py:393
  1440.2 10.4 fusion.52
  1458.3 133.6 %reduce-scatter.31.cloned.1.call-done = bf16[128,4096]{1,0:T(8,128)(2,1)} async-done(((bf16[1024,4096]{1,0:T(8,128)(2,1)}), bf16[128,4096]{1,0:T(8,128)(2,1)}) %reduce-scatter.31.cloned.1.call-update) | async-done | bytes 1048592
  1604.7 35.2 %all-reduce.11 = (bf16[1024]{0:T(1024)(128)(2,1)S(1)}, bf16[1024]{0:T(1024)(128)(2,1)S(1)}, bf16[3072]{0:T(1024)(128)(2,1)S(1)}, bf16[1024]{0:T(1024)(128)(2,1)S...) all-reduce(bf16[1024]{0:T(1024)(128)(2,1)S(1)} %get-tuple-element.4, ...), channel_id=4, replica_groups=mesh['dp'=8,'fsdp'=4] {'dp'}, use_global_device_ids=true, to_apply=%region_20.21.clone | all-reduce | flops 13312 | bytes 53248
  1650.0 17.0 reduce-scatter.23.cloned.1.call-done
  1668.8 25.7 %reduce-scatter.25.cloned.1.call-done = bf16[1024,128]{1,0:T(8,128)(2,1)} async-done(((bf16[4096,128]{1,0:T(8,128)(2,1)}), bf16[1024,128]{1,0:T(8,128)(2,1)}) %reduce-scatter.25.cloned.1.call-update) | async-done | bytes 262160 | tf_op jit(solution)/shard_map/reduce_scatter | solution.py:434
  (664 shorter events, 614.0 us)
Async XLA Ops:
  7.2 18.7 %copy-start.48 = (bf16[128]{0:T(256)(128)(2,1)S(1)}, bf16[128]{0:T(256)(128)(2,1)}, u32[]{:S(2)}) copy-start(bf16[128]{0:T(256)(128)(2,1)} %param.24) | copy-start | bytes 772
  7.2 39.6 %copy-start.49 = (bf16[128]{0:T(256)(128)(2,1)S(1)}, bf16[128]{0:T(256)(128)(2,1)}, u32[]{:S(2)}) copy-start(bf16[128]{0:T(256)(128)(2,1)} %param.25) | copy-start | bytes 772
  7.2 55.8 %copy-start.47 = (bf16[384]{0:T(512)(128)(2,1)S(1)}, bf16[384]{0:T(512)(128)(2,1)}, u32[]{:S(2)}) copy-start(bf16[384]{0:T(512)(128)(2,1)} %param.27) | copy-start | bytes 2308
  7.2 112.5 %all-gather.17.cloned.1.call-start = ((), (), s32[]{:S(2)}) async-start(), calls=%async_computation.8 | async-start | bytes 7077888 | tf_op jit(solution)/shard_map/all_gather | solution.py:223
  19.1 142.2 %all-gather.25.cloned.1.call-start = ((), (), s32[]{:S(2)}) async-start(), calls=%async_computation.12 | async-start | bytes 1310720 | tf_op jit(solution)/shard_map/all_gather | solution.py:206
  19.8 220.1 %all-gather.29.cloned.1.call-start = ((), (), s32[]{:S(2)}) async-start(), calls=%async_computation.14 | async-start | bytes 1310720 | tf_op jit(solution)/shard_map/all_gather | solution.py:207
  20.6 223.7 %all-gather.19.cloned.1.call-start = ((), (), s32[]{:S(2)}) async-start(), calls=%async_computation.9 | async-start | bytes 10567680 | tf_op jit(solution)/shard_map/all_gather | solution.py:272
  25.4 94.4 %copy-start.29 = (f32[516]{0:T(1024)}, f32[516]{0:T(1024)S(1)}, u32[]{:S(2)}) copy-start(f32[516]{0:T(1024)S(1)} %broadcast_multiply_fusion.2) | copy-start | bytes 6196
  25.9 93.9 %copy-start.38 = (f32[516]{0:T(1024)}, f32[516]{0:T(1024)S(1)}, u32[]{:S(2)}) copy-start(f32[516]{0:T(1024)S(1)} %add_rsqrt_fusion.1) | copy-start | bytes 6196
  46.8 73.0 %copy-start.33 = (f32[8,1,128]{2,1,0:T(1,128)}, f32[8,1,128]{2,1,0:T(1,128)S(1)}, u32[]{:S(2)}) copy-start(f32[8,1,128]{2,1,0:T(1,128)S(1)} %convert_element_type.315) | copy-start | bytes 12292
  63.0 56.8 %copy-start.40 = (f32[8,1,128]{2,1,0:T(1,128)}, f32[8,1,128]{2,1,0:T(1,128)S(1)}, u32[]{:S(2)}) copy-start(f32[8,1,128]{2,1,0:T(1,128)S(1)} %convert_element_type.316) | copy-start | bytes 12292
  92.8 50.8 %copy-start.23 = (f32[516,3,10]{0,2,1:T(8,128)}, f32[516,3,10]{0,2,1:T(8,128)S(1)}, u32[]{:S(2)}) copy-start(f32[516,3,10]{0,2,1:T(8,128)S(1)} %get-tuple-element.521) | copy-start | bytes 185764
  149.8 125.6 %all-gather.21.cloned.1.call-start = ((), (), s32[]{:S(2)}) async-start(), calls=%async_computation.10 | async-start | bytes 10567680 | tf_op jit(solution)/shard_map/all_gather | solution.py:273
  154.8 26.1 %copy-start.51 = (bf16[128]{0:T(256)(128)(2,1)S(1)}, bf16[128]{0:T(256)(128)(2,1)}, u32[]{:S(2)}) copy-start(bf16[128]{0:T(256)(128)(2,1)} %param.30) | copy-start | bytes 772
  154.8 42.7 %copy-start.45 = (bf16[512]{0:T(512)(128)(2,1)S(1)}, bf16[512]{0:T(512)(128)(2,1)}, u32[]{:S(2)}) copy-start(bf16[512]{0:T(512)(128)(2,1)} %param.33) | copy-start | bytes 3076
  154.8 68.8 %copy-start.52 = (bf16[128]{0:T(256)(128)(2,1)S(1)}, bf16[128]{0:T(256)(128)(2,1)}, u32[]{:S(2)}) copy-start(bf16[128]{0:T(256)(128)(2,1)} %param.31) | copy-start | bytes 772
  154.8 86.2 %copy-start.22 = (bf16[1,516,16,3,1,10]{1,2,5,4,3,0:T(8,128)(2,1)S(1)}, bf16[1,516,16,3,1,10]{1,2,5,4,3,0:T(8,128)(2,1)}, u32[]{:S(2)}) copy-start(bf16[1,516,16,3,1,10]{1,2,5,4,3,0:T(8,128)(2,1)} %get-tuple-element.525) | copy-start | bytes 1486084
  154.8 285.2 %all-gather.23.cloned.1.call-start = ((), (), s32[]{:S(2)}) async-start(), calls=%async_computation.11 | async-start | bytes 2359296 | tf_op jit(solution)/shard_map/all_gather | solution.py:224
  161.3 292.8 %all-gather.27.cloned.1.call-start = ((), (), s32[]{:S(2)}) async-start(), calls=%async_computation.13 | async-start | bytes 9437184 | tf_op jit(solution)/shard_map/all_gather | solution.py:225
  162.0 417.7 %all-gather.31.cloned.1.call-start = ((), (), s32[]{:S(2)}) async-start(), calls=%async_computation.15 | async-start | bytes 9437184 | tf_op jit(solution)/shard_map/all_gather | solution.py:226
  239.9 855.8 %all-reduce.15.cloned.1.call-start = ((), (), s32[]{:S(2)}) async-start(), calls=%async_computation.24 | async-start | bytes 17825792
  454.1 125.7 %copy-start.18 = (bf16[1,516,1024]{2,1,0:T(8,128)(2,1)S(1)}, bf16[1,516,1024]{2,1,0:T(8,128)(2,1)}, u32[]{:S(2)}) copy-start(bf16[1,516,1024]{2,1,0:T(8,128)(2,1)} %param.21) | copy-start | bytes 3170308
  935.8 231.4 %reduce-scatter.29.cloned.1.call-start = ((), (), s32[]{:S(2)}) async-start(), calls=%async_computation.22 | async-start | bytes 2359296
  945.4 342.3 %reduce-scatter.27.cloned.1.call-start = ((), (), s32[]{:S(2)}) async-start(), calls=%async_computation.21 | async-start | bytes 7077888
  1125.6 314.3 %reduce-scatter.21.cloned.1.call-start = ((), (), s32[]{:S(2)}) async-start(), calls=%async_computation.18 | async-start | bytes 9437184 | tf_op jit(solution)/shard_map/reduce_scatter | solution.py:393
  1137.4 454.5 %reduce-scatter.31.cloned.1.call-start = ((), (), s32[]{:S(2)}) async-start(), calls=%async_computation.23 | async-start | bytes 9437184
  1160.4 129.7 %copy-start.57 = (u32[32]{0:T(128)S(1)}, u32[32]{0:T(128)}, u32[]{:S(2)}) copy-start(u32[32]{0:T(128)} %constant.290) | copy-start | bytes 388
  1160.4 132.2 %copy-start.53 = (bf16[128]{0:T(256)(128)(2,1)S(1)}, bf16[128]{0:T(256)(128)(2,1)}, u32[]{:S(2)}) copy-start(bf16[128]{0:T(256)(128)(2,1)} %param.35) | copy-start | bytes 772
  1160.5 486.3 %reduce-scatter.19.cloned.1.call-start = ((), (), s32[]{:S(2)}) async-start(), calls=%async_computation.17 | async-start | bytes 327680 | tf_op jit(solution)/shard_map/reduce_scatter | solution.py:428
  1168.9 479.4 %reduce-scatter.17.cloned.1.call-start = ((), (), s32[]{:S(2)}) async-start(), calls=%async_computation.16 | async-start | bytes 983040 | tf_op jit(solution)/shard_map/reduce_scatter | solution.py:425
  1290.1 377.0 %reduce-scatter.23.cloned.1.call-start = ((), (), s32[]{:S(2)}) async-start(), calls=%async_computation.19 | async-start | bytes 1310720 | tf_op jit(solution)/shard_map/reduce_scatter | solution.py:431
  1439.9 254.6 %reduce-scatter.25.cloned.1.call-start = ((), (), s32[]{:S(2)}) async-start(), calls=%async_computation.20 | async-start | bytes 1310720 | tf_op jit(solution)/shard_map/reduce_scatter | solution.py:434
  (105 other events, 359.3 us)
Sparse Core Ops, SparseCore 0:
  19.2 100.5 all-gather.16
  121.3 14.8 all-gather.24
  137.8 16.7 all-gather.28
  156.6 58.6 all-gather.18
  216.7 58.6 all-gather.20
  277.3 51.0 all-gather.22
  330.5 123.5 all-gather.26
  456.1 123.5 all-gather.30
  935.9 159.8 all-reduce.14
  1099.2 67.9 reduce-scatter.28
  1170.7 116.9 reduce-scatter.26
  1291.2 148.5 reduce-scatter.20
  1443.9 147.9 reduce-scatter.30
  1594.8 19.0 reduce-scatter.18
  1616.4 23.2 reduce-scatter.16
  1642.1 24.8 reduce-scatter.22
  1669.6 24.8 reduce-scatter.24
where the time goes:
time: 1720 us; the launch traced here: 1700 us
  waiting for transfers between devices  710 us (41%)
  matrix products  437 us (25%)
  local copies, waits for them, and re-layouts  264 us (15%)
  blocking collectives  220 us (13%)
  other arithmetic  49.3 us (3%)
  between operations  19.5 us (1%)
    unnamed x21, waiting for transfers between devices  406 us
    reduce_scatter x1, waiting for transfers between devices, shards(): lax.psum_scatter(expand_weight_grad.astype(jnp.bfloat16), 'dp', scatter_d...  128 us
    all_gather x1, waiting for transfers between devices, shards(): lax.all_gather(reduce_full, 'dp', axis=1, tiled=True)  96.7 us
    dynamic_update_slice x48, local copies, waits for them, and re-layouts, sequence_forward(): lax.map(run_head, (split_heads(query), split_heads(key_all), split_heads(...  74 us
    unnamed x128, local copies, waits for them, and re-layouts  67.8 us
    dot_general x16, matrix products, head_backward(): jnp.einsum('qk,qd->kd', probs.astype(jnp.bfloat16), grad_rows, preferred_...  58.2 us
    dot_general x16, matrix products, head_forward(): jnp.einsum('qk,kd->qd', probs, value_rows, preferred_element_type=jnp.flo...  55.6 us
    dot_general x16, matrix products, head_backward(): jnp.einsum('qd,kd->qk', query, key_rows, preferred_element_type=jnp.float32)  55 us
  transfers between devices with their start and end apart: 17, of which 11 were waited for; matrix products, arithmetic and copies ran while one was open for 21% of the time, Pallas kernels for 0%

commit v1 on v0

v1 whole, which is shorter than its diff:
```python
import functools
import math

import jax
import jax.numpy as jnp
import numpy as np
from jax import lax
from jax.experimental import pallas as pl
from jax.experimental.pallas import tpu as pltpu
from jax.sharding import PartitionSpec as P

D = 1024
HEADS = 16
HEAD = 64
FF = 4096
GRID = 16
PATCHES = GRID * GRID
ROW_FRAME = PATCHES + 2
PAIRS = HEAD // 3 // 2
EXTRA = 16

EPSILON = 1e-06
SCALE2 = 0.125 * math.log2(math.e)
MASKED = -8e9
FAR = 1 << 20
VMEM = 60 * 1024 * 1024
BF = jnp.bfloat16
F32 = jnp.float32


def nn(left, right):
    return lax.dot_general(left, right, (((1,), (0,)), ((), ())), preferred_element_type=F32)


def nt(left, right):
    return lax.dot_general(left, right, (((1,), (1,)), ((), ())), preferred_element_type=F32)


def tn(left, right):
    return lax.dot_general(left, right, (((0,), (0,)), ((), ())), preferred_element_type=F32)


def qkv_kernel(normed, weight, bias, turn, cosine, sine, q_out, k_out, v_out, turned, turned_bias):
    width = q_out.shape[-1]
    half = width // 2

    @pl.when(pl.program_id(0) == 0)
    def _():
        for part in range(2):
            span = slice(part * width, (part + 1) * width)
            turned[:, span] = nn(weight[:, span], turn[...]).astype(BF)
            turned_bias[:, span] = nn(bias[:, span], turn[...])

    rows = normed[0]
    cos = cosine[0]
    sin = sine[0]
    for part, out in ((0, q_out), (1, k_out)):
        span = slice(part * width, (part + 1) * width)
        value = nn(rows, turned[:, span]) + turned_bias[:1, span]
        first = value[:, :half]
        second = value[:, half:]
        out[0, :, :half] = (first * cos - second * sin).astype(BF)
        out[0, :, half:] = (second * cos + first * sin).astype(BF)
    span = slice(2 * width, 3 * width)
    v_out[0] = (nn(rows, weight[:, span]) + bias[:1, span].astype(F32)).astype(BF)


def qkv_call(normed, weight, bias, turn, cosine, sine):
    sources, rows, _ = normed.shape
    width = weight.shape[1] // 3
    half = width // 2
    block = pl.BlockSpec((1, rows, width), lambda s: (s, 0, 0))
    table = pl.BlockSpec((1, rows, half), lambda s: (s, 0, 0))

    def whole(shape):
        return pl.BlockSpec(shape, lambda s: (0,) * len(shape))

    shape = jax.ShapeDtypeStruct((sources, rows, width), BF)
    return pl.pallas_call(
        qkv_kernel,
        grid=(sources,),
        in_specs=[
            pl.BlockSpec((1, rows, D), lambda s: (s, 0, 0)),
            whole(weight.shape),
            whole(bias.shape),
            whole(turn.shape),
            table,
            table,
        ],
        out_specs=[block] * 3,
        out_shape=[shape] * 3,
        scratch_shapes=[pltpu.VMEM((D, 2 * width), BF), pltpu.VMEM((bias.shape[0], 2 * width), F32)],
        compiler_params=pltpu.CompilerParams(vmem_limit_bytes=VMEM),
        cost_estimate=pl.CostEstimate(
            flops=2 * sources * rows * D * 3 * width, bytes_accessed=4 * sources * rows * D, transcendentals=0
        ),
        name="qkv_rotary",
    )(normed, weight, bias, turn, cosine, sine)


def turned_lanes(width, head):
    lane = lax.broadcasted_iota(jnp.int32, (1, width), 1)
    return (lane % (width // 2)) // (HEAD // 2) == head


def plain_lanes(width, head):
    lane = lax.broadcasted_iota(jnp.int32, (1, width), 1)
    return lane // HEAD == head


def pick(mask, array):
    return jnp.where(mask, array, jnp.zeros((), array.dtype))


def head_rows(array, head):
    half = array.shape[0] // 2
    step = HEAD // 2
    return jnp.concatenate(
        [array[head * step : (head + 1) * step], array[half + head * step : half + (head + 1) * step]], 0
    )


def value_total(v, frames_local, sources):
    total = jnp.zeros((1, v.shape[-1]), F32)
    real = lax.broadcasted_iota(jnp.int32, (EXTRA, 1), 0) < 2 * frames_local
    for s in range(sources):
        for l in range(frames_local):
            total = total + jnp.sum(v[s, l * PATCHES : (l + 1) * PATCHES].astype(F32), 0, keepdims=True)
        total = total + jnp.sum(pick(real, v[s, frames_local * PATCHES :].astype(F32)), 0, keepdims=True)
    return total


def attend_kernel(
    frames_local, start, key_frame, query_start, query_frame, query_pad, q, k, v, mixed, exact, logs, logs_extra, v_t, acc, state
):
    sources, _, width = q.shape
    heads = width // HEAD
    frames = sources * frames_local
    patch_rows = frames_local * PATCHES
    length = frames * ROW_FRAME
    extra = sources * EXTRA

    def frame_ref(ref, g):
        return ref[g // frames_local, pl.ds(pl.multiple_of((g % frames_local) * PATCHES, PATCHES), PATCHES), :]

    for g in range(frames):
        s, l = g // frames_local, g % frames_local
        v_t[g] = v[s, l * PATCHES : (l + 1) * PATCHES].T
    k_extra = jnp.concatenate([k[s, patch_rows:] for s in range(sources)], 0)
    v_extra = jnp.concatenate([v[s, patch_rows:] for s in range(sources)], 0)
    v_extra_t = v_extra.T
    uniform = jnp.asarray(1.0 / length, BF).astype(F32) * value_total(v, frames_local, sources)
    key_at = key_frame[:, :1]

    def begin(head, query, allowed, slot):
        scores = jnp.where(allowed, nt(k_extra, query), MASKED)
        top = jnp.max(scores, 0, keepdims=True)
        weights = jnp.exp2((scores - top) * SCALE2)
        total = jnp.sum(weights, 0, keepdims=True)
        lanes = query.shape[0]
        acc[head * HEAD : (head + 1) * HEAD, :lanes] = nn(v_extra_t[head * HEAD : (head + 1) * HEAD], weights.astype(BF))
        state[slot, head : head + 1, :lanes] = top
        state[slot + 1, head : head + 1, :lanes] = total

    def step(head, query, keys, values_t, allowed, slot):
        lanes = query.shape[0]
        scores = nt(keys, query)
        if allowed is not None:
            scores = jnp.where(allowed, scores, MASKED)
        before = state[slot, head : head + 1, :lanes]
        top = jnp.maximum(before, jnp.max(scores, 0, keepdims=True))
        fade = jnp.exp2((before - top) * SCALE2)
        weights = jnp.exp2((scores - top) * SCALE2)
        span = slice(head * HEAD, (head + 1) * HEAD)
        state[slot, head : head + 1, :lanes] = top
        state[slot + 1, head : head + 1, :lanes] = state[slot + 1, head : head + 1, :lanes] * fade + jnp.sum(
            weights, 0, keepdims=True
        )
        acc[span, :lanes] = acc[span, :lanes] * fade + nn(values_t[span], weights.astype(BF))

    def finish(lanes):
        parts = []
        for head in range(heads):
            span = slice(head * HEAD, (head + 1) * HEAD)
            parts.append(acc[span, :lanes] / state[1, head : head + 1, :lanes])
        return jnp.concatenate(parts, 0).T

    def one_frame(g, _):
        query = frame_ref(q, g)
        queries = [pick(turned_lanes(width, head), query) for head in range(heads)]
        first = start[g]
        allowed = (key_at >= first) & (key_at <= g)
        for head in range(heads):
            begin(head, queries[head], allowed, 0)

        def one_key(f, _):
            keys = frame_ref(k, f)
            values_t = v_t[f]
            for head in range(heads):
                step(head, queries[head], keys, values_t, None, 0)
            return 0

        lax.fori_loop(first, g + 1, one_key, 0)
        result = jnp.where(first > frames, jnp.broadcast_to(uniform, (PATCHES, width)), finish(PATCHES))
        rows = pl.ds(pl.multiple_of((g % frames_local) * PATCHES, PATCHES), PATCHES)
        exact[g // frames_local, rows, :] = result
        mixed[g // frames_local, rows, :] = result.astype(BF)
        logs[g] = state[0] + jnp.log2(state[1]) * (1.0 / SCALE2)
        return 0

    state[...] = jnp.ones_like(state)
    lax.fori_loop(0, frames, one_frame, 0)

    q_extra = jnp.concatenate([q[s, patch_rows:] for s in range(sources)], 0)
    queries = [pick(turned_lanes(width, head), q_extra) for head in range(heads)]
    first = query_start[:1]
    last = query_frame[:1]
    allowed = (key_at >= first) & (key_at <= last)
    for head in range(heads):
        begin(head, queries[head], allowed, 0)

    def one_key(f, _):
        keys = frame_ref(k, f)
        values_t = v_t[f]
        visible = (first <= f) & (last >= f)
        for head in range(heads):
            step(head, queries[head], keys, values_t, visible, 0)
        return 0

    lax.fori_loop(0, frames, one_key, 0)
    result = finish(extra)
    result = jnp.where(query_pad[:, :1] > 0, jnp.broadcast_to(uniform, result.shape), result)
    for s in range(sources):
        exact[s, patch_rows:, :] = result[s * EXTRA : (s + 1) * EXTRA]
        mixed[s, patch_rows:, :] = result[s * EXTRA : (s + 1) * EXTRA].astype(BF)
    logs_extra[...] = (state[0] + jnp.log2(state[1]) * (1.0 / SCALE2))[:, :extra]


def attend_call(start, key_frame, query_start, query_frame, query_pad, q, k, v):
    sources, rows, width = q.shape
    frames_local = rows // PATCHES
    frames = sources * frames_local
    extra = sources * EXTRA
    lanes = max(PATCHES, extra)
    heads = width // HEAD
    vmem = pl.BlockSpec(memory_space=pltpu.VMEM)
    return pl.pallas_call(
        functools.partial(attend_kernel, frames_local),
        in_specs=[pl.BlockSpec(memory_space=pltpu.SMEM)] + [vmem] * 7,
        out_specs=[vmem] * 4,
        out_shape=[
            jax.ShapeDtypeStruct(q.shape, BF),
            jax.ShapeDtypeStruct(q.shape, F32),
            jax.ShapeDtypeStruct((frames, 8, lanes), F32),
            jax.ShapeDtypeStruct((8, extra), F32),
        ],
        scratch_shapes=[
            pltpu.VMEM((frames, width, PATCHES), BF),
            pltpu.VMEM((width, lanes), F32),
            pltpu.VMEM((2, 8, lanes), F32),
        ],
        compiler_params=pltpu.CompilerParams(vmem_limit_bytes=VMEM),
        cost_estimate=pl.CostEstimate(
            flops=8 * heads * 256 * frames * frames * PATCHES * PATCHES // 2,
            bytes_accessed=10 * sources * rows * width,
            transcendentals=heads * frames * frames * PATCHES * PATCHES // 2,
        ),
        name="attend",
    )(start, key_frame, query_start, query_frame, query_pad, q, k, v)


def attend_back_kernel(
    frames_local,
    start,
    key_frame,
    query_start,
    query_frame,
    query_pad,
    q,
    k,
    v,
    grad,
    exact,
    logs,
    logs_extra,
    cosine,
    sine,
    out,
    k_t,
    dq_t,
    dk,
    dv,
    dq_extra,
    dk_extra,
    dv_extra,
    centers,
):
    sources, _, width = q.shape
    half = width // 2
    heads = width // HEAD
    frames = sources * frames_local
    patch_rows = frames_local * PATCHES
    length = frames * ROW_FRAME
    step_rows = HEAD // 2

    def frame_ref(ref, g):
        return ref[g // frames_local, pl.ds(pl.multiple_of((g % frames_local) * PATCHES, PATCHES), PATCHES), :]

    which = lax.broadcasted_iota(jnp.int32, (8, width), 0)
    lane = lax.broadcasted_iota(jnp.int32, (8, width), 1)
    groups = (lane // HEAD == which).astype(BF)

    def center_of(grads, exacts):
        product = grads.astype(F32) * exacts
        high = product.astype(BF)
        low = (product - high.astype(F32)).astype(BF)
        return nt(groups, high) + nt(groups, low)

    def gather_extra(ref):
        return jnp.concatenate([ref[s, patch_rows:] for s in range(sources)], 0)

    for g in range(frames):
        s, l = g // frames_local, g % frames_local
        k_t[g] = k[s, l * PATCHES : (l + 1) * PATCHES].T
    q_extra = gather_extra(q)
    k_extra = gather_extra(k)
    v_extra = gather_extra(v)
    g_extra = gather_extra(grad)
    k_extra_t = k_extra.T
    dq_t[...] = jnp.zeros_like(dq_t)
    dk[...] = jnp.zeros_like(dk)
    dv[...] = jnp.zeros_like(dv)
    dq_extra[...] = jnp.zeros_like(dq_extra)
    dk_extra[...] = jnp.zeros_like(dk_extra)
    dv_extra[...] = jnp.zeros_like(dv_extra)
    key_at = key_frame[:, :1]

    def tile(head, query, grads, keys, values, keys_t, log, center, allowed):
        scores = nt(keys, query)
        probs = jnp.exp2((scores - log) * SCALE2)
        if allowed is not None:
            probs = jnp.where(allowed, probs, 0.0)
        inner = nt(values, grads)
        change = (probs * (inner - center)).astype(BF)
        dv_part = nn(probs.astype(BF), grads)
        dk_part = nn(change, query)
        dq_part = nn(head_rows(keys_t, head), change)
        return dv_part, dk_part, dq_part

    def add_dq(ref, head, part):
        first = slice(head * step_rows, (head + 1) * step_rows)
        second = slice(half + head * step_rows, half + (head + 1) * step_rows)
        ref[first] += part[:step_rows]
        ref[second] += part[step_rows:]

    def one_frame(g, pad_grad):
        query = frame_ref(q, g)
        grads = frame_ref(grad, g)
        queries = [pick(turned_lanes(width, head), query) for head in range(heads)]
        grad_heads = [pick(plain_lanes(width, head), grads) for head in range(heads)]
        first = start[g]
        centers[...] = center_of(grads, frame_ref(exact, g))
        allowed = (key_at >= first) & (key_at <= g)
        for head in range(heads):
            dv_part, dk_part, dq_part = tile(
                head,
                queries[head],
                grad_heads[head],
                k_extra,
                v_extra,
                k_extra_t,
                logs[g, head : head + 1, :PATCHES],
                centers[head : head + 1],
                allowed,
            )
            dv_extra[...] += dv_part
            dk_extra[...] += dk_part
            add_dq(dq_t.at[g], head, dq_part)

        def one_key(f, _):
            keys = frame_ref(k, f)
            values = frame_ref(v, f)
            keys_t = k_t[f]
            dv_sum = dv[f]
            dk_sum = dk[f]
            for head in range(heads):
                dv_part, dk_part, dq_part = tile(
                    head,
                    queries[head],
                    grad_heads[head],
                    keys,
                    values,
                    keys_t,
                    logs[g, head : head + 1, :PATCHES],
                    centers[head : head + 1],
                    None,
                )
                dv_sum = dv_sum + dv_part
                dk_sum = dk_sum + dk_part
                add_dq(dq_t.at[g], head, dq_part)
            dv[f] = dv_sum
            dk[f] = dk_sum
            return 0

        lax.fori_loop(first, g + 1, one_key, 0)
        return pad_grad + jnp.where(first > frames, jnp.sum(grads.astype(F32), 0, keepdims=True), 0.0)

    pad_grad = lax.fori_loop(0, frames, one_frame, jnp.zeros((1, width), F32))
    pad_grad = pad_grad + jnp.sum(jnp.where(query_pad[:, :1] > 0, g_extra.astype(F32), 0.0), 0, keepdims=True)
    pad_grad = pad_grad * jnp.asarray(1.0 / length, BF).astype(F32)

    queries = [pick(turned_lanes(width, head), q_extra) for head in range(heads)]
    grad_heads = [pick(plain_lanes(width, head), g_extra) for head in range(heads)]
    first = query_start[:1]
    last = query_frame[:1]
    center = center_of(g_extra, gather_extra(exact))
    allowed = (key_at >= first) & (key_at <= last)
    for head in range(heads):
        dv_part, dk_part, dq_part = tile(
            head,
            queries[head],
            grad_heads[head],
            k_extra,
            v_extra,
            k_extra_t,
            logs_extra[head : head + 1],
            center[head : head + 1],
            allowed,
        )
        dv_extra[...] += dv_part
        dk_extra[...] += dk_part
        add_dq(dq_extra, head, dq_part)

    def extra_key(f, _):
        keys = frame_ref(k, f)
        values = frame_ref(v, f)
        keys_t = k_t[f]
        visible = (first <= f) & (last >= f)
        for head in range(heads):
            dv_part, dk_part, dq_part = tile(
                head,
                queries[head],
                grad_heads[head],
                keys,
                values,
                keys_t,
                logs_extra[head : head + 1],
                center[head : head + 1],
                visible,
            )
            dv[f] += dv_part
            dk[f] += dk_part
            add_dq(dq_extra, head, dq_part)
        return 0

    lax.fori_loop(0, frames, extra_key, 0)

    def emit(s, rows, dq_rows, dk_rows, dv_rows):
        cos = cosine[s, rows]
        sin = sine[s, rows]
        for part, array in ((0, dq_rows), (1, dk_rows)):
            a = array[:, :half] * 0.125
            b = array[:, half:] * 0.125
            at = part * width
            out[s, rows, at : at + half] = (a * cos + b * sin).astype(BF)
            out[s, rows, at + half : at + width] = (b * cos - a * sin).astype(BF)
        out[s, rows, 2 * width :] = (dv_rows + pad_grad).astype(BF)

    def emit_frame(g, _):
        rows = pl.ds(pl.multiple_of((g % frames_local) * PATCHES, PATCHES), PATCHES)
        emit(g // frames_local, rows, dq_t[g].T, dk[g], dv[g])
        return 0

    lax.fori_loop(0, frames, emit_frame, 0)
    dq_rows = dq_extra[...].T
    real = lax.broadcasted_iota(jnp.int32, (EXTRA, 1), 0) < 2 * frames_local
    for s in range(sources):
        at = slice(s * EXTRA, (s + 1) * EXTRA)
        rows = slice(patch_rows, patch_rows + EXTRA)
        emit(s, rows, dq_rows[at], dk_extra[at], dv_extra[at])
        out[s, rows, :] = pick(real, out[s, rows, :])


def attend_back_call(start, key_frame, query_start, query_frame, query_pad, q, k, v, grad, exact, logs, logs_extra, cosine, sine):
    sources, rows, width = q.shape
    frames_local = rows // PATCHES
    frames = sources * frames_local
    extra = sources * EXTRA
    heads = width // HEAD
    vmem = pl.BlockSpec(memory_space=pltpu.VMEM)
    return pl.pallas_call(
        functools.partial(attend_back_kernel, frames_local),
        in_specs=[pl.BlockSpec(memory_space=pltpu.SMEM)] + [vmem] * 13,
        out_specs=vmem,
        out_shape=jax.ShapeDtypeStruct((sources, rows, 3 * width), BF),
        scratch_shapes=[
            pltpu.VMEM((frames, width, PATCHES), BF),
            pltpu.VMEM((frames, width, PATCHES), F32),
            pltpu.VMEM((frames, PATCHES, width), F32),
            pltpu.VMEM((frames, PATCHES, width), F32),
            pltpu.VMEM((width, extra), F32),
            pltpu.VMEM((extra, width), F32),
            pltpu.VMEM((extra, width), F32),
            pltpu.VMEM((8, PATCHES), F32),
        ],
        compiler_params=pltpu.CompilerParams(vmem_limit_bytes=VMEM),
        cost_estimate=pl.CostEstimate(
            flops=20 * heads * 256 * frames * frames * PATCHES * PATCHES // 2,
            bytes_accessed=20 * sources * rows * width,
            transcendentals=heads * frames * frames * PATCHES * PATCHES // 2,
        ),
        name="attend_back",
    )(start, key_frame, query_start, query_frame, query_pad, q, k, v, grad, exact, logs, logs_extra, cosine, sine)


def feed_kernel(
    chunk, second, outer, outer_t, expand, expand_bias, reduce, final, second_grad, d_expand, d_reduce, d_bias, second_t, active, slope
):
    rows = second.shape[0]
    wide = expand.shape[-1]

    @pl.when(pl.program_id(0) == 0)
    def _():
        for r in range(0, rows, chunk):
            second_t[:, r : r + chunk] = second[r : r + chunk].T
        final[...] = jnp.zeros_like(final)
        second_grad[...] = jnp.zeros_like(second_grad)

    weight_in = expand[0]
    weight_out = reduce[0]
    add = expand_bias[0, :1].astype(F32)

    d_bias[...] = jnp.zeros_like(d_bias)
    for r in range(0, rows, chunk):
        at = slice(r, r + chunk)
        hidden = nn(second[at], weight_in) + add
        cdf = 0.5 + 0.5 * lax.erf(hidden * math.sqrt(0.5))
        density = jnp.exp(hidden * hidden * -0.5) * (1.0 / math.sqrt(2.0 * math.pi))
        act = (hidden * cdf).astype(BF)
        grad = (nt(outer[at], weight_out) * (cdf + hidden * density)).astype(BF)
        active[at] = act
        slope[at] = grad
        d_bias[0] += jnp.sum(grad.astype(F32), 0, keepdims=True)
        final[at] += nn(act, weight_out)
        second_grad[at] += nt(grad, weight_in)
    d_expand[0] = nn(second_t[...], slope[...]).astype(BF)
    d_reduce[:, 0] = nn(outer_t[...], active[...]).astype(BF).reshape(d_reduce.shape[0], d_reduce.shape[2], wide)


def feed_call(second, outer, outer_t, expand, expand_bias, reduce, n_dp):
    rows = second.shape[0]
    tiles, _, wide = expand.shape
    chunk = rows // 2
    assert chunk % 16 == 0

    def whole(shape):
        return pl.BlockSpec(shape, lambda t: (0,) * len(shape))

    return pl.pallas_call(
        functools.partial(feed_kernel, chunk),
        grid=(tiles,),
        in_specs=[
            whole((rows, D)),
            whole((rows, D)),
            whole((D, rows)),
            pl.BlockSpec((1, D, wide), lambda t: (t, 0, 0)),
            pl.BlockSpec((1, 1, wide), lambda t: (t, 0, 0)),
            pl.BlockSpec((1, wide, D), lambda t: (t, 0, 0)),
        ],
        out_specs=[
            whole((rows, D)),
            whole((rows, D)),
            pl.BlockSpec((1, D, wide), lambda t: (t, 0, 0)),
            pl.BlockSpec((n_dp, 1, D // n_dp, wide), lambda t: (0, t, 0, 0)),
            pl.BlockSpec((1, 1, wide), lambda t: (t, 0, 0)),
        ],
        out_shape=[
            jax.ShapeDtypeStruct((rows, D), F32),
            jax.ShapeDtypeStruct((rows, D), F32),
            jax.ShapeDtypeStruct((tiles, D, wide), BF),
            jax.ShapeDtypeStruct((n_dp, tiles, D // n_dp, wide), BF),
            jax.ShapeDtypeStruct((tiles, 1, wide), F32),
        ],
        scratch_shapes=[
            pltpu.VMEM((D, rows), BF),
            pltpu.VMEM((rows, wide), BF),
            pltpu.VMEM((rows, wide), BF),
        ],
        compiler_params=pltpu.CompilerParams(vmem_limit_bytes=VMEM),
        cost_estimate=pl.CostEstimate(
            flops=10 * rows * D * wide * tiles,
            bytes_accessed=8 * D * wide * tiles + 14 * rows * D,
            transcendentals=2 * rows * wide * tiles,
        ),
        name="feed_forward",
    )(second, outer, outer_t, expand, expand_bias, reduce)


def norm_parts(values):
    center = values - jnp.mean(values, -1, keepdims=True)
    scale = lax.rsqrt(jnp.mean(center * center, -1, keepdims=True) + EPSILON)
    return center * scale, scale


def norm_back(grad, unit, scale, gain):
    scaled = grad * gain
    mean_one = jnp.mean(scaled, -1, keepdims=True)
    mean_two = jnp.mean(scaled * unit, -1, keepdims=True)
    return scale * (scaled - mean_one - unit * mean_two)


def to_block(array, frames_local):
    split = array.reshape(frames_local, ROW_FRAME, D)
    return jnp.concatenate(
        [
            split[:, 2:].reshape(frames_local * PATCHES, D),
            split[:, :2].reshape(frames_local * 2, D),
            jnp.zeros((EXTRA - 2 * frames_local, D), array.dtype),
        ],
        0,
    )


def from_block(array, frames_local):
    patches = array[: frames_local * PATCHES].reshape(frames_local, PATCHES, D)
    extra = array[frames_local * PATCHES : frames_local * ROW_FRAME].reshape(frames_local, 2, D)
    return jnp.concatenate([extra, patches], 1).reshape(1, frames_local * ROW_FRAME, D)


def rows_of(per_frame, per_extra, sources, frames_local, fill):
    patches = jnp.broadcast_to(per_frame.reshape(sources, frames_local, 1), (sources, frames_local, PATCHES))
    pad = jnp.full((sources, EXTRA - 2 * frames_local), fill, per_frame.dtype)
    return jnp.concatenate(
        [patches.reshape(sources, -1), per_extra.reshape(sources, 2 * frames_local), pad], 1
    )


def tables(counts, present, sources, frames_local, heads):
    frames = sources * frames_local
    at = jnp.arange(frames, dtype=jnp.int32)
    first, second = counts[0], counts[1]
    inside = at < first + second
    start = jnp.where(at < first, 0, first).astype(jnp.int32)
    time = (at - start).astype(F32)
    begin = jnp.where(inside, start, FAR)
    live_extra = inside[:, None] & (present == 1)
    time_rows = rows_of(time, jnp.repeat(time, 2), sources, frames_local, 0.0)
    live_rows = rows_of(inside.astype(F32), live_extra.astype(F32), sources, frames_local, 0.0)

    patch = np.arange(PATCHES)
    grid_row = np.zeros(frames_local * PATCHES + EXTRA, np.float32)
    grid_col = np.zeros(frames_local * PATCHES + EXTRA, np.float32)
    for l in range(frames_local):
        grid_row[l * PATCHES : (l + 1) * PATCHES] = patch // GRID
        grid_col[l * PATCHES : (l + 1) * PATCHES] = patch % GRID
    lanes = np.zeros((3, HEAD // 2), np.float32)
    freq = 10000.0 ** (-np.arange(PAIRS, dtype=np.float32) / PAIRS)
    for a in range(3):
        lanes[a, a * PAIRS : (a + 1) * PAIRS] = freq
    lanes = np.tile(lanes, (1, heads))
    angle = time_rows[:, :, None] * lanes[0] + (grid_row[:, None] * lanes[1] + grid_col[:, None] * lanes[2])[None]

    def extra_of(per_frame, fill):
        both = jnp.repeat(per_frame, 2).reshape(sources, 2 * frames_local)
        pad = jnp.full((sources, EXTRA - 2 * frames_local), fill, both.dtype)
        return jnp.concatenate([both, pad], 1).reshape(-1)

    extra = sources * EXTRA
    key_frame = jnp.where(live_extra, at[:, None], -1).reshape(sources, 2 * frames_local)
    key_frame = jnp.concatenate(
        [key_frame, jnp.full((sources, EXTRA - 2 * frames_local), -1, jnp.int32)], 1
    ).reshape(-1)
    query_start = extra_of(begin, FAR)
    query_frame = extra_of(at, -1)

    def column(vector):
        return jnp.broadcast_to(vector[:, None], (extra, 128))

    def row(vector):
        return jnp.broadcast_to(vector[None], (8, extra))

    return (
        live_rows,
        jnp.cos(angle),
        jnp.sin(angle),
        (begin, column(key_frame), row(query_start), row(query_frame), column((query_start == FAR).astype(jnp.int32))),
    )


def turn_matrix(width):
    turn = np.zeros((width, width), np.float32)
    step = HEAD // 2
    for h in range(width // HEAD):
        for d in range(HEAD):
            if d < 6 * PAIRS:
                a, rest = divmod(d, 2 * PAIRS)
                side, k = divmod(rest, PAIRS)
                to = side * (width // 2) + h * step + a * PAIRS + k
            else:
                side, k = divmod(d - 6 * PAIRS, step - 3 * PAIRS)
                to = side * (width // 2) + h * step + 3 * PAIRS + k
            turn[h * HEAD + d, to] = 1.0
    return turn


def shards(sizes, *args):
    (
        tokens,
        cotangent,
        frame_counts,
        presence,
        attend_gain,
        attend_shift,
        triple_weight,
        triple_bias,
        output_weight,
        output_bias,
        second_gain,
        second_shift,
        expand_weight,
        expand_bias,
        reduce_weight,
        reduce_bias,
    ) = args
    n_dp, n_x = sizes
    n_f = n_x * 2
    heads = HEADS // n_f
    width = heads * HEAD
    local_rows = tokens.shape[1]
    frames_local = local_rows // ROW_FRAME
    rows = frames_local * PATCHES + EXTRA
    core = lax.axis_index("core")
    shard = lax.axis_index("x") * 2 + core
    dp_at = lax.axis_index("dp")
    d_part = D // n_dp
    ff_part = FF // n_dp
    ff_half = ff_part // 2

    def swap(array):
        return lax.ppermute(array, "core", [(0, 1), (1, 0)])

    def both_cores(array, axis=0):
        other = swap(array)
        low = jnp.where(core == 0, array, other)
        high = jnp.where(core == 0, other, array)
        return jnp.concatenate([low, high], axis)

    def mine(pair, which):
        return jnp.where(which == 0, pair[0], pair[1])

    vectors = [attend_gain, attend_shift, output_bias, second_gain, second_shift, reduce_bias, triple_bias, expand_bias]
    flat = jnp.concatenate(vectors)
    qkv_part = 3 * D // n_dp
    flat = jnp.pad(flat, (0, 16 * qkv_part - flat.shape[0])).reshape(16, qkv_part)
    packed = jnp.concatenate([triple_weight, flat], 0)
    packed = lax.all_gather(packed, "dp", axis=0)
    small = packed[:, D // n_f :].reshape(n_dp, -1)
    full = []
    at = 0
    for vector in vectors:
        full.append(small[:, at : at + vector.shape[0]].reshape(-1))
        at += vector.shape[0]
    gain_one, shift_one, output_add, gain_two, shift_two, reduce_add = (v.astype(F32)[None] for v in full[:6])
    triple_add, expand_add = full[6], full[7]
    triple_rows = packed[:, : D // n_f].transpose(1, 0, 2).reshape(D // n_f, 3, n_f, width)
    triple_own = lax.all_to_all(triple_rows.transpose(2, 0, 1, 3), ("x", "core"), 0, 0, tiled=True)
    triple_own = triple_own.reshape(D, 3 * width)
    bias_own = lax.dynamic_index_in_dim(triple_add.reshape(3, n_f, width), shard, 1, False).reshape(1, 3 * width)

    expand_keep = mine([expand_weight[:, :ff_half], expand_weight[:, ff_half:]], core)
    expand_give = mine([expand_weight[:, ff_half:], expand_weight[:, :ff_half]], core)
    expand_other = swap(expand_give)
    expand_chip = jnp.concatenate(
        [jnp.where(core == 0, expand_keep, expand_other), jnp.where(core == 0, expand_other, expand_keep)], 0
    )
    blocks = n_dp // n_f
    reduce_split = reduce_weight.reshape(blocks, 2, ff_half, d_part)
    reduce_keep = mine([reduce_split[:, 0], reduce_split[:, 1]], core)
    reduce_other = swap(mine([reduce_split[:, 1], reduce_split[:, 0]], core))
    reduce_chip = jnp.stack(
        [jnp.where(core == 0, reduce_keep, reduce_other), jnp.where(core == 0, reduce_other, reduce_keep)], 0
    )
    expand_all = lax.all_gather(expand_chip, ("dp", "x"), axis=0)
    expand_all = expand_all.reshape(n_dp, D, ff_half)
    reduce_all = lax.all_gather(reduce_chip, ("dp", "x"), axis=0)
    reduce_all = reduce_all.reshape(n_dp, n_dp, ff_half, d_part).transpose(1, 2, 0, 3).reshape(n_dp, ff_half, D)
    output_all = lax.all_gather(output_weight, ("dp", "x"), axis=0)
    output_all = output_all.reshape(n_dp, n_x * width, d_part).transpose(1, 0, 2).reshape(n_x * width, D)
    expand_add_own = lax.dynamic_index_in_dim(expand_add.reshape(n_dp, 2, 1, ff_half), core, 1, False)

    live_all, cosine, sine, guides = tables(frame_counts[0], presence[0], n_f, frames_local, heads)
    live = lax.dynamic_index_in_dim(live_all, shard, 0, False)[:, None]
    entered = to_block(tokens[0], frames_local).astype(F32) * live
    outer = to_block(cotangent[0], frames_local).astype(F32) * live
    outer_low = outer.astype(BF)
    outer_chip = both_cores(outer_low)
    outer_chip_t = outer_chip.T
    unit_one, scale_one = norm_parts(entered)
    normed = (unit_one * gain_one + shift_one).astype(BF)
    normed_all = lax.all_gather(normed, ("x", "core"), axis=0)

    turn = turn_matrix(width)
    q, k, v = qkv_call(normed_all, triple_own, bias_own, jnp.asarray(turn, BF), cosine, sine)
    mixed, exact, logs, logs_extra = attend_call(*guides, q, k, v)

    def over_x(array):
        return lax.all_to_all(array, "x", 0, 0, tiled=True)

    mixed_chip = over_x(mixed.reshape(n_x, 2 * rows, width)).transpose(1, 0, 2).reshape(2 * rows, n_x * width)
    branch_part = nn(mixed_chip, output_all).reshape(2, rows, D)
    branch = mine(branch_part, core) + swap(mine(branch_part[::-1], core).astype(BF)).astype(F32)
    middle = entered + branch + output_add
    unit_two, scale_two = norm_parts(middle)
    second = (unit_two * gain_two + shift_two).astype(BF)
    second_chip = both_cores(second)
    final, second_grad, d_expand, d_reduce, d_expand_bias = feed_call(
        second_chip, outer_chip, outer_chip_t, expand_all, expand_add_own, reduce_all, n_dp
    )
    second_grad = second_grad.reshape(2, rows, D)
    second_grad = mine(second_grad, core) + swap(mine(second_grad[::-1], core).astype(BF)).astype(F32)
    final = final.reshape(2, rows, D)
    final = mine(final, core) + swap(mine(final[::-1], core).astype(BF)).astype(F32)
    block_output = ((middle + final + reduce_add) * live).astype(BF)

    middle_grad = outer + norm_back(second_grad, unit_two, scale_two, gain_two)
    second_gain_grad = jnp.sum(second_grad * unit_two, 0)
    second_shift_grad = jnp.sum(second_grad, 0)
    branch_low = middle_grad.astype(BF)
    branch_chip = both_cores(branch_low)
    mixed_grad = nt(branch_chip, output_all).astype(BF)
    mixed_grad = over_x(mixed_grad.reshape(2 * rows, n_x, width).transpose(1, 0, 2)).reshape(n_f, rows, width)
    d_output = tn(mixed_chip, branch_chip).astype(BF)
    triple_grad = attend_back_call(*guides, q, k, v, mixed_grad, exact, logs, logs_extra, cosine, sine)
    flat_grad = triple_grad.reshape(n_f * rows, 3 * width)
    turned = jnp.asarray(turn, BF)
    natural = jnp.concatenate(
        [
            nt(flat_grad[:, :width], turned).astype(BF),
            nt(flat_grad[:, width : 2 * width], turned).astype(BF),
            flat_grad[:, 2 * width :],
        ],
        1,
    )
    d_triple = tn(normed_all.reshape(n_f * rows, D), natural).astype(BF)
    d_triple_bias = jnp.sum(natural.astype(F32), 0)
    normed_grad = nt(natural, triple_own).astype(BF)
    normed_grad = lax.psum_scatter(normed_grad, ("x", "core"), scatter_dimension=0, tiled=True).astype(F32)
    attend_gain_grad = jnp.sum(normed_grad * unit_one, 0)
    attend_shift_grad = jnp.sum(normed_grad, 0)
    tokens_grad = (middle_grad + norm_back(normed_grad, unit_one, scale_one, gain_one)) * live

    d_triple = lax.all_to_all(d_triple.reshape(n_f, D // n_f, 3, width), ("x", "core"), 0, 0, tiled=True)
    d_triple = d_triple.transpose(1, 2, 0, 3).reshape(D // n_f, 3 * D)
    triple_weight_grad = lax.psum_scatter(d_triple, "dp", scatter_dimension=1, tiled=True).astype(F32)
    d_output = d_output.reshape(n_x, width, n_dp, d_part).transpose(2, 0, 1, 3).reshape(n_dp * n_x * width, d_part)
    output_weight_grad = lax.psum_scatter(d_output, ("dp", "x"), scatter_dimension=0, tiled=True).astype(F32)
    d_expand = d_expand.reshape(n_dp * n_x * (D // n_x), ff_half)
    d_expand = lax.psum_scatter(d_expand, ("dp", "x"), scatter_dimension=0, tiled=True)
    d_expand = d_expand.reshape(2, D // n_f, ff_half)
    expand_keep = mine(d_expand, core)
    expand_other = swap(mine(d_expand[::-1], core))
    expand_weight_grad = jnp.concatenate(
        [jnp.where(core == 0, expand_keep, expand_other), jnp.where(core == 0, expand_other, expand_keep)], 1
    ).astype(F32)
    d_reduce = d_reduce.reshape(n_dp * n_x * 2 * blocks * d_part, ff_half)
    d_reduce = lax.psum_scatter(d_reduce, ("dp", "x"), scatter_dimension=0, tiled=True)
    d_reduce = d_reduce.reshape(2, blocks, d_part, ff_half)
    reduce_keep = mine(d_reduce, core)
    reduce_other = swap(mine(d_reduce[::-1], core))
    reduce_weight_grad = jnp.stack(
        [jnp.where(core == 0, reduce_keep, reduce_other), jnp.where(core == 0, reduce_other, reduce_keep)], 1
    )
    reduce_weight_grad = reduce_weight_grad.transpose(0, 1, 3, 2).reshape(blocks * 2 * ff_half, d_part).astype(F32)

    zero_qkv = jnp.zeros((3, n_f, width), F32)
    triple_bias_part = lax.dynamic_update_slice(zero_qkv, d_triple_bias.reshape(3, 1, width), (0, shard, 0))
    zero_ff = jnp.zeros((n_dp, 2, ff_half), F32)
    expand_bias_part = lax.dynamic_update_slice(zero_ff, d_expand_bias.reshape(n_dp, 1, ff_half), (0, core, 0))
    sums = [
        attend_gain_grad,
        attend_shift_grad,
        jnp.sum(branch_low.astype(F32), 0),
        second_gain_grad,
        second_shift_grad,
        jnp.sum(outer_low.astype(F32), 0),
        triple_bias_part.reshape(-1),
        expand_bias_part.reshape(-1),
    ]
    sums = jnp.concatenate([s.reshape(n_dp, -1) for s in sums], 1)
    device = dp_at * n_f + shard
    total = n_dp * n_f
    bit = 1
    while bit < total:
        sums = sums + lax.ppermute(sums, ("dp", "x", "core"), [(i, i ^ bit) for i in range(total)])
        bit *= 2
    own = lax.dynamic_index_in_dim(sums, dp_at, 0, False)
    parts = []
    at = 0
    for size in [d_part] * 6 + [qkv_part, ff_part]:
        parts.append(own[at : at + size])
        at += size
    return (
        from_block(block_output, frames_local),
        from_block(tokens_grad, frames_local),
        parts[0],
        parts[1],
        triple_weight_grad,
        parts[6],
        output_weight_grad,
        parts[2],
        parts[3],
        parts[4],
        expand_weight_grad,
        parts[7],
        reduce_weight_grad,
        parts[5],
    )


def solution(mesh):
    n_dp, n_f = mesh.shape["dp"], mesh.shape["fsdp"]
    n_x = n_f // 2
    inner = jax.sharding.Mesh(mesh.devices.reshape(n_dp, n_x, 2), ("dp", "x", "core"))
    fsdp = ("x", "core")
    rows = P("dp", fsdp, None)
    weight = P(fsdp, "dp")
    vector = P("dp")
    return jax.shard_map(
        functools.partial(shards, (n_dp, n_x)),
        mesh=inner,
        in_specs=(
            rows,
            rows,
            P("dp", None),
            P("dp", None, None),
            vector,
            vector,
            weight,
            vector,
            weight,
            vector,
            vector,
            vector,
            weight,
            vector,
            weight,
            vector,
        ),
        out_specs=(
            rows,
            rows,
            vector,
            vector,
            weight,
            vector,
            weight,
            vector,
            vector,
            vector,
            weight,
            vector,
            weight,
            vector,
        ),
        check_vma=False,
    )
```

time: 1720 us -> 921 us (0.54)
  matrix products: 437 us -> 25 us
  waiting for transfers between devices: 710 us -> 448 us
  blocking collectives: 220 us -> 23.6 us
  Pallas kernels: 0 us -> 191 us
  local copies, waits for them, and re-layouts: 264 us -> 118 us
  other arithmetic: 49.3 us -> 69.8 us
  starting transfers between devices: 1.5 us -> 20.4 us
    dot_general x124 -> x7, matrix products: 437 us -> 25 us  [the longest x4 12.8 us: nt(): lax.dot_general(left, right, (((1,), (1,)), ((), ())), preferred_element_...]
    unnamed x21 -> x11, waiting for transfers between devices: 406 us -> 46.1 us
    pallas_call x0 -> x4, Pallas kernels: none -> 191 us  [the longest x1 69.7 us: attend_back_call(): pl.pallas_call(functools.partial(attend_back_kernel, frames_local), in_sp...]
    all_gather x10 -> x0, blocking collectives: 179 us -> none  [the longest x1 28 us: shards(): lax.all_gather(triple_bias, 'dp', axis=0, tiled=True)]
    dynamic_update_slice x48 -> x2, local copies, waits for them, and re-layouts: 74 us -> 0.31 us  [the longest x1 0.31 us: shards(): lax.dynamic_update_slice(zero_qkv, d_triple_bias.reshape(3, 1, width), (0...]
    reduce_scatter x5 -> x4, waiting for transfers between devices: 171 us -> 231 us  [the longest x1 95.7 us: shards(): lax.psum_scatter(d_expand, ('dp', 'x'), scatter_dimension=0, tiled=True)]
    all_to_all x0 -> x3, waiting for transfers between devices: none -> 53.8 us  [the longest x2 27.1 us: over_x(): return lax.all_to_all(array, 'x', 0, 0, tiled=True)]
    unnamed x128 -> x102, local copies, waits for them, and re-layouts: 67.8 us -> 21.2 us
  transfers between devices with their start and end apart: 17 -> 28, of which waited for: 11 -> 17; matrix products, arithmetic and copies ran while one was open for 21% -> 17% of each run, Pallas kernels for 0% -> 15%
where the time goes in v1:
time: 921 us; the launch traced here: 912 us
  waiting for transfers between devices  448 us (49%)
  Pallas kernels  191 us (21%)
  local copies, waits for them, and re-layouts  118 us (13%)
  other arithmetic  69.8 us (8%)
  matrix products  25 us (3%)
  blocking collectives  23.6 us (3%)
  starting transfers between devices  20.4 us (2%)
  between operations  17 us (2%)
    reduce_scatter x1, waiting for transfers between devices, shards(): lax.psum_scatter(d_expand, ('dp', 'x'), scatter_dimension=0, tiled=True)  95.7 us
    reduce_scatter x1, waiting for transfers between devices, shards(): lax.psum_scatter(d_reduce, ('dp', 'x'), scatter_dimension=0, tiled=True)  94.5 us
    pallas_call x1, Pallas kernels, attend_back_call(): pl.pallas_call(functools.partial(attend_back_kernel, frames_local), in_sp...  69.7 us
    pallas_call x1, Pallas kernels, attend_call(): pl.pallas_call(functools.partial(attend_kernel, frames_local), in_specs=[...  61.1 us
    pallas_call x1, Pallas kernels, feed_call(): pl.pallas_call(functools.partial(feed_kernel, chunk), grid=(tiles,), in_s...  52 us
    unnamed x11, waiting for transfers between devices  46.1 us
    all_gather x1, waiting for transfers between devices, shards(): expand_all = lax.all_gather(expand_chip, ('dp', 'x'), axis=0)  45.4 us
    all_gather x1, waiting for transfers between devices, shards(): packed = lax.all_gather(packed, 'dp', axis=0)  41.5 us
  transfers between devices with their start and end apart: 28, of which 17 were waited for; matrix products, arithmetic and copies ran while one was open for 17% of the time, Pallas kernels for 15%

profile of v1, /device:TPU:0, one launch (start us, length us, event | category | flops | bytes accessed | tf_op | source)
XLA Modules:
  0.0 912.4 jit_solution(6575679198420532018)
XLA Ops:
  22.0 41.5 %all-gather.12.cloned.1.call-done = bf16[2176,384]{1,0:T(8,128)(2,1)} async-done(((bf16[272,384]{1,0:T(8,128)(2,1)}), bf16[2176,384]{1,0:T(8,128)(2,1)}) %all-gather.12.cloned.1.call-update) | async-done | bytes 1671184 | tf_op jit(solution)/shard_map/all_gather | solution.py:756
  82.1 5.2 fusion.16
  90.2 26.7 %all-to-all-done = bf16[4,256,3,256]{1,3,2,0:T(8,128)(2,1)S(1)} async-done(((bf16[4,256,3,256]{1,3,2,0:T(8,128)(2,1)}), bf16[4,256,3,256]{1,3,2,0:T(8,128)(2,1)S(1)}, u32[]{:S(2)}, u32[]{:S(2)}) %all-to-all-start) | async-done | bytes 1572896 | tf_op jit(solution)/shard_map/all_to_all | solution.py:766
  120.2 8.1 qkv_rotary.1
  130.8 61.1 %attend.1 = (bf16[4,528,256]{2,1,0:T(8,128)(2,1)}, f32[4,528,256]{2,1,0:T(8,128)}, f32[8,8,256]{2,1,0:T(8,128)}, f32[8,64]{1,0:T(8,128)}) custom-call(s32[8]{0:T(128)} %compare_select_fusion.2.start, s32[64,128]{1,0:T(8,128)} %broadcast_in_dim.111.key_frame, s32[8,64]{1,0:T(8,128)} %broadcast_in_dim.117.query_start, s32[8,64]{1,0:T(8,128)} %broadcast_in_dim.120.query_frame, ...), custom_call_target="tpu_custom_call" | custom-call | flops 17179869184 | bytes 5406720 | tf_op jit(solution)/shard_map/attend/pallas_call | solution.py:247
  191.9 3.9 all-to-all-start.1
  197.4 16.1 %all-to-all-done.1 = bf16[2,1056,256]{2,1,0:T(8,128)(2,1)S(1)} async-done(((bf16[2,1056,256]{2,1,0:T(8,128)(2,1)}), bf16[2,1056,256]{2,1,0:T(8,128)(2,1)S(1)}, u32[]{:S(2)}, u32[]{:S(2)}) %all-to-all-start.1) | async-done | bytes 1081376 | tf_op jit(solution)/shard_map/all_to_all | solution.py:807
  225.6 5.7 convert_reduce_fusion.2
  239.0 17.8 %all-gather.18.cloned.1.call-done = bf16[32,2,256,128]{3,2,1,0:T(8,128)(2,1)} async-done(((bf16[2,2,256,128]{3,2,1,0:T(8,128)(2,1)}), bf16[32,2,256,128]{3,2,1,0:T(8,128)(2,1)}) %all-gather.18.cloned.1.call-update) | async-done | bytes 4194320 | tf_op jit(solution)/shard_map/all_gather | solution.py:785
  256.8 5.3 copy.311
  270.2 4.2 copy.258.outer
  281.2 4.2 copy.257.second
  285.4 3.9 fusion.45.outer_t
  289.2 45.4 %all-gather.16.cloned.1.call-done = bf16[8192,256]{1,0:T(8,128)(2,1)} async-done(((bf16[512,256]{1,0:T(8,128)(2,1)}), bf16[8192,256]{1,0:T(8,128)(2,1)}) %all-gather.16.cloned.1.call-update) | async-done | bytes 4194320 | tf_op jit(solution)/shard_map/all_gather | solution.py:783
  334.7 52.0 %feed_forward.1 = (f32[1056,1024]{1,0:T(8,128)}, f32[1056,1024]{1,0:T(8,128)}, bf16[8,1024,256]{2,1,0:T(8,128)(2,1)}, bf16[8,8,128,256]{3,2,1,0:T(8,128)(2,1)}, f32[8,1,256]{2,1,0:T(1,128)}) custom-call(bf16[1056,1024]{1,0:T(8,128)(2,1)} %copy.257.second, bf16[1056,1024]{1,0:T(8,128)(2,1)} %copy.258.outer, bf16[1024,1056]{1,0:T(8,128)(2,1)} %fusion.45.outer_t, ...), custom_call_target="tpu_custom_call" | custom-call | flops 22145925120 | bytes 31916032 | tf_op jit(solution)/shard_map/feed_forward/pallas_call | solution.py:559
  386.6 5.8 copy.266
  392.4 4.2 select_convert_fusion
  398.9 5.7 copy.260
  404.6 4.2 select_convert_fusion.1
  414.1 4.9 multiply_reduce_fusion
  421.3 6.7 convert_reduce_fusion.3
  438.5 4.6 all-to-all-start.2
  448.1 11.0 %all-to-all-done.2 = bf16[2,1056,256]{2,1,0:T(8,128)(2,1)} async-done(((bf16[2,1056,256]{2,1,0:T(8,128)(2,1)}), bf16[2,1056,256]{2,1,0:T(8,128)(2,1)}, u32[]{:S(2)}, u32[]{:S(2)}) %all-to-all-start.2) | async-done | bytes 1081376 | tf_op jit(solution)/shard_map/all_to_all | solution.py:807
  459.1 69.7 %attend_back.1 = bf16[4,528,768]{2,1,0:T(8,128)(2,1)} custom-call(s32[8]{0:T(128)} %compare_select_fusion.2.start, s32[64,128]{1,0:T(8,128)} %broadcast_in_dim.111.key_frame, s32[8,64]{1,0:T(8,128)} %broadcast_in_dim.117.query_start, s32[8,64]{1,0:T(8,128)} %broadcast_in_dim.120.query_frame, s32[64,128]{1,0:T(8,128)} %broadcast_in_dim.121.query_pad, ...), custom_call_target="tpu_custom_call" | custom-call | flops 42949672960 | bytes 10813440 | tf_op jit(solution)/shard_map/attend_back/pallas_call | solution.py:491
  535.4 7.4 convolution_convert_fusion.4
  542.8 4.2 reshape.587
  549.3 23.6 %all_to_all.20 = bf16[4,256,3,256]{1,3,2,0:T(8,128)(2,1)S(1)} all-to-all(bf16[4,256,3,256]{1,3,2,0:T(8,128)(2,1)} %copy.279), channel_id=1, replica_groups=mesh['dp'=8,'x'=2,'core'=2] {'x','core'}, dimensions={0} | all-to-all | bytes 3145728 | tf_op jit(solution)/shard_map/all_to_all | solution.py:852
  576.4 7.1 convolution_convert_fusion
  595.1 40.4 %reduce-scatter.8.cloned.1.call-done = bf16[256,384]{0,1:T(8,128)(2,1)} async-done(((bf16[256,3072]{0,1:T(8,128)(2,1)}), bf16[256,384]{0,1:T(8,128)(2,1)}) %reduce-scatter.8.cloned.1.call-update) | async-done | bytes 196624 | tf_op jit(solution)/shard_map/reduce_scatter | solution.py:854
  637.3 94.5 %reduce-scatter.14.cloned.1.call-done = bf16[512,256]{1,0:T(8,128)(2,1)} async-done(((bf16[8192,256]{1,0:T(8,128)(2,1)}), bf16[512,256]{1,0:T(8,128)(2,1)}) %reduce-scatter.14.cloned.1.call-update) | async-done | bytes 262160 | tf_op jit(solution)/shard_map/reduce_scatter | solution.py:866
  733.2 95.7 %reduce-scatter.12.cloned.1.call-done = bf16[512,256]{1,0:T(8,128)(2,1)} async-done(((bf16[8192,256]{1,0:T(8,128)(2,1)}), bf16[512,256]{1,0:T(8,128)(2,1)}) %reduce-scatter.12.cloned.1.call-update) | async-done | bytes 262160 | tf_op jit(solution)/shard_map/reduce_scatter | solution.py:858
  832.3 44.0 %reduce-scatter.16.cloned.1.call-done = bf16[528,1024]{1,0:T(8,128)(2,1)} async-done(((bf16[2112,1024]{1,0:T(8,128)(2,1)}), bf16[528,1024]{1,0:T(8,128)(2,1)}) %reduce-scatter.16.cloned.1.call-update) | async-done | bytes 1081360
  (317 shorter events, 160.7 us)
Async XLA Ops:
  7.2 56.4 %all-gather.12.cloned.1.call-start = ((), (), s32[]{:S(2)}) async-start(), calls=%async_computation.14 | async-start | bytes 1880064 | tf_op jit(solution)/shard_map/all_gather | solution.py:756
  15.7 104.5 %all-gather.10.cloned.1.call-start = ((), (), s32[]{:S(2)}) async-start(), calls=%async_computation.9 | async-start | bytes 5406720 | tf_op jit(solution)/shard_map/all_gather | solution.py:800
  67.5 128.4 %all-gather.14.cloned.1.call-start = ((), (), s32[]{:S(2)}) async-start(), calls=%async_computation.15 | async-start | bytes 1114112 | tf_op jit(solution)/shard_map/all_gather | solution.py:787
  68.2 188.6 %all-gather.18.cloned.1.call-start = ((), (), s32[]{:S(2)}) async-start(), calls=%async_computation.17 | async-start | bytes 4456448 | tf_op jit(solution)/shard_map/all_gather | solution.py:785
  68.3 1.4 collective-permute-start.4
  70.5 18.3 %collective-permute-start.3 = (bf16[256,256]{1,0:T(8,128)(2,1)S(1)}, bf16[256,256]{1,0:T(8,128)(2,1)S(1)}, u32[]{:S(2)}, u32[]{:S(2)}) collective-permute-start(bf16[256,256]{1,0:T(8,128)(2,1)S(1)} %broadcast_select_fusion.14), channel_id=1, source_target_pairs={{0,1},{1,0},{2,3},{3,2},{4,5},{5,4},{6,7},{7,6},{8,9},{9,8},{10,11... | collective-permute-start | bytes 393224 | tf_op jit(solution)/shard_map/ppermute | solution.py:740
  77.9 39.0 %all-to-all-start = ((bf16[4,256,3,256]{1,3,2,0:T(8,128)(2,1)}), bf16[4,256,3,256]{1,3,2,0:T(8,128)(2,1)S(1)}, u32[]{:S(2)}, u32[]{:S(2)}) async-start(bf16[4,256,3,256]{1,3,2,0:T(8,128)(2,1)} %copy.232), calls=%async_computation | async-start | bytes 3145728 | tf_op jit(solution)/shard_map/all_to_all | solution.py:766
  81.6 253.1 %all-gather.16.cloned.1.call-start = ((), (), s32[]{:S(2)}) async-start(), calls=%async_computation.16 | async-start | bytes 4456448 | tf_op jit(solution)/shard_map/all_gather | solution.py:783
  191.9 21.5 %all-to-all-start.1 = ((bf16[2,1056,256]{2,1,0:T(8,128)(2,1)}), bf16[2,1056,256]{2,1,0:T(8,128)(2,1)S(1)}, u32[]{:S(2)}, u32[]{:S(2)}) async-start(bf16[2,1056,256]{2,1,0:T(8,128)(2,1)} %bitcast.215), calls=%async_computation.1 | async-start | bytes 2162688 | tf_op jit(solution)/shard_map/all_to_all | solution.py:807
  220.2 3.0 collective-permute-start
  233.7 28.4 %collective-permute-start.2 = (bf16[528,1024]{1,0:T(8,128)(2,1)}, bf16[528,1024]{1,0:T(8,128)(2,1)}, u32[]{:S(2)}, u32[]{:S(2)}) collective-permute-start(bf16[528,1024]{1,0:T(8,128)(2,1)} %copy.248), channel_id=1, source_target_pairs={{0,1},{1,0},{2,3},{3,2},{4,5},{5,4},{6,7},{7,6},{8,9},{9,8},{10,11... | collective-permute-start | bytes 3244040 | tf_op jit(solution)/shard_map/ppermute | solution.py:740
  237.9 36.6 %collective-permute-start.1 = (bf16[528,1024]{1,0:T(8,128)(2,1)}, bf16[528,1024]{1,0:T(8,128)(2,1)}, u32[]{:S(2)}, u32[]{:S(2)}) collective-permute-start(bf16[528,1024]{1,0:T(8,128)(2,1)} %copy.243), channel_id=1, source_target_pairs={{0,1},{1,0},{2,3},{3,2},{4,5},{5,4},{6,7},{7,6},{8,9},{9,8},{10,11... | collective-permute-start | bytes 3244040 | tf_op jit(solution)/shard_map/ppermute | solution.py:740
  398.9 12.7 %collective-permute-start.6 = (bf16[528,1024]{1,0:T(8,128)(2,1)}, bf16[528,1024]{1,0:T(8,128)(2,1)}, u32[]{:S(2)}, u32[]{:S(2)}) collective-permute-start(bf16[528,1024]{1,0:T(8,128)(2,1)} %copy.268), channel_id=1, source_target_pairs={{0,1},{1,0},{2,3},{3,2},{4,5},{5,4},{6,7},{7,6},{8,9},{9,8},{10,11... | collective-permute-start | bytes 3244040 | tf_op jit(solution)/shard_map/ppermute | solution.py:740
  411.2 7.8 collective-permute-start.5
  429.7 2.9 collective-permute-start.7
  438.5 20.6 %all-to-all-start.2 = ((bf16[2,1056,256]{2,1,0:T(8,128)(2,1)}), bf16[2,1056,256]{2,1,0:T(8,128)(2,1)}, u32[]{:S(2)}, u32[]{:S(2)}) async-start(bf16[2,1056,256]{2,1,0:T(8,128)(2,1)} %bitcast.187), calls=%async_computation.2 | async-start | bytes 2162688 | tf_op jit(solution)/shard_map/all_to_all | solution.py:807
  443.1 150.5 %reduce-scatter.10.cloned.1.call-start = ((), (), s32[]{:S(2)}) async-start(), calls=%async_computation.11 | async-start | bytes 1114112 | tf_op jit(solution)/shard_map/reduce_scatter | solution.py:856
  448.1 187.5 %reduce-scatter.8.cloned.1.call-start = ((), (), s32[]{:S(2)}) async-start(), calls=%async_computation.10 | async-start | bytes 1769472 | tf_op jit(solution)/shard_map/reduce_scatter | solution.py:854
  574.2 157.6 %reduce-scatter.14.cloned.1.call-start = ((), (), s32[]{:S(2)}) async-start(), calls=%async_computation.13 | async-start | bytes 4456448 | tf_op jit(solution)/shard_map/reduce_scatter | solution.py:866
  575.0 253.9 %reduce-scatter.12.cloned.1.call-start = ((), (), s32[]{:S(2)}) async-start(), calls=%async_computation.12 | async-start | bytes 4456448 | tf_op jit(solution)/shard_map/reduce_scatter | solution.py:858
  575.7 300.6 %reduce-scatter.16.cloned.1.call-start = ((), (), s32[]{:S(2)}) async-start(), calls=%async_computation.18 | async-start | bytes 5406720
  733.0 97.0 %collective-permute-start.14 = (bf16[2,128,256]{1,2,0:T(8,128)(2,1)S(1)}, bf16[2,128,256]{1,2,0:T(8,128)(2,1)S(1)}, u32[]{:S(2)}, u32[]{:S(2)}) collective-permute-start(bf16[2,128,256]{1,2,0:T(8,128)(2,1)S(1)} %copy.282), channel_id=1, source_target_pairs={{0,1},{1,0},{2,3},{3,2},{4,5},{5,4},{6,7},{7,6},{8,9},{9,8},{10,11... | collective-permute-start | bytes 393224 | tf_op jit(solution)/shard_map/ppermute | solution.py:740
  733.2 144.8 %copy-start.1 = (bf16[512,1024]{0,1:T(8,128)(2,1)S(1)}, bf16[512,1024]{0,1:T(8,128)(2,1)}, u32[]{:S(2)}) copy-start(bf16[512,1024]{0,1:T(8,128)(2,1)} %copy-done) | copy-start | bytes 3145732
  733.2 144.8 %copy-start.29 = (f32[528]{0:T(1024)S(1)}, f32[528]{0:T(1024)}, u32[]{:S(2)}) copy-start(f32[528]{0:T(1024)} %copy-done.28) | copy-start | bytes 6340
  733.2 144.8 %copy-start.31 = (f32[1024]{0:T(1024)S(1)}, f32[1024]{0:T(1024)}, u32[]{:S(2)}) copy-start(f32[1024]{0:T(1024)} %copy-done.30) | copy-start | bytes 12292
  733.2 144.8 %copy-start.33 = (f32[528]{0:T(1024)S(1)}, f32[528]{0:T(1024)}, u32[]{:S(2)}) copy-start(f32[528]{0:T(1024)} %copy-done.32) | copy-start | bytes 6340
  829.9 1.4 collective-permute-start.13
  879.5 1.3 collective-permute-start.8
  880.8 4.2 collective-permute-start.9
  885.1 4.2 collective-permute-start.10
  889.3 6.2 collective-permute-start.11
  895.5 7.8 collective-permute-start.12
  (35 other events, 374.8 us)
Sparse Core Ops, SparseCore 0:
  15.8 47.7 all-gather.11
  67.6 49.4 all-gather.9
  119.8 57.3 all-gather.13
  180.4 76.3 all-gather.17
  260.0 74.6 all-gather.15
  448.2 77.8 reduce-scatter.9
  574.3 61.1 reduce-scatter.7
  637.8 94.0 reduce-scatter.13
  734.2 94.7 reduce-scatter.11
  831.3 44.9 reduce-scatter.15

commit v2 on v1

v2 whole, which is shorter than its diff:
```python
import functools
import math

import jax
import jax.numpy as jnp
import numpy as np
from jax import lax
from jax.experimental import pallas as pl
from jax.experimental.pallas import tpu as pltpu
from jax.sharding import PartitionSpec as P

D = 1024
HEADS = 16
HEAD = 64
FF = 4096
GRID = 16
PATCHES = GRID * GRID
ROW_FRAME = PATCHES + 2
PAIRS = HEAD // 3 // 2
EXTRA = 16

EPSILON = 1e-06
SCALE2 = 0.125 * math.log2(math.e)
MASKED = -8e9
FAR = 1 << 20
VMEM = 60 * 1024 * 1024
BF = jnp.bfloat16
F32 = jnp.float32


def nn(left, right):
    return lax.dot_general(left, right, (((1,), (0,)), ((), ())), preferred_element_type=F32)


def nt(left, right):
    return lax.dot_general(left, right, (((1,), (1,)), ((), ())), preferred_element_type=F32)


def tn(left, right):
    return lax.dot_general(left, right, (((0,), (0,)), ((), ())), preferred_element_type=F32)


def qkv_kernel(normed, weight, bias, turn, cosine, sine, q_out, k_out, v_out, turned, turned_bias):
    width = q_out.shape[-1]
    half = width // 2

    @pl.when(pl.program_id(0) == 0)
    def _():
        for part in range(2):
            span = slice(part * width, (part + 1) * width)
            turned[:, span] = nn(weight[:, span], turn[...]).astype(BF)
            turned_bias[:, span] = nn(bias[:, span], turn[...])

    rows = normed[0]
    cos = cosine[0]
    sin = sine[0]
    for part, out in ((0, q_out), (1, k_out)):
        span = slice(part * width, (part + 1) * width)
        value = nn(rows, turned[:, span]) + turned_bias[:1, span]
        first = value[:, :half]
        second = value[:, half:]
        out[0, :, :half] = (first * cos - second * sin).astype(BF)
        out[0, :, half:] = (second * cos + first * sin).astype(BF)
    span = slice(2 * width, 3 * width)
    v_out[0] = (nn(rows, weight[:, span]) + bias[:1, span].astype(F32)).astype(BF)


def qkv_call(normed, weight, bias, turn, cosine, sine):
    sources, rows, _ = normed.shape
    width = weight.shape[1] // 3
    half = width // 2
    block = pl.BlockSpec((1, rows, width), lambda s: (s, 0, 0))
    table = pl.BlockSpec((1, rows, half), lambda s: (s, 0, 0))

    def whole(shape):
        return pl.BlockSpec(shape, lambda s: (0,) * len(shape))

    shape = jax.ShapeDtypeStruct((sources, rows, width), BF)
    return pl.pallas_call(
        qkv_kernel,
        grid=(sources,),
        in_specs=[
            pl.BlockSpec((1, rows, D), lambda s: (s, 0, 0)),
            whole(weight.shape),
            whole(bias.shape),
            whole(turn.shape),
            table,
            table,
        ],
        out_specs=[block] * 3,
        out_shape=[shape] * 3,
        scratch_shapes=[pltpu.VMEM((D, 2 * width), BF), pltpu.VMEM((bias.shape[0], 2 * width), F32)],
        compiler_params=pltpu.CompilerParams(vmem_limit_bytes=VMEM),
        cost_estimate=pl.CostEstimate(
            flops=2 * sources * rows * D * 3 * width, bytes_accessed=4 * sources * rows * D, transcendentals=0
        ),
        name="qkv_rotary",
    )(normed, weight, bias, turn, cosine, sine)


def turned_lanes(width, head):
    lane = lax.broadcasted_iota(jnp.int32, (1, width), 1)
    return (lane % (width // 2)) // (HEAD // 2) == head


def plain_lanes(width, head):
    lane = lax.broadcasted_iota(jnp.int32, (1, width), 1)
    return lane // HEAD == head


def pick(mask, array):
    return jnp.where(mask, array, jnp.zeros((), array.dtype))


def stack_heads(array, lanes):
    width = array.shape[-1]
    return jnp.concatenate([pick(lanes(width, head), array) for head in range(width // HEAD)], 0)


def unstack_heads(array, lanes):
    width = array.shape[-1]
    heads = width // HEAD
    step = array.shape[0] // heads
    total = pick(lanes(width, 0), array[:step])
    for head in range(1, heads):
        total = total + pick(lanes(width, head), array[head * step : (head + 1) * step])
    return total


def head_rows(array, head):
    half = array.shape[0] // 2
    step = HEAD // 2
    return jnp.concatenate(
        [array[head * step : (head + 1) * step], array[half + head * step : half + (head + 1) * step]], 0
    )


def value_total(v, frames_local, sources):
    total = jnp.zeros((1, v.shape[-1]), F32)
    real = lax.broadcasted_iota(jnp.int32, (EXTRA, 1), 0) < 2 * frames_local
    for s in range(sources):
        for l in range(frames_local):
            total = total + jnp.sum(v[s, l * PATCHES : (l + 1) * PATCHES].astype(F32), 0, keepdims=True)
        total = total + jnp.sum(pick(real, v[s, frames_local * PATCHES :].astype(F32)), 0, keepdims=True)
    return total


def attend_kernel(
    frames_local,
    start,
    key_frame,
    query_start,
    query_frame,
    query_pad,
    q,
    k,
    v,
    mixed,
    exact,
    logs,
    logs_extra,
    v_t,
    queries,
    acc,
    acc_extra,
    state,
    state_extra,
):
    sources, _, width = q.shape
    heads = width // HEAD
    frames = sources * frames_local
    patch_rows = frames_local * PATCHES
    length = frames * ROW_FRAME

    def frame_ref(ref, g):
        return ref[g // frames_local, pl.ds(pl.multiple_of((g % frames_local) * PATCHES, PATCHES), PATCHES), :]

    for g in range(frames):
        s, l = g // frames_local, g % frames_local
        v_t[g] = v[s, l * PATCHES : (l + 1) * PATCHES].T
    k_extra = jnp.concatenate([k[s, patch_rows:] for s in range(sources)], 0)
    v_extra_t = jnp.concatenate([v[s, patch_rows:] for s in range(sources)], 0).T
    uniform = jnp.asarray(1.0 / length, BF).astype(F32) * value_total(v, frames_local, sources)
    key_at = key_frame[:, :1]

    def weigh(scores, top):
        return jnp.exp2((scores - top) * SCALE2)

    def mix(values_t, weights, head):
        return nn(values_t[head * HEAD : (head + 1) * HEAD], weights[:, head * PATCHES : (head + 1) * PATCHES])

    def one_frame(g, _):
        first = start[g]
        queries[...] = stack_heads(frame_ref(q, g), turned_lanes)
        allowed = (key_at >= first) & (key_at <= g)
        scores_extra = jnp.where(allowed, nt(k_extra, queries[...]), MASKED)
        scores = nt(frame_ref(k, g), queries[...])
        top = jnp.maximum(jnp.max(scores_extra, 0, keepdims=True), jnp.max(scores, 0, keepdims=True))
        weights_extra = weigh(scores_extra, top)
        weights = weigh(scores, top)
        state[0:1] = top
        state[1:2] = jnp.sum(weights_extra, 0, keepdims=True) + jnp.sum(weights, 0, keepdims=True)
        weights_extra = weights_extra.astype(BF)
        weights = weights.astype(BF)
        values_t = v_t[g]
        for head in range(heads):
            acc[head] = mix(v_extra_t, weights_extra, head) + mix(values_t, weights, head)

        def one_key(f, _):
            scores = nt(frame_ref(k, f), queries[...])
            before = state[0:1]
            top = jnp.maximum(before, jnp.max(scores, 0, keepdims=True))
            fade = weigh(before, top)
            weights = weigh(scores, top)
            state[0:1] = top
            state[1:2] = state[1:2] * fade + jnp.sum(weights, 0, keepdims=True)
            weights = weights.astype(BF)
            values_t = v_t[f]
            for head in range(heads):
                acc[head] = acc[head] * fade[:, head * PATCHES : (head + 1) * PATCHES] + mix(values_t, weights, head)
            return 0

        lax.fori_loop(first, g, one_key, 0)
        total = state[1:2]
        result = jnp.concatenate(
            [acc[head] / total[:, head * PATCHES : (head + 1) * PATCHES] for head in range(heads)], 0
        ).T
        result = jnp.where(first > frames, jnp.broadcast_to(uniform, result.shape), result)
        rows = pl.ds(pl.multiple_of((g % frames_local) * PATCHES, PATCHES), PATCHES)
        exact[g // frames_local, rows, :] = result
        mixed[g // frames_local, rows, :] = result.astype(BF)
        logs[g] = jnp.broadcast_to(state[0:1] + jnp.log2(total) * (1.0 / SCALE2), (8, heads * PATCHES))
        return 0

    lax.fori_loop(0, frames, one_frame, 0)

    q_extra = stack_heads(jnp.concatenate([q[s, patch_rows:] for s in range(sources)], 0), turned_lanes)
    queries[: q_extra.shape[0]] = q_extra
    first = jnp.concatenate([query_start[:1]] * heads, 1)
    last = jnp.concatenate([query_frame[:1]] * heads, 1)
    scores = jnp.where((key_at >= first) & (key_at <= last), nt(k_extra, q_extra), MASKED)
    top = jnp.max(scores, 0, keepdims=True)
    weights = weigh(scores, top)
    state_extra[0:1] = top
    state_extra[1:2] = jnp.sum(weights, 0, keepdims=True)
    acc_extra[...] = nn(v_extra_t, weights.astype(BF))

    def extra_key(f, _):
        visible = (first <= f) & (last >= f)
        scores = jnp.where(visible, nt(frame_ref(k, f), queries[: q_extra.shape[0]]), MASKED)
        before = state_extra[0:1]
        top = jnp.maximum(before, jnp.max(scores, 0, keepdims=True))
        fade = weigh(before, top)
        weights = weigh(scores, top)
        state_extra[0:1] = top
        state_extra[1:2] = state_extra[1:2] * fade + jnp.sum(weights, 0, keepdims=True)
        acc_extra[...] = acc_extra[...] * fade + nn(v_t[f], weights.astype(BF))
        return 0

    lax.fori_loop(0, frames, extra_key, 0)
    result = unstack_heads((acc_extra[...] / state_extra[1:2]).T, plain_lanes)
    result = jnp.where(query_pad[:, :1] > 0, jnp.broadcast_to(uniform, result.shape), result)
    for s in range(sources):
        exact[s, patch_rows:, :] = result[s * EXTRA : (s + 1) * EXTRA]
        mixed[s, patch_rows:, :] = result[s * EXTRA : (s + 1) * EXTRA].astype(BF)
    logs_extra[...] = jnp.broadcast_to(
        state_extra[0:1] + jnp.log2(state_extra[1:2]) * (1.0 / SCALE2), logs_extra.shape
    )


def attend_call(start, key_frame, query_start, query_frame, query_pad, q, k, v, waits=()):
    sources, rows, width = q.shape
    frames_local = rows // PATCHES
    frames = sources * frames_local
    heads = width // HEAD
    stacked = heads * sources * EXTRA
    vmem = pl.BlockSpec(memory_space=pltpu.VMEM)
    return pl.pallas_call(
        waiting(functools.partial(attend_kernel, frames_local), 8, waits),
        in_specs=[pl.BlockSpec(memory_space=pltpu.SMEM)] + [vmem] * 7 + [ANY_REF] * len(waits),
        out_specs=[vmem] * 4,
        out_shape=[
            jax.ShapeDtypeStruct(q.shape, BF),
            jax.ShapeDtypeStruct(q.shape, F32),
            jax.ShapeDtypeStruct((frames, 8, heads * PATCHES), F32),
            jax.ShapeDtypeStruct((8, stacked), F32),
        ],
        scratch_shapes=[
            pltpu.VMEM((frames, width, PATCHES), BF),
            pltpu.VMEM((heads * PATCHES, width), BF),
            pltpu.VMEM((heads, HEAD, PATCHES), F32),
            pltpu.VMEM((width, stacked), F32),
            pltpu.VMEM((8, heads * PATCHES), F32),
            pltpu.VMEM((8, stacked), F32),
        ],
        compiler_params=pltpu.CompilerParams(vmem_limit_bytes=VMEM),
        cost_estimate=cost(
            flops=8 * heads * 256 * frames * frames * PATCHES * PATCHES // 2,
            bytes_accessed=10 * sources * rows * width,
            transcendentals=heads * frames * frames * PATCHES * PATCHES // 2,
        ),
        name="attend",
    )(start, key_frame, query_start, query_frame, query_pad, q, k, v, *waits)


def attend_back_kernel(
    frames_local,
    start,
    key_frame,
    query_start,
    query_frame,
    query_pad,
    q,
    k,
    v,
    grad,
    exact,
    logs,
    logs_extra,
    cosine,
    sine,
    turn,
    out,
    k_t,
    queries,
    grads,
    dq_t,
    dk,
    dv,
    dq_extra,
    dk_extra,
    dv_extra,
    centers,
):
    sources, _, width = q.shape
    half = width // 2
    heads = width // HEAD
    frames = sources * frames_local
    patch_rows = frames_local * PATCHES
    length = frames * ROW_FRAME
    step_rows = HEAD // 2

    def frame_ref(ref, g):
        return ref[g // frames_local, pl.ds(pl.multiple_of((g % frames_local) * PATCHES, PATCHES), PATCHES), :]

    which = lax.broadcasted_iota(jnp.int32, (8, width), 0)
    lane = lax.broadcasted_iota(jnp.int32, (8, width), 1)
    groups = (lane // HEAD == which).astype(BF)

    def center_of(grad_rows, exact_rows):
        product = grad_rows.astype(F32) * exact_rows
        high = product.astype(BF)
        low = (product - high.astype(F32)).astype(BF)
        center = nt(groups, high) + nt(groups, low)
        return jnp.concatenate([center[head : head + 1] for head in range(heads)], 1)

    def gather_extra(ref):
        return jnp.concatenate([ref[s, patch_rows:] for s in range(sources)], 0)

    for g in range(frames):
        s, l = g // frames_local, g % frames_local
        k_t[g] = k[s, l * PATCHES : (l + 1) * PATCHES].T
    k_extra = gather_extra(k)
    v_extra = gather_extra(v)
    k_extra_t = k_extra.T
    dk[...] = jnp.zeros_like(dk)
    dv[...] = jnp.zeros_like(dv)
    dk_extra[...] = jnp.zeros_like(dk_extra)
    dv_extra[...] = jnp.zeros_like(dv_extra)
    key_at = key_frame[:, :1]

    def tile(keys, values, query, query_grad, log, center, allowed):
        scores = nt(keys, query)
        inner = nt(values, query_grad)
        probs = jnp.exp2((scores - log) * SCALE2)
        if allowed is not None:
            probs = jnp.where(allowed, probs, 0.0)
        change = (probs * (inner - center)).astype(BF)
        return nn(probs.astype(BF), query_grad), nn(change, query), change

    def add_dq(ref, keys_t, change, keep):
        for head in range(heads):
            part = nn(head_rows(keys_t, head), change[:, head * PATCHES : (head + 1) * PATCHES])
            for side in range(2):
                rows = slice(side * half + head * step_rows, side * half + (head + 1) * step_rows)
                piece = part[side * step_rows : (side + 1) * step_rows]
                ref[rows] = ref[rows] + piece if keep else piece

    def one_frame(g, pad_grad):
        first = start[g]
        grad_rows = frame_ref(grad, g)
        queries[...] = stack_heads(frame_ref(q, g), turned_lanes)
        grads[...] = stack_heads(grad_rows, plain_lanes)
        centers[...] = jnp.broadcast_to(center_of(grad_rows, frame_ref(exact, g)), centers.shape)
        allowed = (key_at >= first) & (key_at <= g)
        dv_part, dk_part, change = tile(
            k_extra, v_extra, queries[...], grads[...], logs[g, :1], centers[:1], allowed
        )
        dv_extra[...] += dv_part
        dk_extra[...] += dk_part
        add_dq(dq_t.at[g], k_extra_t, change, False)

        def one_key(f, _):
            dv_part, dk_part, change = tile(
                frame_ref(k, f), frame_ref(v, f), queries[...], grads[...], logs[g, :1], centers[:1], None
            )
            dv[f] += dv_part
            dk[f] += dk_part
            add_dq(dq_t.at[g], k_t[f], change, True)
            return 0

        lax.fori_loop(first, g + 1, one_key, 0)
        return pad_grad + jnp.where(first > frames, jnp.sum(grad_rows.astype(F32), 0, keepdims=True), 0.0)

    pad_grad = lax.fori_loop(0, frames, one_frame, jnp.zeros((1, width), F32))
    g_extra = gather_extra(grad)
    pad_grad = pad_grad + jnp.sum(jnp.where(query_pad[:, :1] > 0, g_extra.astype(F32), 0.0), 0, keepdims=True)
    pad_grad = pad_grad * jnp.asarray(1.0 / length, BF).astype(F32)

    q_stack = stack_heads(gather_extra(q), turned_lanes)
    g_stack = stack_heads(g_extra, plain_lanes)
    stacked = q_stack.shape[0]
    queries[:stacked] = q_stack
    grads[:stacked] = g_stack
    first = jnp.concatenate([query_start[:1]] * heads, 1)
    last = jnp.concatenate([query_frame[:1]] * heads, 1)
    log = logs_extra[:1]
    center = center_of(g_extra, gather_extra(exact))
    allowed = (key_at >= first) & (key_at <= last)
    dv_part, dk_part, change = tile(k_extra, v_extra, q_stack, g_stack, log, center, allowed)
    dv_extra[...] += dv_part
    dk_extra[...] += dk_part
    dq_extra[...] = nn(k_extra_t, change)

    def extra_key(f, _):
        visible = (first <= f) & (last >= f)
        dv_part, dk_part, change = tile(
            frame_ref(k, f), frame_ref(v, f), queries[:stacked], grads[:stacked], log, center, visible
        )
        dv[f] += dv_part
        dk[f] += dk_part
        dq_extra[...] += nn(k_t[f], change)
        return 0

    lax.fori_loop(0, frames, extra_key, 0)

    def emit(s, rows, dq_rows, dk_rows, dv_rows, real=None):
        cos = cosine[s, rows]
        sin = sine[s, rows]
        for part, array in ((0, dq_rows), (1, dk_rows)):
            a = array[:, :half] * 0.125
            b = array[:, half:] * 0.125
            both = jnp.concatenate([(a * cos + b * sin).astype(BF), (b * cos - a * sin).astype(BF)], 1)
            both = nt(both, turn[...])
            if real is not None:
                both = pick(real, both)
            out[s, rows, part * width : (part + 1) * width] = both.astype(BF)
        total = dv_rows + pad_grad
        if real is not None:
            total = pick(real, total)
        out[s, rows, 2 * width :] = total.astype(BF)

    def emit_frame(g, _):
        rows = pl.ds(pl.multiple_of((g % frames_local) * PATCHES, PATCHES), PATCHES)
        emit(g // frames_local, rows, dq_t[g].T, dk[g], dv[g])
        return 0

    lax.fori_loop(0, frames, emit_frame, 0)
    dq_rows = unstack_heads(dq_extra[...].T, turned_lanes)
    real = lax.broadcasted_iota(jnp.int32, (EXTRA, 1), 0) < 2 * frames_local
    for s in range(sources):
        at = slice(s * EXTRA, (s + 1) * EXTRA)
        emit(s, slice(patch_rows, patch_rows + EXTRA), dq_rows[at], dk_extra[at], dv_extra[at], real)


def attend_back_call(
    start, key_frame, query_start, query_frame, query_pad, q, k, v, grad, exact, logs, logs_extra, cosine, sine, turn, waits=()
):
    sources, rows, width = q.shape
    frames_local = rows // PATCHES
    frames = sources * frames_local
    extra = sources * EXTRA
    heads = width // HEAD
    vmem = pl.BlockSpec(memory_space=pltpu.VMEM)
    return pl.pallas_call(
        waiting(functools.partial(attend_back_kernel, frames_local), 15, waits),
        in_specs=[pl.BlockSpec(memory_space=pltpu.SMEM)] + [vmem] * 14 + [ANY_REF] * len(waits),
        out_specs=vmem,
        out_shape=jax.ShapeDtypeStruct((sources, rows, 3 * width), BF),
        scratch_shapes=[
            pltpu.VMEM((frames, width, PATCHES), BF),
            pltpu.VMEM((heads * PATCHES, width), BF),
            pltpu.VMEM((heads * PATCHES, width), BF),
            pltpu.VMEM((frames, width, PATCHES), F32),
            pltpu.VMEM((frames, PATCHES, width), F32),
            pltpu.VMEM((frames, PATCHES, width), F32),
            pltpu.VMEM((width, heads * extra), F32),
            pltpu.VMEM((extra, width), F32),
            pltpu.VMEM((extra, width), F32),
            pltpu.VMEM((8, heads * PATCHES), F32),
        ],
        compiler_params=pltpu.CompilerParams(vmem_limit_bytes=VMEM),
        cost_estimate=cost(
            flops=20 * heads * 256 * frames * frames * PATCHES * PATCHES // 2,
            bytes_accessed=20 * sources * rows * width,
            transcendentals=heads * frames * frames * PATCHES * PATCHES // 2,
        ),
        name="attend_back",
    )(start, key_frame, query_start, query_frame, query_pad, q, k, v, grad, exact, logs, logs_extra, cosine, sine, turn, *waits)


def gelu_parts(hidden):
    base = 1.0 + (0.3275911 * math.sqrt(0.5)) * jnp.abs(hidden)
    guess = pl.reciprocal(base, approx=True)
    t = guess * (2.0 - base * guess)
    bell = jnp.exp2(hidden * hidden * (-0.5 * math.log2(math.e)))
    poly = 0.5 * 1.061405429
    for coefficient in (-1.453152027, 1.421413741, -0.284496736, 0.254829592):
        poly = poly * t + 0.5 * coefficient
    tail = poly * t * bell
    cdf = jnp.where(hidden < 0.0, tail, 1.0 - tail)
    return hidden * cdf, cdf + hidden * bell * (1.0 / math.sqrt(2.0 * math.pi))


def feed_body(chunk, second, outer, outer_t, weight_in, weight_out, add, final, second_grad, d_bias, second_t, active, slope):
    rows = second.shape[0]

    @pl.when(pl.program_id(0) == 0)
    def _():
        for r in range(0, rows, chunk):
            second_t[:, r : r + chunk] = second[r : r + chunk].T
        final[...] = jnp.zeros_like(final)
        second_grad[...] = jnp.zeros_like(second_grad)

    d_bias[...] = jnp.zeros_like(d_bias)
    for r in range(0, rows, chunk):
        at = slice(r, r + chunk)
        act, gradient = gelu_parts(nn(second[at], weight_in[...]) + add)
        act = act.astype(BF)
        grad = (nt(outer[at], weight_out[...]) * gradient).astype(BF)
        active[at] = act
        slope[at] = grad
        d_bias[0] += jnp.sum(grad.astype(F32), 0, keepdims=True)
        final[at] += nn(act, weight_out[...])
        second_grad[at] += nt(grad, weight_in[...])
    return nn(second_t[...], slope[...]).astype(BF), nn(outer_t[...], active[...]).astype(BF)


def feed_plain_kernel(
    chunk, second, outer, outer_t, expand, expand_bias, reduce, final, second_grad, d_bias, d_expand, d_reduce, second_t, active, slope
):
    d_expand[0], d_reduce[0] = feed_body(
        chunk, second, outer, outer_t, expand.at[0], reduce.at[0], expand_bias[0].astype(F32),
        final, second_grad, d_bias, second_t, active, slope,
    )


def feed_call(second, outer, outer_t, expand, expand_bias, reduce):
    rows = second.shape[0]
    tiles, _, wide = expand.shape
    chunk = rows // 2

    def whole(shape):
        return pl.BlockSpec(shape, lambda t: (0,) * len(shape))

    def tiled(shape):
        return pl.BlockSpec((1,) + shape[1:], lambda t: (t, 0, 0))

    return pl.pallas_call(
        functools.partial(feed_plain_kernel, chunk),
        grid=(tiles,),
        in_specs=[
            whole((rows, D)),
            whole((rows, D)),
            whole((D, rows)),
            tiled(expand.shape),
            tiled(expand_bias.shape),
            tiled(reduce.shape),
        ],
        out_specs=[whole((rows, D)), whole((rows, D)), tiled((tiles, 1, wide))] + [tiled((tiles, D, wide))] * 2,
        out_shape=[
            jax.ShapeDtypeStruct((rows, D), F32),
            jax.ShapeDtypeStruct((rows, D), F32),
            jax.ShapeDtypeStruct((tiles, 1, wide), F32),
        ]
        + [jax.ShapeDtypeStruct((tiles, D, wide), BF)] * 2,
        scratch_shapes=[pltpu.VMEM((D, rows), BF), pltpu.VMEM((rows, wide), BF), pltpu.VMEM((rows, wide), BF)],
        compiler_params=pltpu.CompilerParams(vmem_limit_bytes=VMEM),
        cost_estimate=pl.CostEstimate(
            flops=10 * rows * D * wide * tiles,
            bytes_accessed=8 * D * wide * tiles + 14 * rows * D,
            transcendentals=2 * rows * wide * tiles,
        ),
        name="feed_forward",
    )(second, outer, outer_t, expand, expand_bias, reduce)


def norm_parts(values):
    center = values - jnp.mean(values, -1, keepdims=True)
    scale = lax.rsqrt(jnp.mean(center * center, -1, keepdims=True) + EPSILON)
    return center * scale, scale


def norm_back(grad, unit, scale, gain):
    scaled = grad * gain
    mean_one = jnp.mean(scaled, -1, keepdims=True)
    mean_two = jnp.mean(scaled * unit, -1, keepdims=True)
    return scale * (scaled - mean_one - unit * mean_two)


def to_block(array, frames_local):
    split = array.reshape(frames_local, ROW_FRAME, D)
    return jnp.concatenate(
        [
            split[:, 2:].reshape(frames_local * PATCHES, D),
            split[:, :2].reshape(frames_local * 2, D),
            jnp.zeros((EXTRA - 2 * frames_local, D), array.dtype),
        ],
        0,
    )


def from_block(array, frames_local):
    patches = array[: frames_local * PATCHES].reshape(frames_local, PATCHES, D)
    extra = array[frames_local * PATCHES : frames_local * ROW_FRAME].reshape(frames_local, 2, D)
    return jnp.concatenate([extra, patches], 1).reshape(1, frames_local * ROW_FRAME, D)


def rows_of(per_frame, per_extra, sources, frames_local, fill):
    patches = jnp.broadcast_to(per_frame.reshape(sources, frames_local, 1), (sources, frames_local, PATCHES))
    pad = jnp.full((sources, EXTRA - 2 * frames_local), fill, per_frame.dtype)
    return jnp.concatenate(
        [patches.reshape(sources, -1), per_extra.reshape(sources, 2 * frames_local), pad], 1
    )


def tables(counts, present, sources, frames_local, heads):
    frames = sources * frames_local
    at = jnp.arange(frames, dtype=jnp.int32)
    first, second = counts[0], counts[1]
    inside = at < first + second
    start = jnp.where(at < first, 0, first).astype(jnp.int32)
    time = (at - start).astype(F32)
    begin = jnp.where(inside, start, FAR)
    live_extra = inside[:, None] & (present == 1)
    time_rows = rows_of(time, jnp.repeat(time, 2), sources, frames_local, 0.0)
    live_rows = rows_of(inside.astype(F32), live_extra.astype(F32), sources, frames_local, 0.0)

    patch = np.arange(PATCHES)
    grid_row = np.zeros(frames_local * PATCHES + EXTRA, np.float32)
    grid_col = np.zeros(frames_local * PATCHES + EXTRA, np.float32)
    for l in range(frames_local):
        grid_row[l * PATCHES : (l + 1) * PATCHES] = patch // GRID
        grid_col[l * PATCHES : (l + 1) * PATCHES] = patch % GRID
    lanes = np.zeros((3, HEAD // 2), np.float32)
    freq = 10000.0 ** (-np.arange(PAIRS, dtype=np.float32) / PAIRS)
    for a in range(3):
        lanes[a, a * PAIRS : (a + 1) * PAIRS] = freq
    lanes = np.tile(lanes, (1, heads))
    angle = time_rows[:, :, None] * lanes[0] + (grid_row[:, None] * lanes[1] + grid_col[:, None] * lanes[2])[None]

    def extra_of(per_frame, fill):
        both = jnp.repeat(per_frame, 2).reshape(sources, 2 * frames_local)
        pad = jnp.full((sources, EXTRA - 2 * frames_local), fill, both.dtype)
        return jnp.concatenate([both, pad], 1).reshape(-1)

    extra = sources * EXTRA
    key_frame = jnp.where(live_extra, at[:, None], -1).reshape(sources, 2 * frames_local)
    key_frame = jnp.concatenate(
        [key_frame, jnp.full((sources, EXTRA - 2 * frames_local), -1, jnp.int32)], 1
    ).reshape(-1)
    query_start = extra_of(begin, FAR)
    query_frame = extra_of(at, -1)

    def column(vector):
        return jnp.broadcast_to(vector[:, None], (extra, 128))

    def row(vector):
        return jnp.broadcast_to(vector[None], (8, extra))

    return (
        live_rows,
        jnp.cos(angle),
        jnp.sin(angle),
        (begin, column(key_frame), row(query_start), row(query_frame), column((query_start == FAR).astype(jnp.int32))),
    )


def turn_matrix(width):
    turn = np.zeros((width, width), np.float32)
    step = HEAD // 2
    for h in range(width // HEAD):
        for d in range(HEAD):
            if d < 6 * PAIRS:
                a, rest = divmod(d, 2 * PAIRS)
                side, k = divmod(rest, PAIRS)
                to = side * (width // 2) + h * step + a * PAIRS + k
            else:
                side, k = divmod(d - 6 * PAIRS, step - 3 * PAIRS)
                to = side * (width // 2) + h * step + 3 * PAIRS + k
            turn[h * HEAD + d, to] = 1.0
    return turn


SMEM_REF = pl.BlockSpec(memory_space=pltpu.SMEM)
VMEM_REF = pl.BlockSpec(memory_space=pltpu.VMEM)


ANY_REF = pl.BlockSpec(memory_space=pl.ANY)


def cost(flops=0, bytes_accessed=0, transcendentals=0):
    return pl.CostEstimate(flops=flops, bytes_accessed=bytes_accessed, transcendentals=transcendentals)


def waiting(kernel, inputs, waits, carried=0, outputs=None):
    if not waits:
        return kernel

    def run(*refs):
        used = [*refs[:inputs], *refs[inputs + len(waits) :]]
        if carried:
            del used[inputs + outputs : inputs + outputs + carried]
        kernel(*used)

    return run


def local_call(kernel, name, inputs, outputs, scratch=(), smem=0, flops=0, transcendentals=0, waits=(), carry=()):
    first = len(inputs) + len(waits)
    waits = [*waits, *carry]
    size = sum(math.prod(a.shape) * a.dtype.itemsize for a in [*inputs, *outputs])
    return pl.pallas_call(
        waiting(kernel, len(inputs), waits, len(carry), len(outputs)),
        in_specs=[SMEM_REF] * smem + [VMEM_REF] * (len(inputs) - smem) + [ANY_REF] * len(waits),
        out_specs=[VMEM_REF] * len(outputs) + [ANY_REF] * len(carry),
        out_shape=[*outputs] + [shape_of(*c.shape, dtype=c.dtype) for c in carry],
        input_output_aliases={first + i: len(outputs) + i for i in range(len(carry))},
        scratch_shapes=list(scratch),
        compiler_params=pltpu.CompilerParams(vmem_limit_bytes=VMEM),
        cost_estimate=cost(flops=flops, bytes_accessed=size, transcendentals=transcendentals),
        name=name,
    )(*inputs, *waits)


def shape_of(*shape, dtype=BF):
    return jax.ShapeDtypeStruct(shape, dtype)


def stack_kernel(*refs):
    for i, ref in enumerate(refs[:-1]):
        refs[-1][i] = ref[...]


def stack_call(pieces, waits=()):
    return local_call(stack_kernel, "stack", pieces, [shape_of(len(pieces), *pieces[0].shape)], waits=waits)[0]


def copy_kernel(source, out):
    out[...] = source[...]


def copy_call(array, waits):
    return local_call(copy_kernel, "copy", [array], [shape_of(*array.shape)], waits=waits)[0]


def add_kernel(*refs):
    total = refs[0][...].astype(F32)
    for ref in refs[1:-1]:
        total = total + ref[...].astype(F32)
    refs[-1][...] = total.astype(refs[-1].dtype)


def add_call(pieces, waits=(), dtype=BF):
    return local_call(add_kernel, "add", pieces, [shape_of(*pieces[0].shape, dtype=dtype)], waits=waits)[0]


def span(index, size):
    return pl.ds(pl.multiple_of(index * size, size), size)


def front_kernel(*refs):
    *parts, entered, near, entered_out = refs
    for s, ref in enumerate(parts):
        near[s] = ref[...]
    entered_out[...] = entered[...]


def pack_kernel(n_z, place, near, far, own, one, two, three, vectors, bias, expand_bias):
    y, z, shard = place[1], place[2], place[4]
    rows = own.shape[0]
    width = bias.shape[1] // 3
    part = near.shape[2]
    chunks = part // 128
    d_part = D // (2 * n_z)
    outs = (own, one, two, three)

    def source(dp):
        return (dp % 2) ^ y, (z - dp // 2 + n_z) % n_z

    for m in range(4):
        target = shard ^ m
        for i in range(3 * width // 128):
            j = (i // 2) * (D // 128) + 2 * target + i % 2
            side, s = source(j // chunks)
            lanes = pl.ds(pl.multiple_of((j % chunks) * 128, 128), 128)
            at = slice(i * 128, (i + 1) * 128)

            @pl.when(side == 0)
            def _(m=m, s=s, lanes=lanes, at=at):
                outs[m][:, at] = near[s, :rows, lanes]

            @pl.when(side == 1)
            def _(m=m, s=s, lanes=lanes, at=at):
                outs[m][:, at] = far[s, :rows, lanes]

            if m == 0:

                @pl.when(side == 0)
                def _(s=s, lanes=lanes, at=at):
                    bias[:, at] = near[s, rows + 6 : rows + 7, lanes].astype(F32)

                @pl.when(side == 1)
                def _(s=s, lanes=lanes, at=at):
                    bias[:, at] = far[s, rows + 6 : rows + 7, lanes].astype(F32)

    quarter = FF // (8 * n_z)
    for s in range(n_z):
        for side, ref in ((0, near), (1, far)):
            dp = 2 * ((z - s + n_z) % n_z) + (y ^ side)
            block = ref[s, rows : rows + 16].astype(F32)
            vectors[:, span(dp, d_part)] = block[:8, :d_part]
            picked = block[7:8, :quarter]
            for f in range(1, 4):
                picked = jnp.where(shard == f, block[7 + f : 8 + f, :quarter], picked)
            expand_bias[s, :, side * quarter : (side + 1) * quarter] = picked


def enter_kernel(place, e0, e1, e2, e3, w0, w1, w2, w3, bias, vectors, turn, cosine, sine, q, k, v, normed, triple, scratch, entered, weight, add):
    shard = place[4]
    width = q.shape[-1]
    half = width // 2
    step = pl.program_id(0)

    @pl.when(step == 0)
    def _():
        for m, ref in enumerate((w0, w1, w2, w3)):
            rows = span(shard ^ m, ref.shape[0])
            triple[rows, :] = ref[...]
            for part in range(2):
                at = slice(part * width, (part + 1) * width)
                weight[rows, at] = nn(ref[:, at], turn[...]).astype(BF)
            weight[rows, 2 * width :] = ref[:, 2 * width :]
        low = jnp.broadcast_to(bias[...], (8, 3 * width)).astype(BF)
        for part in range(2):
            at = slice(part * width, (part + 1) * width)
            add[:, at] = nn(low[:, at], turn[...])
        add[:, 2 * width :] = low[:, 2 * width :].astype(F32)

    for m, ref in enumerate((e0, e1, e2, e3)):

        @pl.when(step == m)
        def _(ref=ref):
            entered[...] = ref[...]

    values = entered[...].astype(F32)
    unit, _ = norm_parts(values)
    rows = (unit * vectors[0:1] + vectors[1:2]).astype(BF)
    normed[0] = rows
    scratch[...] = rows
    cos = cosine[0]
    sin = sine[0]
    for part, out in ((0, q), (1, k)):
        at = slice(part * width, (part + 1) * width)
        value = nn(scratch[...], weight[:, at]) + add[:1, at]
        first = value[:, :half]
        second = value[:, half:]
        out[0, :, :half] = (first * cos - second * sin).astype(BF)
        out[0, :, half:] = (second * cos + first * sin).astype(BF)
    v[0] = (nn(scratch[...], weight[:, 2 * width :]) + add[:1, 2 * width :]).astype(BF)


def enter_call(place, entered, weights, bias, vectors, turn, cosine, sine, waits):
    rows = entered[0].shape[0]
    width = bias.shape[-1] // 3

    def whole(array):
        return pl.BlockSpec(array.shape, lambda m, p: (0,) * array.ndim)

    def moved(*shape):
        return pl.BlockSpec((1,) + shape, lambda m, p: (p[4] ^ m, 0, 0))

    flat = [*entered, *weights, bias, vectors, turn]
    return pl.pallas_call(
        waiting(enter_kernel, 3 + len(flat), waits),
        grid_spec=pltpu.PrefetchScalarGridSpec(
            num_scalar_prefetch=1,
            grid=(4,),
            in_specs=[whole(a) for a in flat] + [moved(rows, width // 2)] * 2 + [ANY_REF] * len(waits),
            out_specs=[moved(rows, width)] * 3
            + [moved(rows, D), pl.BlockSpec((D, 3 * width), lambda m, p: (0, 0))],
            scratch_shapes=[
                pltpu.VMEM((rows, D), BF),
                pltpu.VMEM((rows, D), BF),
                pltpu.VMEM((D, 3 * width), BF),
                pltpu.VMEM((8, 3 * width), F32),
            ],
        ),
        out_shape=[shape_of(4, rows, width)] * 3 + [shape_of(4, rows, D), shape_of(D, 3 * width)],
        compiler_params=pltpu.CompilerParams(vmem_limit_bytes=VMEM),
        cost_estimate=cost(flops=8 * rows * D * 3 * width, bytes_accessed=30 * rows * D, transcendentals=0),
        name="enter",
    )(place, *flat, cosine, sine, *waits)


def part_kernel(place, mixed, own, far):
    x = place[0]
    for core in range(2):
        own[core] = mixed[2 * x + core]
        far[core] = mixed[2 * (1 - x) + core]


def project_kernel(place, own, far, output, keep, give, weight):
    x, core = place[0], place[3]
    _, rows, width = own.shape
    n_z = output.shape[0]
    d_part = output.shape[-1]
    for z in range(n_z):
        for y in range(2):
            at = (2 * z + y) * d_part
            for source in range(2):
                weight[source * width : (source + 1) * width, at : at + d_part] = output[z, y, source]

    def part(at):
        return nn(own[at], weight[span(x, width), :]) + nn(far[at], weight[span(1 - x, width), :])

    give[...] = part(1 - core).astype(BF)
    keep[...] = part(core)


def middle_kernel(entered, keep, other, vectors, middle, second):
    values = entered[...].astype(F32) + keep[...] + other[...].astype(F32) + vectors[2:3]
    middle[...] = values
    unit, _ = norm_parts(values)
    second[...] = (unit * vectors[3:4] + vectors[4:5]).astype(BF)


def rows_call(kernel, name, inputs, outputs, blocks=3, waits=()):
    rows = max(a.shape[0] for a in inputs)
    step = rows // blocks

    def spec(array):
        if array.shape[0] == 8:
            return pl.BlockSpec(array.shape, lambda i: (0, 0))
        return pl.BlockSpec((step, array.shape[1]), lambda i: (i, 0))

    size = sum(math.prod(a.shape) * a.dtype.itemsize for a in [*inputs, *outputs])
    return pl.pallas_call(
        waiting(kernel, len(inputs), waits),
        grid=(blocks,),
        in_specs=[spec(a) for a in inputs] + [ANY_REF] * len(waits),
        out_specs=[spec(a) for a in outputs],
        out_shape=list(outputs),
        compiler_params=pltpu.CompilerParams(vmem_limit_bytes=VMEM),
        cost_estimate=cost(flops=20 * rows * D, bytes_accessed=size, transcendentals=0),
        name=name,
    )(*inputs, *waits)


def add_rows(ref, rows):
    @pl.when(pl.program_id(0) == 0)
    def _():
        ref[...] = jnp.zeros_like(ref)

    for i, row in enumerate(rows):
        ref[i : i + 1] += jnp.sum(row, 0, keepdims=True)


def middle_back_kernel(middle, outer, keep, other, far, vectors, middle_grad, branch, sums):
    unit, scale = norm_parts(middle[...])
    grad = keep[...] + other[...].astype(F32) + far[...].astype(F32)
    result = outer[...].astype(F32) + norm_back(grad, unit, scale, vectors[3:4])
    middle_grad[...] = result
    low = result.astype(BF)
    branch[...] = low
    add_rows(sums, (low.astype(F32), grad * unit, grad, outer[...].astype(F32)))


def leave_rows(values, frames_local):
    pieces = []
    for l in range(frames_local):
        at = frames_local * PATCHES + 2 * l
        pieces += [values[at : at + 2], values[l * PATCHES : (l + 1) * PATCHES]]
    return jnp.concatenate(pieces, 0)


def output_kernel(frames_local, middle, keep, other, far, live, vectors, out):
    values = middle[...] + keep[...] + other[...].astype(F32) + far[...].astype(F32) + vectors[5:6]
    values = values * live[...]
    out[...] = leave_rows(values, frames_local).astype(BF)


def mixed_grad_kernel(place, branch, branch_other, weight, own, far):
    x, core = place[0], place[3]
    width = own.shape[-1]
    for at, rows in ((core, branch), (1 - core, branch_other)):
        own[at] = nt(rows[...], weight[span(x, width), :]).astype(BF)
        far[at] = nt(rows[...], weight[span(1 - x, width), :]).astype(BF)


def output_grad_kernel(place, own, far, branch, branch_other, near_y, far_y, rows_all, held):
    y, z, core = place[1], place[2], place[3]
    _, rows, width = own.shape
    _, n_z, _, d_part = near_y.shape
    rows_all[span(core, rows), :] = branch[...]
    rows_all[span(1 - core, rows), :] = branch_other[...]
    for i, ref in enumerate((own, far)):
        held[...] = tn(ref[...].reshape(2 * rows, width), rows_all[...]).astype(BF)
        for s in range(n_z):
            for flip, out in ((0, near_y), (1, far_y)):
                out[i, s] = held[:, span(2 * ((z + s) % n_z) + (y ^ flip), d_part)]


def triple_kernel(
    place, normed, triple_grad, grad_rows, triple, e0, e1, e2, e3, own, one, two, three, rows_own, rows_far, rows_give, bias, sums, entered
):
    step = pl.program_id(0)
    count, rows, wide = triple_grad.shape
    flat = triple_grad[...].reshape(count * rows, wide)
    grad = tn(normed[...].reshape(count * rows, normed.shape[-1]), flat).astype(BF)
    back = nt(grad_rows[0], triple[...])
    low = back.astype(BF)
    outs = (own, one, two, three)
    rows_outs = (rows_own, rows_give.at[0], rows_far, rows_give.at[1])
    for m, ref in enumerate((e0, e1, e2, e3)):

        @pl.when(step == m)
        def _(m=m, ref=ref):
            outs[m][...] = grad
            rows_outs[m][...] = low
            entered[...] = ref[...]

    @pl.when(step == 0)
    def _():
        bias[...] = jnp.zeros_like(bias)
        sums[...] = jnp.zeros_like(sums)

    bias[...] += jnp.sum(grad_rows[0].astype(F32), 0, keepdims=True)
    unit, _ = norm_parts(entered[...].astype(F32))
    sums[0:1] += jnp.sum(back * unit, 0, keepdims=True)
    sums[1:2] += jnp.sum(back, 0, keepdims=True)


def triple_call(place, normed, triple_grad, triple, entered, waits):
    count, rows, wide = triple_grad.shape
    part = D // count

    def fixed(shape):
        return pl.BlockSpec(shape, lambda m, p: (0,) * len(shape), pipeline_mode=pl.Buffered(1))

    outs = [shape_of(part, wide)] * 4 + [shape_of(rows, D)] * 2
    outs += [shape_of(2, rows, D), shape_of(1, wide, dtype=F32), shape_of(8, D, dtype=F32)]
    return pl.pallas_call(
        waiting(triple_kernel, 5 + len(entered), waits),
        grid_spec=pltpu.PrefetchScalarGridSpec(
            num_scalar_prefetch=1,
            grid=(count,),
            in_specs=[
                pl.BlockSpec((count, rows, part), lambda m, p: (0, 0, p[4] ^ m)),
                fixed(triple_grad.shape),
                pl.BlockSpec((1, rows, wide), lambda m, p: (p[4] ^ m, 0, 0)),
                fixed(triple.shape),
            ]
            + [fixed(e.shape) for e in entered]
            + [ANY_REF] * len(waits),
            out_specs=[fixed(o.shape) for o in outs],
            scratch_shapes=[pltpu.VMEM((rows, D), BF)],
        ),
        out_shape=outs,
        compiler_params=pltpu.CompilerParams(vmem_limit_bytes=VMEM),
        cost_estimate=cost(flops=4 * count * rows * wide * D, bytes_accessed=20 * rows * D, transcendentals=0),
        name="triple_grads",
    )(place, normed, triple_grad, triple_grad, triple, *entered, *waits)


def normed_sum_kernel(own, far, got, own_out, far_out):
    own_out[...] = (own[...].astype(F32) + got[0].astype(F32)).astype(BF)
    far_out[...] = (far[...].astype(F32) + got[1].astype(F32)).astype(BF)


def tail_sum_kernel(near, near_got, out, out_got, total):
    part = near.shape[-1]
    total[:, :, :part] = (near[...].astype(F32) + near_got[...].astype(F32)).astype(BF)
    total[:, :, part:] = (out[...].astype(F32) + out_got[...].astype(F32)).astype(BF)


def unpack_kernel(n_z, place, p0, p1, p2, p3, near, far, held):
    y, z, shard = place[1], place[2], place[4]
    part = near.shape[2]
    chunks = part // 128
    for m, ref in enumerate((p0, p1, p2, p3)):
        held[shard ^ m] = ref[...]
    for j in range(3 * D // 128):
        dp, c = divmod(j, chunks)
        per = D // 128
        at = (j // per) * 256 + (j % 2) * 128
        chunk = held[(j % per) // 2, :, at : at + 128]
        s = (dp // 2 - z + n_z) % n_z

        @pl.when(y == dp % 2)
        def _(chunk=chunk, s=s, c=c):
            near[s, :, c * 128 : (c + 1) * 128] = chunk

        @pl.when(y != dp % 2)
        def _(chunk=chunk, s=s, c=c):
            far[s, :, c * 128 : (c + 1) * 128] = chunk


def tail_kernel(*refs):
    total = refs[0][...].astype(F32)
    for ref in refs[1:-2]:
        total = total + ref[...].astype(F32)
    part = refs[-2].shape[-1]
    refs[-2][...] = total[:, :part]
    refs[-1][...] = total[:, part:]


def leave_kernel(frames_local, entered, keep, other, middle_grad, live, vectors, out):
    unit, scale = norm_parts(entered[...].astype(F32))
    grad = keep[...].astype(F32) + other[...].astype(F32)
    result = (middle_grad[...] + norm_back(grad, unit, scale, vectors[0:1])) * live[...]
    out[...] = leave_rows(result, frames_local)


def split_kernel(place, expand, reduce, own, one, two, three):
    shard = place[4]
    rows = expand.shape[0]
    part = own.shape[1]
    blocks = reduce.shape[0] // (4 * part)
    for m, ref in enumerate((own, one, two, three)):
        to = shard ^ m
        ref[:rows] = expand[:, span(to, part)]
        for p in range(blocks):
            ref[rows + p * part : rows + (p + 1) * part] = reduce[span(p * 4 + to, part), :]


def join_kernel(place, own, one, two, three, expand, reduce):
    shard = place[4]
    rows = expand.shape[0]
    part = own.shape[1]
    blocks = reduce.shape[0] // (4 * part)
    for m, ref in enumerate((own, one, two, three)):
        at = shard ^ m
        expand[:, span(at, part)] = ref[:rows].astype(F32)
        for p in range(blocks):
            reduce[span(p * 4 + at, part), :] = ref[rows + p * part : rows + (p + 1) * part].astype(F32)


def fill_weights(place, step, parts, weight_in, weight_out):
    y, z, shard = place[1], place[2], place[4]
    n_z = len(parts)
    part = parts[0].shape[-1]
    rows = D // 4
    unit = (z - step + n_z) % n_z
    if weight_in is not None:
        for s, ref in enumerate(parts):

            @pl.when(step == s)
            def _(ref=ref):
                for side in range(2):
                    for m in range(4):
                        weight_in[span(shard ^ m, rows), side * part : (side + 1) * part] = ref[side, m, :rows]

    for side in range(2):
        at = pl.ds(pl.multiple_of(rows + (y ^ side) * part, part), part)
        for s, ref in enumerate(parts):
            for flip in range(2):
                features = span(2 * ((z - s + n_z) % n_z) + (y ^ flip), part)
                weight_out[side * part : (side + 1) * part, features] = ref[flip, unit ^ shard, at, :]


def feed_kernel(
    place, normal, normal_other, cot, cot_other, p0, p1, p2, p3, bias, active, slope, keep, give, d_bias, give_acc, weight_in, weight_out
):
    step = pl.program_id(0)
    rows = normal.shape[0]
    fill_weights(place, step, (p0, p1, p2, p3), weight_in, weight_out)

    @pl.when(step == 0)
    def _():
        keep[...] = jnp.zeros_like(keep)
        give_acc[...] = jnp.zeros_like(give_acc)

    d_bias[...] = jnp.zeros_like(d_bias)
    for i, values, outer, total in ((0, normal, cot, keep), (1, normal_other, cot_other, give_acc)):
        act, gradient = gelu_parts(nn(values[...], weight_in[...]) + bias[0])
        grad = (nt(outer[...], weight_out[...]) * gradient).astype(BF)
        active[i * rows : (i + 1) * rows] = act.astype(BF)
        slope[i * rows : (i + 1) * rows] = grad
        d_bias[0] += jnp.sum(grad.astype(F32), 0, keepdims=True)
        total[...] += nt(grad, weight_in[...])

    @pl.when(step == pl.num_programs(0) - 1)
    def _():
        give[...] = give_acc[...].astype(BF)


def feed_grad_kernel(
    place,
    n0,
    n1,
    n2,
    n3,
    c0,
    c1,
    c2,
    c3,
    active,
    active_far,
    slope,
    slope_far,
    p0,
    p1,
    p2,
    p3,
    keep,
    give,
    keep_far,
    give_far,
    d0,
    d1,
    d2,
    d3,
    normal_t,
    cot_all,
    give_acc,
    keep_far_acc,
    give_far_acc,
    weight_out,
    held,
    active_all,
    slope_all,
):
    y, z, shard = place[1], place[2], place[4]
    step = pl.program_id(0)
    grads = (d0, d1, d2, d3)
    n_z = len(grads)
    part = p0.shape[-1]
    rows = n0.shape[0]
    deep = D // 4
    totals = (keep, give_acc, keep_far_acc, give_far_acc)
    fill_weights(place, step, (p0, p1, p2, p3), None, weight_out)

    @pl.when(step == 0)
    def _():
        for i, (normal, cot) in enumerate(((n0, c0), (n1, c1), (n2, c2), (n3, c3))):
            normal_t[:, i * rows : (i + 1) * rows] = normal[...].T
            cot_all[i * rows : (i + 1) * rows] = cot[...]
            totals[i][...] = jnp.zeros_like(totals[i])

    for i, (act, grad) in enumerate(((active, slope), (active_far, slope_far))):
        at = slice(i * 2 * rows, (i + 1) * 2 * rows)
        active_all[at] = act[...]
        slope_all[at] = grad[...]
        for j in range(2):
            totals[2 * i + j][...] += nn(act[j * rows : (j + 1) * rows], weight_out[...])

    held[...] = nn(normal_t[...], slope_all[...]).astype(BF)
    for s, ref in enumerate(grads):

        @pl.when((n_z - step) % n_z == s)
        def _(ref=ref):
            for side in range(2):
                for m in range(4):
                    ref[side, m, :deep] = held[span(shard ^ m, deep), side * part : (side + 1) * part]

    weight_out[...] = tn(active_all[...], cot_all[...]).astype(BF)
    unit = (z - step + n_z) % n_z
    for side in range(2):
        at = pl.ds(pl.multiple_of(deep + (y ^ side) * part, part), part)
        for s, ref in enumerate(grads):
            for flip in range(2):
                features = span(2 * ((z + s) % n_z) + (y ^ flip), part)
                ref[flip, unit ^ shard, at, :] = weight_out[side * part : (side + 1) * part, features]

    @pl.when(step == pl.num_programs(0) - 1)
    def _():
        give[...] = give_acc[...].astype(BF)
        keep_far[...] = keep_far_acc[...].astype(BF)
        give_far[...] = give_far_acc[...].astype(BF)


def feed_specs(place, n_z):
    def whole(array):
        return pl.BlockSpec(array.shape, lambda t, p: (0,) * len(array.shape), pipeline_mode=pl.Buffered(1))

    def lanes(rows, wide):
        return pl.BlockSpec((rows, wide), lambda t, p: (0, t))

    return whole, lanes


def feed_split_call(place, normal, cot, parts, bias, waits=()):
    rows = normal[0].shape[0]
    n_z = len(parts)
    wide = bias.shape[-1]
    whole, lanes = feed_specs(place, n_z)
    row = pl.BlockSpec((1, 1, wide), lambda t, p: (t, 0, 0))
    block = (rows, D)
    outs = [shape_of(2 * rows, n_z * wide)] * 2 + [shape_of(*block, dtype=F32), shape_of(*block)]
    outs += [shape_of(n_z, 1, wide, dtype=F32)]
    inputs = [*normal, *cot, *parts]
    return pl.pallas_call(
        waiting(feed_kernel, 2 + len(inputs), waits),
        grid_spec=pltpu.PrefetchScalarGridSpec(
            num_scalar_prefetch=1,
            grid=(n_z,),
            in_specs=[whole(a) for a in inputs] + [row] + [ANY_REF] * len(waits),
            out_specs=[lanes(2 * rows, wide)] * 2 + [whole(o) for o in outs[2:4]] + [row],
            scratch_shapes=[pltpu.VMEM(block, F32), pltpu.VMEM((D, wide), BF), pltpu.VMEM((wide, D), BF)],
        ),
        out_shape=outs,
        compiler_params=pltpu.CompilerParams(vmem_limit_bytes=VMEM),
        cost_estimate=cost(
            flops=12 * rows * D * wide * n_z, bytes_accessed=20 * rows * D, transcendentals=4 * rows * wide * n_z
        ),
        name="feed_forward",
    )(place, *inputs, bias, *waits)


def feed_grad_call(place, normal, cot, active, slope, parts, waits=()):
    rows = normal[0].shape[0]
    n_z = len(parts)
    wide = active[0].shape[1] // n_z
    whole, lanes = feed_specs(place, n_z)
    block = (rows, D)
    outs = [shape_of(*block, dtype=F32)] + [shape_of(*block)] * 3 + [shape_of(*p.shape) for p in parts]
    first = [*normal, *cot]
    tiles = [*active, *slope]
    return pl.pallas_call(
        waiting(feed_grad_kernel, 1 + len(first) + len(tiles) + n_z, waits),
        grid_spec=pltpu.PrefetchScalarGridSpec(
            num_scalar_prefetch=1,
            grid=(n_z,),
            in_specs=[whole(a) for a in first]
            + [lanes(2 * rows, wide)] * 4
            + [whole(p) for p in parts]
            + [ANY_REF] * len(waits),
            out_specs=[whole(o) for o in outs],
            scratch_shapes=[
                pltpu.VMEM((D, 4 * rows), BF),
                pltpu.VMEM((4 * rows, D), BF),
                pltpu.VMEM(block, F32),
                pltpu.VMEM(block, F32),
                pltpu.VMEM(block, F32),
                pltpu.VMEM((wide, D), BF),
                pltpu.VMEM((D, wide), BF),
                pltpu.VMEM((4 * rows, wide), BF),
                pltpu.VMEM((4 * rows, wide), BF),
            ],
        ),
        out_shape=outs,
        compiler_params=pltpu.CompilerParams(vmem_limit_bytes=VMEM),
        cost_estimate=cost(flops=24 * rows * D * wide * n_z, bytes_accessed=40 * rows * D),
        name="feed_grads",
    )(place, *first, *tiles, *parts, *waits)


def torus_shards(sizes, *args):
    (
        tokens,
        cotangent,
        frame_counts,
        presence,
        attend_gain,
        attend_shift,
        triple_weight,
        triple_bias,
        output_weight,
        output_bias,
        second_gain,
        second_shift,
        expand_weight,
        expand_bias,
        reduce_weight,
        reduce_bias,
    ) = args
    n_z, n_y, n_x = sizes
    n_dp = n_z * n_y
    n_f = n_x * 2
    width = D // n_f
    local_rows = tokens.shape[1]
    frames_local = local_rows // ROW_FRAME
    rows = frames_local * PATCHES + EXTRA
    z, y, x, core = (lax.axis_index(name) for name in ("z", "y", "x", "core"))
    shard = x * 2 + core
    place = jnp.stack([x, y, z, core, shard]).astype(jnp.int32)
    d_part = D // n_dp
    qkv_part = 3 * D // n_dp
    ff_part = FF // n_dp
    quarter = ff_part // 4

    def swap(array, axis="core"):
        return lax.ppermute(array, axis, [(0, 1), (1, 0)])

    def cross_over(array):
        return lax.ppermute(array, ("x", "core"), [(i, i ^ 3) for i in range(4)])

    def to_z(array, s):
        return lax.ppermute(array, "z", [(i, (i + s) % n_z) for i in range(n_z)])

    def take(array, index, axis=0):
        return lax.dynamic_index_in_dim(array, index, axis, False)

    def gather_z(array):
        return [array] + [to_z(array, s) for s in range(1, n_z)]

    def scatter_z(array, waits=(), dtype=BF):
        return add_call([array[0]] + [to_z(array[s], s) for s in range(1, n_z)], waits, dtype)

    def lane_row(vector):
        return jnp.pad(vector, (0, qkv_part - vector.shape[0]))[None]

    vectors = [attend_gain, attend_shift, output_bias, second_gain, second_shift, reduce_bias, triple_bias]
    vectors += [expand_bias[f * quarter : (f + 1) * quarter] for f in range(4)]
    packed = jnp.concatenate(
        [triple_weight] + [lane_row(v) for v in vectors] + [jnp.zeros((16 - len(vectors), qkv_part), BF)], 0
    )

    live_all, cosine, sine, guides = tables(frame_counts[0], presence[0], n_f, frames_local, width // HEAD)
    live = take(live_all, shard)[:, None]
    entered = to_block(tokens[0], frames_local) * live.astype(BF)
    outer = to_block(cotangent[0], frames_local) * live.astype(BF)

    own, one, two, three = local_call(
        split_kernel,
        "split",
        [place, expand_weight, reduce_weight],
        [shape_of(2 * (D // n_f), d_part)] * 4,
        smem=1,
    )
    feed = stack_call([own, swap(one), swap(two, "x"), cross_over(three)])
    feed_y = swap(feed, "y")
    near, entered = local_call(
        front_kernel,
        "front",
        [*gather_z(packed), entered],
        [shape_of(n_z, *packed.shape), shape_of(*entered.shape)],
        waits=[feed],
    )
    far = swap(near, "y")
    entered_x = swap(entered, "x")
    entered_all = [entered, swap(entered), entered_x]
    output_all = lax.all_gather(output_weight, ("z", "y", "x"), axis=0).reshape(n_z, n_y, n_x, width, d_part)

    own, one, two, three, vectors, bias, expand_add = local_call(
        functools.partial(pack_kernel, n_z),
        "pack",
        [place, near, far],
        [shape_of(D // n_f, 3 * width)] * 4
        + [shape_of(8, D, dtype=F32), shape_of(1, 3 * width, dtype=F32), shape_of(n_z, 1, 2 * quarter, dtype=F32)],
        smem=1,
        waits=[entered_x],
    )
    weights = [own, swap(one), swap(two, "x"), cross_over(three)]
    entered_all.append(swap(copy_call(entered_x, [own])))
    feed = stack_call([feed, feed_y], [own])
    feed_parts = [feed, to_z(feed, 1)]
    turn = jnp.asarray(turn_matrix(width), BF)
    q, k, v, normed, triple = enter_call(
        place, entered_all, weights, bias, vectors, turn, cosine, sine, [feed]
    )
    feed_parts += [to_z(feed_parts[1], 1), to_z(feed, 3)]
    outer = copy_call(outer, [normed])
    outer_x = swap(outer, "x")
    outer_all = [outer, swap(outer), outer_x]
    mixed, exact, logs, logs_extra = attend_call(*guides, q, k, v)
    mixed_own, mixed_far, outer_x = local_call(
        part_kernel,
        "mixed_parts",
        [place, mixed],
        [shape_of(2, rows, width)] * 2,
        smem=1,
        waits=[*feed_parts[2:], outer_all[1]],
        carry=[outer_x],
    )
    mixed_far = swap(mixed_far, "x")
    outer_all = [*outer_all[:2], outer_x, swap(outer_x)]
    keep, give = local_call(
        project_kernel,
        "project",
        [place, mixed_own, mixed_far, output_all],
        [shape_of(rows, D, dtype=F32), shape_of(rows, D)],
        [pltpu.VMEM((D // 2, D), BF)],
        smem=1,
        flops=4 * rows * D * D // 2,
        waits=[outer_all[3]],
    )
    output_full = output_all.transpose(2, 3, 0, 1, 4).reshape(D // 2, D)
    middle, second = rows_call(
        middle_kernel,
        "middle",
        [entered, keep, swap(give), vectors],
        [shape_of(rows, D, dtype=F32), shape_of(rows, D)],
    )
    second_all = [second, swap(second)]
    feed_both = [feed_parts, expand_add]
    active, slope, back, back_give, d_bias = feed_split_call(place, second_all, outer_all[:2], *feed_both)
    second_x = swap(second, "x")
    second_all += [second_x, swap(copy_call(second_x, [active]))]
    active_far, slope_far, back_far, back_far_give, d_bias_far = feed_split_call(
        place, second_all[2:], outer_all[2:], *feed_both, waits=[back_give]
    )
    back_give = swap(back_give)
    back_far = swap(add_call([back_far, swap(back_far_give)]), "x")
    final, final_give, final_far, final_far_give, *d_feed = feed_grad_call(
        place, second_all, outer_all, [active, active_far], [slope, slope_far], feed_parts
    )
    middle_grad, branch, sums_two = rows_call(
        middle_back_kernel,
        "middle_back",
        [middle, outer, back, back_give, back_far, vectors],
        [shape_of(rows, D, dtype=F32), shape_of(rows, D), shape_of(8, D, dtype=F32)],
        waits=[d_feed[0]],
    )
    branch_other = swap(branch)
    grad_own, grad_far = local_call(
        mixed_grad_kernel,
        "mixed_grad",
        [place, branch, branch_other, output_full],
        [shape_of(2, rows, width)] * 2,
        smem=1,
        flops=4 * rows * D * D // 2,
    )
    grad_far = swap(grad_far, "x")
    out_near, out_far = local_call(
        output_grad_kernel,
        "output_weight_grad",
        [place, mixed_own, mixed_far, branch, branch_other],
        [shape_of(n_x, n_z, width, d_part)] * 2,
        [pltpu.VMEM((2 * rows, D), BF), pltpu.VMEM((width, D), BF)],
        smem=1,
        flops=4 * rows * D * D // 2,
        waits=[grad_own],
    )
    out_far = swap(out_far, "y")
    final_far = add_call([final_far, swap(final_far_give)], [grad_own])
    final_far = swap(final_far, "x")
    final_give = swap(final_give)
    mixed_grad = jnp.where(
        x == 0, jnp.concatenate([grad_own, grad_far], 0), jnp.concatenate([grad_far, grad_own], 0)
    )
    triple_grad = attend_back_call(
        *guides, q, k, v, mixed_grad, exact, logs, logs_extra, cosine, sine, turn, waits=[out_near, final_give]
    )
    back_feed = add_call([d_feed[2], to_z(d_feed[3], 1)], [triple_grad])
    tri_own, tri_one, tri_two, tri_three, normed_own, normed_far, normed_give, d_triple_bias, sums_one = triple_call(
        place, normed, triple_grad, triple, entered_all, [back_feed, out_far, final_far]
    )
    pieces = [tri_own, swap(tri_one), swap(tri_two, "x"), cross_over(tri_three)]
    zero_qkv = jnp.zeros((3, n_f, width), F32)
    triple_bias_part = lax.dynamic_update_slice(zero_qkv, d_triple_bias.reshape(3, 1, width), (0, shard, 0))
    expand_bias_part = jnp.zeros((n_z, n_y, n_f, quarter), F32)
    d_bias = (d_bias + d_bias_far).reshape(n_z, n_y, quarter)
    for s in range(n_z):
        for side in range(n_y):
            expand_bias_part = lax.dynamic_update_slice(
                expand_bias_part, d_bias[s, side].reshape(1, 1, 1, quarter), ((z - s) % n_z, y ^ side, shard, 0)
            )
    sums = [sums_one[0], sums_one[1], sums_two[0], sums_two[1], sums_two[2], sums_two[3], triple_bias_part, expand_bias_part]
    sums = jnp.concatenate([piece.reshape(n_dp, -1) for piece in sums], 1)
    back_feed = to_z(back_feed, 1)
    normed_own, normed_far = local_call(
        normed_sum_kernel,
        "normed_sum",
        [normed_own, normed_far, swap(normed_give)],
        [shape_of(rows, D)] * 2,
        waits=[*pieces[1:], back_feed],
    )
    normed_far = swap(normed_far, "x")
    tri_near, tri_far = local_call(
        functools.partial(unpack_kernel, n_z),
        "unpack",
        [place, *pieces],
        [shape_of(n_z, D // n_f, qkv_part)] * 2,
        [pltpu.VMEM((4, D // n_f, 3 * width), BF)],
        smem=1,
        waits=[normed_own],
    )
    tri_far = swap(tri_far, "y")
    back_feed = add_call([d_feed[1], back_feed], [tri_near])
    back_feed = to_z(back_feed, 1)
    out_near = add_call([out_near, out_far], [tri_near])
    out_far = swap(out_near[1], "x")
    block_output = local_call(
        functools.partial(output_kernel, frames_local),
        "block_output",
        [middle, final, final_give, final_far, live, vectors],
        [shape_of(local_rows, D)],
        waits=[out_near],
    )[0]
    tail, sums = local_call(
        tail_sum_kernel,
        "tail_sum",
        [tri_near, tri_far, out_near[0], out_far],
        [shape_of(n_z, D // n_f, qkv_part + d_part)],
        waits=[normed_far, block_output, back_feed],
        carry=[sums],
    )
    tail_parts = [tail[0]] + [to_z(tail[s], s) for s in range(1, n_z)]
    d_feed = add_call([d_feed[0], back_feed], [tail])
    d_feed_far = swap(d_feed[1], "y")
    tokens_grad = local_call(
        functools.partial(leave_kernel, frames_local),
        "tokens_grad",
        [entered, normed_own, normed_far, middle_grad, live, vectors],
        [shape_of(local_rows, D, dtype=F32)],
        waits=[d_feed],
    )[0]
    d_feed = add_call([d_feed[0], d_feed_far], [tokens_grad])
    expand_weight_grad, reduce_weight_grad = local_call(
        join_kernel,
        "join",
        [place, d_feed[0], swap(d_feed[1]), swap(d_feed[2], "x"), cross_over(d_feed[3])],
        [shape_of(D // n_f, ff_part, dtype=F32), shape_of(FF // n_f, d_part, dtype=F32)],
        smem=1,
    )
    triple_weight_grad, output_weight_grad = local_call(
        tail_kernel,
        "tail",
        tail_parts,
        [shape_of(D // n_f, qkv_part, dtype=F32), shape_of(D // n_f, d_part, dtype=F32)],
        waits=[d_feed],
    )

    for bit in (1, 2, 4, 8, 16):
        sums = sums + lax.ppermute(sums, ("z", "y", "x", "core"), [(i, i ^ bit) for i in range(32)])
    sums = take(sums, z * n_y + y)
    parts = [sums[i * d_part : (i + 1) * d_part] for i in range(6)]
    rest = sums[6 * d_part :]
    return (
        block_output[None],
        tokens_grad[None],
        parts[0],
        parts[1],
        triple_weight_grad,
        rest[:qkv_part],
        output_weight_grad,
        parts[2],
        parts[3],
        parts[4],
        expand_weight_grad,
        rest[qkv_part:],
        reduce_weight_grad,
        parts[5],
    )


def general_shards(sizes, *args):
    (
        tokens,
        cotangent,
        frame_counts,
        presence,
        attend_gain,
        attend_shift,
        triple_weight,
        triple_bias,
        output_weight,
        output_bias,
        second_gain,
        second_shift,
        expand_weight,
        expand_bias,
        reduce_weight,
        reduce_bias,
    ) = args
    n_z, n_y, n_x = sizes
    n_dp = n_z * n_y
    n_f = n_x * 2
    heads = HEADS // n_f
    width = heads * HEAD
    local_rows = tokens.shape[1]
    frames_local = local_rows // ROW_FRAME
    rows = frames_local * PATCHES + EXTRA
    z, y, x, core = (lax.axis_index(name) for name in ("z", "y", "x", "core"))
    shard = x * 2 + core
    d_part = D // n_dp
    ff_part = FF // n_dp
    ff_half = ff_part // 2
    blocks = n_dp // n_f

    def swap(array, axis="core"):
        return lax.ppermute(array, axis, [(0, 1), (1, 0)])

    def take(array, index, axis=0):
        return lax.dynamic_index_in_dim(array, index, axis, False)

    def ordered(index, own, other, axis=0):
        low = jnp.where(index == 0, own, other)
        high = jnp.where(index == 0, other, own)
        return jnp.concatenate([low, high], axis)

    def both_cores(array, axis=0):
        return ordered(core, array, swap(array), axis)

    def exchange_f(array):
        return lax.all_to_all(array, ("x", "core"), 0, 0, tiled=True)

    def over_x(array):
        return lax.all_to_all(array, "x", 0, 0, tiled=True)

    vectors = [attend_gain, attend_shift, output_bias, second_gain, second_shift, reduce_bias, triple_bias, expand_bias]
    flat = jnp.concatenate(vectors)
    qkv_part = 3 * D // n_dp
    flat = jnp.pad(flat, (0, 16 * qkv_part - flat.shape[0])).reshape(16, qkv_part)
    packed = jnp.concatenate([triple_weight, flat], 0)
    packed = lax.all_gather(packed, ("z", "y"), axis=0)
    small = packed[:, D // n_f :].reshape(n_dp, -1)
    full = []
    at = 0
    for vector in vectors:
        full.append(small[:, at : at + vector.shape[0]].reshape(-1))
        at += vector.shape[0]
    gain_one, shift_one, output_add, gain_two, shift_two, reduce_add = (v.astype(F32)[None] for v in full[:6])
    triple_add, expand_add = full[6], full[7]
    triple_rows = packed[:, : D // n_f].transpose(1, 0, 2).reshape(D // n_f, 3, n_f, width)
    triple_own = exchange_f(triple_rows.transpose(2, 0, 1, 3)).reshape(D, 3 * width)
    bias_own = take(triple_add.reshape(3, n_f, width), shard, 1).reshape(1, 3 * width)

    expand_split = expand_weight.reshape(D // n_f, 2, ff_half)
    expand_chip = ordered(core, take(expand_split, core, 1), swap(take(expand_split, 1 - core, 1)))
    reduce_split = reduce_weight.reshape(blocks, 2, ff_half, d_part)
    reduce_chip = ordered(core, take(reduce_split, core, 1)[None], swap(take(reduce_split, 1 - core, 1))[None])
    expand_add_own = take(expand_add.reshape(n_z, n_y, 2, ff_half), core, 2)
    expand_all = lax.all_gather(expand_chip, ("z", "y", "x"), axis=0).reshape(n_z, n_y, D, ff_half)
    expand_pieces = [expand_all.transpose(0, 2, 1, 3).reshape(n_z, D, n_y * ff_half)]
    reduce_all = lax.all_gather(reduce_chip, ("z", "y", "x"), axis=0)
    reduce_pieces = [
        reduce_all.reshape(n_dp, n_dp, ff_half, d_part).transpose(1, 2, 0, 3).reshape(n_z, n_y * ff_half, D)
    ]
    expand_add_own = expand_add_own.reshape(n_z, 1, n_y * ff_half)
    output_all = lax.all_gather(output_weight, ("z", "y", "x"), axis=0)
    output_all = output_all.reshape(n_dp, n_x * width, d_part).transpose(1, 0, 2).reshape(n_x * width, D)

    live_all, cosine, sine, guides = tables(frame_counts[0], presence[0], n_f, frames_local, heads)
    live = take(live_all, shard)[:, None]
    entered = to_block(tokens[0], frames_local).astype(F32) * live
    outer = to_block(cotangent[0], frames_local).astype(F32) * live
    outer_low = outer.astype(BF)
    outer_chip = both_cores(outer_low)
    outer_chip_t = outer_chip.T
    unit_one, scale_one = norm_parts(entered)
    normed = (unit_one * gain_one + shift_one).astype(BF)
    normed_all = lax.all_gather(normed, ("x", "core"), axis=0)

    turned = jnp.asarray(turn_matrix(width), BF)
    q, k, v = qkv_call(normed_all, triple_own, bias_own, turned, cosine, sine)
    mixed, exact, logs, logs_extra = attend_call(*guides, q, k, v)

    mixed_chip = over_x(mixed.reshape(n_x, 2 * rows, width)).transpose(1, 0, 2).reshape(2 * rows, n_x * width)
    branch_part = nn(mixed_chip, output_all).reshape(2, rows, D)
    branch = take(branch_part, core) + swap(take(branch_part, 1 - core).astype(BF)).astype(F32)
    middle = entered + branch + output_add
    unit_two, scale_two = norm_parts(middle)
    second = (unit_two * gain_two + shift_two).astype(BF)
    second_chip = both_cores(second)
    final, second_grad, d_expand_bias, *d_feed = feed_call(
        second_chip, outer_chip, outer_chip_t, expand_pieces[0], expand_add_own, reduce_pieces[0]
    )
    second_grad = second_grad.reshape(2, rows, D)
    second_grad = take(second_grad, core) + swap(take(second_grad, 1 - core).astype(BF)).astype(F32)
    final = final.reshape(2, rows, D)
    final = take(final, core) + swap(take(final, 1 - core).astype(BF)).astype(F32)
    block_output = ((middle + final + reduce_add) * live).astype(BF)

    middle_grad = outer + norm_back(second_grad, unit_two, scale_two, gain_two)
    second_gain_grad = jnp.sum(second_grad * unit_two, 0)
    second_shift_grad = jnp.sum(second_grad, 0)
    branch_low = middle_grad.astype(BF)
    branch_chip = both_cores(branch_low)
    mixed_grad = nt(branch_chip, output_all).astype(BF)
    mixed_grad = over_x(mixed_grad.reshape(2 * rows, n_x, width).transpose(1, 0, 2)).reshape(n_f, rows, width)
    d_output = tn(mixed_chip, branch_chip).astype(BF)
    triple_grad = attend_back_call(*guides, q, k, v, mixed_grad, exact, logs, logs_extra, cosine, sine, turned)
    natural = triple_grad.reshape(n_f * rows, 3 * width)
    d_triple = tn(normed_all.reshape(n_f * rows, D), natural).astype(BF)
    d_triple_bias = jnp.sum(natural.astype(F32), 0)
    normed_grad = nt(natural, triple_own).astype(BF)
    normed_grad = lax.psum_scatter(normed_grad, ("x", "core"), scatter_dimension=0, tiled=True).astype(F32)
    attend_gain_grad = jnp.sum(normed_grad * unit_one, 0)
    attend_shift_grad = jnp.sum(normed_grad, 0)
    tokens_grad = (middle_grad + norm_back(normed_grad, unit_one, scale_one, gain_one)) * live

    d_triple = exchange_f(d_triple.reshape(n_f, D // n_f, 3, width))
    d_triple = d_triple.transpose(1, 2, 0, 3).reshape(D // n_f, n_z, n_y, qkv_part)
    d_triple = d_triple.reshape(D // n_f, 3 * D)
    triple_weight_grad = lax.psum_scatter(d_triple, ("z", "y"), scatter_dimension=1, tiled=True).astype(F32)
    d_output = d_output.reshape(n_x, width, n_dp, d_part).transpose(2, 0, 1, 3).reshape(n_dp * n_x * width, d_part)
    output_weight_grad = lax.psum_scatter(d_output, ("z", "y", "x"), scatter_dimension=0, tiled=True).astype(F32)
    d_expand, d_reduce = d_feed
    d_expand = d_expand.reshape(n_z, D, n_y, ff_half).transpose(0, 2, 1, 3).reshape(n_dp * D, ff_half)
    d_expand = lax.psum_scatter(d_expand, ("z", "y", "x"), scatter_dimension=0, tiled=True)
    d_expand = d_expand.reshape(2, D // n_f, ff_half)
    d_reduce = d_reduce.reshape(n_z, n_dp, d_part, n_y, ff_half).transpose(1, 0, 3, 2, 4).reshape(-1, ff_half)
    d_reduce = lax.psum_scatter(d_reduce, ("z", "y", "x"), scatter_dimension=0, tiled=True)
    d_reduce = d_reduce.reshape(2, blocks, d_part, ff_half)
    expand_weight_grad = ordered(core, take(d_expand, core), swap(take(d_expand, 1 - core)), 1).astype(F32)
    reduce_weight_grad = jnp.stack(
        [
            jnp.where(core == 0, take(d_reduce, core), swap(take(d_reduce, 1 - core))),
            jnp.where(core == 0, swap(take(d_reduce, 1 - core)), take(d_reduce, core)),
        ],
        1,
    )
    reduce_weight_grad = reduce_weight_grad.transpose(0, 1, 3, 2).reshape(blocks * 2 * ff_half, d_part).astype(F32)

    zero_qkv = jnp.zeros((3, n_f, width), F32)
    triple_bias_part = lax.dynamic_update_slice(zero_qkv, d_triple_bias.reshape(3, 1, width), (0, shard, 0))
    d_expand_bias = d_expand_bias.reshape(n_z, n_y, ff_half)
    zero_ff = jnp.zeros((n_dp, 2, ff_half), F32)
    expand_bias_part = lax.dynamic_update_slice(zero_ff, d_expand_bias.reshape(n_dp, 1, ff_half), (0, core, 0))
    sums = [
        attend_gain_grad,
        attend_shift_grad,
        jnp.sum(branch_low.astype(F32), 0),
        second_gain_grad,
        second_shift_grad,
        jnp.sum(outer_low.astype(F32), 0),
        triple_bias_part.reshape(-1),
        expand_bias_part.reshape(-1),
    ]
    sums = jnp.concatenate([s.reshape(n_dp, -1) for s in sums], 1)
    total = n_dp * n_f
    bit = 1
    while bit < total:
        sums = sums + lax.ppermute(sums, ("z", "y", "x", "core"), [(i, i ^ bit) for i in range(total)])
        bit *= 2
    own = take(sums, z * n_y + y)
    parts = []
    at = 0
    for size in [d_part] * 6 + [qkv_part, ff_part]:
        parts.append(own[at : at + size])
        at += size
    return (
        from_block(block_output, frames_local),
        from_block(tokens_grad, frames_local),
        parts[0],
        parts[1],
        triple_weight_grad,
        parts[6],
        output_weight_grad,
        parts[2],
        parts[3],
        parts[4],
        expand_weight_grad,
        parts[7],
        reduce_weight_grad,
        parts[5],
    )


def solution(mesh):
    n_dp, n_f = mesh.shape["dp"], mesh.shape["fsdp"]
    sizes = (n_dp // 2, 2, n_f // 2)
    inner = jax.sharding.Mesh(mesh.devices.reshape(*sizes, 2), ("z", "y", "x", "core"))
    dp = ("z", "y")
    fsdp = ("x", "core")
    rows = P(dp, fsdp, None)
    weight = P(fsdp, dp)
    vector = P(dp)
    return jax.shard_map(
        functools.partial(torus_shards if sizes == (4, 2, 2) else general_shards, sizes),
        mesh=inner,
        in_specs=(
            rows,
            rows,
            P(dp, None),
            P(dp, None, None),
            vector,
            vector,
            weight,
            vector,
            weight,
            vector,
            vector,
            vector,
            weight,
            vector,
            weight,
            vector,
        ),
        out_specs=(
            rows,
            rows,
            vector,
            vector,
            weight,
            vector,
            weight,
            vector,
            vector,
            vector,
            weight,
            vector,
            weight,
            vector,
        ),
        check_vma=False,
    )
```

time: 921 us -> 552 us (0.60)
  waiting for transfers between devices: 448 us -> 129 us
  Pallas kernels: 191 us -> 288 us
  local copies, waits for them, and re-layouts: 118 us -> 55.5 us
  other arithmetic: 69.8 us -> 12.8 us
  matrix products: 25 us -> 0 us
  starting transfers between devices: 20.4 us -> 44.7 us
  blocking collectives: 23.6 us -> 0 us
    reduce_scatter x4 -> x0, waiting for transfers between devices: 231 us -> none  [the longest x1 95.7 us: shards(): lax.psum_scatter(d_expand, ('dp', 'x'), scatter_dimension=0, tiled=True)]
    ppermute x15 -> x56, waiting for transfers between devices: 12.5 us -> 129 us  [the longest x35 83.3 us: swap(): return lax.ppermute(array, axis, [(0, 1), (1, 0)])]
    all_gather x5 -> x1, waiting for transfers between devices: 105 us -> 0.01 us  [torus_shards(): lax.all_gather(output_weight, ('z', 'y', 'x'), axis=0)]
    pallas_call x4 -> x35, Pallas kernels: 191 us -> 288 us  [the longest x26 78.7 us: local_call(): pl.pallas_call(waiting(kernel, len(inputs), waits, len(carry), len(output...]
    all_to_all x3 -> x0, waiting for transfers between devices: 53.8 us -> none  [the longest x2 27.1 us: over_x(): return lax.all_to_all(array, 'x', 0, 0, tiled=True)]
    unnamed x11 -> x1, waiting for transfers between devices: 46.1 us -> 0.02 us
    ppermute x15 -> x56, starting transfers between devices: 7.56 us -> 44.6 us  [the longest x35 21.4 us: swap(): return lax.ppermute(array, axis, [(0, 1), (1, 0)])]
    dot_general x7 -> x0, matrix products: 25 us -> none  [the longest x4 12.8 us: nt(): lax.dot_general(left, right, (((1,), (1,)), ((), ())), preferred_element_...]
  transfers between devices with their start and end apart: 28 -> 57, of which waited for: 17 -> 20; matrix products, arithmetic and copies ran while one was open for 17% -> 7% of each run, Pallas kernels for 15% -> 39%
where the time goes in v2:
time: 552 us; the launch traced here: 546 us
  Pallas kernels  288 us (52%)
  waiting for transfers between devices  129 us (23%)
  local copies, waits for them, and re-layouts  55.5 us (10%)
  starting transfers between devices  44.7 us (8%)
  between operations  16.4 us (3%)
  other arithmetic  12.8 us (2%)
    ppermute x35, waiting for transfers between devices, swap(): return lax.ppermute(array, axis, [(0, 1), (1, 0)])  83.3 us
    pallas_call x26, Pallas kernels, local_call(): pl.pallas_call(waiting(kernel, len(inputs), waits, len(carry), len(output...  78.7 us
    pallas_call x1, Pallas kernels, attend_back_call(): pl.pallas_call(waiting(functools.partial(attend_back_kernel, frames_local...  48 us
    pallas_call x1, Pallas kernels, feed_grad_call(): pl.pallas_call(waiting(feed_grad_kernel, 1 + len(first) + len(tiles) + n_...  41.4 us
    pallas_call x2, Pallas kernels, feed_split_call(): pl.pallas_call(waiting(feed_kernel, 2 + len(inputs), waits), grid_spec=pl...  38.5 us
    pallas_call x1, Pallas kernels, attend_call(): pl.pallas_call(waiting(functools.partial(attend_kernel, frames_local), 8,...  37.3 us
    ppermute x12, waiting for transfers between devices, to_z(): return lax.ppermute(array, 'z', [(i, (i + s) % n_z) for i in range(n_z)])  28.3 us
    unnamed x126, local copies, waits for them, and re-layouts  27.5 us
  transfers between devices with their start and end apart: 57, of which 20 were waited for; matrix products, arithmetic and copies ran while one was open for 7% of the time, Pallas kernels for 39%

profile of v2, /device:TPU:0, one launch (start us, length us, event | category | flops | bytes accessed | tf_op | source)
XLA Modules:
  0.0 545.8 jit_solution(14396458078537010786)
XLA Ops:
  33.3 3.4 collective-permute-done.5.refs_3_
  45.9 19.2 %collective-permute-done.8.refs_2_ = bf16[4,272,384]{2,1,0:T(8,128)(2,1)S(1)} collective-permute-done((bf16[4,272,384]{2,1,0:T(8,128)(2,1)}, bf16[4,272,384]{2,1,0:T(8,128)(2,1)S(1)}, u32[]{:S(2)}, u32[]{:S(2)}) %collective-permute-start.8) | collective-permute-done | bytes 835616 | tf_op jit(solution)/shard_map/ppermute | solution.py:1404
  65.1 3.9 collective-permute-done.7.refs_3_.refs_0_.refs_7_
  70.0 3.6 pack.1
  83.9 5.1 fusion
  91.8 21.4 %collective-permute-done.14.p1.refs_6_ = bf16[2,4,512,128]{3,2,1,0:T(8,128)(2,1)} collective-permute-done((bf16[2,4,512,128]{3,2,1,0:T(8,128)(2,1)}, bf16[2,4,512,128]{3,2,1,0:T(8,128)(2,1)}, u32[]{:S(2)}, u32[]{:S(2)}) %collective-permute-start.14) | collective-permute-done | bytes 1048608 | tf_op jit(solution)/shard_map/ppermute | solution.py:1410
  115.2 11.9 %enter.1 = (bf16[4,528,256]{2,1,0:T(8,128)(2,1)}, bf16[4,528,256]{2,1,0:T(8,128)(2,1)}, bf16[4,528,256]{2,1,0:T(8,128)(2,1)}, bf16[4,528,1024]{2,1,0:T(8,128)(2,1)}, bf16[1024,768]{1,0:T(8,128)(2,1)}) custom-call(s32[5]{0:T(128)} %stack.25.place.refs_0_, bf16[528,1024]{1,0:T(8,128)(2,1)} %get-tuple-element.91.refs_1_.entered.refs_5_.refs_0_, ...), custom_call_target="tpu_custom_call" | custom-call | flops 3321888768 | bytes 16220160 | tf_op jit(solution)/shard_map/enter/pallas_call | solution.py:894
  133.6 37.3 %attend.1 = (bf16[4,528,256]{2,1,0:T(8,128)(2,1)}, f32[4,528,256]{2,1,0:T(8,128)}, f32[8,8,1024]{2,1,0:T(8,128)}, f32[8,256]{1,0:T(8,128)}) custom-call(s32[8]{0:T(128)} %compare_select_fusion.2.start.refs_0_, s32[64,128]{1,0:T(8,128)} %broadcast_in_dim.153.key_frame.refs_1_, s32[8,64]{1,0:T(8,128)} %broadcast_in_dim.159.query_start.refs_2_, ...), custom_call_target="tpu_custom_call" | custom-call | flops 17179869184 | bytes 5406720 | tf_op jit(solution)/shard_map/attend/pallas_call | solution.py:278
  175.2 14.2 %collective-permute-done.19.refs_2_ = bf16[2,528,256]{2,1,0:T(8,128)(2,1)S(1)} collective-permute-done((bf16[2,528,256]{2,1,0:T(8,128)(2,1)}, bf16[2,528,256]{2,1,0:T(8,128)(2,1)S(1)}, u32[]{:S(2)}, u32[]{:S(2)}) %collective-permute-start.19) | collective-permute-done | bytes 540704 | tf_op jit(solution)/shard_map/ppermute | solution.py:1404
  190.6 4.6 project.1
  199.1 4.8 middle.1
  207.8 19.2 %feed_forward.2 = (bf16[1056,1024]{1,0:T(8,128)(2,1)}, bf16[1056,1024]{1,0:T(8,128)(2,1)}, f32[528,1024]{1,0:T(8,128)}, bf16[528,1024]{1,0:T(8,128)(2,1)}, f32[4,1,256]{2,1,0:T(1,128)}) custom-call(s32[5]{0:T(128)} %stack.25.place.refs_0_, bf16[528,1024]{1,0:T(8,128)(2,1)} %get-tuple-element.110.normal.n0, bf16[528,1024]{1,0:T(8,128)(2,1)} %copy-done.46, ...), custom_call_target="tpu_custom_call" | custom-call | flops 6643777536 | bytes 10813440 | tf_op jit(solution)/shard_map/feed_forward/pallas_call | solution.py:1313
  227.1 3.3 collective-permute-done.23.refs_0_.refs_1_.n2
  237.6 19.3 %feed_forward.3 = (bf16[1056,1024]{1,0:T(8,128)(2,1)}, bf16[1056,1024]{1,0:T(8,128)(2,1)}, f32[528,1024]{1,0:T(8,128)}, bf16[528,1024]{1,0:T(8,128)(2,1)}, f32[4,1,256]{2,1,0:T(1,128)}) custom-call(s32[5]{0:T(128)} %stack.25.place.refs_0_, bf16[528,1024]{1,0:T(8,128)(2,1)} %copy-done.16, bf16[528,1024]{1,0:T(8,128)(2,1)} %copy-done.48, ...), custom_call_target="tpu_custom_call" | custom-call | flops 6643777536 | bytes 10813440 | tf_op jit(solution)/shard_map/feed_forward/pallas_call | solution.py:1313
  264.5 41.4 %feed_grads.1 = (f32[528,1024]{1,0:T(8,128)}, bf16[528,1024]{1,0:T(8,128)(2,1)}, bf16[528,1024]{1,0:T(8,128)(2,1)}, bf16[528,1024]{1,0:T(8,128)(2,1)}, bf16[2,4,...) custom-call(s32[5]{0:T(128)} %stack.25.place.refs_0_, ...), custom_call_target="tpu_custom_call" | custom-call | flops 13287555072 | bytes 21626880 | tf_op jit(solution)/shard_map/feed_grads/pallas_call | solution.py:1340
  307.2 6.8 %middle_back.1 = (f32[528,1024]{1,0:T(8,128)}, bf16[528,1024]{1,0:T(8,128)(2,1)}, f32[8,1024]{1,0:T(8,128)}) custom-call(f32[528,1024]{1,0:T(8,128)} %get-tuple-element.109.refs_0_, bf16[528,1024]{1,0:T(8,128)(2,1)} %copy.87.cot.c0.refs_1_, f32[528,1024]{1,0:T(8,128)} %get-tuple-element.121.refs_2_, bf16[528,1024]{1,0:T(8,128)(2,1)} %copy-done.13, ...), custom_call_target="tpu_custom_call" | custom-call | flops 10813440 | bytes 10878976 | tf_op jit(solution)/shard_map/middle_back/pallas_call | solution.py:958
  318.6 4.3 mixed_grad.1
  324.5 4.8 output_weight_grad.1
  335.1 3.2 collective-permute-done.33
  341.7 48.0 %attend_back.1.refs_2_.refs_3_ = bf16[4,528,768]{2,1,0:T(8,128)(2,1)} custom-call(s32[8]{0:T(128)} %compare_select_fusion.2.start.refs_0_, s32[64,128]{1,0:T(8,128)} %broadcast_in_dim.153.key_frame.refs_1_, s32[8,64]{1,0:T(8,128)} %broadcast_in_dim.159.query_start.refs_2_, s32[8,64]{1,0:T(8,128)} %broadcast_in_dim.162.query_frame.refs_3_, ...), custom_call_target="tpu_custom_call" | custom-call | flops 42949672960 | bytes 10813440 | tf_op jit(solution)/shard_map/attend_back/pallas_call | solution.py:485
  393.5 20.3 %triple_grads.1 = (bf16[256,768]{1,0:T(8,128)(2,1)}, bf16[256,768]{1,0:T(8,128)(2,1)}, bf16[256,768]{1,0:T(8,128)(2,1)}, bf16[256,768]{1,0:T(8,128)(2,1)}, bf16[...) custom-call(s32[5]{0:T(128)} %stack.25.place.refs_0_, ...), custom_call_target="tpu_custom_call" | custom-call | flops 6643777536 | bytes 10813440 | tf_op jit(solution)/shard_map/triple_grads/pallas_call | solution.py:1063
  418.9 8.9 %collective-permute-done.36.refs_4_.refs_3_ = bf16[256,768]{1,0:T(8,128)(2,1)S(1)} collective-permute-done((bf16[256,768]{1,0:T(8,128)(2,1)}, bf16[256,768]{1,0:T(8,128)(2,1)S(1)}, u32[]{:S(2)}, u32[]{:S(2)}) %collective-permute-start.36) | collective-permute-done | bytes 393248 | tf_op jit(solution)/shard_map/ppermute | solution.py:1404
  427.8 6.8 %collective-permute-done.37.refs_5_.refs_4_ = bf16[256,768]{1,0:T(8,128)(2,1)S(1)} collective-permute-done((bf16[256,768]{1,0:T(8,128)(2,1)}, bf16[256,768]{1,0:T(8,128)(2,1)S(1)}, u32[]{:S(2)}, u32[]{:S(2)}) %collective-permute-start.37) | collective-permute-done | bytes 393248 | tf_op jit(solution)/shard_map/ppermute | solution.py:1407
  434.6 6.8 %collective-permute-done.39.refs_6_.refs_1_ = bf16[2,4,512,128]{3,2,1,0:T(8,128)(2,1)S(1)} collective-permute-done((bf16[2,4,512,128]{3,2,1,0:T(8,128)(2,1)}, bf16[2,4,512,128]{3,2,1,0:T(8,128)(2,1)S(1)}, u32[]{:S(2)}, u32[]{:S(2)}) %collective-permute-start.39) | collective-permute-done | bytes 1048608 | tf_op jit(solution)/shard_map/ppermute | solution.py:1410
  443.2 3.9 normed_sum.1
  447.1 3.4 unpack.1
  460.8 4.6 block_output.1.refs_5_
  465.4 19.1 %collective-permute-done.43.refs_3_ = bf16[4,256,128]{2,1,0:T(8,128)(2,1)S(1)} collective-permute-done((bf16[4,256,128]{2,1,0:T(8,128)(2,1)S(1)}, bf16[4,256,128]{2,1,0:T(8,128)(2,1)S(1)}, u32[]{:S(2)}, u32[]{:S(2)}) %collective-permute-start.43) | collective-permute-done | bytes 262176 | tf_op jit(solution)/shard_map/ppermute | solution.py:1404
  492.2 3.1 collective-permute-done.45
  503.9 3.5 collective-permute-start.48
  512.0 5.8 %tokens_grad.1.refs_2_ = f32[516,1024]{1,0:T(8,128)} custom-call(bf16[528,1024]{1,0:T(8,128)(2,1)} %get-tuple-element.91.refs_1_.entered.refs_5_.refs_0_, bf16[528,1024]{1,0:T(8,128)(2,1)} %get-tuple-element.143.refs_5_.refs_1_, bf16[528,1024]{1,0:T(8,128)(2,1)} %copy-done.1, f32[528,1024]{1,0:T(8,128)} %get-tuple-element.146.refs_3_, ...), custom_call_target="tpu_custom_call" | custom-call | bytes 7555136 | tf_op jit(solution)/shard_map/tokens_grad/pallas_call | solution.py:733
  517.8 5.1 copy.61
  (351 shorter events, 158.7 us)
Async XLA Ops:
  7.2 168.0 %all-gather.3.cloned.1.call-start = ((), (), s32[]{:S(2)}) async-start(), calls=%async_computation | async-start | bytes 1114112 | tf_op jit(solution)/shard_map/all_gather | solution.py:1454
  14.5 24.8 %collective-permute-start = (bf16[272,384]{1,0:T(8,128)(2,1)S(1)}, bf16[272,384]{1,0:T(8,128)(2,1)}, u32[]{:S(2)}, u32[]{:S(2)}) collective-permute-start(bf16[272,384]{1,0:T(8,128)(2,1)S(1)} %concatenate.33.refs_0_), channel_id=1, source_target_pairs={{0,8},{8,16},{16,24},{24,0},{1,9},{9,17},{17,25},{25,1},{2,10},{10... | collective-permute-start | bytes 626696 | tf_op jit(solution)/shard_map/ppermute | solution.py:1410
  17.6 21.7 %collective-permute-start.1 = (bf16[272,384]{1,0:T(8,128)(2,1)S(1)}, bf16[272,384]{1,0:T(8,128)(2,1)}, u32[]{:S(2)}, u32[]{:S(2)}) collective-permute-start(bf16[272,384]{1,0:T(8,128)(2,1)S(1)} %concatenate.33.refs_0_), channel_id=1, source_target_pairs={{0,16},{8,24},{16,0},{24,8},{1,17},{9,25},{17,1},{25,9},{2,18},{10... | collective-permute-start | bytes 626696 | tf_op jit(solution)/shard_map/ppermute | solution.py:1410
  42.4 26.6 %collective-permute-start.7 = (bf16[528,1024]{1,0:T(8,128)(2,1)}, bf16[528,1024]{1,0:T(8,128)(2,1)S(1)}, u32[]{:S(2)}, u32[]{:S(2)}) collective-permute-start(bf16[528,1024]{1,0:T(8,128)(2,1)} %get-tuple-element.91.refs_1_.entered.refs_5_.refs_0_), channel_id=1, source_target_pairs={{0,2},{2,0},{1,3},{3,1},{4,6},{6,4},{5,7},{7,5},{8,10},{10,8},{9,1... | collective-permute-start | bytes 3244040 | tf_op jit(solution)/shard_map/ppermute | solution.py:1404
  43.0 22.1 %collective-permute-start.8 = (bf16[4,272,384]{2,1,0:T(8,128)(2,1)}, bf16[4,272,384]{2,1,0:T(8,128)(2,1)S(1)}, u32[]{:S(2)}, u32[]{:S(2)}) collective-permute-start(bf16[4,272,384]{2,1,0:T(8,128)(2,1)} %get-tuple-element.92.refs_1_), channel_id=1, source_target_pairs={{0,4},{4,0},{1,5},{5,1},{2,6},{6,2},{3,7},{7,3},{8,12},{12,8},{9,1... | collective-permute-start | bytes 2506760 | tf_op jit(solution)/shard_map/ppermute | solution.py:1404
  44.5 31.8 %collective-permute-start.13 = (bf16[4,512,128]{2,1,0:T(8,128)(2,1)S(1)}, bf16[4,512,128]{2,1,0:T(8,128)(2,1)S(1)}, u32[]{:S(2)}, u32[]{:S(2)}) collective-permute-start(bf16[4,512,128]{2,1,0:T(8,128)(2,1)S(1)} %copy-done), channel_id=1, source_target_pairs={{0,4},{4,0},{1,5},{5,1},{2,6},{6,2},{3,7},{7,3},{8,12},{12,8},{9,1... | collective-permute-start | bytes 1572872 | tf_op jit(solution)/shard_map/ppermute | solution.py:1404
  45.0 37.4 %collective-permute-start.6 = (bf16[528,1024]{1,0:T(8,128)(2,1)}, bf16[528,1024]{1,0:T(8,128)(2,1)}, u32[]{:S(2)}, u32[]{:S(2)}) collective-permute-start(bf16[528,1024]{1,0:T(8,128)(2,1)} %get-tuple-element.91.refs_1_.entered.refs_5_.refs_0_), channel_id=1, source_target_pairs={{0,1},{1,0},{2,3},{3,2},{4,5},{5,4},{6,7},{7,6},{8,9},{9,8},{10,11... | collective-permute-start | bytes 3244040 | tf_op jit(solution)/shard_map/ppermute | solution.py:1404
  75.9 37.5 %collective-permute-start.9 = (bf16[528,1024]{1,0:T(8,128)(2,1)}, bf16[528,1024]{1,0:T(8,128)(2,1)S(1)}, u32[]{:S(2)}, u32[]{:S(2)}) collective-permute-start(bf16[528,1024]{1,0:T(8,128)(2,1)} %copy.86), channel_id=1, source_target_pairs={{0,1},{1,0},{2,3},{3,2},{4,5},{5,4},{6,7},{7,6},{8,9},{9,8},{10,11... | collective-permute-start | bytes 3244040 | tf_op jit(solution)/shard_map/ppermute | solution.py:1404
  79.4 33.9 %collective-permute-start.14 = (bf16[2,4,512,128]{3,2,1,0:T(8,128)(2,1)}, bf16[2,4,512,128]{3,2,1,0:T(8,128)(2,1)}, u32[]{:S(2)}, u32[]{:S(2)}) collective-permute-start(bf16[2,4,512,128]{3,2,1,0:T(8,128)(2,1)} %stack.27.refs_14_.p0.refs_5_), channel_id=1, source_target_pairs={{0,8},{8,16},{16,24},{24,0},{1,9},{9,17},{17,25},{25,1},{2,10},{10... | collective-permute-start | bytes 3145736 | tf_op jit(solution)/shard_map/ppermute | solution.py:1410
  81.1 32.3 %collective-permute-start.11 = (bf16[256,768]{1,0:T(8,128)(2,1)S(1)}, bf16[256,768]{1,0:T(8,128)(2,1)S(1)}, u32[]{:S(2)}, u32[]{:S(2)}) collective-permute-start(bf16[256,768]{1,0:T(8,128)(2,1)S(1)} %copy-done.51), channel_id=1, source_target_pairs={{0,2},{2,0},{1,3},{3,1},{4,6},{6,4},{5,7},{7,5},{8,10},{10,8},{9,1... | collective-permute-start | bytes 1179656 | tf_op jit(solution)/shard_map/ppermute | solution.py:1404
  82.4 31.0 %collective-permute-start.12 = (bf16[256,768]{1,0:T(8,128)(2,1)S(1)}, bf16[256,768]{1,0:T(8,128)(2,1)S(1)}, u32[]{:S(2)}, u32[]{:S(2)}) collective-permute-start(bf16[256,768]{1,0:T(8,128)(2,1)S(1)} %copy-done.50), channel_id=1, source_target_pairs={{0,3},{1,2},{2,1},{3,0},{4,7},{5,6},{6,5},{7,4},{8,11},{9,10},{10,... | collective-permute-start | bytes 1179656 | tf_op jit(solution)/shard_map/ppermute | solution.py:1407
  89.0 81.8 %collective-permute-start.16 = (bf16[2,4,512,128]{3,2,1,0:T(8,128)(2,1)}, bf16[2,4,512,128]{3,2,1,0:T(8,128)(2,1)}, u32[]{:S(2)}, u32[]{:S(2)}) collective-permute-start(bf16[2,4,512,128]{3,2,1,0:T(8,128)(2,1)} %stack.27.refs_14_.p0.refs_5_), channel_id=1, source_target_pairs={{0,24},{8,0},{16,8},{24,16},{1,25},{9,1},{17,9},{25,17},{2,26},{10... | collective-permute-start | bytes 3145736 | tf_op jit(solution)/shard_map/ppermute | solution.py:1410
  113.2 57.6 %collective-permute-start.15 = (bf16[2,4,512,128]{3,2,1,0:T(8,128)(2,1)}, bf16[2,4,512,128]{3,2,1,0:T(8,128)(2,1)}, u32[]{:S(2)}, u32[]{:S(2)}) collective-permute-start(bf16[2,4,512,128]{3,2,1,0:T(8,128)(2,1)} %collective-permute-done.14.p1.refs_6_), channel_id=1, source_target_pairs={{0,8},{8,16},{16,24},{24,0},{1,9},{9,17},{17,25},{25,1},{2,10},{10... | collective-permute-start | bytes 3145736 | tf_op jit(solution)/shard_map/ppermute | solution.py:1410
  129.5 41.4 %collective-permute-start.17 = (bf16[528,1024]{1,0:T(8,128)(2,1)}, bf16[528,1024]{1,0:T(8,128)(2,1)S(1)}, u32[]{:S(2)}, u32[]{:S(2)}) collective-permute-start(bf16[528,1024]{1,0:T(8,128)(2,1)} %copy.87.cot.c0.refs_1_), channel_id=1, source_target_pairs={{0,1},{1,0},{2,3},{3,2},{4,5},{5,4},{6,7},{7,6},{8,9},{9,8},{10,11... | collective-permute-start | bytes 3244040 | tf_op jit(solution)/shard_map/ppermute | solution.py:1404
  129.5 41.4 %collective-permute-start.18 = (bf16[528,1024]{1,0:T(8,128)(2,1)}, bf16[528,1024]{1,0:T(8,128)(2,1)S(1)}, u32[]{:S(2)}, u32[]{:S(2)}) collective-permute-start(bf16[528,1024]{1,0:T(8,128)(2,1)} %copy.87.cot.c0.refs_1_), channel_id=1, source_target_pairs={{0,2},{2,0},{1,3},{3,1},{4,6},{6,4},{5,7},{7,5},{8,10},{10,8},{9,1... | collective-permute-start | bytes 3244040 | tf_op jit(solution)/shard_map/ppermute | solution.py:1404
  204.0 26.4 %collective-permute-start.23 = (bf16[528,1024]{1,0:T(8,128)(2,1)}, bf16[528,1024]{1,0:T(8,128)(2,1)S(1)}, u32[]{:S(2)}, u32[]{:S(2)}) collective-permute-start(bf16[528,1024]{1,0:T(8,128)(2,1)} %get-tuple-element.110.normal.n0), channel_id=1, source_target_pairs={{0,2},{2,0},{1,3},{3,1},{4,6},{6,4},{5,7},{7,5},{8,10},{10,8},{9,1... | collective-permute-start | bytes 3244040 | tf_op jit(solution)/shard_map/ppermute | solution.py:1404
  257.0 48.8 %collective-permute-start.27 = (bf16[528,1024]{1,0:T(8,128)(2,1)S(1)}, bf16[528,1024]{1,0:T(8,128)(2,1)S(1)}, u32[]{:S(2)}, u32[]{:S(2)}) collective-permute-start(bf16[528,1024]{1,0:T(8,128)(2,1)S(1)} %copy-done.47), channel_id=1, source_target_pairs={{0,1},{1,0},{2,3},{3,2},{4,5},{5,4},{6,7},{7,6},{8,9},{9,8},{10,11... | collective-permute-start | bytes 3244040 | tf_op jit(solution)/shard_map/ppermute | solution.py:1404
  264.0 41.9 %collective-permute-start.29 = (bf16[528,1024]{1,0:T(8,128)(2,1)}, bf16[528,1024]{1,0:T(8,128)(2,1)S(1)}, u32[]{:S(2)}, u32[]{:S(2)}) collective-permute-start(bf16[528,1024]{1,0:T(8,128)(2,1)} %add.181), channel_id=1, source_target_pairs={{0,2},{2,0},{1,3},{3,1},{4,6},{6,4},{5,7},{7,5},{8,10},{10,8},{9,1... | collective-permute-start | bytes 3244040 | tf_op jit(solution)/shard_map/ppermute | solution.py:1404
  314.5 26.2 %collective-permute-start.25 = (bf16[528,1024]{1,0:T(8,128)(2,1)}, bf16[528,1024]{1,0:T(8,128)(2,1)S(1)}, u32[]{:S(2)}, u32[]{:S(2)}) collective-permute-start(bf16[528,1024]{1,0:T(8,128)(2,1)} %get-tuple-element.118), channel_id=1, source_target_pairs={{0,1},{1,0},{2,3},{3,2},{4,5},{5,4},{6,7},{7,6},{8,9},{9,8},{10,11... | collective-permute-start | bytes 3244040 | tf_op jit(solution)/shard_map/ppermute | solution.py:1404
  324.5 65.3 %collective-permute-start.34 = (bf16[2,4,512,128]{3,2,1,0:T(8,128)(2,1)}, bf16[2,4,512,128]{3,2,1,0:T(8,128)(2,1)}, u32[]{:S(2)}, u32[]{:S(2)}) collective-permute-start(bf16[2,4,512,128]{3,2,1,0:T(8,128)(2,1)} %get-tuple-element.135), channel_id=1, source_target_pairs={{0,8},{8,16},{16,24},{24,0},{1,9},{9,17},{17,25},{25,1},{2,10},{10... | collective-permute-start | bytes 3145736 | tf_op jit(solution)/shard_map/ppermute | solution.py:1410
  329.2 63.2 %collective-permute-start.32 = (bf16[2,4,256,128]{3,2,1,0:T(8,128)(2,1)}, bf16[2,4,256,128]{3,2,1,0:T(8,128)(2,1)}, u32[]{:S(2)}, u32[]{:S(2)}) collective-permute-start(bf16[2,4,256,128]{3,2,1,0:T(8,128)(2,1)} %get-tuple-element.128), channel_id=1, source_target_pairs={{0,4},{4,0},{1,5},{5,1},{2,6},{6,2},{3,7},{7,3},{8,12},{12,8},{9,1... | collective-permute-start | bytes 1572872 | tf_op jit(solution)/shard_map/ppermute | solution.py:1404
  334.6 57.9 %collective-permute-start.31 = (bf16[528,1024]{1,0:T(8,128)(2,1)}, bf16[528,1024]{1,0:T(8,128)(2,1)S(1)}, u32[]{:S(2)}, u32[]{:S(2)}) collective-permute-start(bf16[528,1024]{1,0:T(8,128)(2,1)} %add.182), channel_id=1, source_target_pairs={{0,2},{2,0},{1,3},{3,1},{4,6},{6,4},{5,7},{7,5},{8,10},{10,8},{9,1... | collective-permute-start | bytes 3244040 | tf_op jit(solution)/shard_map/ppermute | solution.py:1404
  413.8 27.7 %collective-permute-start.38 = (bf16[2,528,1024]{2,1,0:T(8,128)(2,1)}, bf16[2,528,1024]{2,1,0:T(8,128)(2,1)S(1)}, u32[]{:S(2)}, u32[]{:S(2)}) collective-permute-start(bf16[2,528,1024]{2,1,0:T(8,128)(2,1)} %get-tuple-element.142), channel_id=1, source_target_pairs={{0,1},{1,0},{2,3},{3,2},{4,5},{5,4},{6,7},{7,6},{8,9},{9,8},{10,11... | collective-permute-start | bytes 6488072 | tf_op jit(solution)/shard_map/ppermute | solution.py:1404
  413.9 27.6 %collective-permute-start.39 = (bf16[2,4,512,128]{3,2,1,0:T(8,128)(2,1)}, bf16[2,4,512,128]{3,2,1,0:T(8,128)(2,1)S(1)}, u32[]{:S(2)}, u32[]{:S(2)}) collective-permute-start(bf16[2,4,512,128]{3,2,1,0:T(8,128)(2,1)} %add.183.refs_9_), channel_id=1, source_target_pairs={{0,8},{8,16},{16,24},{24,0},{1,9},{9,17},{17,25},{25,1},{2,10},{10... | collective-permute-start | bytes 3145736 | tf_op jit(solution)/shard_map/ppermute | solution.py:1410
  453.2 31.3 %collective-permute-start.41 = (bf16[2,4,512,128]{3,2,1,0:T(8,128)(2,1)}, bf16[2,4,512,128]{3,2,1,0:T(8,128)(2,1)S(1)}, u32[]{:S(2)}, u32[]{:S(2)}) collective-permute-start(bf16[2,4,512,128]{3,2,1,0:T(8,128)(2,1)} %add.185), channel_id=1, source_target_pairs={{0,8},{8,16},{16,24},{24,0},{1,9},{9,17},{17,25},{25,1},{2,10},{10... | collective-permute-start | bytes 3145736 | tf_op jit(solution)/shard_map/ppermute | solution.py:1410
  453.2 31.3 %collective-permute-start.40 = (bf16[528,1024]{1,0:T(8,128)(2,1)}, bf16[528,1024]{1,0:T(8,128)(2,1)S(1)}, u32[]{:S(2)}, u32[]{:S(2)}) collective-permute-start(bf16[528,1024]{1,0:T(8,128)(2,1)} %get-tuple-element.145), channel_id=1, source_target_pairs={{0,2},{2,0},{1,3},{3,1},{4,6},{6,4},{5,7},{7,5},{8,10},{10,8},{9,1... | collective-permute-start | bytes 3244040 | tf_op jit(solution)/shard_map/ppermute | solution.py:1404
  454.4 30.1 %collective-permute-start.42 = (bf16[4,256,384]{2,1,0:T(8,128)(2,1)}, bf16[4,256,384]{2,1,0:T(8,128)(2,1)S(1)}, u32[]{:S(2)}, u32[]{:S(2)}) collective-permute-start(bf16[4,256,384]{2,1,0:T(8,128)(2,1)} %get-tuple-element.148), channel_id=1, source_target_pairs={{0,4},{4,0},{1,5},{5,1},{2,6},{6,2},{3,7},{7,3},{8,12},{12,8},{9,1... | collective-permute-start | bytes 2359304 | tf_op jit(solution)/shard_map/ppermute | solution.py:1404
  459.8 24.6 %collective-permute-start.43 = (bf16[4,256,128]{2,1,0:T(8,128)(2,1)S(1)}, bf16[4,256,128]{2,1,0:T(8,128)(2,1)S(1)}, u32[]{:S(2)}, u32[]{:S(2)}) collective-permute-start(bf16[4,256,128]{2,1,0:T(8,128)(2,1)S(1)} %get-tuple-element.200), channel_id=1, source_target_pairs={{0,2},{2,0},{1,3},{3,1},{4,6},{6,4},{5,7},{7,5},{8,10},{10,8},{9,1... | collective-permute-start | bytes 786440 | tf_op jit(solution)/shard_map/ppermute | solution.py:1404
  501.9 21.0 %collective-permute-start.52 = (bf16[4,512,128]{2,1,0:T(8,128)(2,1)S(1)}, bf16[4,512,128]{2,1,0:T(8,128)(2,1)S(1)}, u32[]{:S(2)}, u32[]{:S(2)}) collective-permute-start(bf16[4,512,128]{2,1,0:T(8,128)(2,1)S(1)} %get-tuple-element.190), channel_id=1, source_target_pairs={{0,4},{4,0},{1,5},{5,1},{2,6},{6,2},{3,7},{7,3},{8,12},{12,8},{9,1... | collective-permute-start | bytes 1572872 | tf_op jit(solution)/shard_map/ppermute | solution.py:1404
  508.2 20.5 %collective-permute-start.49 = (bf16[256,512]{1,0:T(8,128)(2,1)S(1)}, bf16[256,512]{1,0:T(8,128)(2,1)S(1)}, u32[]{:S(2)}, u32[]{:S(2)}) collective-permute-start(bf16[256,512]{1,0:T(8,128)(2,1)S(1)} %get-tuple-element.194), channel_id=1, source_target_pairs={{0,8},{8,16},{16,24},{24,0},{1,9},{9,17},{17,25},{25,1},{2,10},{10... | collective-permute-start | bytes 786440 | tf_op jit(solution)/shard_map/ppermute | solution.py:1410
  508.9 22.3 %collective-permute-start.50 = (bf16[256,512]{1,0:T(8,128)(2,1)S(1)}, bf16[256,512]{1,0:T(8,128)(2,1)S(1)}, u32[]{:S(2)}, u32[]{:S(2)}) collective-permute-start(bf16[256,512]{1,0:T(8,128)(2,1)S(1)} %get-tuple-element.193), channel_id=1, source_target_pairs={{0,16},{8,24},{16,0},{24,8},{1,17},{9,25},{17,1},{25,9},{2,18},{10... | collective-permute-start | bytes 786440 | tf_op jit(solution)/shard_map/ppermute | solution.py:1410
  509.0 22.2 %collective-permute-start.51 = (bf16[256,512]{1,0:T(8,128)(2,1)S(1)}, bf16[256,512]{1,0:T(8,128)(2,1)S(1)}, u32[]{:S(2)}, u32[]{:S(2)}) collective-permute-start(bf16[256,512]{1,0:T(8,128)(2,1)S(1)} %get-tuple-element.192), channel_id=1, source_target_pairs={{0,24},{8,0},{16,8},{24,16},{1,25},{9,1},{17,9},{25,17},{2,26},{10... | collective-permute-start | bytes 786440 | tf_op jit(solution)/shard_map/ppermute | solution.py:1410
  (81 other events, 497.8 us)
Sparse Core Ops, SparseCore 0:
  45.1 70.5 all-gather.2

commit v3 on v2

--- a/solution.py
+++ b/solution.py
@@ -162,9 +162,7 @@
     v_t,
     queries,
     acc,
-    acc_extra,
     state,
-    state_extra,
 ):
     sources, _, width = q.shape
     heads = width // HEAD
@@ -206,21 +204,37 @@
         for head in range(heads):
             acc[head] = mix(v_extra_t, weights_extra, head) + mix(values_t, weights, head)
 
-        def one_key(f, _):
-            scores = nt(frame_ref(k, f), queries[...])
+        def some_keys(which):
+            scores = [nt(frame_ref(k, f), queries[...]) for f in which]
             before = state[0:1]
-            top = jnp.maximum(before, jnp.max(scores, 0, keepdims=True))
+            top = before
+            for s in scores:
+                top = jnp.maximum(top, jnp.max(s, 0, keepdims=True))
             fade = weigh(before, top)
-            weights = weigh(scores, top)
+            weights = [weigh(s, top) for s in scores]
             state[0:1] = top
-            state[1:2] = state[1:2] * fade + jnp.sum(weights, 0, keepdims=True)
-            weights = weights.astype(BF)
-            values_t = v_t[f]
+            total = state[1:2] * fade
+            for w in weights:
+                total = total + jnp.sum(w, 0, keepdims=True)
+            state[1:2] = total
+            weights = [w.astype(BF) for w in weights]
             for head in range(heads):
-                acc[head] = acc[head] * fade[:, head * PATCHES : (head + 1) * PATCHES] + mix(values_t, weights, head)
+                out = acc[head] * fade[:, head * PATCHES : (head + 1) * PATCHES]
+                for f, w in zip(which, weights):
+                    out = out + mix(v_t[f], w, head)
+                acc[head] = out
+
+        def pair(i, _):
+            some_keys([first + 2 * i, first + 2 * i + 1])
             return 0
 
-        lax.fori_loop(first, g, one_key, 0)
+        count = jnp.maximum(g - first, 0)
+        lax.fori_loop(0, count // 2, pair, 0)
+
+        @pl.when(count % 2 == 1)
+        def _():
+            some_keys([g - 1])
+
         total = state[1:2]
         result = jnp.concatenate(
             [acc[head] / total[:, head * PATCHES : (head + 1) * PATCHES] for head in range(heads)], 0
@@ -235,37 +249,26 @@
     lax.fori_loop(0, frames, one_frame, 0)
 
     q_extra = stack_heads(jnp.concatenate([q[s, patch_rows:] for s in range(sources)], 0), turned_lanes)
-    queries[: q_extra.shape[0]] = q_extra
     first = jnp.concatenate([query_start[:1]] * heads, 1)
     last = jnp.concatenate([query_frame[:1]] * heads, 1)
-    scores = jnp.where((key_at >= first) & (key_at <= last), nt(k_extra, q_extra), MASKED)
-    top = jnp.max(scores, 0, keepdims=True)
-    weights = weigh(scores, top)
-    state_extra[0:1] = top
-    state_extra[1:2] = jnp.sum(weights, 0, keepdims=True)
-    acc_extra[...] = nn(v_extra_t, weights.astype(BF))
-
-    def extra_key(f, _):
-        visible = (first <= f) & (last >= f)
-        scores = jnp.where(visible, nt(frame_ref(k, f), queries[: q_extra.shape[0]]), MASKED)
-        before = state_extra[0:1]
-        top = jnp.maximum(before, jnp.max(scores, 0, keepdims=True))
-        fade = weigh(before, top)
+    every = [jnp.where((key_at >= first) & (key_at <= last), nt(k_extra, q_extra), MASKED)]
+    for f in range(frames):
+        every.append(jnp.where((first <= f) & (last >= f), nt(frame_ref(k, f), q_extra), MASKED))
+    top = jnp.max(every[0], 0, keepdims=True)
+    for scores in every[1:]:
+        top = jnp.maximum(top, jnp.max(scores, 0, keepdims=True))
+    total = jnp.zeros_like(top)
+    result = jnp.zeros((width, q_extra.shape[0]), F32)
+    for scores, values_t in zip(every, [v_extra_t] + [v_t[f] for f in range(frames)]):
         weights = weigh(scores, top)
-        state_extra[0:1] = top
-        state_extra[1:2] = state_extra[1:2] * fade + jnp.sum(weights, 0, keepdims=True)
-        acc_extra[...] = acc_extra[...] * fade + nn(v_t[f], weights.astype(BF))
-        return 0
-
-    lax.fori_loop(0, frames, extra_key, 0)
-    result = unstack_heads((acc_extra[...] / state_extra[1:2]).T, plain_lanes)
+        total = total + jnp.sum(weights, 0, keepdims=True)
+        result = result + nn(values_t, weights.astype(BF))
+    result = unstack_heads((result / total).T, plain_lanes)
     result = jnp.where(query_pad[:, :1] > 0, jnp.broadcast_to(uniform, result.shape), result)
     for s in range(sources):
         exact[s, patch_rows:, :] = result[s * EXTRA : (s + 1) * EXTRA]
         mixed[s, patch_rows:, :] = result[s * EXTRA : (s + 1) * EXTRA].astype(BF)
-    logs_extra[...] = jnp.broadcast_to(
-        state_extra[0:1] + jnp.log2(state_extra[1:2]) * (1.0 / SCALE2), logs_extra.shape
-    )
+    logs_extra[...] = jnp.broadcast_to(top + jnp.log2(total) * (1.0 / SCALE2), logs_extra.shape)
 
 
 def attend_call(start, key_frame, query_start, query_frame, query_pad, q, k, v, waits=()):
@@ -289,9 +292,7 @@
             pltpu.VMEM((frames, width, PATCHES), BF),
             pltpu.VMEM((heads * PATCHES, width), BF),
             pltpu.VMEM((heads, HEAD, PATCHES), F32),
-            pltpu.VMEM((width, stacked), F32),
             pltpu.VMEM((8, heads * PATCHES), F32),
-            pltpu.VMEM((8, stacked), F32),
         ],
         compiler_params=pltpu.CompilerParams(vmem_limit_bytes=VMEM),
         cost_estimate=cost(
@@ -305,6 +306,8 @@
 
 def attend_back_kernel(
     frames_local,
+    chips,
+    flip,
     start,
     key_frame,
     query_start,
@@ -313,26 +316,33 @@
     q,
     k,
     v,
-    grad,
-    exact,
-    logs,
-    logs_extra,
-    cosine,
-    sine,
-    turn,
-    out,
-    k_t,
-    queries,
-    grads,
-    dq_t,
-    dk,
-    dv,
-    dq_extra,
-    dk_extra,
-    dv_extra,
-    centers,
+    *rest,
 ):
+    pieces = rest[:chips]
+    (
+        exact,
+        logs,
+        logs_extra,
+        cosine,
+        sine,
+        turn,
+        out,
+        grad,
+        k_t,
+        queries,
+        grads,
+        dq_t,
+        dk,
+        dv,
+        dq_extra,
+        dk_extra,
+        dv_extra,
+        centers,
+    ) = rest[chips:]
     sources, _, width = q.shape
+    for i in range(chips):
+        for core in range(2):
+            grad[2 * (i ^ flip[0]) + core] = pieces[i][core]
     half = width // 2
     heads = width // HEAD
     frames = sources * frames_local
@@ -363,8 +373,6 @@
     k_extra = gather_extra(k)
     v_extra = gather_extra(v)
     k_extra_t = k_extra.T
-    dk[...] = jnp.zeros_like(dk)
-    dv[...] = jnp.zeros_like(dv)
     dk_extra[...] = jnp.zeros_like(dk_extra)
     dv_extra[...] = jnp.zeros_like(dv_extra)
     key_at = key_frame[:, :1]
@@ -393,23 +401,40 @@
         grads[...] = stack_heads(grad_rows, plain_lanes)
         centers[...] = jnp.broadcast_to(center_of(grad_rows, frame_ref(exact, g)), centers.shape)
         allowed = (key_at >= first) & (key_at <= g)
-        dv_part, dk_part, change = tile(
-            k_extra, v_extra, queries[...], grads[...], logs[g, :1], centers[:1], allowed
-        )
+        query, query_grad, log, center = queries[...], grads[...], logs[g, :1], centers[:1]
+        dv_part, dk_part, change = tile(k_extra, v_extra, query, query_grad, log, center, allowed)
         dv_extra[...] += dv_part
         dk_extra[...] += dk_part
         add_dq(dq_t.at[g], k_extra_t, change, False)
-
-        def one_key(f, _):
-            dv_part, dk_part, change = tile(
-                frame_ref(k, f), frame_ref(v, f), queries[...], grads[...], logs[g, :1], centers[:1], None
-            )
-            dv[f] += dv_part
-            dk[f] += dk_part
-            add_dq(dq_t.at[g], k_t[f], change, True)
+        dv_part, dk_part, change = tile(
+            frame_ref(k, g), frame_ref(v, g), query, query_grad, log, center, jnp.broadcast_to(first <= g, log.shape)
+        )
+        dv[g] = dv_part
+        dk[g] = dk_part
+        add_dq(dq_t.at[g], k_t[g], change, True)
+
+        def some_keys(which):
+            parts = [
+                tile(frame_ref(k, f), frame_ref(v, f), queries[...], grads[...], logs[g, :1], centers[:1], None)
+                for f in which
+            ]
+            for f, (dv_part, dk_part, _) in zip(which, parts):
+                dv[f] += dv_part
+                dk[f] += dk_part
+            for f, (_, _, change) in zip(which, parts):
+                add_dq(dq_t.at[g], k_t[f], change, True)
+
+        def pair(i, _):
+            some_keys([first + 2 * i, first + 2 * i + 1])
             return 0
 
-        lax.fori_loop(first, g + 1, one_key, 0)
+        count = jnp.maximum(g - first, 0)
+        lax.fori_loop(0, count // 2, pair, 0)
+
+        @pl.when(count % 2 == 1)
+        def _():
+            some_keys([g - 1])
+
         return pad_grad + jnp.where(first > frames, jnp.sum(grad_rows.astype(F32), 0, keepdims=True), 0.0)
 
     pad_grad = lax.fori_loop(0, frames, one_frame, jnp.zeros((1, width), F32))
@@ -432,17 +457,23 @@
     dk_extra[...] += dk_part
     dq_extra[...] = nn(k_extra_t, change)
 
-    def extra_key(f, _):
-        visible = (first <= f) & (last >= f)
-        dv_part, dk_part, change = tile(
-            frame_ref(k, f), frame_ref(v, f), queries[:stacked], grads[:stacked], log, center, visible
-        )
-        dv[f] += dv_part
-        dk[f] += dk_part
-        dq_extra[...] += nn(k_t[f], change)
+    def extra_keys(i, _):
+        which = [2 * i, 2 * i + 1]
+        parts = [
+            tile(
+                frame_ref(k, f), frame_ref(v, f), queries[:stacked], grads[:stacked], log, center, (first <= f) & (last >= f)
+            )
+            for f in which
+        ]
+        total = dq_extra[...]
+        for f, (dv_part, dk_part, change) in zip(which, parts):
+            dv[f] += dv_part
+            dk[f] += dk_part
+            total = total + nn(k_t[f], change)
+        dq_extra[...] = total
         return 0
 
-    lax.fori_loop(0, frames, extra_key, 0)
+    lax.fori_loop(0, frames // 2, extra_keys, 0)
 
     def emit(s, rows, dq_rows, dk_rows, dv_rows, real=None):
         cos = cosine[s, rows]
@@ -474,8 +505,9 @@
 
 
 def attend_back_call(
-    start, key_frame, query_start, query_frame, query_pad, q, k, v, grad, exact, logs, logs_extra, cosine, sine, turn, waits=()
+    flip, start, key_frame, query_start, query_frame, query_pad, q, k, v, grad, exact, logs, logs_extra, cosine, sine, turn, waits=()
 ):
+    chips = len(grad)
     sources, rows, width = q.shape
     frames_local = rows // PATCHES
     frames = sources * frames_local
@@ -483,11 +515,12 @@
     heads = width // HEAD
     vmem = pl.BlockSpec(memory_space=pltpu.VMEM)
     return pl.pallas_call(
-        waiting(functools.partial(attend_back_kernel, frames_local), 15, waits),
-        in_specs=[pl.BlockSpec(memory_space=pltpu.SMEM)] + [vmem] * 14 + [ANY_REF] * len(waits),
+        waiting(functools.partial(attend_back_kernel, frames_local, chips), 15 + chips, waits),
+        in_specs=[pl.BlockSpec(memory_space=pltpu.SMEM)] * 2 + [vmem] * (13 + chips) + [ANY_REF] * len(waits),
         out_specs=vmem,
         out_shape=jax.ShapeDtypeStruct((sources, rows, 3 * width), BF),
         scratch_shapes=[
+            pltpu.VMEM((sources, rows, width), BF),
             pltpu.VMEM((frames, width, PATCHES), BF),
             pltpu.VMEM((heads * PATCHES, width), BF),
             pltpu.VMEM((heads * PATCHES, width), BF),
@@ -506,7 +539,9 @@
             transcendentals=heads * frames * frames * PATCHES * PATCHES // 2,
         ),
         name="attend_back",
-    )(start, key_frame, query_start, query_frame, query_pad, q, k, v, grad, exact, logs, logs_extra, cosine, sine, turn, *waits)
+    )(
+        flip, start, key_frame, query_start, query_frame, query_pad, q, k, v, *grad, exact, logs, logs_extra, cosine, sine, turn, *waits
+    )
 
 
 def gelu_parts(hidden):
@@ -738,7 +773,7 @@
         input_output_aliases={first + i: len(outputs) + i for i in range(len(carry))},
         scratch_shapes=list(scratch),
         compiler_params=pltpu.CompilerParams(vmem_limit_bytes=VMEM),
-        cost_estimate=cost(flops=flops, bytes_accessed=size, transcendentals=transcendentals),
+        cost_estimate=cost(flops=1, bytes_accessed=1, transcendentals=0),
         name=name,
     )(*inputs, *waits)
 
@@ -754,6 +789,45 @@
 
 def stack_call(pieces, waits=()):
     return local_call(stack_kernel, "stack", pieces, [shape_of(len(pieces), *pieces[0].shape)], waits=waits)[0]
+
+
+def add_piece_kernel(pieces, other, *outs):
+    if len(outs) == 1:
+        outs[0][...] = (pieces[0].astype(F32) + other[...].astype(F32)).astype(BF)
+    else:
+        for i, out in enumerate(outs):
+            out[...] = (pieces[0, i].astype(F32) + other[i].astype(F32)).astype(BF)
+
+
+def add_apart_kernel(one, two, *outs):
+    for i, out in enumerate(outs):
+        out[...] = (one[i].astype(F32) + two[i].astype(F32)).astype(BF)
+
+
+def add_apart_call(one, two, waits, carry=()):
+    return local_call(
+        add_apart_kernel, "add", [one, two], [shape_of(*one.shape[1:])] * one.shape[0], waits=waits, carry=carry
+    )
+
+
+def add_piece_call(pieces, index, other, waits, apart=False):
+    outs = [other.shape[1:]] * other.shape[0] if apart else [other.shape]
+    block = pl.BlockSpec((1,) + other.shape, lambda i: (index,) + (0,) * other.ndim)
+
+    def whole(shape):
+        return pl.BlockSpec(shape, lambda i: (0,) * len(shape))
+
+    result = pl.pallas_call(
+        waiting(add_piece_kernel, 2, waits),
+        grid=(1,),
+        in_specs=[block, whole(other.shape)] + [ANY_REF] * len(waits),
+        out_specs=[whole(o) for o in outs],
+        out_shape=[shape_of(*o) for o in outs],
+        compiler_params=pltpu.CompilerParams(vmem_limit_bytes=VMEM),
+        cost_estimate=cost(flops=1, bytes_accessed=1, transcendentals=0),
+        name="add_piece",
+    )(pieces, other, *waits)
+    return result if apart else result[0]
 
 
 def copy_kernel(source, out):
@@ -780,10 +854,9 @@
 
 
 def front_kernel(*refs):
-    *parts, entered, near, entered_out = refs
+    *parts, near = refs
     for s, ref in enumerate(parts):
         near[s] = ref[...]
-    entered_out[...] = entered[...]
 
 
 def pack_kernel(n_z, place, near, far, own, one, two, three, vectors, bias, expand_bias):
@@ -962,7 +1035,7 @@
         out_specs=[spec(a) for a in outputs],
         out_shape=list(outputs),
         compiler_params=pltpu.CompilerParams(vmem_limit_bytes=VMEM),
-        cost_estimate=cost(flops=20 * rows * D, bytes_accessed=size, transcendentals=0),
+        cost_estimate=cost(flops=1, bytes_accessed=1, transcendentals=0),
         name=name,
     )(*inputs, *waits)
 
@@ -1022,33 +1095,38 @@
 
 
 def triple_kernel(
-    place, normed, triple_grad, grad_rows, triple, e0, e1, e2, e3, own, one, two, three, rows_own, rows_far, rows_give, bias, sums, entered
+    place, normed, triple_grad, grad_rows, triple, e0, e1, e2, e3, own, one, two, three, rows_own, rows_far, rows_give, bias, sums, entered, held
 ):
     step = pl.program_id(0)
     count, rows, wide = triple_grad.shape
-    flat = triple_grad[...].reshape(count * rows, wide)
-    grad = tn(normed[...].reshape(count * rows, normed.shape[-1]), flat).astype(BF)
-    back = nt(grad_rows[0], triple[...])
-    low = back.astype(BF)
     outs = (own, one, two, three)
     rows_outs = (rows_own, rows_give.at[0], rows_far, rows_give.at[1])
-    for m, ref in enumerate((e0, e1, e2, e3)):
-
-        @pl.when(step == m)
-        def _(m=m, ref=ref):
-            outs[m][...] = grad
-            rows_outs[m][...] = low
-            entered[...] = ref[...]
 
     @pl.when(step == 0)
     def _():
         bias[...] = jnp.zeros_like(bias)
         sums[...] = jnp.zeros_like(sums)
 
-    bias[...] += jnp.sum(grad_rows[0].astype(F32), 0, keepdims=True)
+    for m, ref in enumerate((e0, e1, e2, e3)):
+
+        @pl.when(step == m)
+        def _(ref=ref):
+            entered[...] = ref[...]
+
+    flat = triple_grad[...].reshape(count * rows, wide)
+    held[...] = tn(normed[...].reshape(count * rows, normed.shape[-1]), flat).astype(BF)
+    back = nt(grad_rows[0], triple[...])
     unit, _ = norm_parts(entered[...].astype(F32))
     sums[0:1] += jnp.sum(back * unit, 0, keepdims=True)
     sums[1:2] += jnp.sum(back, 0, keepdims=True)
+    entered[...] = back.astype(BF)
+    bias[...] += jnp.sum(grad_rows[0].astype(F32), 0, keepdims=True)
+    for m in range(4):
+
+        @pl.when(step == m)
+        def _(m=m):
+            outs[m][...] = held[...]
+            rows_outs[m][...] = entered[...]
 
 
 def triple_call(place, normed, triple_grad, triple, entered, waits):
@@ -1074,7 +1152,7 @@
             + [fixed(e.shape) for e in entered]
             + [ANY_REF] * len(waits),
             out_specs=[fixed(o.shape) for o in outs],
-            scratch_shapes=[pltpu.VMEM((rows, D), BF)],
+            scratch_shapes=[pltpu.VMEM((rows, D), BF), pltpu.VMEM((part, wide), BF)],
         ),
         out_shape=outs,
         compiler_params=pltpu.CompilerParams(vmem_limit_bytes=VMEM),
@@ -1088,10 +1166,11 @@
     far_out[...] = (far[...].astype(F32) + got[1].astype(F32)).astype(BF)
 
 
-def tail_sum_kernel(near, near_got, out, out_got, total):
+def tail_sum_kernel(near, near_got, out, out_got, *totals):
     part = near.shape[-1]
-    total[:, :, :part] = (near[...].astype(F32) + near_got[...].astype(F32)).astype(BF)
-    total[:, :, part:] = (out[...].astype(F32) + out_got[...].astype(F32)).astype(BF)
+    for s, total in enumerate(totals):
+        total[:, :part] = (near[s].astype(F32) + near_got[s].astype(F32)).astype(BF)
+        total[:, part:] = (out[0, s].astype(F32) + out_got[s].astype(F32)).astype(BF)
 
 
 def unpack_kernel(n_z, place, p0, p1, p2, p3, near, far, held):
@@ -1156,49 +1235,44 @@
             reduce[span(p * 4 + at, part), :] = ref[rows + p * part : rows + (p + 1) * part].astype(F32)
 
 
-def fill_weights(place, step, parts, weight_in, weight_out):
+def fill_weights(place, near, far, weight_in, weight_out):
     y, z, shard = place[1], place[2], place[4]
-    n_z = len(parts)
-    part = parts[0].shape[-1]
+    n_z = len(near)
+    part = near[0].shape[-1]
     rows = D // 4
-    unit = (z - step + n_z) % n_z
-    if weight_in is not None:
-        for s, ref in enumerate(parts):
-
-            @pl.when(step == s)
-            def _(ref=ref):
-                for side in range(2):
-                    for m in range(4):
-                        weight_in[span(shard ^ m, rows), side * part : (side + 1) * part] = ref[side, m, :rows]
-
-    for side in range(2):
-        at = pl.ds(pl.multiple_of(rows + (y ^ side) * part, part), part)
-        for s, ref in enumerate(parts):
-            for flip in range(2):
-                features = span(2 * ((z - s + n_z) % n_z) + (y ^ flip), part)
-                weight_out[side * part : (side + 1) * part, features] = ref[flip, unit ^ shard, at, :]
+    for s in range(n_z):
+        for side, ref in ((0, near[s]), (1, far[s])):
+            if weight_in is not None:
+                for m in range(4):
+                    weight_in[s, span(shard ^ m, rows), side * part : (side + 1) * part] = ref[m, :rows]
+            features = span(2 * ((z - s + n_z) % n_z) + (y ^ side), part)
+            for tile in range(n_z):
+                unit = (z - tile + n_z) % n_z
+                for flip in range(2):
+                    at = pl.ds(pl.multiple_of(rows + (y ^ flip) * part, part), part)
+                    weight_out[tile, flip * part : (flip + 1) * part, features] = ref[unit ^ shard, at, :]
 
 
 def feed_kernel(
-    place, normal, normal_other, cot, cot_other, p0, p1, p2, p3, bias, active, slope, keep, give, d_bias, give_acc, weight_in, weight_out
+    place, normal, normal_other, cot, cot_other, p0, p1, p2, p3, f0, f1, f2, f3, bias, active, slope, keep, give, d_bias, give_acc, weight_in, weight_out
 ):
     step = pl.program_id(0)
     rows = normal.shape[0]
-    fill_weights(place, step, (p0, p1, p2, p3), weight_in, weight_out)
 
     @pl.when(step == 0)
     def _():
+        fill_weights(place, (p0, p1, p2, p3), (f0, f1, f2, f3), weight_in, weight_out)
         keep[...] = jnp.zeros_like(keep)
         give_acc[...] = jnp.zeros_like(give_acc)
 
     d_bias[...] = jnp.zeros_like(d_bias)
     for i, values, outer, total in ((0, normal, cot, keep), (1, normal_other, cot_other, give_acc)):
-        act, gradient = gelu_parts(nn(values[...], weight_in[...]) + bias[0])
-        grad = (nt(outer[...], weight_out[...]) * gradient).astype(BF)
+        act, gradient = gelu_parts(nn(values[...], weight_in[step]) + bias[0])
+        grad = (nt(outer[...], weight_out[step]) * gradient).astype(BF)
         active[i * rows : (i + 1) * rows] = act.astype(BF)
         slope[i * rows : (i + 1) * rows] = grad
         d_bias[0] += jnp.sum(grad.astype(F32), 0, keepdims=True)
-        total[...] += nt(grad, weight_in[...])
+        total[...] += nt(grad, weight_in[step])
 
     @pl.when(step == pl.num_programs(0) - 1)
     def _():
@@ -1223,14 +1297,16 @@
     p1,
     p2,
     p3,
+    f0,
+    f1,
+    f2,
+    f3,
     keep,
     give,
     keep_far,
     give_far,
-    d0,
-    d1,
-    d2,
-    d3,
+    grads,
+    sent,
     normal_t,
     cot_all,
     give_acc,
@@ -1243,16 +1319,15 @@
 ):
     y, z, shard = place[1], place[2], place[4]
     step = pl.program_id(0)
-    grads = (d0, d1, d2, d3)
-    n_z = len(grads)
+    n_z = grads.shape[0]
     part = p0.shape[-1]
     rows = n0.shape[0]
     deep = D // 4
     totals = (keep, give_acc, keep_far_acc, give_far_acc)
-    fill_weights(place, step, (p0, p1, p2, p3), None, weight_out)
 
     @pl.when(step == 0)
     def _():
+        fill_weights(place, (p0, p1, p2, p3), (f0, f1, f2, f3), None, weight_out)
         for i, (normal, cot) in enumerate(((n0, c0), (n1, c1), (n2, c2), (n3, c3))):
             normal_t[:, i * rows : (i + 1) * rows] = normal[...].T
             cot_all[i * rows : (i + 1) * rows] = cot[...]
@@ -1263,31 +1338,28 @@
         active_all[at] = act[...]
         slope_all[at] = grad[...]
         for j in range(2):
-            totals[2 * i + j][...] += nn(act[j * rows : (j + 1) * rows], weight_out[...])
+            totals[2 * i + j][...] += nn(act[j * rows : (j + 1) * rows], weight_out[step])
 
     held[...] = nn(normal_t[...], slope_all[...]).astype(BF)
-    for s, ref in enumerate(grads):
-
-        @pl.when((n_z - step) % n_z == s)
-        def _(ref=ref):
-            for side in range(2):
-                for m in range(4):
-                    ref[side, m, :deep] = held[span(shard ^ m, deep), side * part : (side + 1) * part]
-
-    weight_out[...] = tn(active_all[...], cot_all[...]).astype(BF)
+    for side in range(2):
+        for m in range(4):
+            grads[(n_z - step) % n_z, side, m, :deep] = held[span(shard ^ m, deep), side * part : (side + 1) * part]
+    held_t = weight_out.at[step]
+    held_t[...] = tn(active_all[...], cot_all[...]).astype(BF)
     unit = (z - step + n_z) % n_z
     for side in range(2):
         at = pl.ds(pl.multiple_of(deep + (y ^ side) * part, part), part)
-        for s, ref in enumerate(grads):
+        for s in range(n_z):
             for flip in range(2):
                 features = span(2 * ((z + s) % n_z) + (y ^ flip), part)
-                ref[flip, unit ^ shard, at, :] = weight_out[side * part : (side + 1) * part, features]
+                grads[s, flip, unit ^ shard, at, :] = held_t[side * part : (side + 1) * part, features]
 
     @pl.when(step == pl.num_programs(0) - 1)
     def _():
         give[...] = give_acc[...].astype(BF)
         keep_far[...] = keep_far_acc[...].astype(BF)
         give_far[...] = give_far_acc[...].astype(BF)
+        sent[...] = grads[n_z - 1]
 
 
 def feed_specs(place, n_z):
@@ -1302,7 +1374,7 @@
 
 def feed_split_call(place, normal, cot, parts, bias, waits=()):
     rows = normal[0].shape[0]
-    n_z = len(parts)
+    n_z = len(parts) // 2
     wide = bias.shape[-1]
     whole, lanes = feed_specs(place, n_z)
     row = pl.BlockSpec((1, 1, wide), lambda t, p: (t, 0, 0))
@@ -1317,7 +1389,7 @@
             grid=(n_z,),
             in_specs=[whole(a) for a in inputs] + [row] + [ANY_REF] * len(waits),
             out_specs=[lanes(2 * rows, wide)] * 2 + [whole(o) for o in outs[2:4]] + [row],
-            scratch_shapes=[pltpu.VMEM(block, F32), pltpu.VMEM((D, wide), BF), pltpu.VMEM((wide, D), BF)],
+            scratch_shapes=[pltpu.VMEM(block, F32), pltpu.VMEM((n_z, D, wide), BF), pltpu.VMEM((n_z, wide, D), BF)],
         ),
         out_shape=outs,
         compiler_params=pltpu.CompilerParams(vmem_limit_bytes=VMEM),
@@ -1330,15 +1402,15 @@
 
 def feed_grad_call(place, normal, cot, active, slope, parts, waits=()):
     rows = normal[0].shape[0]
-    n_z = len(parts)
+    n_z = len(parts) // 2
     wide = active[0].shape[1] // n_z
     whole, lanes = feed_specs(place, n_z)
     block = (rows, D)
-    outs = [shape_of(*block, dtype=F32)] + [shape_of(*block)] * 3 + [shape_of(*p.shape) for p in parts]
+    outs = [shape_of(*block, dtype=F32)] + [shape_of(*block)] * 3 + [shape_of(n_z, 2, *parts[0].shape), shape_of(2, *parts[0].shape)]
     first = [*normal, *cot]
     tiles = [*active, *slope]
     return pl.pallas_call(
-        waiting(feed_grad_kernel, 1 + len(first) + len(tiles) + n_z, waits),
+        waiting(feed_grad_kernel, 1 + len(first) + len(tiles) + 2 * n_z, waits),
         grid_spec=pltpu.PrefetchScalarGridSpec(
             num_scalar_prefetch=1,
             grid=(n_z,),
@@ -1353,7 +1425,7 @@
                 pltpu.VMEM(block, F32),
                 pltpu.VMEM(block, F32),
                 pltpu.VMEM(block, F32),
-                pltpu.VMEM((wide, D), BF),
+                pltpu.VMEM((n_z, wide, D), BF),
                 pltpu.VMEM((D, wide), BF),
                 pltpu.VMEM((4 * rows, wide), BF),
                 pltpu.VMEM((4 * rows, wide), BF),
@@ -1427,51 +1499,54 @@
         [triple_weight] + [lane_row(v) for v in vectors] + [jnp.zeros((16 - len(vectors), qkv_part), BF)], 0
     )
 
-    live_all, cosine, sine, guides = tables(frame_counts[0], presence[0], n_f, frames_local, width // HEAD)
+    live_all = tables(frame_counts[0], presence[0], n_f, frames_local, width // HEAD)[0]
     live = take(live_all, shard)[:, None]
     entered = to_block(tokens[0], frames_local) * live.astype(BF)
     outer = to_block(cotangent[0], frames_local) * live.astype(BF)
 
-    own, one, two, three = local_call(
+    own, one, two, three, packed = local_call(
         split_kernel,
         "split",
         [place, expand_weight, reduce_weight],
         [shape_of(2 * (D // n_f), d_part)] * 4,
         smem=1,
-    )
-    feed = stack_call([own, swap(one), swap(two, "x"), cross_over(three)])
-    feed_y = swap(feed, "y")
-    near, entered = local_call(
+        carry=[packed],
+    )
+    packed_parts = gather_z(packed)
+    feed = stack_call([own, swap(one), swap(two, "x"), cross_over(three)], [packed_parts[1]])
+    near = local_call(
         front_kernel,
         "front",
-        [*gather_z(packed), entered],
-        [shape_of(n_z, *packed.shape), shape_of(*entered.shape)],
-        waits=[feed],
-    )
+        packed_parts,
+        [shape_of(n_z, *packed.shape)],
+    )[0]
     far = swap(near, "y")
+    entered = copy_call(entered, [near, feed])
     entered_x = swap(entered, "x")
     entered_all = [entered, swap(entered), entered_x]
     output_all = lax.all_gather(output_weight, ("z", "y", "x"), axis=0).reshape(n_z, n_y, n_x, width, d_part)
 
-    own, one, two, three, vectors, bias, expand_add = local_call(
+    own, one, two, three, vectors, bias, expand_add, counts = local_call(
         functools.partial(pack_kernel, n_z),
         "pack",
         [place, near, far],
         [shape_of(D // n_f, 3 * width)] * 4
         + [shape_of(8, D, dtype=F32), shape_of(1, 3 * width, dtype=F32), shape_of(n_z, 1, 2 * quarter, dtype=F32)],
         smem=1,
-        waits=[entered_x],
-    )
+        waits=[entered_all[1]],
+        carry=[frame_counts],
+    )
+    _, cosine, sine, guides = tables(counts[0], presence[0], n_f, frames_local, width // HEAD)
     weights = [own, swap(one), swap(two, "x"), cross_over(three)]
-    entered_all.append(swap(copy_call(entered_x, [own])))
-    feed = stack_call([feed, feed_y], [own])
-    feed_parts = [feed, to_z(feed, 1)]
+    entered_all.append(swap(copy_call(entered_x, weights[1:])))
+    feed_near = gather_z(feed)
     turn = jnp.asarray(turn_matrix(width), BF)
     q, k, v, normed, triple = enter_call(
-        place, entered_all, weights, bias, vectors, turn, cosine, sine, [feed]
-    )
-    feed_parts += [to_z(feed_parts[1], 1), to_z(feed, 3)]
-    outer = copy_call(outer, [normed])
+        place, entered_all, weights, bias, vectors, turn, cosine, sine, feed_near[1:2]
+    )
+    outer = copy_call(outer, [normed, *feed_near[2:]])
+    feed_far = [swap(part, "y") for part in feed_near]
+    feed_parts = [*feed_near, *feed_far]
     outer_x = swap(outer, "x")
     outer_all = [outer, swap(outer), outer_x]
     mixed, exact, logs, logs_extra = attend_call(*guides, q, k, v)
@@ -1481,7 +1556,7 @@
         [place, mixed],
         [shape_of(2, rows, width)] * 2,
         smem=1,
-        waits=[*feed_parts[2:], outer_all[1]],
+        waits=[*feed_far[:3], outer_all[1]],
         carry=[outer_x],
     )
     mixed_far = swap(mixed_far, "x")
@@ -1494,7 +1569,7 @@
         [pltpu.VMEM((D // 2, D), BF)],
         smem=1,
         flops=4 * rows * D * D // 2,
-        waits=[outer_all[3]],
+        waits=[outer_all[3], feed_far[3]],
     )
     output_full = output_all.transpose(2, 3, 0, 1, 4).reshape(D // 2, D)
     middle, second = rows_call(
@@ -1513,7 +1588,7 @@
     )
     back_give = swap(back_give)
     back_far = swap(add_call([back_far, swap(back_far_give)]), "x")
-    final, final_give, final_far, final_far_give, *d_feed = feed_grad_call(
+    final, final_give, final_far, final_far_give, d_feed, d_sent = feed_grad_call(
         place, second_all, outer_all, [active, active_far], [slope, slope_far], feed_parts
     )
     middle_grad, branch, sums_two = rows_call(
@@ -1521,7 +1596,7 @@
         "middle_back",
         [middle, outer, back, back_give, back_far, vectors],
         [shape_of(rows, D, dtype=F32), shape_of(rows, D), shape_of(8, D, dtype=F32)],
-        waits=[d_feed[0]],
+        waits=[d_sent],
     )
     branch_other = swap(branch)
     grad_own, grad_far = local_call(
@@ -1547,13 +1622,10 @@
     final_far = add_call([final_far, swap(final_far_give)], [grad_own])
     final_far = swap(final_far, "x")
     final_give = swap(final_give)
-    mixed_grad = jnp.where(
-        x == 0, jnp.concatenate([grad_own, grad_far], 0), jnp.concatenate([grad_far, grad_own], 0)
-    )
     triple_grad = attend_back_call(
-        *guides, q, k, v, mixed_grad, exact, logs, logs_extra, cosine, sine, turn, waits=[out_near, final_give]
-    )
-    back_feed = add_call([d_feed[2], to_z(d_feed[3], 1)], [triple_grad])
+        x.reshape(1), *guides, q, k, v, [grad_own, grad_far], exact, logs, logs_extra, cosine, sine, turn, waits=[out_near, final_give]
+    )
+    back_feed = to_z(d_sent, 1)
     tri_own, tri_one, tri_two, tri_three, normed_own, normed_far, normed_give, d_triple_bias, sums_one = triple_call(
         place, normed, triple_grad, triple, entered_all, [back_feed, out_far, final_far]
     )
@@ -1569,29 +1641,16 @@
             )
     sums = [sums_one[0], sums_one[1], sums_two[0], sums_two[1], sums_two[2], sums_two[3], triple_bias_part, expand_bias_part]
     sums = jnp.concatenate([piece.reshape(n_dp, -1) for piece in sums], 1)
+
+    def butterfly(sums, bits):
+        for bit in bits:
+            sums = sums + lax.ppermute(sums, ("z", "y", "x", "core"), [(i, i ^ bit) for i in range(32)])
+        return sums
+
+    back_feed = add_piece_call(d_feed, 2, back_feed, pieces[1:3])
     back_feed = to_z(back_feed, 1)
-    normed_own, normed_far = local_call(
-        normed_sum_kernel,
-        "normed_sum",
-        [normed_own, normed_far, swap(normed_give)],
-        [shape_of(rows, D)] * 2,
-        waits=[*pieces[1:], back_feed],
-    )
-    normed_far = swap(normed_far, "x")
-    tri_near, tri_far = local_call(
-        functools.partial(unpack_kernel, n_z),
-        "unpack",
-        [place, *pieces],
-        [shape_of(n_z, D // n_f, qkv_part)] * 2,
-        [pltpu.VMEM((4, D // n_f, 3 * width), BF)],
-        smem=1,
-        waits=[normed_own],
-    )
-    tri_far = swap(tri_far, "y")
-    back_feed = add_call([d_feed[1], back_feed], [tri_near])
-    back_feed = to_z(back_feed, 1)
-    out_near = add_call([out_near, out_far], [tri_near])
-    out_far = swap(out_near[1], "x")
+    out_near, out_send = add_apart_call(out_near, out_far, [tri_own])
+    out_far = swap(out_send, "x")
     block_output = local_call(
         functools.partial(output_kernel, frames_local),
         "block_output",
@@ -1599,25 +1658,53 @@
         [shape_of(local_rows, D)],
         waits=[out_near],
     )[0]
-    tail, sums = local_call(
+    normed_own, normed_far = local_call(
+        normed_sum_kernel,
+        "normed_sum",
+        [normed_own, normed_far, swap(normed_give)],
+        [shape_of(rows, D)] * 2,
+        waits=pieces[1:],
+    )
+    normed_far = swap(normed_far, "x")
+    tri_near, tri_far, sums = local_call(
+        functools.partial(unpack_kernel, n_z),
+        "unpack",
+        [place, *pieces],
+        [shape_of(n_z, D // n_f, qkv_part)] * 2,
+        [pltpu.VMEM((4, D // n_f, 3 * width), BF)],
+        smem=1,
+        waits=[block_output, normed_own, out_far],
+        carry=[sums],
+    )
+    tri_far = swap(tri_far, "y")
+    back_feed = add_piece_call(d_feed, 1, back_feed, [tri_near])
+    back_feed = to_z(back_feed, 1)
+    sums = butterfly(sums, (1, 4))
+    tail = local_call(
         tail_sum_kernel,
         "tail_sum",
-        [tri_near, tri_far, out_near[0], out_far],
-        [shape_of(n_z, D // n_f, qkv_part + d_part)],
-        waits=[normed_far, block_output, back_feed],
-        carry=[sums],
+        [tri_near, tri_far, out_near[None], out_far],
+        [shape_of(D // n_f, qkv_part + d_part)] * n_z,
+        waits=[sums],
     )
     tail_parts = [tail[0]] + [to_z(tail[s], s) for s in range(1, n_z)]
-    d_feed = add_call([d_feed[0], back_feed], [tail])
-    d_feed_far = swap(d_feed[1], "y")
+    d_near, d_send = add_piece_call(d_feed, 0, back_feed, tail_parts[1:3], True)
     tokens_grad = local_call(
         functools.partial(leave_kernel, frames_local),
         "tokens_grad",
         [entered, normed_own, normed_far, middle_grad, live, vectors],
         [shape_of(local_rows, D, dtype=F32)],
-        waits=[d_feed],
+        waits=[tail[0], d_near],
     )[0]
-    d_feed = add_call([d_feed[0], d_feed_far], [tokens_grad])
+    triple_weight_grad, output_weight_grad = local_call(
+        tail_kernel,
+        "tail",
+        tail_parts,
+        [shape_of(D // n_f, qkv_part, dtype=F32), shape_of(D // n_f, d_part, dtype=F32)],
+        waits=[tokens_grad],
+    )
+    *d_feed, sums = add_apart_call(d_near, swap(d_send, "y"), [triple_weight_grad], [sums])
+    sums = butterfly(sums, (2, 8, 16))
     expand_weight_grad, reduce_weight_grad = local_call(
         join_kernel,
         "join",
@@ -1625,16 +1712,7 @@
         [shape_of(D // n_f, ff_part, dtype=F32), shape_of(FF // n_f, d_part, dtype=F32)],
         smem=1,
     )
-    triple_weight_grad, output_weight_grad = local_call(
-        tail_kernel,
-        "tail",
-        tail_parts,
-        [shape_of(D // n_f, qkv_part, dtype=F32), shape_of(D // n_f, d_part, dtype=F32)],
-        waits=[d_feed],
-    )
-
-    for bit in (1, 2, 4, 8, 16):
-        sums = sums + lax.ppermute(sums, ("z", "y", "x", "core"), [(i, i ^ bit) for i in range(32)])
+
     sums = take(sums, z * n_y + y)
     parts = [sums[i * d_part : (i + 1) * d_part] for i in range(6)]
     rest = sums[6 * d_part :]
@@ -1782,7 +1860,8 @@
     mixed_grad = nt(branch_chip, output_all).astype(BF)
     mixed_grad = over_x(mixed_grad.reshape(2 * rows, n_x, width).transpose(1, 0, 2)).reshape(n_f, rows, width)
     d_output = tn(mixed_chip, branch_chip).astype(BF)
-    triple_grad = attend_back_call(*guides, q, k, v, mixed_grad, exact, logs, logs_extra, cosine, sine, turned)
+    triple_grad = attend_back_call(
+        jnp.zeros((1,), jnp.int32), *guides, q, k, v, list(mixed_grad.reshape(n_x, 2, rows, width)), exact, logs, logs_extra, cosine, sine, turned)
     natural = triple_grad.reshape(n_f * rows, 3 * width)
     d_triple = tn(normed_all.reshape(n_f * rows, D), natural).astype(BF)
     d_triple_bias = jnp.sum(natural.astype(F32), 0)

time: 552 us -> 518 us (0.938)
  Pallas kernels: 288 us -> 264 us
  waiting for transfers between devices: 129 us -> 122 us
    ppermute x35 -> x38, waiting for transfers between devices: 83.3 us -> 56.9 us  [swap(): return lax.ppermute(array, axis, [(0, 1), (1, 0)])]
    ppermute x12, waiting for transfers between devices: 28.3 us -> 44.6 us  [to_z(): return lax.ppermute(array, 'z', [(i, (i + s) % n_z) for i in range(n_z)])]
    ppermute x5, waiting for transfers between devices: 5.13 us -> 17.1 us  [butterfly(): lax.ppermute(sums, ('z', 'y', 'x', 'core'), [(i, i ^ bit) for i in range(...]
    pallas_call x26 -> x23, Pallas kernels: 78.7 us -> 69 us  [local_call(): pl.pallas_call(waiting(kernel, len(inputs), waits, len(carry), len(output...]
    ppermute x4, waiting for transfers between devices: 12.1 us -> 3.69 us  [cross_over(): return lax.ppermute(array, ('x', 'core'), [(i, i ^ 3) for i in range(4)])]
    ppermute x12, starting transfers between devices: 14.9 us -> 21.9 us  [to_z(): return lax.ppermute(array, 'z', [(i, (i + s) % n_z) for i in range(n_z)])]
    squeeze x4 -> x0, local copies, waits for them, and re-layouts: 6.47 us -> none  [the longest x1 2.14 us: torus_shards(): d_feed_far = swap(d_feed[1], 'y')]
    pallas_call x1, Pallas kernels: 37.3 us -> 31.3 us  [attend_call(): pl.pallas_call(waiting(functools.partial(attend_kernel, frames_local), 8,...]
  transfers between devices with their start and end apart: 57 -> 60, of which waited for: 20 -> 24; matrix products, arithmetic and copies ran while one was open for 7% -> 5% of each run, Pallas kernels for 39% -> 39%
where the time goes in v3:
time: 518 us; the launch traced here: 513 us
  Pallas kernels  264 us (51%)
  waiting for transfers between devices  122 us (24%)
  local copies, waits for them, and re-layouts  51.1 us (10%)
  starting transfers between devices  46.3 us (9%)
  between operations  17.7 us (3%)
  other arithmetic  12.2 us (2%)
    pallas_call x23, Pallas kernels, local_call(): pl.pallas_call(waiting(kernel, len(inputs), waits, len(carry), len(output...  69 us
    ppermute x38, waiting for transfers between devices, swap(): return lax.ppermute(array, axis, [(0, 1), (1, 0)])  56.9 us
    ppermute x12, waiting for transfers between devices, to_z(): return lax.ppermute(array, 'z', [(i, (i + s) % n_z) for i in range(n_z)])  44.6 us
    pallas_call x1, Pallas kernels, attend_back_call(): pl.pallas_call(waiting(functools.partial(attend_back_kernel, frames_local...  44 us
    pallas_call x2, Pallas kernels, feed_split_call(): pl.pallas_call(waiting(feed_kernel, 2 + len(inputs), waits), grid_spec=pl...  39 us
    pallas_call x1, Pallas kernels, attend_call(): pl.pallas_call(waiting(functools.partial(attend_kernel, frames_local), 8,...  31.3 us
    pallas_call x1, Pallas kernels, feed_grad_call(): pl.pallas_call(waiting(feed_grad_kernel, 1 + len(first) + len(tiles) + 2...  31 us
    unnamed x138, local copies, waits for them, and re-layouts  28.7 us
  transfers between devices with their start and end apart: 60, of which 24 were waited for; matrix products, arithmetic and copies ran while one was open for 5% of the time, Pallas kernels for 39%

profile of v3, /device:TPU:0, one launch (start us, length us, event | category | flops | bytes accessed | tf_op | source)
XLA Modules:
  0.0 513.3 jit_solution(3557881543508590954)
XLA Ops:
  49.5 5.0 collective-permute-start.13
  56.4 11.7 %collective-permute-done.6.refs_2_ = bf16[4,272,384]{2,1,0:T(8,128)(2,1)} collective-permute-done((bf16[4,272,384]{2,1,0:T(8,128)(2,1)S(1)}, bf16[4,272,384]{2,1,0:T(8,128)(2,1)}, u32[]{:S(2)}, u32[]{:S(2)}) %collective-permute-start.6) | collective-permute-done | bytes 835616 | tf_op jit(solution)/shard_map/ppermute | solution.py:1476
  69.0 3.6 pack.1
  78.3 13.2 %collective-permute-done.16.refs_2_.p2.refs_7_ = bf16[4,512,128]{2,1,0:T(8,128)(2,1)} collective-permute-done((bf16[4,512,128]{2,1,0:T(8,128)(2,1)S(1)}, bf16[4,512,128]{2,1,0:T(8,128)(2,1)}, u32[]{:S(2)}, u32[]{:S(2)}) %collective-permute-start.16) | collective-permute-done | bytes 524320 | tf_op jit(solution)/shard_map/ppermute | solution.py:1482
  99.8 5.1 fusion
  105.9 11.9 %enter.1 = (bf16[4,528,256]{2,1,0:T(8,128)(2,1)}, bf16[4,528,256]{2,1,0:T(8,128)(2,1)}, bf16[4,528,256]{2,1,0:T(8,128)(2,1)}, bf16[4,528,1024]{2,1,0:T(8,128)(2,1)}, bf16[1024,768]{1,0:T(8,128)(2,1)}) custom-call(s32[5]{0:T(128)} %stack.24.refs_0_.place, bf16[528,1024]{1,0:T(8,128)(2,1)} %copy.96.refs_1_.entered.refs_5_.refs_0_, ...), custom_call_target="tpu_custom_call" | custom-call | flops 3321888768 | bytes 16220160 | tf_op jit(solution)/shard_map/enter/pallas_call | solution.py:967
  125.1 31.3 %attend.1 = (bf16[4,528,256]{2,1,0:T(8,128)(2,1)}, f32[4,528,256]{2,1,0:T(8,128)}, f32[8,8,1024]{2,1,0:T(8,128)}, f32[8,256]{1,0:T(8,128)}) custom-call(s32[8]{0:T(128)} %compare_select_fusion.2.start.refs_1_, s32[64,128]{1,0:T(8,128)} %broadcast_in_dim.157.key_frame.refs_2_, s32[8,64]{1,0:T(8,128)} %broadcast_in_dim.163.query_start.refs_3_, ...), custom_call_target="tpu_custom_call" | custom-call | flops 17179869184 | bytes 5406720 | tf_op jit(solution)/shard_map/attend/pallas_call | solution.py:281
  161.0 14.1 %collective-permute-done.23.refs_5_.f3.refs_12_ = bf16[4,512,128]{2,1,0:T(8,128)(2,1)S(1)} collective-permute-done((bf16[4,512,128]{2,1,0:T(8,128)(2,1)S(1)}, bf16[4,512,128]{2,1,0:T(8,128)(2,1)S(1)}, u32[]{:S(2)}, u32[]{:S(2)}) %collective-permute-start.23) | collective-permute-done | bytes 524320 | tf_op jit(solution)/shard_map/ppermute | solution.py:1476
  176.4 4.5 project.1
  184.8 4.8 middle.1
  193.6 19.5 %feed_forward.2 = (bf16[1056,1024]{1,0:T(8,128)(2,1)}, bf16[1056,1024]{1,0:T(8,128)(2,1)}, f32[528,1024]{1,0:T(8,128)}, bf16[528,1024]{1,0:T(8,128)(2,1)}, f32[4,1,256]{2,1,0:T(1,128)}) custom-call(s32[5]{0:T(128)} %stack.24.refs_0_.place, bf16[528,1024]{1,0:T(8,128)(2,1)} %get-tuple-element.120.normal.n0, bf16[528,1024]{1,0:T(8,128)(2,1)} %copy-done.56, ...), custom_call_target="tpu_custom_call" | custom-call | flops 6643777536 | bytes 10813440 | tf_op jit(solution)/shard_map/feed_forward/pallas_call | solution.py:1385
  223.4 19.4 %feed_forward.3 = (bf16[1056,1024]{1,0:T(8,128)(2,1)}, bf16[1056,1024]{1,0:T(8,128)(2,1)}, f32[528,1024]{1,0:T(8,128)}, bf16[528,1024]{1,0:T(8,128)(2,1)}, f32[4,1,256]{2,1,0:T(1,128)}) custom-call(s32[5]{0:T(128)} %stack.24.refs_0_.place, bf16[528,1024]{1,0:T(8,128)(2,1)} %copy-done.19, bf16[528,1024]{1,0:T(8,128)(2,1)} %copy-done.58, ...), custom_call_target="tpu_custom_call" | custom-call | flops 6643777536 | bytes 10813440 | tf_op jit(solution)/shard_map/feed_forward/pallas_call | solution.py:1385
  251.1 31.0 %feed_grads.1 = (f32[528,1024]{1,0:T(8,128)}, bf16[528,1024]{1,0:T(8,128)(2,1)}, bf16[528,1024]{1,0:T(8,128)(2,1)}, bf16[528,1024]{1,0:T(8,128)(2,1)}, bf16[4,2,...) custom-call(s32[5]{0:T(128)} %stack.24.refs_0_.place, bf16[528,1024]{1,0:T(8,128)(2,1)} %get-tuple-element.120.normal.n0, ...), custom_call_target="tpu_custom_call" | custom-call | flops 13287555072 | bytes 21626880 | tf_op jit(solution)/shard_map/feed_grads/pallas_call | solution.py:1412
  283.5 6.8 %middle_back.1 = (f32[528,1024]{1,0:T(8,128)}, bf16[528,1024]{1,0:T(8,128)(2,1)}, f32[8,1024]{1,0:T(8,128)}) custom-call(f32[528,1024]{1,0:T(8,128)} %get-tuple-element.119.refs_0_, bf16[528,1024]{1,0:T(8,128)(2,1)} %copy.98.cot.c0.refs_1_, f32[528,1024]{1,0:T(8,128)} %get-tuple-element.131.refs_2_, bf16[528,1024]{1,0:T(8,128)(2,1)} %copy-done.13, ...), custom_call_target="tpu_custom_call" | custom-call | flops 1 | bytes 1 | tf_op jit(solution)/shard_map/middle_back/pallas_call | solution.py:1031
  295.1 4.2 mixed_grad.1
  300.4 4.8 output_weight_grad.1
  310.5 4.3 collective-permute-done.36.refs_10_
  314.8 44.0 %attend_back.1.refs_2_.refs_3_ = bf16[4,528,768]{2,1,0:T(8,128)(2,1)} custom-call(s32[1]{0:T(128)} %bitcast.2.refs_0_, s32[8]{0:T(128)} %compare_select_fusion.2.start.refs_1_, s32[64,128]{1,0:T(8,128)} %broadcast_in_dim.157.key_frame.refs_2_, s32[8,64]{1,0:T(8,128)} %broadcast_in_dim.163.query_start.refs_3_, s32[8,64]{1,0:T(8,128)} %broadcast_in_dim.166.query_frame.refs_4_, ...), custom_call_target="tpu_custom_call" | custom-call | flops 42949672960 | bytes 10813440 | tf_op jit(solution)/shard_map/attend_back/pallas_call | solution.py:517
  360.4 17.6 %triple_grads.1 = (bf16[256,768]{1,0:T(8,128)(2,1)}, bf16[256,768]{1,0:T(8,128)(2,1)}, bf16[256,768]{1,0:T(8,128)(2,1)}, bf16[256,768]{1,0:T(8,128)(2,1)}, bf16[...) custom-call(s32[5]{0:T(128)} %stack.24.refs_0_.place, ...), custom_call_target="tpu_custom_call" | custom-call | flops 6643777536 | bytes 10813440 | tf_op jit(solution)/shard_map/triple_grads/pallas_call | solution.py:1141
  383.1 7.8 %collective-permute-done.40.refs_4_.refs_3_ = bf16[256,768]{1,0:T(8,128)(2,1)S(1)} collective-permute-done((bf16[256,768]{1,0:T(8,128)(2,1)}, bf16[256,768]{1,0:T(8,128)(2,1)S(1)}, u32[]{:S(2)}, u32[]{:S(2)}) %collective-permute-start.40) | collective-permute-done | bytes 393248 | tf_op jit(solution)/shard_map/ppermute | solution.py:1476
  398.5 4.6 block_output.1.refs_5_
  403.1 3.7 collective-permute-done.41.refs_5_.refs_4_
  408.2 3.9 normed_sum.1
  415.9 6.8 %collective-permute-done.47.refs_1_ = bf16[2,4,512,128]{3,2,1,0:T(8,128)(2,1)} collective-permute-done((bf16[2,4,512,128]{3,2,1,0:T(8,128)(2,1)}, bf16[2,4,512,128]{3,2,1,0:T(8,128)(2,1)}, u32[]{:S(2)}, u32[]{:S(2)}) %collective-permute-start.47) | collective-permute-done | bytes 1048608 | tf_op jit(solution)/shard_map/ppermute | solution.py:1482
  427.3 9.4 %collective-permute-done.46 = f32[8,1664]{1,0:T(8,128)S(1)} collective-permute-done((f32[8,1664]{1,0:T(8,128)S(1)}, f32[8,1664]{1,0:T(8,128)S(1)}, u32[]{:S(2)}, u32[]{:S(2)}) %collective-permute-start.46) | collective-permute-done | bytes 53280 | tf_op jit(solution)/shard_map/ppermute | solution.py:1647
  440.7 3.5 collective-permute-start.49
  446.7 6.9 %collective-permute-done.48.refs_1_ = bf16[2,4,512,128]{3,2,1,0:T(8,128)(2,1)S(1)} collective-permute-done((bf16[2,4,512,128]{3,2,1,0:T(8,128)(2,1)}, bf16[2,4,512,128]{3,2,1,0:T(8,128)(2,1)S(1)}, u32[]{:S(2)}, u32[]{:S(2)}) %collective-permute-start.48) | collective-permute-done | bytes 1048608 | tf_op jit(solution)/shard_map/ppermute | solution.py:1482
  453.6 5.6 %collective-permute-done.49.refs_2_.refs_1_ = bf16[256,512]{1,0:T(8,128)(2,1)S(1)} collective-permute-done((bf16[256,512]{1,0:T(8,128)(2,1)}, bf16[256,512]{1,0:T(8,128)(2,1)S(1)}, u32[]{:S(2)}, u32[]{:S(2)}) %collective-permute-start.49) | collective-permute-done | bytes 262176 | tf_op jit(solution)/shard_map/ppermute | solution.py:1482
  459.2 8.7 %collective-permute-done.50.refs_3_.refs_2_ = bf16[256,512]{1,0:T(8,128)(2,1)S(1)} collective-permute-done((bf16[256,512]{1,0:T(8,128)(2,1)}, bf16[256,512]{1,0:T(8,128)(2,1)S(1)}, u32[]{:S(2)}, u32[]{:S(2)}) %collective-permute-start.50) | collective-permute-done | bytes 262176 | tf_op jit(solution)/shard_map/ppermute | solution.py:1482
  473.0 5.8 %tokens_grad.1.refs_4_ = f32[516,1024]{1,0:T(8,128)} custom-call(bf16[528,1024]{1,0:T(8,128)(2,1)} %copy.96.refs_1_.entered.refs_5_.refs_0_, bf16[528,1024]{1,0:T(8,128)(2,1)} %get-tuple-element.152.refs_6_.refs_1_, bf16[528,1024]{1,0:T(8,128)(2,1)} %copy-done.12, f32[528,1024]{1,0:T(8,128)} %get-tuple-element.154.refs_3_, f32[528,1]{1,0:T(8,128)} %copy.64.refs_4_, ...), custom_call_target="tpu_custom_call" | custom-call | flops 1 | bytes 1 | tf_op jit(solution)/shard_map/tokens_grad/pallas_call | solution.py:768
  493.8 4.1 collective-permute-done.54
  498.0 3.5 copy.67
  (371 shorter events, 164.5 us)
Async XLA Ops:
  7.2 167.8 %all-gather.3.cloned.1.call-start = ((), (), s32[]{:S(2)}) async-start(), calls=%async_computation | async-start | bytes 1114112 | tf_op jit(solution)/shard_map/all_gather | solution.py:1527
  22.6 16.6 %collective-permute-start.1 = (bf16[272,384]{1,0:T(8,128)(2,1)}, bf16[272,384]{1,0:T(8,128)(2,1)}, u32[]{:S(2)}, u32[]{:S(2)}) collective-permute-start(bf16[272,384]{1,0:T(8,128)(2,1)} %get-tuple-element.97.refs_0_), channel_id=1, source_target_pairs={{0,16},{8,24},{16,0},{24,8},{1,17},{9,25},{17,1},{25,9},{2,18},{10... | collective-permute-start | bytes 626696 | tf_op jit(solution)/shard_map/ppermute | solution.py:1482
  46.5 21.6 %collective-permute-start.7 = (bf16[528,1024]{1,0:T(8,128)(2,1)}, bf16[528,1024]{1,0:T(8,128)(2,1)S(1)}, u32[]{:S(2)}, u32[]{:S(2)}) collective-permute-start(bf16[528,1024]{1,0:T(8,128)(2,1)} %copy.96.refs_1_.entered.refs_5_.refs_0_), channel_id=1, source_target_pairs={{0,1},{1,0},{2,3},{3,2},{4,5},{5,4},{6,7},{7,6},{8,9},{9,8},{10,11... | collective-permute-start | bytes 3244040 | tf_op jit(solution)/shard_map/ppermute | solution.py:1476
  46.5 21.6 %collective-permute-start.6 = (bf16[4,272,384]{2,1,0:T(8,128)(2,1)S(1)}, bf16[4,272,384]{2,1,0:T(8,128)(2,1)}, u32[]{:S(2)}, u32[]{:S(2)}) collective-permute-start(bf16[4,272,384]{2,1,0:T(8,128)(2,1)S(1)} %copy-done.1), channel_id=1, source_target_pairs={{0,4},{4,0},{1,5},{5,1},{2,6},{6,2},{3,7},{7,3},{8,12},{12,8},{9,1... | collective-permute-start | bytes 2506760 | tf_op jit(solution)/shard_map/ppermute | solution.py:1476
  48.0 44.9 %collective-permute-start.8 = (bf16[528,1024]{1,0:T(8,128)(2,1)}, bf16[528,1024]{1,0:T(8,128)(2,1)S(1)}, u32[]{:S(2)}, u32[]{:S(2)}) collective-permute-start(bf16[528,1024]{1,0:T(8,128)(2,1)} %copy.96.refs_1_.entered.refs_5_.refs_0_), channel_id=1, source_target_pairs={{0,2},{2,0},{1,3},{3,1},{4,6},{6,4},{5,7},{7,5},{8,10},{10,8},{9,1... | collective-permute-start | bytes 3244040 | tf_op jit(solution)/shard_map/ppermute | solution.py:1476
  49.5 24.7 %collective-permute-start.13 = (bf16[4,512,128]{2,1,0:T(8,128)(2,1)S(1)}, bf16[4,512,128]{2,1,0:T(8,128)(2,1)}, u32[]{:S(2)}, u32[]{:S(2)}) collective-permute-start(bf16[4,512,128]{2,1,0:T(8,128)(2,1)S(1)} %copy-done.8), channel_id=1, source_target_pairs={{0,8},{8,16},{16,24},{24,0},{1,9},{9,17},{17,25},{25,1},{2,10},{10... | collective-permute-start | bytes 1572872 | tf_op jit(solution)/shard_map/ppermute | solution.py:1482
  54.5 37.0 %collective-permute-start.16 = (bf16[4,512,128]{2,1,0:T(8,128)(2,1)S(1)}, bf16[4,512,128]{2,1,0:T(8,128)(2,1)}, u32[]{:S(2)}, u32[]{:S(2)}) collective-permute-start(bf16[4,512,128]{2,1,0:T(8,128)(2,1)S(1)} %copy-done.8), channel_id=1, source_target_pairs={{0,16},{8,24},{16,0},{24,8},{1,17},{9,25},{17,1},{25,9},{2,18},{10... | collective-permute-start | bytes 1572872 | tf_op jit(solution)/shard_map/ppermute | solution.py:1482
  72.7 20.8 %collective-permute-start.10 = (bf16[256,768]{1,0:T(8,128)(2,1)}, bf16[256,768]{1,0:T(8,128)(2,1)S(1)}, u32[]{:S(2)}, u32[]{:S(2)}) collective-permute-start(bf16[256,768]{1,0:T(8,128)(2,1)} %get-tuple-element.104), channel_id=1, source_target_pairs={{0,2},{2,0},{1,3},{3,1},{4,6},{6,4},{5,7},{7,5},{8,10},{10,8},{9,1... | collective-permute-start | bytes 1179656 | tf_op jit(solution)/shard_map/ppermute | solution.py:1476
  74.2 20.8 %collective-permute-start.11 = (bf16[256,768]{1,0:T(8,128)(2,1)}, bf16[256,768]{1,0:T(8,128)(2,1)S(1)}, u32[]{:S(2)}, u32[]{:S(2)}) collective-permute-start(bf16[256,768]{1,0:T(8,128)(2,1)} %get-tuple-element.105), channel_id=1, source_target_pairs={{0,3},{1,2},{2,1},{3,0},{4,7},{5,6},{6,5},{7,4},{8,11},{9,10},{10,... | collective-permute-start | bytes 1179656 | tf_op jit(solution)/shard_map/ppermute | solution.py:1479
  74.2 21.3 %collective-permute-start.9 = (bf16[256,768]{1,0:T(8,128)(2,1)}, bf16[256,768]{1,0:T(8,128)(2,1)}, u32[]{:S(2)}, u32[]{:S(2)}) collective-permute-start(bf16[256,768]{1,0:T(8,128)(2,1)} %get-tuple-element.103), channel_id=1, source_target_pairs={{0,1},{1,0},{2,3},{3,2},{4,5},{5,4},{6,7},{7,6},{8,9},{9,8},{10,11... | collective-permute-start | bytes 1179656 | tf_op jit(solution)/shard_map/ppermute | solution.py:1476
  91.5 26.3 %collective-permute-start.18 = (bf16[4,512,128]{2,1,0:T(8,128)(2,1)S(1)}, bf16[4,512,128]{2,1,0:T(8,128)(2,1)S(1)}, u32[]{:S(2)}, u32[]{:S(2)}) collective-permute-start(bf16[4,512,128]{2,1,0:T(8,128)(2,1)S(1)} %copy-done.8), channel_id=1, source_target_pairs={{0,24},{8,0},{16,8},{24,16},{1,25},{9,1},{17,9},{25,17},{2,26},{10... | collective-permute-start | bytes 1572872 | tf_op jit(solution)/shard_map/ppermute | solution.py:1482
  92.9 63.5 %collective-permute-start.14 = (bf16[4,512,128]{2,1,0:T(8,128)(2,1)S(1)}, bf16[4,512,128]{2,1,0:T(8,128)(2,1)}, u32[]{:S(2)}, u32[]{:S(2)}) collective-permute-start(bf16[4,512,128]{2,1,0:T(8,128)(2,1)S(1)} %copy-done.8), channel_id=1, source_target_pairs={{0,4},{4,0},{1,5},{5,1},{2,6},{6,2},{3,7},{7,3},{8,12},{12,8},{9,1... | collective-permute-start | bytes 1572872 | tf_op jit(solution)/shard_map/ppermute | solution.py:1476
  93.4 63.0 %collective-permute-start.15 = (bf16[4,512,128]{2,1,0:T(8,128)(2,1)}, bf16[4,512,128]{2,1,0:T(8,128)(2,1)}, u32[]{:S(2)}, u32[]{:S(2)}) collective-permute-start(bf16[4,512,128]{2,1,0:T(8,128)(2,1)} %collective-permute-done.13.refs_14_.p1.refs_6_), channel_id=1, source_target_pairs={{0,4},{4,0},{1,5},{5,1},{2,6},{6,2},{3,7},{7,3},{8,12},{12,8},{9,1... | collective-permute-start | bytes 1572872 | tf_op jit(solution)/shard_map/ppermute | solution.py:1476
  95.0 61.5 %collective-permute-start.17 = (bf16[4,512,128]{2,1,0:T(8,128)(2,1)}, bf16[4,512,128]{2,1,0:T(8,128)(2,1)}, u32[]{:S(2)}, u32[]{:S(2)}) collective-permute-start(bf16[4,512,128]{2,1,0:T(8,128)(2,1)} %collective-permute-done.16.refs_2_.p2.refs_7_), channel_id=1, source_target_pairs={{0,4},{4,0},{1,5},{5,1},{2,6},{6,2},{3,7},{7,3},{8,12},{12,8},{9,1... | collective-permute-start | bytes 1572872 | tf_op jit(solution)/shard_map/ppermute | solution.py:1476
  120.9 35.6 %collective-permute-start.19 = (bf16[528,1024]{1,0:T(8,128)(2,1)}, bf16[528,1024]{1,0:T(8,128)(2,1)S(1)}, u32[]{:S(2)}, u32[]{:S(2)}) collective-permute-start(bf16[528,1024]{1,0:T(8,128)(2,1)} %copy.98.cot.c0.refs_1_), channel_id=1, source_target_pairs={{0,1},{1,0},{2,3},{3,2},{4,5},{5,4},{6,7},{7,6},{8,9},{9,8},{10,11... | collective-permute-start | bytes 3244040 | tf_op jit(solution)/shard_map/ppermute | solution.py:1476
  121.4 35.1 %collective-permute-start.20 = (bf16[528,1024]{1,0:T(8,128)(2,1)}, bf16[528,1024]{1,0:T(8,128)(2,1)S(1)}, u32[]{:S(2)}, u32[]{:S(2)}) collective-permute-start(bf16[528,1024]{1,0:T(8,128)(2,1)} %copy.98.cot.c0.refs_1_), channel_id=1, source_target_pairs={{0,2},{2,0},{1,3},{3,1},{4,6},{6,4},{5,7},{7,5},{8,10},{10,8},{9,1... | collective-permute-start | bytes 3244040 | tf_op jit(solution)/shard_map/ppermute | solution.py:1476
  189.8 26.4 %collective-permute-start.26 = (bf16[528,1024]{1,0:T(8,128)(2,1)}, bf16[528,1024]{1,0:T(8,128)(2,1)S(1)}, u32[]{:S(2)}, u32[]{:S(2)}) collective-permute-start(bf16[528,1024]{1,0:T(8,128)(2,1)} %get-tuple-element.120.normal.n0), channel_id=1, source_target_pairs={{0,2},{2,0},{1,3},{3,1},{4,6},{6,4},{5,7},{7,5},{8,10},{10,8},{9,1... | collective-permute-start | bytes 3244040 | tf_op jit(solution)/shard_map/ppermute | solution.py:1476
  243.0 39.2 %collective-permute-start.30 = (bf16[528,1024]{1,0:T(8,128)(2,1)S(1)}, bf16[528,1024]{1,0:T(8,128)(2,1)S(1)}, u32[]{:S(2)}, u32[]{:S(2)}) collective-permute-start(bf16[528,1024]{1,0:T(8,128)(2,1)S(1)} %copy-done.57), channel_id=1, source_target_pairs={{0,1},{1,0},{2,3},{3,2},{4,5},{5,4},{6,7},{7,6},{8,9},{9,8},{10,11... | collective-permute-start | bytes 3244040 | tf_op jit(solution)/shard_map/ppermute | solution.py:1476
  249.9 32.3 %collective-permute-start.32 = (bf16[528,1024]{1,0:T(8,128)(2,1)}, bf16[528,1024]{1,0:T(8,128)(2,1)S(1)}, u32[]{:S(2)}, u32[]{:S(2)}) collective-permute-start(bf16[528,1024]{1,0:T(8,128)(2,1)} %add.187), channel_id=1, source_target_pairs={{0,2},{2,0},{1,3},{3,1},{4,6},{6,4},{5,7},{7,5},{8,10},{10,8},{9,1... | collective-permute-start | bytes 3244040 | tf_op jit(solution)/shard_map/ppermute | solution.py:1476
  290.4 15.8 %collective-permute-start.29 = (bf16[528,1024]{1,0:T(8,128)(2,1)}, bf16[528,1024]{1,0:T(8,128)(2,1)}, u32[]{:S(2)}, u32[]{:S(2)}) collective-permute-start(bf16[528,1024]{1,0:T(8,128)(2,1)} %get-tuple-element.130), channel_id=1, source_target_pairs={{0,1},{1,0},{2,3},{3,2},{4,5},{5,4},{6,7},{7,6},{8,9},{9,8},{10,11... | collective-permute-start | bytes 3244040 | tf_op jit(solution)/shard_map/ppermute | solution.py:1476
  290.9 19.5 %collective-permute-start.28 = (bf16[528,1024]{1,0:T(8,128)(2,1)}, bf16[528,1024]{1,0:T(8,128)(2,1)}, u32[]{:S(2)}, u32[]{:S(2)}) collective-permute-start(bf16[528,1024]{1,0:T(8,128)(2,1)} %get-tuple-element.128), channel_id=1, source_target_pairs={{0,1},{1,0},{2,3},{3,2},{4,5},{5,4},{6,7},{7,6},{8,9},{9,8},{10,11... | collective-permute-start | bytes 3244040 | tf_op jit(solution)/shard_map/ppermute | solution.py:1476
  299.4 15.4 %collective-permute-start.36 = (bf16[2,528,256]{2,1,0:T(8,128)(2,1)}, bf16[2,528,256]{2,1,0:T(8,128)(2,1)}, u32[]{:S(2)}, u32[]{:S(2)}) collective-permute-start(bf16[2,528,256]{2,1,0:T(8,128)(2,1)} %get-tuple-element.139), channel_id=1, source_target_pairs={{0,2},{2,0},{1,3},{3,1},{4,6},{6,4},{5,7},{7,5},{8,10},{10,8},{9,1... | collective-permute-start | bytes 1622024 | tf_op jit(solution)/shard_map/ppermute | solution.py:1476
  300.2 58.6 %collective-permute-start.37 = (bf16[2,4,512,128]{3,2,1,0:T(8,128)(2,1)S(1)}, bf16[2,4,512,128]{3,2,1,0:T(8,128)(2,1)S(1)}, u32[]{:S(2)}, u32[]{:S(2)}) collective-permute-start(bf16[2,4,512,128]{3,2,1,0:T(8,128)(2,1)S(1)} %copy-done.25), channel_id=1, source_target_pairs={{0,8},{8,16},{16,24},{24,0},{1,9},{9,17},{17,25},{25,1},{2,10},{10... | collective-permute-start | bytes 3145736 | tf_op jit(solution)/shard_map/ppermute | solution.py:1482
  305.1 53.7 %collective-permute-start.35 = (bf16[2,4,256,128]{3,2,1,0:T(8,128)(2,1)}, bf16[2,4,256,128]{3,2,1,0:T(8,128)(2,1)S(1)}, u32[]{:S(2)}, u32[]{:S(2)}) collective-permute-start(bf16[2,4,256,128]{3,2,1,0:T(8,128)(2,1)} %get-tuple-element.138), channel_id=1, source_target_pairs={{0,4},{4,0},{1,5},{5,1},{2,6},{6,2},{3,7},{7,3},{8,12},{12,8},{9,1... | collective-permute-start | bytes 1572872 | tf_op jit(solution)/shard_map/ppermute | solution.py:1476
  309.0 49.9 %collective-permute-start.34 = (bf16[528,1024]{1,0:T(8,128)(2,1)}, bf16[528,1024]{1,0:T(8,128)(2,1)S(1)}, u32[]{:S(2)}, u32[]{:S(2)}) collective-permute-start(bf16[528,1024]{1,0:T(8,128)(2,1)} %add.188), channel_id=1, source_target_pairs={{0,2},{2,0},{1,3},{3,1},{4,6},{6,4},{5,7},{7,5},{8,10},{10,8},{9,1... | collective-permute-start | bytes 3244040 | tf_op jit(solution)/shard_map/ppermute | solution.py:1476
  378.0 28.8 %collective-permute-start.38 = (bf16[2,528,1024]{2,1,0:T(8,128)(2,1)}, bf16[2,528,1024]{2,1,0:T(8,128)(2,1)S(1)}, u32[]{:S(2)}, u32[]{:S(2)}) collective-permute-start(bf16[2,528,1024]{2,1,0:T(8,128)(2,1)} %get-tuple-element.148), channel_id=1, source_target_pairs={{0,1},{1,0},{2,3},{3,2},{4,5},{5,4},{6,7},{7,6},{8,9},{9,8},{10,11... | collective-permute-start | bytes 6488072 | tf_op jit(solution)/shard_map/ppermute | solution.py:1476
  394.3 28.3 %collective-permute-start.47 = (bf16[2,4,512,128]{3,2,1,0:T(8,128)(2,1)}, bf16[2,4,512,128]{3,2,1,0:T(8,128)(2,1)}, u32[]{:S(2)}, u32[]{:S(2)}) collective-permute-start(bf16[2,4,512,128]{3,2,1,0:T(8,128)(2,1)} %add_piece.3), channel_id=1, source_target_pairs={{0,8},{8,16},{16,24},{24,0},{1,9},{9,17},{17,25},{25,1},{2,10},{10... | collective-permute-start | bytes 3145736 | tf_op jit(solution)/shard_map/ppermute | solution.py:1482
  415.9 21.4 %collective-permute-start.44 = (bf16[4,256,384]{2,1,0:T(8,128)(2,1)}, bf16[4,256,384]{2,1,0:T(8,128)(2,1)S(1)}, u32[]{:S(2)}, u32[]{:S(2)}) collective-permute-start(bf16[4,256,384]{2,1,0:T(8,128)(2,1)} %get-tuple-element.162), channel_id=1, source_target_pairs={{0,4},{4,0},{1,5},{5,1},{2,6},{6,2},{3,7},{7,3},{8,12},{12,8},{9,1... | collective-permute-start | bytes 2359304 | tf_op jit(solution)/shard_map/ppermute | solution.py:1476
  425.4 28.2 %collective-permute-start.48 = (bf16[2,4,512,128]{3,2,1,0:T(8,128)(2,1)}, bf16[2,4,512,128]{3,2,1,0:T(8,128)(2,1)S(1)}, u32[]{:S(2)}, u32[]{:S(2)}) collective-permute-start(bf16[2,4,512,128]{3,2,1,0:T(8,128)(2,1)} %add_piece.4), channel_id=1, source_target_pairs={{0,8},{8,16},{16,24},{24,0},{1,9},{9,17},{17,25},{25,1},{2,10},{10... | collective-permute-start | bytes 3145736 | tf_op jit(solution)/shard_map/ppermute | solution.py:1482
  425.4 46.6 %collective-permute-start.42 = (bf16[528,1024]{1,0:T(8,128)(2,1)}, bf16[528,1024]{1,0:T(8,128)(2,1)S(1)}, u32[]{:S(2)}, u32[]{:S(2)}) collective-permute-start(bf16[528,1024]{1,0:T(8,128)(2,1)} %get-tuple-element.153), channel_id=1, source_target_pairs={{0,2},{2,0},{1,3},{3,1},{4,6},{6,4},{5,7},{7,5},{8,10},{10,8},{9,1... | collective-permute-start | bytes 3244040 | tf_op jit(solution)/shard_map/ppermute | solution.py:1476
  440.7 18.5 %collective-permute-start.49 = (bf16[256,512]{1,0:T(8,128)(2,1)}, bf16[256,512]{1,0:T(8,128)(2,1)S(1)}, u32[]{:S(2)}, u32[]{:S(2)}) collective-permute-start(bf16[256,512]{1,0:T(8,128)(2,1)} %get-tuple-element.166), channel_id=1, source_target_pairs={{0,8},{8,16},{16,24},{24,0},{1,9},{9,17},{17,25},{25,1},{2,10},{10... | collective-permute-start | bytes 786440 | tf_op jit(solution)/shard_map/ppermute | solution.py:1482
  444.2 23.8 %collective-permute-start.50 = (bf16[256,512]{1,0:T(8,128)(2,1)}, bf16[256,512]{1,0:T(8,128)(2,1)S(1)}, u32[]{:S(2)}, u32[]{:S(2)}) collective-permute-start(bf16[256,512]{1,0:T(8,128)(2,1)} %get-tuple-element.167), channel_id=1, source_target_pairs={{0,16},{8,24},{16,0},{24,8},{1,17},{9,25},{17,1},{25,9},{2,18},{10... | collective-permute-start | bytes 786440 | tf_op jit(solution)/shard_map/ppermute | solution.py:1482
  (90 other events, 585.7 us)
Sparse Core Ops, SparseCore 0:
  54.6 73.9 all-gather.2

commit v4 on v3

--- a/solution.py
+++ b/solution.py
@@ -953,7 +953,7 @@
     v[0] = (nn(scratch[...], weight[:, 2 * width :]) + add[:1, 2 * width :]).astype(BF)
 
 
-def enter_call(place, entered, weights, bias, vectors, turn, cosine, sine, waits):
+def enter_call(place, entered, weights, bias, vectors, turn, cosine, sine, waits, carry):
     rows = entered[0].shape[0]
     width = bias.shape[-1] // 3
 
@@ -964,14 +964,15 @@
         return pl.BlockSpec((1,) + shape, lambda m, p: (p[4] ^ m, 0, 0))
 
     flat = [*entered, *weights, bias, vectors, turn]
+    waits = [*waits, carry]
     return pl.pallas_call(
-        waiting(enter_kernel, 3 + len(flat), waits),
+        waiting(enter_kernel, 3 + len(flat), waits, 1, 5),
         grid_spec=pltpu.PrefetchScalarGridSpec(
             num_scalar_prefetch=1,
             grid=(4,),
             in_specs=[whole(a) for a in flat] + [moved(rows, width // 2)] * 2 + [ANY_REF] * len(waits),
             out_specs=[moved(rows, width)] * 3
-            + [moved(rows, D), pl.BlockSpec((D, 3 * width), lambda m, p: (0, 0))],
+            + [moved(rows, D), pl.BlockSpec((D, 3 * width), lambda m, p: (0, 0)), ANY_REF],
             scratch_shapes=[
                 pltpu.VMEM((rows, D), BF),
                 pltpu.VMEM((rows, D), BF),
@@ -979,7 +980,9 @@
                 pltpu.VMEM((8, 3 * width), F32),
             ],
         ),
-        out_shape=[shape_of(4, rows, width)] * 3 + [shape_of(4, rows, D), shape_of(D, 3 * width)],
+        out_shape=[shape_of(4, rows, width)] * 3
+        + [shape_of(4, rows, D), shape_of(D, 3 * width), shape_of(*carry.shape)],
+        input_output_aliases={2 + len(flat) + len(waits): 5},
         compiler_params=pltpu.CompilerParams(vmem_limit_bytes=VMEM),
         cost_estimate=cost(flops=8 * rows * D * 3 * width, bytes_accessed=30 * rows * D, transcendentals=0),
         name="enter",
@@ -1538,18 +1541,17 @@
     )
     _, cosine, sine, guides = tables(counts[0], presence[0], n_f, frames_local, width // HEAD)
     weights = [own, swap(one), swap(two, "x"), cross_over(three)]
-    entered_all.append(swap(copy_call(entered_x, weights[1:])))
+    entered_all.append(swap(copy_call(entered_x, [own])))
     feed_near = gather_z(feed)
     turn = jnp.asarray(turn_matrix(width), BF)
-    q, k, v, normed, triple = enter_call(
-        place, entered_all, weights, bias, vectors, turn, cosine, sine, feed_near[1:2]
-    )
-    outer = copy_call(outer, [normed, *feed_near[2:]])
+    q, k, v, normed, triple, outer = enter_call(
+        place, entered_all, weights, bias, vectors, turn, cosine, sine, feed_near[1:2], outer
+    )
     feed_far = [swap(part, "y") for part in feed_near]
     feed_parts = [*feed_near, *feed_far]
     outer_x = swap(outer, "x")
     outer_all = [outer, swap(outer), outer_x]
-    mixed, exact, logs, logs_extra = attend_call(*guides, q, k, v)
+    mixed, exact, logs, logs_extra = attend_call(*guides, q, k, v, waits=feed_near[2:])
     mixed_own, mixed_far, outer_x = local_call(
         part_kernel,
         "mixed_parts",
@@ -1647,7 +1649,7 @@
             sums = sums + lax.ppermute(sums, ("z", "y", "x", "core"), [(i, i ^ bit) for i in range(32)])
         return sums
 
-    back_feed = add_piece_call(d_feed, 2, back_feed, pieces[1:3])
+    back_feed = add_piece_call(d_feed, 2, back_feed, [tri_own])
     back_feed = to_z(back_feed, 1)
     out_near, out_send = add_apart_call(out_near, out_far, [tri_own])
     out_far = swap(out_send, "x")
@@ -1688,7 +1690,7 @@
         waits=[sums],
     )
     tail_parts = [tail[0]] + [to_z(tail[s], s) for s in range(1, n_z)]
-    d_near, d_send = add_piece_call(d_feed, 0, back_feed, tail_parts[1:3], True)
+    d_near, d_send = add_piece_call(d_feed, 0, back_feed, [tail[0]], True)
     tokens_grad = local_call(
         functools.partial(leave_kernel, frames_local),
         "tokens_grad",

time: 518 us -> 510 us (0.985)
  waiting for transfers between devices: 122 us -> 98 us
  starting transfers between devices: 46.3 us -> 62.3 us
    ppermute x12, waiting for transfers between devices: 44.6 us -> 20.1 us  [to_z(): return lax.ppermute(array, 'z', [(i, (i + s) % n_z) for i in range(n_z)])]
    ppermute x38, waiting for transfers between devices: 56.9 us -> 43.2 us  [swap(): return lax.ppermute(array, axis, [(0, 1), (1, 0)])]
    ppermute x12, starting transfers between devices: 21.9 us -> 29.6 us  [to_z(): return lax.ppermute(array, 'z', [(i, (i + s) % n_z) for i in range(n_z)])]
    ppermute x4, waiting for transfers between devices: 3.69 us -> 11.3 us  [cross_over(): return lax.ppermute(array, ('x', 'core'), [(i, i ^ 3) for i in range(4)])]
    ppermute x5, starting transfers between devices: 0.71 us -> 7.84 us  [butterfly(): lax.ppermute(sums, ('z', 'y', 'x', 'core'), [(i, i ^ bit) for i in range(...]
    ppermute x5, waiting for transfers between devices: 17.1 us -> 23.3 us  [butterfly(): lax.ppermute(sums, ('z', 'y', 'x', 'core'), [(i, i ^ bit) for i in range(...]
    pallas_call x23 -> x22, Pallas kernels: 69 us -> 66.8 us  [local_call(): pl.pallas_call(waiting(kernel, len(inputs), waits, len(carry), len(output...]
    unnamed x138 -> x144, local copies, waits for them, and re-layouts: 28.7 us -> 29.1 us
  transfers between devices with their start and end apart: 60 -> 60, of which waited for: 24 -> 22; matrix products, arithmetic and copies ran while one was open for 5% -> 5% of each run, Pallas kernels for 39% -> 39%
where the time goes in v4:
time: 510 us; the launch traced here: 503 us
  Pallas kernels  262 us (51%)
  waiting for transfers between devices  98 us (19%)
  starting transfers between devices  62.3 us (12%)
  local copies, waits for them, and re-layouts  51.6 us (10%)
  between operations  17.7 us (3%)
  other arithmetic  12.2 us (2%)
    pallas_call x22, Pallas kernels, local_call(): pl.pallas_call(waiting(kernel, len(inputs), waits, len(carry), len(output...  66.8 us
    pallas_call x1, Pallas kernels, attend_back_call(): pl.pallas_call(waiting(functools.partial(attend_back_kernel, frames_local...  44.2 us
    ppermute x38, waiting for transfers between devices, swap(): return lax.ppermute(array, axis, [(0, 1), (1, 0)])  43.2 us
    pallas_call x2, Pallas kernels, feed_split_call(): pl.pallas_call(waiting(feed_kernel, 2 + len(inputs), waits), grid_spec=pl...  38.9 us
    pallas_call x1, Pallas kernels, attend_call(): pl.pallas_call(waiting(functools.partial(attend_kernel, frames_local), 8,...  31.3 us
    pallas_call x1, Pallas kernels, feed_grad_call(): pl.pallas_call(waiting(feed_grad_kernel, 1 + len(first) + len(tiles) + 2...  31 us
    ppermute x12, starting transfers between devices, to_z(): return lax.ppermute(array, 'z', [(i, (i + s) % n_z) for i in range(n_z)])  29.6 us
    unnamed x144, local copies, waits for them, and re-layouts  29.1 us
  transfers between devices with their start and end apart: 60, of which 22 were waited for; matrix products, arithmetic and copies ran while one was open for 5% of the time, Pallas kernels for 39%

profile of v4, /device:TPU:0, one launch (start us, length us, event | category | flops | bytes accessed | tf_op | source)
XLA Modules:
  0.0 503.4 jit_solution(14931206519620687460)
XLA Ops:
  49.8 5.0 collective-permute-start.13
  56.3 11.7 %collective-permute-done.6.refs_2_ = bf16[4,272,384]{2,1,0:T(8,128)(2,1)} collective-permute-done((bf16[4,272,384]{2,1,0:T(8,128)(2,1)S(1)}, bf16[4,272,384]{2,1,0:T(8,128)(2,1)}, u32[]{:S(2)}, u32[]{:S(2)}) %collective-permute-start.6) | collective-permute-done | bytes 835616 | tf_op jit(solution)/shard_map/ppermute | solution.py:1479
  69.1 3.6 pack.1
  81.8 5.1 %fusion = (f32[4,528,128]{2,1,0:T(8,128)}, f32[4,528,128]{2,1,0:T(8,128)}) fusion(f32[528,128]{1,0:T(8,128)S(1)} %copy-done.35, f32[128]{0:T(128)S(1)} %copy-done.52, f32[4,528]{1,0:T(4,128)S(1)} %maximum_maximum_fusion), kind=kLoop, calls=%fused_computation.3 | loop fusion | flops 540672 | bytes 2441984 | tf_op jit(solution)/shard_map/sin | solution.py:719
  88.4 4.4 collective-permute-done.14.refs_8_.p2.refs_7_
  96.6 4.1 collective-permute-done.12.refs_8_
  103.2 11.9 %enter.1 = (bf16[4,528,256]{2,1,0:T(8,128)(2,1)}, bf16[4,528,256]{2,1,0:T(8,128)(2,1)}, bf16[4,528,256]{2,1,0:T(8,128)(2,1)}, bf16[4,528,1024]{2,1,0:T(8,128)(2,...) custom-call(s32[5]{0:T(128)} %stack.24.refs_0_.place, ...), custom_call_target="tpu_custom_call", output_to_operand_aliasing={{5}: (15, {})} | custom-call | flops 3321888768 | bytes 16220160 | tf_op jit(solution)/shard_map/enter/pallas_call | solution.py:968
  119.9 31.3 %attend.1 = (bf16[4,528,256]{2,1,0:T(8,128)(2,1)}, f32[4,528,256]{2,1,0:T(8,128)}, f32[8,8,1024]{2,1,0:T(8,128)}, f32[8,256]{1,0:T(8,128)}) custom-call(s32[8]{0:T(128)} %compare_select_fusion.2.refs_0_.refs_1_, s32[64,128]{1,0:T(8,128)} %broadcast_in_dim.157.refs_1_.refs_2_, s32[8,64]{1,0:T(8,128)} %broadcast_in_dim.163.refs_2_.refs_3_, ...), custom_call_target="tpu_custom_call" | custom-call | flops 17179869184 | bytes 5406720 | tf_op jit(solution)/shard_map/attend/pallas_call | solution.py:281
  155.8 14.3 %collective-permute-done.23.refs_5_.f3.refs_12_ = bf16[4,512,128]{2,1,0:T(8,128)(2,1)S(1)} collective-permute-done((bf16[4,512,128]{2,1,0:T(8,128)(2,1)}, bf16[4,512,128]{2,1,0:T(8,128)(2,1)S(1)}, u32[]{:S(2)}, u32[]{:S(2)}) %collective-permute-start.23) | collective-permute-done | bytes 524320 | tf_op jit(solution)/shard_map/ppermute | solution.py:1479
  171.4 4.5 project.1
  179.8 4.9 middle.1
  188.6 19.5 %feed_forward.2 = (bf16[1056,1024]{1,0:T(8,128)(2,1)}, bf16[1056,1024]{1,0:T(8,128)(2,1)}, f32[528,1024]{1,0:T(8,128)}, bf16[528,1024]{1,0:T(8,128)(2,1)}, f32[4,1,256]{2,1,0:T(1,128)}) custom-call(s32[5]{0:T(128)} %stack.24.refs_0_.place, bf16[528,1024]{1,0:T(8,128)(2,1)} %get-tuple-element.121.normal.n0, bf16[528,1024]{1,0:T(8,128)(2,1)} %copy-done.54, ...), custom_call_target="tpu_custom_call" | custom-call | flops 6643777536 | bytes 10813440 | tf_op jit(solution)/shard_map/feed_forward/pallas_call | solution.py:1388
  208.1 3.1 collective-permute-done.26.refs_0_.refs_1_.n2
  218.4 19.4 %feed_forward.3 = (bf16[1056,1024]{1,0:T(8,128)(2,1)}, bf16[1056,1024]{1,0:T(8,128)(2,1)}, f32[528,1024]{1,0:T(8,128)}, bf16[528,1024]{1,0:T(8,128)(2,1)}, f32[4,1,256]{2,1,0:T(1,128)}) custom-call(s32[5]{0:T(128)} %stack.24.refs_0_.place, bf16[528,1024]{1,0:T(8,128)(2,1)} %copy-done.19, bf16[528,1024]{1,0:T(8,128)(2,1)} %copy-done.56, ...), custom_call_target="tpu_custom_call" | custom-call | flops 6643777536 | bytes 10813440 | tf_op jit(solution)/shard_map/feed_forward/pallas_call | solution.py:1388
  246.4 31.0 %feed_grads.1 = (f32[528,1024]{1,0:T(8,128)}, bf16[528,1024]{1,0:T(8,128)(2,1)}, bf16[528,1024]{1,0:T(8,128)(2,1)}, bf16[528,1024]{1,0:T(8,128)(2,1)}, bf16[4,2,...) custom-call(s32[5]{0:T(128)} %stack.24.refs_0_.place, bf16[528,1024]{1,0:T(8,128)(2,1)} %get-tuple-element.121.normal.n0, ...), custom_call_target="tpu_custom_call" | custom-call | flops 13287555072 | bytes 21626880 | tf_op jit(solution)/shard_map/feed_grads/pallas_call | solution.py:1415
  278.8 6.9 %middle_back.1 = (f32[528,1024]{1,0:T(8,128)}, bf16[528,1024]{1,0:T(8,128)(2,1)}, f32[8,1024]{1,0:T(8,128)}) custom-call(f32[528,1024]{1,0:T(8,128)} %get-tuple-element.120.refs_0_, bf16[528,1024]{1,0:T(8,128)(2,1)} %get-tuple-element.114.cot.c0.refs_1_, f32[528,1024]{1,0:T(8,128)} %get-tuple-element.132.refs_2_, bf16[528,1024]{1,0:T(8,128)(2,1)} %copy-done.13, ...), custom_call_target="tpu_custom_call" | custom-call | flops 1 | bytes 1 | tf_op jit(solution)/shard_map/middle_back/pallas_call | solution.py:1034
  290.5 4.2 mixed_grad.1
  295.3 5.1 %collective-permute-start.37 = (bf16[2,4,512,128]{3,2,1,0:T(8,128)(2,1)S(1)}, bf16[2,4,512,128]{3,2,1,0:T(8,128)(2,1)S(1)}, u32[]{:S(2)}, u32[]{:S(2)}) collective-permute-start(bf16[2,4,512,128]{3,2,1,0:T(8,128)(2,1)S(1)} %copy-done.25), channel_id=1, source_target_pairs={{0,8},{8,16},{16,24},{24,0},{1,9},{9,17},{17,25},{25,1},{2,10},{10... | collective-permute-start | bytes 3145736 | tf_op jit(solution)/shard_map/ppermute | solution.py:1485
  300.3 4.8 output_weight_grad.1
  309.7 44.2 %attend_back.1.refs_2_.refs_3_ = bf16[4,528,768]{2,1,0:T(8,128)(2,1)} custom-call(s32[1]{0:T(128)} %bitcast.2.refs_0_, s32[8]{0:T(128)} %compare_select_fusion.2.refs_0_.refs_1_, s32[64,128]{1,0:T(8,128)} %broadcast_in_dim.157.refs_1_.refs_2_, s32[8,64]{1,0:T(8,128)} %broadcast_in_dim.163.refs_2_.refs_3_, s32[8,64]{1,0:T(8,128)} %broadcast_in_dim.166.refs_3_.refs_4_, ...), custom_call_target="tpu_custom_call" | custom-call | flops 42949672960 | bytes 10813440 | tf_op jit(solution)/shard_map/attend_back/pallas_call | solution.py:517
  355.4 17.6 %triple_grads.1 = (bf16[256,768]{1,0:T(8,128)(2,1)}, bf16[256,768]{1,0:T(8,128)(2,1)}, bf16[256,768]{1,0:T(8,128)(2,1)}, bf16[256,768]{1,0:T(8,128)(2,1)}, bf16[...) custom-call(s32[5]{0:T(128)} %stack.24.refs_0_.place, ...), custom_call_target="tpu_custom_call" | custom-call | flops 6643777536 | bytes 10813440 | tf_op jit(solution)/shard_map/triple_grads/pallas_call | solution.py:1144
  377.2 5.4 %collective-permute-start.47 = (bf16[2,4,512,128]{3,2,1,0:T(8,128)(2,1)}, bf16[2,4,512,128]{3,2,1,0:T(8,128)(2,1)}, u32[]{:S(2)}, u32[]{:S(2)}) collective-permute-start(bf16[2,4,512,128]{3,2,1,0:T(8,128)(2,1)} %add_piece.3), channel_id=1, source_target_pairs={{0,8},{8,16},{16,24},{24,0},{1,9},{9,17},{17,25},{25,1},{2,10},{10... | collective-permute-start | bytes 3145736 | tf_op jit(solution)/shard_map/ppermute | solution.py:1485
  388.1 4.6 block_output.1.refs_5_
  392.6 3.1 collective-permute-done.40.refs_4_.refs_3_
  395.7 7.3 %collective-permute-done.41.refs_5_.refs_4_ = bf16[256,768]{1,0:T(8,128)(2,1)S(1)} collective-permute-done((bf16[256,768]{1,0:T(8,128)(2,1)}, bf16[256,768]{1,0:T(8,128)(2,1)S(1)}, u32[]{:S(2)}, u32[]{:S(2)}) %collective-permute-start.41) | collective-permute-done | bytes 393248 | tf_op jit(solution)/shard_map/ppermute | solution.py:1482
  404.4 3.9 normed_sum.1
  409.9 3.1 unpack.1
  419.4 17.5 %collective-permute-done.46 = f32[8,1664]{1,0:T(8,128)S(1)} collective-permute-done((f32[8,1664]{1,0:T(8,128)S(1)}, f32[8,1664]{1,0:T(8,128)S(1)}, u32[]{:S(2)}, u32[]{:S(2)}) %collective-permute-start.46) | collective-permute-done | bytes 53280 | tf_op jit(solution)/shard_map/ppermute | solution.py:1649
  452.0 5.8 %tokens_grad.1.refs_4_ = f32[516,1024]{1,0:T(8,128)} custom-call(bf16[528,1024]{1,0:T(8,128)(2,1)} %copy.97.refs_1_.entered.refs_5_.refs_0_, bf16[528,1024]{1,0:T(8,128)(2,1)} %get-tuple-element.154.refs_6_.refs_1_, bf16[528,1024]{1,0:T(8,128)(2,1)} %copy-done.12, f32[528,1024]{1,0:T(8,128)} %get-tuple-element.156.refs_3_, f32[528,1]{1,0:T(8,128)} %copy.64.refs_4_, ...), custom_call_target="tpu_custom_call" | custom-call | flops 1 | bytes 1 | tf_op jit(solution)/shard_map/tokens_grad/pallas_call | solution.py:768
  458.4 10.0 %collective-permute-done.51.refs_2_ = bf16[256,512]{1,0:T(8,128)(2,1)S(1)} collective-permute-done((bf16[256,512]{1,0:T(8,128)(2,1)S(1)}, bf16[256,512]{1,0:T(8,128)(2,1)S(1)}, u32[]{:S(2)}, u32[]{:S(2)}) %collective-permute-start.51) | collective-permute-done | bytes 262176 | tf_op jit(solution)/shard_map/ppermute | solution.py:1485
  480.6 4.3 collective-permute-start.54
  488.2 3.5 copy.67
  (376 shorter events, 160.9 us)
Async XLA Ops:
  7.2 162.8 %all-gather.3.cloned.1.call-start = ((), (), s32[]{:S(2)}) async-start(), calls=%async_computation | async-start | bytes 1114112 | tf_op jit(solution)/shard_map/all_gather | solution.py:1530
  46.5 21.6 %collective-permute-start.7 = (bf16[528,1024]{1,0:T(8,128)(2,1)}, bf16[528,1024]{1,0:T(8,128)(2,1)S(1)}, u32[]{:S(2)}, u32[]{:S(2)}) collective-permute-start(bf16[528,1024]{1,0:T(8,128)(2,1)} %copy.97.refs_1_.entered.refs_5_.refs_0_), channel_id=1, source_target_pairs={{0,1},{1,0},{2,3},{3,2},{4,5},{5,4},{6,7},{7,6},{8,9},{9,8},{10,11... | collective-permute-start | bytes 3244040 | tf_op jit(solution)/shard_map/ppermute | solution.py:1479
  46.5 21.6 %collective-permute-start.6 = (bf16[4,272,384]{2,1,0:T(8,128)(2,1)S(1)}, bf16[4,272,384]{2,1,0:T(8,128)(2,1)}, u32[]{:S(2)}, u32[]{:S(2)}) collective-permute-start(bf16[4,272,384]{2,1,0:T(8,128)(2,1)S(1)} %copy-done.1), channel_id=1, source_target_pairs={{0,4},{4,0},{1,5},{5,1},{2,6},{6,2},{3,7},{7,3},{8,12},{12,8},{9,1... | collective-permute-start | bytes 2506760 | tf_op jit(solution)/shard_map/ppermute | solution.py:1479
  48.0 28.2 %collective-permute-start.8 = (bf16[528,1024]{1,0:T(8,128)(2,1)}, bf16[528,1024]{1,0:T(8,128)(2,1)S(1)}, u32[]{:S(2)}, u32[]{:S(2)}) collective-permute-start(bf16[528,1024]{1,0:T(8,128)(2,1)} %copy.97.refs_1_.entered.refs_5_.refs_0_), channel_id=1, source_target_pairs={{0,2},{2,0},{1,3},{3,1},{4,6},{6,4},{5,7},{7,5},{8,10},{10,8},{9,1... | collective-permute-start | bytes 3244040 | tf_op jit(solution)/shard_map/ppermute | solution.py:1479
  49.8 37.1 %collective-permute-start.13 = (bf16[4,512,128]{2,1,0:T(8,128)(2,1)S(1)}, bf16[4,512,128]{2,1,0:T(8,128)(2,1)}, u32[]{:S(2)}, u32[]{:S(2)}) collective-permute-start(bf16[4,512,128]{2,1,0:T(8,128)(2,1)S(1)} %copy-done.6), channel_id=1, source_target_pairs={{0,8},{8,16},{16,24},{24,0},{1,9},{9,17},{17,25},{25,1},{2,10},{10... | collective-permute-start | bytes 1572872 | tf_op jit(solution)/shard_map/ppermute | solution.py:1485
  54.8 38.0 %collective-permute-start.14 = (bf16[4,512,128]{2,1,0:T(8,128)(2,1)S(1)}, bf16[4,512,128]{2,1,0:T(8,128)(2,1)}, u32[]{:S(2)}, u32[]{:S(2)}) collective-permute-start(bf16[4,512,128]{2,1,0:T(8,128)(2,1)S(1)} %copy-done.6), channel_id=1, source_target_pairs={{0,16},{8,24},{16,0},{24,8},{1,17},{9,25},{17,1},{25,9},{2,18},{10... | collective-permute-start | bytes 1572872 | tf_op jit(solution)/shard_map/ppermute | solution.py:1485
  79.5 22.7 %collective-permute-start.9 = (bf16[528,1024]{1,0:T(8,128)(2,1)}, bf16[528,1024]{1,0:T(8,128)(2,1)S(1)}, u32[]{:S(2)}, u32[]{:S(2)}) collective-permute-start(bf16[528,1024]{1,0:T(8,128)(2,1)} %copy.98), channel_id=1, source_target_pairs={{0,1},{1,0},{2,3},{3,2},{4,5},{5,4},{6,7},{7,6},{8,9},{9,8},{10,11... | collective-permute-start | bytes 3244040 | tf_op jit(solution)/shard_map/ppermute | solution.py:1479
  92.8 23.1 %collective-permute-start.15 = (bf16[4,512,128]{2,1,0:T(8,128)(2,1)S(1)}, bf16[4,512,128]{2,1,0:T(8,128)(2,1)}, u32[]{:S(2)}, u32[]{:S(2)}) collective-permute-start(bf16[4,512,128]{2,1,0:T(8,128)(2,1)S(1)} %copy-done.6), channel_id=1, source_target_pairs={{0,24},{8,0},{16,8},{24,16},{1,25},{9,1},{17,9},{25,17},{2,26},{10... | collective-permute-start | bytes 1572872 | tf_op jit(solution)/shard_map/ppermute | solution.py:1485
  94.5 56.7 %collective-permute-start.16 = (bf16[4,512,128]{2,1,0:T(8,128)(2,1)S(1)}, bf16[4,512,128]{2,1,0:T(8,128)(2,1)S(1)}, u32[]{:S(2)}, u32[]{:S(2)}) collective-permute-start(bf16[4,512,128]{2,1,0:T(8,128)(2,1)S(1)} %copy-done.6), channel_id=1, source_target_pairs={{0,4},{4,0},{1,5},{5,1},{2,6},{6,2},{3,7},{7,3},{8,12},{12,8},{9,1... | collective-permute-start | bytes 1572872 | tf_op jit(solution)/shard_map/ppermute | solution.py:1479
  96.1 55.1 %collective-permute-start.17 = (bf16[4,512,128]{2,1,0:T(8,128)(2,1)}, bf16[4,512,128]{2,1,0:T(8,128)(2,1)S(1)}, u32[]{:S(2)}, u32[]{:S(2)}) collective-permute-start(bf16[4,512,128]{2,1,0:T(8,128)(2,1)} %collective-permute-done.13.refs_14_.p1.refs_6_), channel_id=1, source_target_pairs={{0,4},{4,0},{1,5},{5,1},{2,6},{6,2},{3,7},{7,3},{8,12},{12,8},{9,1... | collective-permute-start | bytes 1572872 | tf_op jit(solution)/shard_map/ppermute | solution.py:1479
  100.7 50.5 %collective-permute-start.18 = (bf16[4,512,128]{2,1,0:T(8,128)(2,1)}, bf16[4,512,128]{2,1,0:T(8,128)(2,1)}, u32[]{:S(2)}, u32[]{:S(2)}) collective-permute-start(bf16[4,512,128]{2,1,0:T(8,128)(2,1)} %collective-permute-done.14.refs_8_.p2.refs_7_), channel_id=1, source_target_pairs={{0,4},{4,0},{1,5},{5,1},{2,6},{6,2},{3,7},{7,3},{8,12},{12,8},{9,1... | collective-permute-start | bytes 1572872 | tf_op jit(solution)/shard_map/ppermute | solution.py:1479
  115.1 36.2 %collective-permute-start.19 = (bf16[528,1024]{1,0:T(8,128)(2,1)}, bf16[528,1024]{1,0:T(8,128)(2,1)S(1)}, u32[]{:S(2)}, u32[]{:S(2)}) collective-permute-start(bf16[528,1024]{1,0:T(8,128)(2,1)} %get-tuple-element.114.cot.c0.refs_1_), channel_id=1, source_target_pairs={{0,1},{1,0},{2,3},{3,2},{4,5},{5,4},{6,7},{7,6},{8,9},{9,8},{10,11... | collective-permute-start | bytes 3244040 | tf_op jit(solution)/shard_map/ppermute | solution.py:1479
  115.9 35.4 %collective-permute-start.20 = (bf16[528,1024]{1,0:T(8,128)(2,1)}, bf16[528,1024]{1,0:T(8,128)(2,1)S(1)}, u32[]{:S(2)}, u32[]{:S(2)}) collective-permute-start(bf16[528,1024]{1,0:T(8,128)(2,1)} %get-tuple-element.114.cot.c0.refs_1_), channel_id=1, source_target_pairs={{0,2},{2,0},{1,3},{3,1},{4,6},{6,4},{5,7},{7,5},{8,10},{10,8},{9,1... | collective-permute-start | bytes 3244040 | tf_op jit(solution)/shard_map/ppermute | solution.py:1479
  184.8 26.4 %collective-permute-start.26 = (bf16[528,1024]{1,0:T(8,128)(2,1)}, bf16[528,1024]{1,0:T(8,128)(2,1)S(1)}, u32[]{:S(2)}, u32[]{:S(2)}) collective-permute-start(bf16[528,1024]{1,0:T(8,128)(2,1)} %get-tuple-element.121.normal.n0), channel_id=1, source_target_pairs={{0,2},{2,0},{1,3},{3,1},{4,6},{6,4},{5,7},{7,5},{8,10},{10,8},{9,1... | collective-permute-start | bytes 3244040 | tf_op jit(solution)/shard_map/ppermute | solution.py:1479
  238.0 39.4 %collective-permute-start.30 = (bf16[528,1024]{1,0:T(8,128)(2,1)S(1)}, bf16[528,1024]{1,0:T(8,128)(2,1)S(1)}, u32[]{:S(2)}, u32[]{:S(2)}) collective-permute-start(bf16[528,1024]{1,0:T(8,128)(2,1)S(1)} %copy-done.55), channel_id=1, source_target_pairs={{0,1},{1,0},{2,3},{3,2},{4,5},{5,4},{6,7},{7,6},{8,9},{9,8},{10,11... | collective-permute-start | bytes 3244040 | tf_op jit(solution)/shard_map/ppermute | solution.py:1479
  244.9 32.5 %collective-permute-start.32 = (bf16[528,1024]{1,0:T(8,128)(2,1)}, bf16[528,1024]{1,0:T(8,128)(2,1)S(1)}, u32[]{:S(2)}, u32[]{:S(2)}) collective-permute-start(bf16[528,1024]{1,0:T(8,128)(2,1)} %add.187), channel_id=1, source_target_pairs={{0,2},{2,0},{1,3},{3,1},{4,6},{6,4},{5,7},{7,5},{8,10},{10,8},{9,1... | collective-permute-start | bytes 3244040 | tf_op jit(solution)/shard_map/ppermute | solution.py:1479
  285.8 19.6 %collective-permute-start.29 = (bf16[528,1024]{1,0:T(8,128)(2,1)}, bf16[528,1024]{1,0:T(8,128)(2,1)}, u32[]{:S(2)}, u32[]{:S(2)}) collective-permute-start(bf16[528,1024]{1,0:T(8,128)(2,1)} %get-tuple-element.131), channel_id=1, source_target_pairs={{0,1},{1,0},{2,3},{3,2},{4,5},{5,4},{6,7},{7,6},{8,9},{9,8},{10,11... | collective-permute-start | bytes 3244040 | tf_op jit(solution)/shard_map/ppermute | solution.py:1479
  286.3 23.4 %collective-permute-start.28 = (bf16[528,1024]{1,0:T(8,128)(2,1)}, bf16[528,1024]{1,0:T(8,128)(2,1)}, u32[]{:S(2)}, u32[]{:S(2)}) collective-permute-start(bf16[528,1024]{1,0:T(8,128)(2,1)} %get-tuple-element.129), channel_id=1, source_target_pairs={{0,1},{1,0},{2,3},{3,2},{4,5},{5,4},{6,7},{7,6},{8,9},{9,8},{10,11... | collective-permute-start | bytes 3244040 | tf_op jit(solution)/shard_map/ppermute | solution.py:1479
  295.3 58.7 %collective-permute-start.37 = (bf16[2,4,512,128]{3,2,1,0:T(8,128)(2,1)S(1)}, bf16[2,4,512,128]{3,2,1,0:T(8,128)(2,1)S(1)}, u32[]{:S(2)}, u32[]{:S(2)}) collective-permute-start(bf16[2,4,512,128]{3,2,1,0:T(8,128)(2,1)S(1)} %copy-done.25), channel_id=1, source_target_pairs={{0,8},{8,16},{16,24},{24,0},{1,9},{9,17},{17,25},{25,1},{2,10},{10... | collective-permute-start | bytes 3145736 | tf_op jit(solution)/shard_map/ppermute | solution.py:1485
  305.1 48.9 %collective-permute-start.35 = (bf16[2,4,256,128]{3,2,1,0:T(8,128)(2,1)}, bf16[2,4,256,128]{3,2,1,0:T(8,128)(2,1)S(1)}, u32[]{:S(2)}, u32[]{:S(2)}) collective-permute-start(bf16[2,4,256,128]{3,2,1,0:T(8,128)(2,1)} %get-tuple-element.139), channel_id=1, source_target_pairs={{0,4},{4,0},{1,5},{5,1},{2,6},{6,2},{3,7},{7,3},{8,12},{12,8},{9,1... | collective-permute-start | bytes 1572872 | tf_op jit(solution)/shard_map/ppermute | solution.py:1479
  308.2 45.8 %collective-permute-start.34 = (bf16[528,1024]{1,0:T(8,128)(2,1)}, bf16[528,1024]{1,0:T(8,128)(2,1)S(1)}, u32[]{:S(2)}, u32[]{:S(2)}) collective-permute-start(bf16[528,1024]{1,0:T(8,128)(2,1)} %add.188), channel_id=1, source_target_pairs={{0,2},{2,0},{1,3},{3,1},{4,6},{6,4},{5,7},{7,5},{8,10},{10,8},{9,1... | collective-permute-start | bytes 3244040 | tf_op jit(solution)/shard_map/ppermute | solution.py:1479
  373.1 29.9 %collective-permute-start.38 = (bf16[2,528,1024]{2,1,0:T(8,128)(2,1)}, bf16[2,528,1024]{2,1,0:T(8,128)(2,1)S(1)}, u32[]{:S(2)}, u32[]{:S(2)}) collective-permute-start(bf16[2,528,1024]{2,1,0:T(8,128)(2,1)} %get-tuple-element.150), channel_id=1, source_target_pairs={{0,1},{1,0},{2,3},{3,2},{4,5},{5,4},{6,7},{7,6},{8,9},{9,8},{10,11... | collective-permute-start | bytes 6488072 | tf_op jit(solution)/shard_map/ppermute | solution.py:1479
  377.2 35.8 %collective-permute-start.47 = (bf16[2,4,512,128]{3,2,1,0:T(8,128)(2,1)}, bf16[2,4,512,128]{3,2,1,0:T(8,128)(2,1)}, u32[]{:S(2)}, u32[]{:S(2)}) collective-permute-start(bf16[2,4,512,128]{3,2,1,0:T(8,128)(2,1)} %add_piece.3), channel_id=1, source_target_pairs={{0,8},{8,16},{16,24},{24,0},{1,9},{9,17},{17,25},{25,1},{2,10},{10... | collective-permute-start | bytes 3145736 | tf_op jit(solution)/shard_map/ppermute | solution.py:1485
  383.8 19.2 %collective-permute-start.41 = (bf16[256,768]{1,0:T(8,128)(2,1)}, bf16[256,768]{1,0:T(8,128)(2,1)S(1)}, u32[]{:S(2)}, u32[]{:S(2)}) collective-permute-start(bf16[256,768]{1,0:T(8,128)(2,1)} %get-tuple-element.153), channel_id=1, source_target_pairs={{0,3},{1,2},{2,1},{3,0},{4,7},{5,6},{6,5},{7,4},{8,11},{9,10},{10,... | collective-permute-start | bytes 1179656 | tf_op jit(solution)/shard_map/ppermute | solution.py:1482
  387.7 21.5 %collective-permute-start.43 = (bf16[4,256,128]{2,1,0:T(8,128)(2,1)}, bf16[4,256,128]{2,1,0:T(8,128)(2,1)S(1)}, u32[]{:S(2)}, u32[]{:S(2)}) collective-permute-start(bf16[4,256,128]{2,1,0:T(8,128)(2,1)} %get-tuple-element.157), channel_id=1, source_target_pairs={{0,2},{2,0},{1,3},{3,1},{4,6},{6,4},{5,7},{7,5},{8,10},{10,8},{9,1... | collective-permute-start | bytes 786440 | tf_op jit(solution)/shard_map/ppermute | solution.py:1479
  415.8 27.6 %collective-permute-start.48 = (bf16[2,4,512,128]{3,2,1,0:T(8,128)(2,1)}, bf16[2,4,512,128]{3,2,1,0:T(8,128)(2,1)S(1)}, u32[]{:S(2)}, u32[]{:S(2)}) collective-permute-start(bf16[2,4,512,128]{3,2,1,0:T(8,128)(2,1)} %add_piece.4), channel_id=1, source_target_pairs={{0,8},{8,16},{16,24},{24,0},{1,9},{9,17},{17,25},{25,1},{2,10},{10... | collective-permute-start | bytes 3145736 | tf_op jit(solution)/shard_map/ppermute | solution.py:1485
  415.8 21.7 %collective-permute-start.44 = (bf16[4,256,384]{2,1,0:T(8,128)(2,1)S(1)}, bf16[4,256,384]{2,1,0:T(8,128)(2,1)S(1)}, u32[]{:S(2)}, u32[]{:S(2)}) collective-permute-start(bf16[4,256,384]{2,1,0:T(8,128)(2,1)S(1)} %copy-done.57), channel_id=1, source_target_pairs={{0,4},{4,0},{1,5},{5,1},{2,6},{6,2},{3,7},{7,3},{8,12},{12,8},{9,1... | collective-permute-start | bytes 2359304 | tf_op jit(solution)/shard_map/ppermute | solution.py:1479
  415.8 35.1 %collective-permute-start.42 = (bf16[528,1024]{1,0:T(8,128)(2,1)}, bf16[528,1024]{1,0:T(8,128)(2,1)S(1)}, u32[]{:S(2)}, u32[]{:S(2)}) collective-permute-start(bf16[528,1024]{1,0:T(8,128)(2,1)} %get-tuple-element.155), channel_id=1, source_target_pairs={{0,2},{2,0},{1,3},{3,1},{4,6},{6,4},{5,7},{7,5},{8,10},{10,8},{9,1... | collective-permute-start | bytes 3244040 | tf_op jit(solution)/shard_map/ppermute | solution.py:1479
  417.4 19.5 %collective-permute-start.46 = (f32[8,1664]{1,0:T(8,128)S(1)}, f32[8,1664]{1,0:T(8,128)S(1)}, u32[]{:S(2)}, u32[]{:S(2)}) collective-permute-start(f32[8,1664]{1,0:T(8,128)S(1)} %add.170), channel_id=1, source_target_pairs={{0,4},{1,5},{2,6},{3,7},{4,0},{5,1},{6,2},{7,3},{8,12},{9,13},{10,... | collective-permute-start | bytes 159752 | tf_op jit(solution)/shard_map/ppermute | solution.py:1649
  447.1 25.0 %collective-permute-start.49 = (bf16[4,512,128]{2,1,0:T(8,128)(2,1)}, bf16[4,512,128]{2,1,0:T(8,128)(2,1)S(1)}, u32[]{:S(2)}, u32[]{:S(2)}) collective-permute-start(bf16[4,512,128]{2,1,0:T(8,128)(2,1)} %get-tuple-element.169), channel_id=1, source_target_pairs={{0,4},{4,0},{1,5},{5,1},{2,6},{6,2},{3,7},{7,3},{8,12},{12,8},{9,1... | collective-permute-start | bytes 1572872 | tf_op jit(solution)/shard_map/ppermute | solution.py:1479
  447.1 21.3 %collective-permute-start.51 = (bf16[256,512]{1,0:T(8,128)(2,1)S(1)}, bf16[256,512]{1,0:T(8,128)(2,1)S(1)}, u32[]{:S(2)}, u32[]{:S(2)}) collective-permute-start(bf16[256,512]{1,0:T(8,128)(2,1)S(1)} %copy-done.62), channel_id=1, source_target_pairs={{0,16},{8,24},{16,0},{24,8},{1,17},{9,25},{17,1},{25,9},{2,18},{10... | collective-permute-start | bytes 786440 | tf_op jit(solution)/shard_map/ppermute | solution.py:1485
  449.1 19.4 %collective-permute-start.52 = (bf16[256,512]{1,0:T(8,128)(2,1)S(1)}, bf16[256,512]{1,0:T(8,128)(2,1)S(1)}, u32[]{:S(2)}, u32[]{:S(2)}) collective-permute-start(bf16[256,512]{1,0:T(8,128)(2,1)S(1)} %copy-done.61), channel_id=1, source_target_pairs={{0,24},{8,0},{16,8},{24,16},{1,25},{9,1},{17,9},{25,17},{2,26},{10... | collective-permute-start | bytes 786440 | tf_op jit(solution)/shard_map/ppermute | solution.py:1485
  (93 other events, 588.0 us)
Sparse Core Ops, SparseCore 0:
  49.6 81.0 all-gather.2

commit v5 on v4

--- a/solution.py
+++ b/solution.py
@@ -1493,15 +1493,17 @@
     def scatter_z(array, waits=(), dtype=BF):
         return add_call([array[0]] + [to_z(array[s], s) for s in range(1, n_z)], waits, dtype)
 
-    def lane_row(vector):
-        return jnp.pad(vector, (0, qkv_part - vector.shape[0]))[None]
-
-    vectors = [attend_gain, attend_shift, output_bias, second_gain, second_shift, reduce_bias, triple_bias]
-    vectors += [expand_bias[f * quarter : (f + 1) * quarter] for f in range(4)]
+    small = [attend_gain, attend_shift, output_bias, second_gain, second_shift, reduce_bias]
+    small = jnp.concatenate([v.reshape(1, d_part) for v in small], 0)
     packed = jnp.concatenate(
-        [triple_weight] + [lane_row(v) for v in vectors] + [jnp.zeros((16 - len(vectors), qkv_part), BF)], 0
-    )
-
+        [
+            triple_weight,
+            jnp.pad(small, ((0, 0), (0, qkv_part - d_part))),
+            triple_bias.reshape(1, qkv_part),
+            jnp.pad(expand_bias.reshape(4, quarter), ((0, 5), (0, qkv_part - quarter))),
+        ],
+        0,
+    )
     live_all = tables(frame_counts[0], presence[0], n_f, frames_local, width // HEAD)[0]
     live = take(live_all, shard)[:, None]
     entered = to_block(tokens[0], frames_local) * live.astype(BF)

time: 510 us -> 503 us (0.986)
  local copies, waits for them, and re-layouts: 51.6 us -> 44.7 us
where the time goes in v5:
time: 503 us; the launch traced here: 497 us
  Pallas kernels  262 us (52%)
  waiting for transfers between devices  97.3 us (19%)
  starting transfers between devices  62.6 us (12%)
  local copies, waits for them, and re-layouts  44.7 us (9%)
  between operations  17.8 us (4%)
  other arithmetic  13.2 us (3%)
    pallas_call x22, Pallas kernels, local_call(): pl.pallas_call(waiting(kernel, len(inputs), waits, len(carry), len(output...  66.7 us
    pallas_call x1, Pallas kernels, attend_back_call(): pl.pallas_call(waiting(functools.partial(attend_back_kernel, frames_local...  44.2 us
    ppermute x38, waiting for transfers between devices, swap(): return lax.ppermute(array, axis, [(0, 1), (1, 0)])  42.8 us
    pallas_call x2, Pallas kernels, feed_split_call(): pl.pallas_call(waiting(feed_kernel, 2 + len(inputs), waits), grid_spec=pl...  39.2 us
    pallas_call x1, Pallas kernels, attend_call(): pl.pallas_call(waiting(functools.partial(attend_kernel, frames_local), 8,...  31.3 us
    pallas_call x1, Pallas kernels, feed_grad_call(): pl.pallas_call(waiting(feed_grad_kernel, 1 + len(first) + len(tiles) + 2...  30.8 us
    ppermute x12, starting transfers between devices, to_z(): return lax.ppermute(array, 'z', [(i, (i + s) % n_z) for i in range(n_z)])  30.1 us
    unnamed x144, local copies, waits for them, and re-layouts  29.1 us
  transfers between devices with their start and end apart: 60, of which 22 were waited for; matrix products, arithmetic and copies ran while one was open for 5% of the time, Pallas kernels for 39%

profile of v5, /device:TPU:0, one launch (start us, length us, event | category | flops | bytes accessed | tf_op | source)
XLA Modules:
  0.0 497.3 jit_solution(11125126048048035501)
XLA Ops:
  43.8 5.0 collective-permute-start.13
  50.3 11.7 %collective-permute-done.6.refs_2_ = bf16[4,272,384]{2,1,0:T(8,128)(2,1)} collective-permute-done((bf16[4,272,384]{2,1,0:T(8,128)(2,1)S(1)}, bf16[4,272,384]{2,1,0:T(8,128)(2,1)}, u32[]{:S(2)}, u32[]{:S(2)}) %collective-permute-start.6) | collective-permute-done | bytes 835616 | tf_op jit(solution)/shard_map/ppermute | solution.py:1479
  63.1 3.6 pack.1
  75.8 5.2 %fusion = (f32[4,528,128]{2,1,0:T(8,128)}, f32[4,528,128]{2,1,0:T(8,128)}) fusion(f32[528,128]{1,0:T(8,128)S(1)} %copy-done.35, f32[128]{0:T(128)S(1)} %copy-done.52, f32[4,528]{1,0:T(4,128)S(1)} %maximum_maximum_fusion), kind=kLoop, calls=%fused_computation.3 | loop fusion | flops 540672 | bytes 2441984 | tf_op jit(solution)/shard_map/sin | solution.py:719
  82.4 4.3 collective-permute-done.14.refs_8_.p2.refs_7_
  90.8 3.9 collective-permute-done.12.refs_8_
  97.2 11.9 %enter.1 = (bf16[4,528,256]{2,1,0:T(8,128)(2,1)}, bf16[4,528,256]{2,1,0:T(8,128)(2,1)}, bf16[4,528,256]{2,1,0:T(8,128)(2,1)}, bf16[4,528,1024]{2,1,0:T(8,128)(2,...) custom-call(s32[5]{0:T(128)} %stack.24.refs_0_.place, ...), custom_call_target="tpu_custom_call", output_to_operand_aliasing={{5}: (15, {})} | custom-call | flops 3321888768 | bytes 16220160 | tf_op jit(solution)/shard_map/enter/pallas_call | solution.py:968
  113.9 31.3 %attend.1 = (bf16[4,528,256]{2,1,0:T(8,128)(2,1)}, f32[4,528,256]{2,1,0:T(8,128)}, f32[8,8,1024]{2,1,0:T(8,128)}, f32[8,256]{1,0:T(8,128)}) custom-call(s32[8]{0:T(128)} %compare_select_fusion.2.refs_0_.refs_1_, s32[64,128]{1,0:T(8,128)} %broadcast_in_dim.109.refs_1_.refs_2_, s32[8,64]{1,0:T(8,128)} %broadcast_in_dim.115.refs_2_.refs_3_, ...), custom_call_target="tpu_custom_call" | custom-call | flops 17179869184 | bytes 5406720 | tf_op jit(solution)/shard_map/attend/pallas_call | solution.py:281
  149.8 14.3 %collective-permute-done.23.refs_5_.f3.refs_12_ = bf16[4,512,128]{2,1,0:T(8,128)(2,1)S(1)} collective-permute-done((bf16[4,512,128]{2,1,0:T(8,128)(2,1)}, bf16[4,512,128]{2,1,0:T(8,128)(2,1)S(1)}, u32[]{:S(2)}, u32[]{:S(2)}) %collective-permute-start.23) | collective-permute-done | bytes 524320 | tf_op jit(solution)/shard_map/ppermute | solution.py:1479
  165.4 4.5 project.1
  173.8 4.8 middle.1
  182.5 19.8 %feed_forward.2 = (bf16[1056,1024]{1,0:T(8,128)(2,1)}, bf16[1056,1024]{1,0:T(8,128)(2,1)}, f32[528,1024]{1,0:T(8,128)}, bf16[528,1024]{1,0:T(8,128)(2,1)}, f32[4,1,256]{2,1,0:T(1,128)}) custom-call(s32[5]{0:T(128)} %stack.24.refs_0_.place, bf16[528,1024]{1,0:T(8,128)(2,1)} %get-tuple-element.121.normal.n0, bf16[528,1024]{1,0:T(8,128)(2,1)} %copy-done.54, ...), custom_call_target="tpu_custom_call" | custom-call | flops 6643777536 | bytes 10813440 | tf_op jit(solution)/shard_map/feed_forward/pallas_call | solution.py:1388
  212.3 19.4 %feed_forward.3 = (bf16[1056,1024]{1,0:T(8,128)(2,1)}, bf16[1056,1024]{1,0:T(8,128)(2,1)}, f32[528,1024]{1,0:T(8,128)}, bf16[528,1024]{1,0:T(8,128)(2,1)}, f32[4,1,256]{2,1,0:T(1,128)}) custom-call(s32[5]{0:T(128)} %stack.24.refs_0_.place, bf16[528,1024]{1,0:T(8,128)(2,1)} %copy-done.19, bf16[528,1024]{1,0:T(8,128)(2,1)} %copy-done.56, ...), custom_call_target="tpu_custom_call" | custom-call | flops 6643777536 | bytes 10813440 | tf_op jit(solution)/shard_map/feed_forward/pallas_call | solution.py:1388
  235.7 3.1 add.173
  240.4 30.8 %feed_grads.1 = (f32[528,1024]{1,0:T(8,128)}, bf16[528,1024]{1,0:T(8,128)(2,1)}, bf16[528,1024]{1,0:T(8,128)(2,1)}, bf16[528,1024]{1,0:T(8,128)(2,1)}, bf16[4,2,...) custom-call(s32[5]{0:T(128)} %stack.24.refs_0_.place, bf16[528,1024]{1,0:T(8,128)(2,1)} %get-tuple-element.121.normal.n0, ...), custom_call_target="tpu_custom_call" | custom-call | flops 13287555072 | bytes 21626880 | tf_op jit(solution)/shard_map/feed_grads/pallas_call | solution.py:1415
  272.6 6.9 %middle_back.1 = (f32[528,1024]{1,0:T(8,128)}, bf16[528,1024]{1,0:T(8,128)(2,1)}, f32[8,1024]{1,0:T(8,128)}) custom-call(f32[528,1024]{1,0:T(8,128)} %get-tuple-element.120.refs_0_, bf16[528,1024]{1,0:T(8,128)(2,1)} %get-tuple-element.114.cot.c0.refs_1_, f32[528,1024]{1,0:T(8,128)} %get-tuple-element.132.refs_2_, bf16[528,1024]{1,0:T(8,128)(2,1)} %copy-done.13, ...), custom_call_target="tpu_custom_call" | custom-call | flops 1 | bytes 1 | tf_op jit(solution)/shard_map/middle_back/pallas_call | solution.py:1034
  284.3 4.2 mixed_grad.1
  288.9 5.3 %collective-permute-start.37 = (bf16[2,4,512,128]{3,2,1,0:T(8,128)(2,1)S(1)}, bf16[2,4,512,128]{3,2,1,0:T(8,128)(2,1)S(1)}, u32[]{:S(2)}, u32[]{:S(2)}) collective-permute-start(bf16[2,4,512,128]{3,2,1,0:T(8,128)(2,1)S(1)} %copy-done.25), channel_id=1, source_target_pairs={{0,8},{8,16},{16,24},{24,0},{1,9},{9,17},{17,25},{25,1},{2,10},{10... | collective-permute-start | bytes 3145736 | tf_op jit(solution)/shard_map/ppermute | solution.py:1485
  294.1 4.8 output_weight_grad.1
  303.3 44.2 %attend_back.1.refs_2_.refs_3_ = bf16[4,528,768]{2,1,0:T(8,128)(2,1)} custom-call(s32[1]{0:T(128)} %bitcast.2.refs_0_, s32[8]{0:T(128)} %compare_select_fusion.2.refs_0_.refs_1_, s32[64,128]{1,0:T(8,128)} %broadcast_in_dim.109.refs_1_.refs_2_, s32[8,64]{1,0:T(8,128)} %broadcast_in_dim.115.refs_2_.refs_3_, s32[8,64]{1,0:T(8,128)} %broadcast_in_dim.118.refs_3_.refs_4_, ...), custom_call_target="tpu_custom_call" | custom-call | flops 42949672960 | bytes 10813440 | tf_op jit(solution)/shard_map/attend_back/pallas_call | solution.py:517
  349.0 17.6 %triple_grads.1 = (bf16[256,768]{1,0:T(8,128)(2,1)}, bf16[256,768]{1,0:T(8,128)(2,1)}, bf16[256,768]{1,0:T(8,128)(2,1)}, bf16[256,768]{1,0:T(8,128)(2,1)}, bf16[...) custom-call(s32[5]{0:T(128)} %stack.24.refs_0_.place, ...), custom_call_target="tpu_custom_call" | custom-call | flops 6643777536 | bytes 10813440 | tf_op jit(solution)/shard_map/triple_grads/pallas_call | solution.py:1144
  370.8 5.5 %collective-permute-start.47 = (bf16[2,4,512,128]{3,2,1,0:T(8,128)(2,1)}, bf16[2,4,512,128]{3,2,1,0:T(8,128)(2,1)}, u32[]{:S(2)}, u32[]{:S(2)}) collective-permute-start(bf16[2,4,512,128]{3,2,1,0:T(8,128)(2,1)} %add_piece.3), channel_id=1, source_target_pairs={{0,8},{8,16},{16,24},{24,0},{1,9},{9,17},{17,25},{25,1},{2,10},{10... | collective-permute-start | bytes 3145736 | tf_op jit(solution)/shard_map/ppermute | solution.py:1485
  381.8 4.6 block_output.1.refs_5_
  386.4 3.0 collective-permute-done.40.refs_4_.refs_3_
  389.4 7.3 %collective-permute-done.41.refs_5_.refs_4_ = bf16[256,768]{1,0:T(8,128)(2,1)S(1)} collective-permute-done((bf16[256,768]{1,0:T(8,128)(2,1)}, bf16[256,768]{1,0:T(8,128)(2,1)S(1)}, u32[]{:S(2)}, u32[]{:S(2)}) %collective-permute-start.41) | collective-permute-done | bytes 393248 | tf_op jit(solution)/shard_map/ppermute | solution.py:1482
  398.2 3.9 normed_sum.1
  403.6 3.1 unpack.1
  413.2 17.5 %collective-permute-done.46 = f32[8,1664]{1,0:T(8,128)S(1)} collective-permute-done((f32[8,1664]{1,0:T(8,128)S(1)}, f32[8,1664]{1,0:T(8,128)S(1)}, u32[]{:S(2)}, u32[]{:S(2)}) %collective-permute-start.46) | collective-permute-done | bytes 53280 | tf_op jit(solution)/shard_map/ppermute | solution.py:1651
  445.7 5.8 %tokens_grad.1.refs_4_ = f32[516,1024]{1,0:T(8,128)} custom-call(bf16[528,1024]{1,0:T(8,128)(2,1)} %copy.97.refs_1_.entered.refs_5_.refs_0_, bf16[528,1024]{1,0:T(8,128)(2,1)} %get-tuple-element.154.refs_6_.refs_1_, bf16[528,1024]{1,0:T(8,128)(2,1)} %copy-done.12, f32[528,1024]{1,0:T(8,128)} %get-tuple-element.156.refs_3_, f32[528,1]{1,0:T(8,128)} %copy.64.refs_4_, ...), custom_call_target="tpu_custom_call" | custom-call | flops 1 | bytes 1 | tf_op jit(solution)/shard_map/tokens_grad/pallas_call | solution.py:768
  452.1 10.0 %collective-permute-done.51.refs_2_ = bf16[256,512]{1,0:T(8,128)(2,1)S(1)} collective-permute-done((bf16[256,512]{1,0:T(8,128)(2,1)S(1)}, bf16[256,512]{1,0:T(8,128)(2,1)S(1)}, u32[]{:S(2)}, u32[]{:S(2)}) %collective-permute-start.51) | collective-permute-done | bytes 262176 | tf_op jit(solution)/shard_map/ppermute | solution.py:1485
  474.4 4.3 collective-permute-start.54
  481.9 3.5 copy.67
  (355 shorter events, 154.6 us)
Async XLA Ops:
  7.2 156.8 %all-gather.3.cloned.1.call-start = ((), (), s32[]{:S(2)}) async-start(), calls=%async_computation | async-start | bytes 1114112 | tf_op jit(solution)/shard_map/all_gather | solution.py:1532
  40.5 21.6 %collective-permute-start.7 = (bf16[528,1024]{1,0:T(8,128)(2,1)}, bf16[528,1024]{1,0:T(8,128)(2,1)S(1)}, u32[]{:S(2)}, u32[]{:S(2)}) collective-permute-start(bf16[528,1024]{1,0:T(8,128)(2,1)} %copy.97.refs_1_.entered.refs_5_.refs_0_), channel_id=1, source_target_pairs={{0,1},{1,0},{2,3},{3,2},{4,5},{5,4},{6,7},{7,6},{8,9},{9,8},{10,11... | collective-permute-start | bytes 3244040 | tf_op jit(solution)/shard_map/ppermute | solution.py:1479
  40.5 21.6 %collective-permute-start.6 = (bf16[4,272,384]{2,1,0:T(8,128)(2,1)S(1)}, bf16[4,272,384]{2,1,0:T(8,128)(2,1)}, u32[]{:S(2)}, u32[]{:S(2)}) collective-permute-start(bf16[4,272,384]{2,1,0:T(8,128)(2,1)S(1)} %copy-done.1), channel_id=1, source_target_pairs={{0,4},{4,0},{1,5},{5,1},{2,6},{6,2},{3,7},{7,3},{8,12},{12,8},{9,1... | collective-permute-start | bytes 2506760 | tf_op jit(solution)/shard_map/ppermute | solution.py:1479
  42.0 28.2 %collective-permute-start.8 = (bf16[528,1024]{1,0:T(8,128)(2,1)}, bf16[528,1024]{1,0:T(8,128)(2,1)S(1)}, u32[]{:S(2)}, u32[]{:S(2)}) collective-permute-start(bf16[528,1024]{1,0:T(8,128)(2,1)} %copy.97.refs_1_.entered.refs_5_.refs_0_), channel_id=1, source_target_pairs={{0,2},{2,0},{1,3},{3,1},{4,6},{6,4},{5,7},{7,5},{8,10},{10,8},{9,1... | collective-permute-start | bytes 3244040 | tf_op jit(solution)/shard_map/ppermute | solution.py:1479
  43.8 37.1 %collective-permute-start.13 = (bf16[4,512,128]{2,1,0:T(8,128)(2,1)S(1)}, bf16[4,512,128]{2,1,0:T(8,128)(2,1)}, u32[]{:S(2)}, u32[]{:S(2)}) collective-permute-start(bf16[4,512,128]{2,1,0:T(8,128)(2,1)S(1)} %copy-done.6), channel_id=1, source_target_pairs={{0,8},{8,16},{16,24},{24,0},{1,9},{9,17},{17,25},{25,1},{2,10},{10... | collective-permute-start | bytes 1572872 | tf_op jit(solution)/shard_map/ppermute | solution.py:1485
  48.7 38.0 %collective-permute-start.14 = (bf16[4,512,128]{2,1,0:T(8,128)(2,1)S(1)}, bf16[4,512,128]{2,1,0:T(8,128)(2,1)}, u32[]{:S(2)}, u32[]{:S(2)}) collective-permute-start(bf16[4,512,128]{2,1,0:T(8,128)(2,1)S(1)} %copy-done.6), channel_id=1, source_target_pairs={{0,16},{8,24},{16,0},{24,8},{1,17},{9,25},{17,1},{25,9},{2,18},{10... | collective-permute-start | bytes 1572872 | tf_op jit(solution)/shard_map/ppermute | solution.py:1485
  73.5 22.7 %collective-permute-start.9 = (bf16[528,1024]{1,0:T(8,128)(2,1)}, bf16[528,1024]{1,0:T(8,128)(2,1)S(1)}, u32[]{:S(2)}, u32[]{:S(2)}) collective-permute-start(bf16[528,1024]{1,0:T(8,128)(2,1)} %copy.98), channel_id=1, source_target_pairs={{0,1},{1,0},{2,3},{3,2},{4,5},{5,4},{6,7},{7,6},{8,9},{9,8},{10,11... | collective-permute-start | bytes 3244040 | tf_op jit(solution)/shard_map/ppermute | solution.py:1479
  86.8 23.1 %collective-permute-start.15 = (bf16[4,512,128]{2,1,0:T(8,128)(2,1)S(1)}, bf16[4,512,128]{2,1,0:T(8,128)(2,1)}, u32[]{:S(2)}, u32[]{:S(2)}) collective-permute-start(bf16[4,512,128]{2,1,0:T(8,128)(2,1)S(1)} %copy-done.6), channel_id=1, source_target_pairs={{0,24},{8,0},{16,8},{24,16},{1,25},{9,1},{17,9},{25,17},{2,26},{10... | collective-permute-start | bytes 1572872 | tf_op jit(solution)/shard_map/ppermute | solution.py:1485
  88.7 56.5 %collective-permute-start.16 = (bf16[4,512,128]{2,1,0:T(8,128)(2,1)S(1)}, bf16[4,512,128]{2,1,0:T(8,128)(2,1)S(1)}, u32[]{:S(2)}, u32[]{:S(2)}) collective-permute-start(bf16[4,512,128]{2,1,0:T(8,128)(2,1)S(1)} %copy-done.6), channel_id=1, source_target_pairs={{0,4},{4,0},{1,5},{5,1},{2,6},{6,2},{3,7},{7,3},{8,12},{12,8},{9,1... | collective-permute-start | bytes 1572872 | tf_op jit(solution)/shard_map/ppermute | solution.py:1479
  90.3 54.9 %collective-permute-start.17 = (bf16[4,512,128]{2,1,0:T(8,128)(2,1)}, bf16[4,512,128]{2,1,0:T(8,128)(2,1)S(1)}, u32[]{:S(2)}, u32[]{:S(2)}) collective-permute-start(bf16[4,512,128]{2,1,0:T(8,128)(2,1)} %collective-permute-done.13.refs_14_.p1.refs_6_), channel_id=1, source_target_pairs={{0,4},{4,0},{1,5},{5,1},{2,6},{6,2},{3,7},{7,3},{8,12},{12,8},{9,1... | collective-permute-start | bytes 1572872 | tf_op jit(solution)/shard_map/ppermute | solution.py:1479
  94.7 50.6 %collective-permute-start.18 = (bf16[4,512,128]{2,1,0:T(8,128)(2,1)}, bf16[4,512,128]{2,1,0:T(8,128)(2,1)}, u32[]{:S(2)}, u32[]{:S(2)}) collective-permute-start(bf16[4,512,128]{2,1,0:T(8,128)(2,1)} %collective-permute-done.14.refs_8_.p2.refs_7_), channel_id=1, source_target_pairs={{0,4},{4,0},{1,5},{5,1},{2,6},{6,2},{3,7},{7,3},{8,12},{12,8},{9,1... | collective-permute-start | bytes 1572872 | tf_op jit(solution)/shard_map/ppermute | solution.py:1479
  109.1 36.2 %collective-permute-start.19 = (bf16[528,1024]{1,0:T(8,128)(2,1)}, bf16[528,1024]{1,0:T(8,128)(2,1)S(1)}, u32[]{:S(2)}, u32[]{:S(2)}) collective-permute-start(bf16[528,1024]{1,0:T(8,128)(2,1)} %get-tuple-element.114.cot.c0.refs_1_), channel_id=1, source_target_pairs={{0,1},{1,0},{2,3},{3,2},{4,5},{5,4},{6,7},{7,6},{8,9},{9,8},{10,11... | collective-permute-start | bytes 3244040 | tf_op jit(solution)/shard_map/ppermute | solution.py:1479
  109.9 35.4 %collective-permute-start.20 = (bf16[528,1024]{1,0:T(8,128)(2,1)}, bf16[528,1024]{1,0:T(8,128)(2,1)S(1)}, u32[]{:S(2)}, u32[]{:S(2)}) collective-permute-start(bf16[528,1024]{1,0:T(8,128)(2,1)} %get-tuple-element.114.cot.c0.refs_1_), channel_id=1, source_target_pairs={{0,2},{2,0},{1,3},{3,1},{4,6},{6,4},{5,7},{7,5},{8,10},{10,8},{9,1... | collective-permute-start | bytes 3244040 | tf_op jit(solution)/shard_map/ppermute | solution.py:1479
  178.8 26.4 %collective-permute-start.26 = (bf16[528,1024]{1,0:T(8,128)(2,1)}, bf16[528,1024]{1,0:T(8,128)(2,1)S(1)}, u32[]{:S(2)}, u32[]{:S(2)}) collective-permute-start(bf16[528,1024]{1,0:T(8,128)(2,1)} %get-tuple-element.121.normal.n0), channel_id=1, source_target_pairs={{0,2},{2,0},{1,3},{3,1},{4,6},{6,4},{5,7},{7,5},{8,10},{10,8},{9,1... | collective-permute-start | bytes 3244040 | tf_op jit(solution)/shard_map/ppermute | solution.py:1479
  232.0 39.3 %collective-permute-start.30 = (bf16[528,1024]{1,0:T(8,128)(2,1)S(1)}, bf16[528,1024]{1,0:T(8,128)(2,1)S(1)}, u32[]{:S(2)}, u32[]{:S(2)}) collective-permute-start(bf16[528,1024]{1,0:T(8,128)(2,1)S(1)} %copy-done.55), channel_id=1, source_target_pairs={{0,1},{1,0},{2,3},{3,2},{4,5},{5,4},{6,7},{7,6},{8,9},{9,8},{10,11... | collective-permute-start | bytes 3244040 | tf_op jit(solution)/shard_map/ppermute | solution.py:1479
  238.8 32.5 %collective-permute-start.32 = (bf16[528,1024]{1,0:T(8,128)(2,1)}, bf16[528,1024]{1,0:T(8,128)(2,1)S(1)}, u32[]{:S(2)}, u32[]{:S(2)}) collective-permute-start(bf16[528,1024]{1,0:T(8,128)(2,1)} %add.173), channel_id=1, source_target_pairs={{0,2},{2,0},{1,3},{3,1},{4,6},{6,4},{5,7},{7,5},{8,10},{10,8},{9,1... | collective-permute-start | bytes 3244040 | tf_op jit(solution)/shard_map/ppermute | solution.py:1479
  279.6 19.6 %collective-permute-start.29 = (bf16[528,1024]{1,0:T(8,128)(2,1)}, bf16[528,1024]{1,0:T(8,128)(2,1)}, u32[]{:S(2)}, u32[]{:S(2)}) collective-permute-start(bf16[528,1024]{1,0:T(8,128)(2,1)} %get-tuple-element.131), channel_id=1, source_target_pairs={{0,1},{1,0},{2,3},{3,2},{4,5},{5,4},{6,7},{7,6},{8,9},{9,8},{10,11... | collective-permute-start | bytes 3244040 | tf_op jit(solution)/shard_map/ppermute | solution.py:1479
  280.1 23.3 %collective-permute-start.28 = (bf16[528,1024]{1,0:T(8,128)(2,1)}, bf16[528,1024]{1,0:T(8,128)(2,1)}, u32[]{:S(2)}, u32[]{:S(2)}) collective-permute-start(bf16[528,1024]{1,0:T(8,128)(2,1)} %get-tuple-element.129), channel_id=1, source_target_pairs={{0,1},{1,0},{2,3},{3,2},{4,5},{5,4},{6,7},{7,6},{8,9},{9,8},{10,11... | collective-permute-start | bytes 3244040 | tf_op jit(solution)/shard_map/ppermute | solution.py:1479
  288.9 58.6 %collective-permute-start.37 = (bf16[2,4,512,128]{3,2,1,0:T(8,128)(2,1)S(1)}, bf16[2,4,512,128]{3,2,1,0:T(8,128)(2,1)S(1)}, u32[]{:S(2)}, u32[]{:S(2)}) collective-permute-start(bf16[2,4,512,128]{3,2,1,0:T(8,128)(2,1)S(1)} %copy-done.25), channel_id=1, source_target_pairs={{0,8},{8,16},{16,24},{24,0},{1,9},{9,17},{17,25},{25,1},{2,10},{10... | collective-permute-start | bytes 3145736 | tf_op jit(solution)/shard_map/ppermute | solution.py:1485
  298.9 48.6 %collective-permute-start.35 = (bf16[2,4,256,128]{3,2,1,0:T(8,128)(2,1)}, bf16[2,4,256,128]{3,2,1,0:T(8,128)(2,1)S(1)}, u32[]{:S(2)}, u32[]{:S(2)}) collective-permute-start(bf16[2,4,256,128]{3,2,1,0:T(8,128)(2,1)} %get-tuple-element.139), channel_id=1, source_target_pairs={{0,4},{4,0},{1,5},{5,1},{2,6},{6,2},{3,7},{7,3},{8,12},{12,8},{9,1... | collective-permute-start | bytes 1572872 | tf_op jit(solution)/shard_map/ppermute | solution.py:1479
  301.9 45.6 %collective-permute-start.34 = (bf16[528,1024]{1,0:T(8,128)(2,1)}, bf16[528,1024]{1,0:T(8,128)(2,1)S(1)}, u32[]{:S(2)}, u32[]{:S(2)}) collective-permute-start(bf16[528,1024]{1,0:T(8,128)(2,1)} %add.174), channel_id=1, source_target_pairs={{0,2},{2,0},{1,3},{3,1},{4,6},{6,4},{5,7},{7,5},{8,10},{10,8},{9,1... | collective-permute-start | bytes 3244040 | tf_op jit(solution)/shard_map/ppermute | solution.py:1479
  366.6 30.1 %collective-permute-start.38 = (bf16[2,528,1024]{2,1,0:T(8,128)(2,1)}, bf16[2,528,1024]{2,1,0:T(8,128)(2,1)S(1)}, u32[]{:S(2)}, u32[]{:S(2)}) collective-permute-start(bf16[2,528,1024]{2,1,0:T(8,128)(2,1)} %get-tuple-element.150), channel_id=1, source_target_pairs={{0,1},{1,0},{2,3},{3,2},{4,5},{5,4},{6,7},{7,6},{8,9},{9,8},{10,11... | collective-permute-start | bytes 6488072 | tf_op jit(solution)/shard_map/ppermute | solution.py:1479
  370.8 35.9 %collective-permute-start.47 = (bf16[2,4,512,128]{3,2,1,0:T(8,128)(2,1)}, bf16[2,4,512,128]{3,2,1,0:T(8,128)(2,1)}, u32[]{:S(2)}, u32[]{:S(2)}) collective-permute-start(bf16[2,4,512,128]{3,2,1,0:T(8,128)(2,1)} %add_piece.3), channel_id=1, source_target_pairs={{0,8},{8,16},{16,24},{24,0},{1,9},{9,17},{17,25},{25,1},{2,10},{10... | collective-permute-start | bytes 3145736 | tf_op jit(solution)/shard_map/ppermute | solution.py:1485
  377.5 19.2 %collective-permute-start.41 = (bf16[256,768]{1,0:T(8,128)(2,1)}, bf16[256,768]{1,0:T(8,128)(2,1)S(1)}, u32[]{:S(2)}, u32[]{:S(2)}) collective-permute-start(bf16[256,768]{1,0:T(8,128)(2,1)} %get-tuple-element.153), channel_id=1, source_target_pairs={{0,3},{1,2},{2,1},{3,0},{4,7},{5,6},{6,5},{7,4},{8,11},{9,10},{10,... | collective-permute-start | bytes 1179656 | tf_op jit(solution)/shard_map/ppermute | solution.py:1482
  381.4 21.5 %collective-permute-start.43 = (bf16[4,256,128]{2,1,0:T(8,128)(2,1)}, bf16[4,256,128]{2,1,0:T(8,128)(2,1)S(1)}, u32[]{:S(2)}, u32[]{:S(2)}) collective-permute-start(bf16[4,256,128]{2,1,0:T(8,128)(2,1)} %get-tuple-element.157), channel_id=1, source_target_pairs={{0,2},{2,0},{1,3},{3,1},{4,6},{6,4},{5,7},{7,5},{8,10},{10,8},{9,1... | collective-permute-start | bytes 786440 | tf_op jit(solution)/shard_map/ppermute | solution.py:1479
  409.5 27.6 %collective-permute-start.48 = (bf16[2,4,512,128]{3,2,1,0:T(8,128)(2,1)}, bf16[2,4,512,128]{3,2,1,0:T(8,128)(2,1)S(1)}, u32[]{:S(2)}, u32[]{:S(2)}) collective-permute-start(bf16[2,4,512,128]{3,2,1,0:T(8,128)(2,1)} %add_piece.4), channel_id=1, source_target_pairs={{0,8},{8,16},{16,24},{24,0},{1,9},{9,17},{17,25},{25,1},{2,10},{10... | collective-permute-start | bytes 3145736 | tf_op jit(solution)/shard_map/ppermute | solution.py:1485
  409.6 21.7 %collective-permute-start.44 = (bf16[4,256,384]{2,1,0:T(8,128)(2,1)S(1)}, bf16[4,256,384]{2,1,0:T(8,128)(2,1)S(1)}, u32[]{:S(2)}, u32[]{:S(2)}) collective-permute-start(bf16[4,256,384]{2,1,0:T(8,128)(2,1)S(1)} %copy-done.57), channel_id=1, source_target_pairs={{0,4},{4,0},{1,5},{5,1},{2,6},{6,2},{3,7},{7,3},{8,12},{12,8},{9,1... | collective-permute-start | bytes 2359304 | tf_op jit(solution)/shard_map/ppermute | solution.py:1479
  409.6 35.2 %collective-permute-start.42 = (bf16[528,1024]{1,0:T(8,128)(2,1)}, bf16[528,1024]{1,0:T(8,128)(2,1)S(1)}, u32[]{:S(2)}, u32[]{:S(2)}) collective-permute-start(bf16[528,1024]{1,0:T(8,128)(2,1)} %get-tuple-element.155), channel_id=1, source_target_pairs={{0,2},{2,0},{1,3},{3,1},{4,6},{6,4},{5,7},{7,5},{8,10},{10,8},{9,1... | collective-permute-start | bytes 3244040 | tf_op jit(solution)/shard_map/ppermute | solution.py:1479
  411.2 19.5 %collective-permute-start.46 = (f32[8,1664]{1,0:T(8,128)S(1)}, f32[8,1664]{1,0:T(8,128)S(1)}, u32[]{:S(2)}, u32[]{:S(2)}) collective-permute-start(f32[8,1664]{1,0:T(8,128)S(1)} %add.156), channel_id=1, source_target_pairs={{0,4},{1,5},{2,6},{3,7},{4,0},{5,1},{6,2},{7,3},{8,12},{9,13},{10,... | collective-permute-start | bytes 159752 | tf_op jit(solution)/shard_map/ppermute | solution.py:1651
  440.8 25.0 %collective-permute-start.49 = (bf16[4,512,128]{2,1,0:T(8,128)(2,1)}, bf16[4,512,128]{2,1,0:T(8,128)(2,1)S(1)}, u32[]{:S(2)}, u32[]{:S(2)}) collective-permute-start(bf16[4,512,128]{2,1,0:T(8,128)(2,1)} %get-tuple-element.169), channel_id=1, source_target_pairs={{0,4},{4,0},{1,5},{5,1},{2,6},{6,2},{3,7},{7,3},{8,12},{12,8},{9,1... | collective-permute-start | bytes 1572872 | tf_op jit(solution)/shard_map/ppermute | solution.py:1479
  440.8 21.4 %collective-permute-start.51 = (bf16[256,512]{1,0:T(8,128)(2,1)S(1)}, bf16[256,512]{1,0:T(8,128)(2,1)S(1)}, u32[]{:S(2)}, u32[]{:S(2)}) collective-permute-start(bf16[256,512]{1,0:T(8,128)(2,1)S(1)} %copy-done.62), channel_id=1, source_target_pairs={{0,16},{8,24},{16,0},{24,8},{1,17},{9,25},{17,1},{25,9},{2,18},{10... | collective-permute-start | bytes 786440 | tf_op jit(solution)/shard_map/ppermute | solution.py:1485
  442.8 19.4 %collective-permute-start.52 = (bf16[256,512]{1,0:T(8,128)(2,1)S(1)}, bf16[256,512]{1,0:T(8,128)(2,1)S(1)}, u32[]{:S(2)}, u32[]{:S(2)}) collective-permute-start(bf16[256,512]{1,0:T(8,128)(2,1)S(1)} %copy-done.61), channel_id=1, source_target_pairs={{0,24},{8,0},{16,8},{24,16},{1,25},{9,1},{17,9},{25,17},{2,26},{10... | collective-permute-start | bytes 786440 | tf_op jit(solution)/shard_map/ppermute | solution.py:1485
  (93 other events, 575.8 us)
Sparse Core Ops, SparseCore 0:
  43.6 81.1 all-gather.2

commit v6 on v5

--- a/solution.py
+++ b/solution.py
@@ -854,9 +854,11 @@
 
 
 def front_kernel(*refs):
-    *parts, near = refs
-    for s, ref in enumerate(parts):
-        near[s] = ref[...]
+    *sources, entered, near, feed, entered_out = refs
+    for s in range(4):
+        near[s] = sources[s][...]
+        feed[s] = sources[4 + s][...]
+    entered_out[...] = entered[...]
 
 
 def pack_kernel(n_z, place, near, far, own, one, two, three, vectors, bias, expand_bias):
@@ -1518,15 +1520,14 @@
         carry=[packed],
     )
     packed_parts = gather_z(packed)
-    feed = stack_call([own, swap(one), swap(two, "x"), cross_over(three)], [packed_parts[1]])
-    near = local_call(
+    feed = [own, swap(one), swap(two, "x"), cross_over(three)]
+    near, feed, entered = local_call(
         front_kernel,
         "front",
-        packed_parts,
-        [shape_of(n_z, *packed.shape)],
-    )[0]
+        [*packed_parts, *feed, entered],
+        [shape_of(n_z, *packed.shape), shape_of(4, *own.shape), shape_of(*entered.shape)],
+    )
     far = swap(near, "y")
-    entered = copy_call(entered, [near, feed])
     entered_x = swap(entered, "x")
     entered_all = [entered, swap(entered), entered_x]
     output_all = lax.all_gather(output_weight, ("z", "y", "x"), axis=0).reshape(n_z, n_y, n_x, width, d_part)

time: 503 us -> 500 us (level)
    ppermute x38, starting transfers between devices: 22.5 us -> 32.9 us  [swap(): return lax.ppermute(array, axis, [(0, 1), (1, 0)])]
    ppermute x12, starting transfers between devices: 30.1 us -> 21.7 us  [to_z(): return lax.ppermute(array, 'z', [(i, (i + s) % n_z) for i in range(n_z)])]
    ppermute x12, waiting for transfers between devices: 20.1 us -> 12.1 us  [to_z(): return lax.ppermute(array, 'z', [(i, (i + s) % n_z) for i in range(n_z)])]
    pallas_call x22 -> x20, Pallas kernels: 66.7 us -> 63.6 us  [local_call(): pl.pallas_call(waiting(kernel, len(inputs), waits, len(carry), len(output...]
  transfers between devices with their start and end apart: 60 -> 60, of which waited for: 22 -> 20; matrix products, arithmetic and copies ran while one was open for 5% -> 5% of each run, Pallas kernels for 39% -> 39%
where the time goes in v6:
time: 500 us; the launch traced here: 494 us
  Pallas kernels  259 us (52%)
  waiting for transfers between devices  96.5 us (19%)
  starting transfers between devices  62.2 us (12%)
  local copies, waits for them, and re-layouts  45.7 us (9%)
  between operations  17.8 us (4%)
  other arithmetic  13.1 us (3%)
    pallas_call x20, Pallas kernels, local_call(): pl.pallas_call(waiting(kernel, len(inputs), waits, len(carry), len(output...  63.6 us
    ppermute x38, waiting for transfers between devices, swap(): return lax.ppermute(array, axis, [(0, 1), (1, 0)])  45 us
    pallas_call x1, Pallas kernels, attend_back_call(): pl.pallas_call(waiting(functools.partial(attend_back_kernel, frames_local...  44.1 us
    pallas_call x2, Pallas kernels, feed_split_call(): pl.pallas_call(waiting(feed_kernel, 2 + len(inputs), waits), grid_spec=pl...  39.2 us
    ppermute x38, starting transfers between devices, swap(): return lax.ppermute(array, axis, [(0, 1), (1, 0)])  32.9 us
    pallas_call x1, Pallas kernels, attend_call(): pl.pallas_call(waiting(functools.partial(attend_kernel, frames_local), 8,...  31.3 us
    pallas_call x1, Pallas kernels, feed_grad_call(): pl.pallas_call(waiting(feed_grad_kernel, 1 + len(first) + len(tiles) + 2...  30.8 us
    unnamed x144, local copies, waits for them, and re-layouts  30.1 us
  transfers between devices with their start and end apart: 60, of which 20 were waited for; matrix products, arithmetic and copies ran while one was open for 5% of the time, Pallas kernels for 39%

profile of v6, /device:TPU:0, one launch (start us, length us, event | category | flops | bytes accessed | tf_op | source)
XLA Modules:
  0.0 493.9 jit_solution(5339176531710995939)
XLA Ops:
  30.5 3.4 collective-permute-done.5.refs_7_
  34.7 3.3 front.1
  40.7 4.1 collective-permute-start.13
  46.4 13.3 %collective-permute-done.6.refs_2_ = bf16[4,272,384]{2,1,0:T(8,128)(2,1)S(1)} collective-permute-done((bf16[4,272,384]{2,1,0:T(8,128)(2,1)}, bf16[4,272,384]{2,1,0:T(8,128)(2,1)S(1)}, u32[]{:S(2)}, u32[]{:S(2)}) %collective-permute-start.6) | collective-permute-done | bytes 835616 | tf_op jit(solution)/shard_map/ppermute | solution.py:1481
  61.6 3.7 pack.1
  73.4 5.1 %fusion = (f32[4,528,128]{2,1,0:T(8,128)}, f32[4,528,128]{2,1,0:T(8,128)}) fusion(f32[528,128]{1,0:T(8,128)S(1)} %copy-done.34, f32[128]{0:T(128)S(1)} %copy-done.52, f32[4,528]{1,0:T(4,128)S(1)} %maximum_maximum_fusion), kind=kLoop, calls=%fused_computation.3 | loop fusion | flops 540672 | bytes 2441984 | tf_op jit(solution)/shard_map/sin | solution.py:719
  88.1 5.2 %collective-permute-done.12.refs_8_ = bf16[256,768]{1,0:T(8,128)(2,1)} collective-permute-done((bf16[256,768]{1,0:T(8,128)(2,1)S(1)}, bf16[256,768]{1,0:T(8,128)(2,1)}, u32[]{:S(2)}, u32[]{:S(2)}) %collective-permute-start.12) | collective-permute-done | bytes 393248 | tf_op jit(solution)/shard_map/ppermute | solution.py:1484
  95.8 11.9 %enter.1 = (bf16[4,528,256]{2,1,0:T(8,128)(2,1)}, bf16[4,528,256]{2,1,0:T(8,128)(2,1)}, bf16[4,528,256]{2,1,0:T(8,128)(2,1)}, bf16[4,528,1024]{2,1,0:T(8,128)(2,...) custom-call(s32[5]{0:T(128)} %stack.23.refs_0_.place, ...), custom_call_target="tpu_custom_call", output_to_operand_aliasing={{5}: (15, {})} | custom-call | flops 3321888768 | bytes 16220160 | tf_op jit(solution)/shard_map/enter/pallas_call | solution.py:970
  111.6 31.3 %attend.1 = (bf16[4,528,256]{2,1,0:T(8,128)(2,1)}, f32[4,528,256]{2,1,0:T(8,128)}, f32[8,8,1024]{2,1,0:T(8,128)}, f32[8,256]{1,0:T(8,128)}) custom-call(s32[8]{0:T(128)} %compare_select_fusion.2.refs_0_.refs_1_, s32[64,128]{1,0:T(8,128)} %broadcast_in_dim.109.refs_1_.refs_2_, s32[8,64]{1,0:T(8,128)} %broadcast_in_dim.115.refs_2_.refs_3_, ...), custom_call_target="tpu_custom_call" | custom-call | flops 17179869184 | bytes 5406720 | tf_op jit(solution)/shard_map/attend/pallas_call | solution.py:281
  148.5 14.3 %collective-permute-done.23.refs_5_.f3.refs_12_ = bf16[4,512,128]{2,1,0:T(8,128)(2,1)S(1)} collective-permute-done((bf16[4,512,128]{2,1,0:T(8,128)(2,1)}, bf16[4,512,128]{2,1,0:T(8,128)(2,1)S(1)}, u32[]{:S(2)}, u32[]{:S(2)}) %collective-permute-start.23) | collective-permute-done | bytes 524320 | tf_op jit(solution)/shard_map/ppermute | solution.py:1481
  164.1 4.6 project.1
  172.6 4.9 middle.1
  181.4 19.8 %feed_forward.2 = (bf16[1056,1024]{1,0:T(8,128)(2,1)}, bf16[1056,1024]{1,0:T(8,128)(2,1)}, f32[528,1024]{1,0:T(8,128)}, bf16[528,1024]{1,0:T(8,128)(2,1)}, f32[4,1,256]{2,1,0:T(1,128)}) custom-call(s32[5]{0:T(128)} %stack.23.refs_0_.place, bf16[528,1024]{1,0:T(8,128)(2,1)} %get-tuple-element.127.normal.n0, bf16[528,1024]{1,0:T(8,128)(2,1)} %copy-done.54, ...), custom_call_target="tpu_custom_call" | custom-call | flops 6643777536 | bytes 10813440 | tf_op jit(solution)/shard_map/feed_forward/pallas_call | solution.py:1390
  211.2 19.4 %feed_forward.3 = (bf16[1056,1024]{1,0:T(8,128)(2,1)}, bf16[1056,1024]{1,0:T(8,128)(2,1)}, f32[528,1024]{1,0:T(8,128)}, bf16[528,1024]{1,0:T(8,128)(2,1)}, f32[4,1,256]{2,1,0:T(1,128)}) custom-call(s32[5]{0:T(128)} %stack.23.refs_0_.place, bf16[528,1024]{1,0:T(8,128)(2,1)} %copy-done.17, bf16[528,1024]{1,0:T(8,128)(2,1)} %copy-done.56, ...), custom_call_target="tpu_custom_call" | custom-call | flops 6643777536 | bytes 10813440 | tf_op jit(solution)/shard_map/feed_forward/pallas_call | solution.py:1390
  234.6 3.1 add.173
  238.3 30.8 %feed_grads.1 = (f32[528,1024]{1,0:T(8,128)}, bf16[528,1024]{1,0:T(8,128)(2,1)}, bf16[528,1024]{1,0:T(8,128)(2,1)}, bf16[528,1024]{1,0:T(8,128)(2,1)}, bf16[4,2,...) custom-call(s32[5]{0:T(128)} %stack.23.refs_0_.place, bf16[528,1024]{1,0:T(8,128)(2,1)} %get-tuple-element.127.normal.n0, ...), custom_call_target="tpu_custom_call" | custom-call | flops 13287555072 | bytes 21626880 | tf_op jit(solution)/shard_map/feed_grads/pallas_call | solution.py:1417
  270.4 6.8 %middle_back.1 = (f32[528,1024]{1,0:T(8,128)}, bf16[528,1024]{1,0:T(8,128)(2,1)}, f32[8,1024]{1,0:T(8,128)}) custom-call(f32[528,1024]{1,0:T(8,128)} %get-tuple-element.126.refs_0_, bf16[528,1024]{1,0:T(8,128)(2,1)} %get-tuple-element.120.cot.c0.refs_1_, f32[528,1024]{1,0:T(8,128)} %get-tuple-element.138.refs_2_, bf16[528,1024]{1,0:T(8,128)(2,1)} %copy-done.11, ...), custom_call_target="tpu_custom_call" | custom-call | flops 1 | bytes 1 | tf_op jit(solution)/shard_map/middle_back/pallas_call | solution.py:1036
  282.0 4.2 mixed_grad.1
  290.1 4.8 output_weight_grad.1
  301.0 44.1 %attend_back.1.refs_2_.refs_3_ = bf16[4,528,768]{2,1,0:T(8,128)(2,1)} custom-call(s32[1]{0:T(128)} %bitcast.refs_0_, s32[8]{0:T(128)} %compare_select_fusion.2.refs_0_.refs_1_, s32[64,128]{1,0:T(8,128)} %broadcast_in_dim.109.refs_1_.refs_2_, s32[8,64]{1,0:T(8,128)} %broadcast_in_dim.115.refs_2_.refs_3_, s32[8,64]{1,0:T(8,128)} %broadcast_in_dim.118.refs_3_.refs_4_, ...), custom_call_target="tpu_custom_call" | custom-call | flops 42949672960 | bytes 10813440 | tf_op jit(solution)/shard_map/attend_back/pallas_call | solution.py:517
  346.6 17.7 %triple_grads.1 = (bf16[256,768]{1,0:T(8,128)(2,1)}, bf16[256,768]{1,0:T(8,128)(2,1)}, bf16[256,768]{1,0:T(8,128)(2,1)}, bf16[256,768]{1,0:T(8,128)(2,1)}, bf16[...) custom-call(s32[5]{0:T(128)} %stack.23.refs_0_.place, ...), custom_call_target="tpu_custom_call" | custom-call | flops 6643777536 | bytes 10813440 | tf_op jit(solution)/shard_map/triple_grads/pallas_call | solution.py:1146
  374.6 4.6 block_output.1.refs_5_
  381.8 7.0 %collective-permute-done.41.refs_5_.refs_4_ = bf16[256,768]{1,0:T(8,128)(2,1)S(1)} collective-permute-done((bf16[256,768]{1,0:T(8,128)(2,1)}, bf16[256,768]{1,0:T(8,128)(2,1)S(1)}, u32[]{:S(2)}, u32[]{:S(2)}) %collective-permute-start.41) | collective-permute-done | bytes 393248 | tf_op jit(solution)/shard_map/ppermute | solution.py:1484
  390.3 3.9 normed_sum.1
  395.7 3.1 unpack.1
  401.7 5.6 %collective-permute-start.44 = (bf16[4,256,384]{2,1,0:T(8,128)(2,1)S(1)}, bf16[4,256,384]{2,1,0:T(8,128)(2,1)S(1)}, u32[]{:S(2)}, u32[]{:S(2)}) collective-permute-start(bf16[4,256,384]{2,1,0:T(8,128)(2,1)S(1)} %copy-done.57), channel_id=1, source_target_pairs={{0,4},{4,0},{1,5},{5,1},{2,6},{6,2},{3,7},{7,3},{8,12},{12,8},{9,1... | collective-permute-start | bytes 2359304 | tf_op jit(solution)/shard_map/ppermute | solution.py:1481
  409.0 17.7 %collective-permute-done.46 = f32[8,1664]{1,0:T(8,128)S(1)} collective-permute-done((f32[8,1664]{1,0:T(8,128)S(1)}, f32[8,1664]{1,0:T(8,128)S(1)}, u32[]{:S(2)}, u32[]{:S(2)}) %collective-permute-start.46) | collective-permute-done | bytes 53280 | tf_op jit(solution)/shard_map/ppermute | solution.py:1652
  434.4 3.8 collective-permute-start.49
  443.0 5.8 %tokens_grad.1.refs_4_ = f32[516,1024]{1,0:T(8,128)} custom-call(bf16[528,1024]{1,0:T(8,128)(2,1)} %get-tuple-element.106.refs_1_.entered.refs_5_.refs_0_, bf16[528,1024]{1,0:T(8,128)(2,1)} %get-tuple-element.160.refs_6_.refs_1_, bf16[528,1024]{1,0:T(8,128)(2,1)} %copy-done.10, f32[528,1024]{1,0:T(8,128)} %get-tuple-element.162.refs_3_, ...), custom_call_target="tpu_custom_call" | custom-call | flops 1 | bytes 1 | tf_op jit(solution)/shard_map/tokens_grad/pallas_call | solution.py:768
  449.5 9.3 %collective-permute-done.51.refs_2_ = bf16[256,512]{1,0:T(8,128)(2,1)S(1)} collective-permute-done((bf16[256,512]{1,0:T(8,128)(2,1)S(1)}, bf16[256,512]{1,0:T(8,128)(2,1)S(1)}, u32[]{:S(2)}, u32[]{:S(2)}) %collective-permute-start.51) | collective-permute-done | bytes 262176 | tf_op jit(solution)/shard_map/ppermute | solution.py:1487
  471.0 4.2 collective-permute-start.54
  478.4 3.5 copy.66
  (353 shorter events, 152.0 us)
Async XLA Ops:
  7.2 155.6 %all-gather.3.cloned.1.call-start = ((), (), s32[]{:S(2)}) async-start(), calls=%async_computation | async-start | bytes 1114112 | tf_op jit(solution)/shard_map/all_gather | solution.py:1533
  13.6 20.4 %collective-permute-start = (bf16[272,384]{1,0:T(8,128)(2,1)}, bf16[272,384]{1,0:T(8,128)(2,1)S(1)}, u32[]{:S(2)}, u32[]{:S(2)}) collective-permute-start(bf16[272,384]{1,0:T(8,128)(2,1)} %get-tuple-element.101.refs_0_), channel_id=1, source_target_pairs={{0,8},{8,16},{16,24},{24,0},{1,9},{9,17},{17,25},{25,1},{2,10},{10... | collective-permute-start | bytes 626696 | tf_op jit(solution)/shard_map/ppermute | solution.py:1487
  38.0 21.7 %collective-permute-start.7 = (bf16[528,1024]{1,0:T(8,128)(2,1)}, bf16[528,1024]{1,0:T(8,128)(2,1)S(1)}, u32[]{:S(2)}, u32[]{:S(2)}) collective-permute-start(bf16[528,1024]{1,0:T(8,128)(2,1)} %get-tuple-element.106.refs_1_.entered.refs_5_.refs_0_), channel_id=1, source_target_pairs={{0,1},{1,0},{2,3},{3,2},{4,5},{5,4},{6,7},{7,6},{8,9},{9,8},{10,11... | collective-permute-start | bytes 3244040 | tf_op jit(solution)/shard_map/ppermute | solution.py:1481
  38.1 21.5 %collective-permute-start.6 = (bf16[4,272,384]{2,1,0:T(8,128)(2,1)}, bf16[4,272,384]{2,1,0:T(8,128)(2,1)S(1)}, u32[]{:S(2)}, u32[]{:S(2)}) collective-permute-start(bf16[4,272,384]{2,1,0:T(8,128)(2,1)} %get-tuple-element.107.refs_1_), channel_id=1, source_target_pairs={{0,4},{4,0},{1,5},{5,1},{2,6},{6,2},{3,7},{7,3},{8,12},{12,8},{9,1... | collective-permute-start | bytes 2506760 | tf_op jit(solution)/shard_map/ppermute | solution.py:1481
  39.7 29.0 %collective-permute-start.8 = (bf16[528,1024]{1,0:T(8,128)(2,1)}, bf16[528,1024]{1,0:T(8,128)(2,1)S(1)}, u32[]{:S(2)}, u32[]{:S(2)}) collective-permute-start(bf16[528,1024]{1,0:T(8,128)(2,1)} %get-tuple-element.106.refs_1_.entered.refs_5_.refs_0_), channel_id=1, source_target_pairs={{0,2},{2,0},{1,3},{3,1},{4,6},{6,4},{5,7},{7,5},{8,10},{10,8},{9,1... | collective-permute-start | bytes 3244040 | tf_op jit(solution)/shard_map/ppermute | solution.py:1481
  40.7 37.8 %collective-permute-start.13 = (bf16[4,512,128]{2,1,0:T(8,128)(2,1)}, bf16[4,512,128]{2,1,0:T(8,128)(2,1)}, u32[]{:S(2)}, u32[]{:S(2)}) collective-permute-start(bf16[4,512,128]{2,1,0:T(8,128)(2,1)} %get-tuple-element.115.p0.refs_5_), channel_id=1, source_target_pairs={{0,8},{8,16},{16,24},{24,0},{1,9},{9,17},{17,25},{25,1},{2,10},{10... | collective-permute-start | bytes 1572872 | tf_op jit(solution)/shard_map/ppermute | solution.py:1487
  44.8 38.2 %collective-permute-start.14 = (bf16[4,512,128]{2,1,0:T(8,128)(2,1)}, bf16[4,512,128]{2,1,0:T(8,128)(2,1)}, u32[]{:S(2)}, u32[]{:S(2)}) collective-permute-start(bf16[4,512,128]{2,1,0:T(8,128)(2,1)} %get-tuple-element.115.p0.refs_5_), channel_id=1, source_target_pairs={{0,16},{8,24},{16,0},{24,8},{1,17},{9,25},{17,1},{25,9},{2,18},{10... | collective-permute-start | bytes 1572872 | tf_op jit(solution)/shard_map/ppermute | solution.py:1487
  72.1 22.8 %collective-permute-start.9 = (bf16[528,1024]{1,0:T(8,128)(2,1)}, bf16[528,1024]{1,0:T(8,128)(2,1)S(1)}, u32[]{:S(2)}, u32[]{:S(2)}) collective-permute-start(bf16[528,1024]{1,0:T(8,128)(2,1)} %copy.96), channel_id=1, source_target_pairs={{0,1},{1,0},{2,3},{3,2},{4,5},{5,4},{6,7},{7,6},{8,9},{9,8},{10,11... | collective-permute-start | bytes 3244040 | tf_op jit(solution)/shard_map/ppermute | solution.py:1481
  83.0 25.4 %collective-permute-start.15 = (bf16[4,512,128]{2,1,0:T(8,128)(2,1)}, bf16[4,512,128]{2,1,0:T(8,128)(2,1)}, u32[]{:S(2)}, u32[]{:S(2)}) collective-permute-start(bf16[4,512,128]{2,1,0:T(8,128)(2,1)} %get-tuple-element.115.p0.refs_5_), channel_id=1, source_target_pairs={{0,24},{8,0},{16,8},{24,16},{1,25},{9,1},{17,9},{25,17},{2,26},{10... | collective-permute-start | bytes 1572872 | tf_op jit(solution)/shard_map/ppermute | solution.py:1487
  85.8 57.1 %collective-permute-start.16 = (bf16[4,512,128]{2,1,0:T(8,128)(2,1)}, bf16[4,512,128]{2,1,0:T(8,128)(2,1)S(1)}, u32[]{:S(2)}, u32[]{:S(2)}) collective-permute-start(bf16[4,512,128]{2,1,0:T(8,128)(2,1)} %get-tuple-element.115.p0.refs_5_), channel_id=1, source_target_pairs={{0,4},{4,0},{1,5},{5,1},{2,6},{6,2},{3,7},{7,3},{8,12},{12,8},{9,1... | collective-permute-start | bytes 1572872 | tf_op jit(solution)/shard_map/ppermute | solution.py:1481
  87.3 55.6 %collective-permute-start.17 = (bf16[4,512,128]{2,1,0:T(8,128)(2,1)}, bf16[4,512,128]{2,1,0:T(8,128)(2,1)S(1)}, u32[]{:S(2)}, u32[]{:S(2)}) collective-permute-start(bf16[4,512,128]{2,1,0:T(8,128)(2,1)} %collective-permute-done.13.refs_14_.p1.refs_6_), channel_id=1, source_target_pairs={{0,4},{4,0},{1,5},{5,1},{2,6},{6,2},{3,7},{7,3},{8,12},{12,8},{9,1... | collective-permute-start | bytes 1572872 | tf_op jit(solution)/shard_map/ppermute | solution.py:1481
  93.3 49.6 %collective-permute-start.18 = (bf16[4,512,128]{2,1,0:T(8,128)(2,1)}, bf16[4,512,128]{2,1,0:T(8,128)(2,1)S(1)}, u32[]{:S(2)}, u32[]{:S(2)}) collective-permute-start(bf16[4,512,128]{2,1,0:T(8,128)(2,1)} %collective-permute-done.14.refs_8_.p2.refs_7_), channel_id=1, source_target_pairs={{0,4},{4,0},{1,5},{5,1},{2,6},{6,2},{3,7},{7,3},{8,12},{12,8},{9,1... | collective-permute-start | bytes 1572872 | tf_op jit(solution)/shard_map/ppermute | solution.py:1481
  107.7 35.2 %collective-permute-start.19 = (bf16[528,1024]{1,0:T(8,128)(2,1)}, bf16[528,1024]{1,0:T(8,128)(2,1)S(1)}, u32[]{:S(2)}, u32[]{:S(2)}) collective-permute-start(bf16[528,1024]{1,0:T(8,128)(2,1)} %get-tuple-element.120.cot.c0.refs_1_), channel_id=1, source_target_pairs={{0,1},{1,0},{2,3},{3,2},{4,5},{5,4},{6,7},{7,6},{8,9},{9,8},{10,11... | collective-permute-start | bytes 3244040 | tf_op jit(solution)/shard_map/ppermute | solution.py:1481
  108.5 34.5 %collective-permute-start.20 = (bf16[528,1024]{1,0:T(8,128)(2,1)}, bf16[528,1024]{1,0:T(8,128)(2,1)S(1)}, u32[]{:S(2)}, u32[]{:S(2)}) collective-permute-start(bf16[528,1024]{1,0:T(8,128)(2,1)} %get-tuple-element.120.cot.c0.refs_1_), channel_id=1, source_target_pairs={{0,2},{2,0},{1,3},{3,1},{4,6},{6,4},{5,7},{7,5},{8,10},{10,8},{9,1... | collective-permute-start | bytes 3244040 | tf_op jit(solution)/shard_map/ppermute | solution.py:1481
  177.6 26.4 %collective-permute-start.26 = (bf16[528,1024]{1,0:T(8,128)(2,1)}, bf16[528,1024]{1,0:T(8,128)(2,1)S(1)}, u32[]{:S(2)}, u32[]{:S(2)}) collective-permute-start(bf16[528,1024]{1,0:T(8,128)(2,1)} %get-tuple-element.127.normal.n0), channel_id=1, source_target_pairs={{0,2},{2,0},{1,3},{3,1},{4,6},{6,4},{5,7},{7,5},{8,10},{10,8},{9,1... | collective-permute-start | bytes 3244040 | tf_op jit(solution)/shard_map/ppermute | solution.py:1481
  230.8 38.3 %collective-permute-start.30 = (bf16[528,1024]{1,0:T(8,128)(2,1)S(1)}, bf16[528,1024]{1,0:T(8,128)(2,1)S(1)}, u32[]{:S(2)}, u32[]{:S(2)}) collective-permute-start(bf16[528,1024]{1,0:T(8,128)(2,1)S(1)} %copy-done.55), channel_id=1, source_target_pairs={{0,1},{1,0},{2,3},{3,2},{4,5},{5,4},{6,7},{7,6},{8,9},{9,8},{10,11... | collective-permute-start | bytes 3244040 | tf_op jit(solution)/shard_map/ppermute | solution.py:1481
  237.7 31.4 %collective-permute-start.32 = (bf16[528,1024]{1,0:T(8,128)(2,1)}, bf16[528,1024]{1,0:T(8,128)(2,1)S(1)}, u32[]{:S(2)}, u32[]{:S(2)}) collective-permute-start(bf16[528,1024]{1,0:T(8,128)(2,1)} %add.173), channel_id=1, source_target_pairs={{0,2},{2,0},{1,3},{3,1},{4,6},{6,4},{5,7},{7,5},{8,10},{10,8},{9,1... | collective-permute-start | bytes 3244040 | tf_op jit(solution)/shard_map/ppermute | solution.py:1481
  277.3 19.4 %collective-permute-start.29 = (bf16[528,1024]{1,0:T(8,128)(2,1)}, bf16[528,1024]{1,0:T(8,128)(2,1)}, u32[]{:S(2)}, u32[]{:S(2)}) collective-permute-start(bf16[528,1024]{1,0:T(8,128)(2,1)} %get-tuple-element.137), channel_id=1, source_target_pairs={{0,1},{1,0},{2,3},{3,2},{4,5},{5,4},{6,7},{7,6},{8,9},{9,8},{10,11... | collective-permute-start | bytes 3244040 | tf_op jit(solution)/shard_map/ppermute | solution.py:1481
  277.8 23.2 %collective-permute-start.28 = (bf16[528,1024]{1,0:T(8,128)(2,1)}, bf16[528,1024]{1,0:T(8,128)(2,1)}, u32[]{:S(2)}, u32[]{:S(2)}) collective-permute-start(bf16[528,1024]{1,0:T(8,128)(2,1)} %get-tuple-element.135), channel_id=1, source_target_pairs={{0,1},{1,0},{2,3},{3,2},{4,5},{5,4},{6,7},{7,6},{8,9},{9,8},{10,11... | collective-permute-start | bytes 3244040 | tf_op jit(solution)/shard_map/ppermute | solution.py:1481
  287.7 57.4 %collective-permute-start.37 = (bf16[2,4,512,128]{3,2,1,0:T(8,128)(2,1)S(1)}, bf16[2,4,512,128]{3,2,1,0:T(8,128)(2,1)S(1)}, u32[]{:S(2)}, u32[]{:S(2)}) collective-permute-start(bf16[2,4,512,128]{3,2,1,0:T(8,128)(2,1)S(1)} %copy-done.23), channel_id=1, source_target_pairs={{0,8},{8,16},{16,24},{24,0},{1,9},{9,17},{17,25},{25,1},{2,10},{10... | collective-permute-start | bytes 3145736 | tf_op jit(solution)/shard_map/ppermute | solution.py:1487
  294.9 50.2 %collective-permute-start.35 = (bf16[2,4,256,128]{3,2,1,0:T(8,128)(2,1)}, bf16[2,4,256,128]{3,2,1,0:T(8,128)(2,1)S(1)}, u32[]{:S(2)}, u32[]{:S(2)}) collective-permute-start(bf16[2,4,256,128]{3,2,1,0:T(8,128)(2,1)} %get-tuple-element.145), channel_id=1, source_target_pairs={{0,4},{4,0},{1,5},{5,1},{2,6},{6,2},{3,7},{7,3},{8,12},{12,8},{9,1... | collective-permute-start | bytes 1572872 | tf_op jit(solution)/shard_map/ppermute | solution.py:1481
  299.5 45.6 %collective-permute-start.34 = (bf16[528,1024]{1,0:T(8,128)(2,1)}, bf16[528,1024]{1,0:T(8,128)(2,1)S(1)}, u32[]{:S(2)}, u32[]{:S(2)}) collective-permute-start(bf16[528,1024]{1,0:T(8,128)(2,1)} %add.174), channel_id=1, source_target_pairs={{0,2},{2,0},{1,3},{3,1},{4,6},{6,4},{5,7},{7,5},{8,10},{10,8},{9,1... | collective-permute-start | bytes 3244040 | tf_op jit(solution)/shard_map/ppermute | solution.py:1481
  364.3 24.6 %collective-permute-start.38 = (bf16[2,528,1024]{2,1,0:T(8,128)(2,1)}, bf16[2,528,1024]{2,1,0:T(8,128)(2,1)S(1)}, u32[]{:S(2)}, u32[]{:S(2)}) collective-permute-start(bf16[2,528,1024]{2,1,0:T(8,128)(2,1)} %get-tuple-element.156), channel_id=1, source_target_pairs={{0,1},{1,0},{2,3},{3,2},{4,5},{5,4},{6,7},{7,6},{8,9},{9,8},{10,11... | collective-permute-start | bytes 6488072 | tf_op jit(solution)/shard_map/ppermute | solution.py:1481
  368.4 30.4 %collective-permute-start.47 = (bf16[2,4,512,128]{3,2,1,0:T(8,128)(2,1)}, bf16[2,4,512,128]{3,2,1,0:T(8,128)(2,1)}, u32[]{:S(2)}, u32[]{:S(2)}) collective-permute-start(bf16[2,4,512,128]{3,2,1,0:T(8,128)(2,1)} %add_piece.3), channel_id=1, source_target_pairs={{0,8},{8,16},{16,24},{24,0},{1,9},{9,17},{17,25},{25,1},{2,10},{10... | collective-permute-start | bytes 3145736 | tf_op jit(solution)/shard_map/ppermute | solution.py:1487
  370.6 18.2 %collective-permute-start.41 = (bf16[256,768]{1,0:T(8,128)(2,1)}, bf16[256,768]{1,0:T(8,128)(2,1)S(1)}, u32[]{:S(2)}, u32[]{:S(2)}) collective-permute-start(bf16[256,768]{1,0:T(8,128)(2,1)} %get-tuple-element.159), channel_id=1, source_target_pairs={{0,3},{1,2},{2,1},{3,0},{4,7},{5,6},{6,5},{7,4},{8,11},{9,10},{10,... | collective-permute-start | bytes 1179656 | tf_op jit(solution)/shard_map/ppermute | solution.py:1484
  373.5 21.5 %collective-permute-start.43 = (bf16[4,256,128]{2,1,0:T(8,128)(2,1)}, bf16[4,256,128]{2,1,0:T(8,128)(2,1)S(1)}, u32[]{:S(2)}, u32[]{:S(2)}) collective-permute-start(bf16[4,256,128]{2,1,0:T(8,128)(2,1)} %get-tuple-element.163), channel_id=1, source_target_pairs={{0,2},{2,0},{1,3},{3,1},{4,6},{6,4},{5,7},{7,5},{8,10},{10,8},{9,1... | collective-permute-start | bytes 786440 | tf_op jit(solution)/shard_map/ppermute | solution.py:1481
  401.7 29.0 %collective-permute-start.48 = (bf16[2,4,512,128]{3,2,1,0:T(8,128)(2,1)}, bf16[2,4,512,128]{3,2,1,0:T(8,128)(2,1)S(1)}, u32[]{:S(2)}, u32[]{:S(2)}) collective-permute-start(bf16[2,4,512,128]{3,2,1,0:T(8,128)(2,1)} %add_piece.4), channel_id=1, source_target_pairs={{0,8},{8,16},{16,24},{24,0},{1,9},{9,17},{17,25},{25,1},{2,10},{10... | collective-permute-start | bytes 3145736 | tf_op jit(solution)/shard_map/ppermute | solution.py:1487
  401.7 25.6 %collective-permute-start.44 = (bf16[4,256,384]{2,1,0:T(8,128)(2,1)S(1)}, bf16[4,256,384]{2,1,0:T(8,128)(2,1)S(1)}, u32[]{:S(2)}, u32[]{:S(2)}) collective-permute-start(bf16[4,256,384]{2,1,0:T(8,128)(2,1)S(1)} %copy-done.57), channel_id=1, source_target_pairs={{0,4},{4,0},{1,5},{5,1},{2,6},{6,2},{3,7},{7,3},{8,12},{12,8},{9,1... | collective-permute-start | bytes 2359304 | tf_op jit(solution)/shard_map/ppermute | solution.py:1481
  407.3 34.7 %collective-permute-start.42 = (bf16[528,1024]{1,0:T(8,128)(2,1)}, bf16[528,1024]{1,0:T(8,128)(2,1)S(1)}, u32[]{:S(2)}, u32[]{:S(2)}) collective-permute-start(bf16[528,1024]{1,0:T(8,128)(2,1)} %get-tuple-element.161), channel_id=1, source_target_pairs={{0,2},{2,0},{1,3},{3,1},{4,6},{6,4},{5,7},{7,5},{8,10},{10,8},{9,1... | collective-permute-start | bytes 3244040 | tf_op jit(solution)/shard_map/ppermute | solution.py:1481
  434.4 28.1 %collective-permute-start.49 = (bf16[4,512,128]{2,1,0:T(8,128)(2,1)}, bf16[4,512,128]{2,1,0:T(8,128)(2,1)S(1)}, u32[]{:S(2)}, u32[]{:S(2)}) collective-permute-start(bf16[4,512,128]{2,1,0:T(8,128)(2,1)} %get-tuple-element.175), channel_id=1, source_target_pairs={{0,4},{4,0},{1,5},{5,1},{2,6},{6,2},{3,7},{7,3},{8,12},{12,8},{9,1... | collective-permute-start | bytes 1572872 | tf_op jit(solution)/shard_map/ppermute | solution.py:1481
  438.1 20.6 %collective-permute-start.51 = (bf16[256,512]{1,0:T(8,128)(2,1)S(1)}, bf16[256,512]{1,0:T(8,128)(2,1)S(1)}, u32[]{:S(2)}, u32[]{:S(2)}) collective-permute-start(bf16[256,512]{1,0:T(8,128)(2,1)S(1)} %copy-done.62), channel_id=1, source_target_pairs={{0,16},{8,24},{16,0},{24,8},{1,17},{9,25},{17,1},{25,9},{2,18},{10... | collective-permute-start | bytes 786440 | tf_op jit(solution)/shard_map/ppermute | solution.py:1487
  439.8 19.0 %collective-permute-start.52 = (bf16[256,512]{1,0:T(8,128)(2,1)S(1)}, bf16[256,512]{1,0:T(8,128)(2,1)S(1)}, u32[]{:S(2)}, u32[]{:S(2)}) collective-permute-start(bf16[256,512]{1,0:T(8,128)(2,1)S(1)} %copy-done.61), channel_id=1, source_target_pairs={{0,24},{8,0},{16,8},{24,16},{1,25},{9,1},{17,9},{25,17},{2,26},{10... | collective-permute-start | bytes 786440 | tf_op jit(solution)/shard_map/ppermute | solution.py:1487
  (93 other events, 561.2 us)
Sparse Core Ops, SparseCore 0:
  40.5 81.2 all-gather.2
